TPU v7x, 32 devices: a whole 2x2x4 slice. The times are simulated.
32 devices in a mesh: dp: 8 (over z, x), head: 4 (over y, core).
Axes of the slice: x: 2, y: 2, z: 4, core: 2. Of those that a mesh axis runs over, the one named last changes fastest.
Arguments:
- tokens: bfloat16 [16384, 1536], P('dp', 'head'), may hold values from -6 to 6
- cotangent: bfloat16 [16384, 1536], P('dp', 'head'), may hold values from -6 to 6
- order: int32 [8, 2048], P('dp'), may hold values from 0 to 2047, each once within a row
- lengths: int32 [16], P('dp'), may hold values from 128 to 1024, as said below
- norm_gain: bfloat16 [1536], P('dp'), may hold values from 0.5 to 1.5
- w_zx: bfloat16 [1536, 2, 3072], P('dp', None, 'head'), may hold values from -0.15625 to 0.15625
- w_bc: bfloat16 [1536, 256], P('dp'), may hold values from -0.15625 to 0.15625
- w_dt: bfloat16 [1536, 48], P('dp', 'head'), may hold values from -0.15625 to 0.15625
- w_out: bfloat16 [1536, 3072], P('dp', 'head'), may hold values from -0.109375 to 0.109375
- conv_x: float32 [5, 3072], P(None, 'head'), may hold values from -0.5 to 0.5
- conv_bc: float32 [5, 256], replicated, may hold values from -0.5 to 0.5
- head_params: float32 [3, 48], P(None, 'head'), may hold values from -8 to 3
- gate_gain: float32 [3072], P('head'), may hold values from 0.5 to 1.5
Outputs:
- block_output: bfloat16 [16384, 1536], P('dp', 'head')
- input_grad: bfloat16 [16384, 1536], P('dp', 'head')
- norm_gain_grad: float32 [1536], P('dp')
- w_zx_grad: float32 [1536, 2, 3072], P('dp', None, 'head')
- w_bc_grad: float32 [1536, 256], P('dp')
- w_dt_grad: float32 [1536, 48], P('dp', 'head')
- w_out_grad: float32 [1536, 3072], P('dp', 'head')
- conv_x_grad: float32 [5, 3072], P(None, 'head')
- conv_bc_grad: float32 [5, 256], replicated
- head_params_grad: float32 [3, 48], P(None, 'head')
- gate_gain_grad: float32 [3072], P('head')
Inputs may be any that keep to these rules, and one draw needn't show every extreme that they name: Each row of order is a permutation of 0 to 2047. `lengths`: rows of a slot at or past its length are padding.
All inputs are finite; a program needn't handle non-finite values.
Results may differ from a plain program's by a relative error of at most 0.0076.
Values may be sent and summed in bfloat16 or wider, within the bound.
A program may use at most 320 MiB of HBM per device.

v0:
```python
from functools import partial

import jax
import jax.numpy as jnp
from jax import lax
from jax.sharding import PartitionSpec as P

E = 3072
Q = 256
LEN = 1024
MICRO = 2


epsilon = 1e-05
highest = lax.Precision.HIGHEST


def causal_conv(values, taps):
    width = taps.shape[0] - 1
    length = values.shape[0]
    padded = jnp.pad(values, ((width - 1, 0), (0, 0)))
    total = taps[width] + jnp.zeros_like(values)
    for offset in range(width):
        total = total + taps[offset] * padded[offset : offset + length]
    return total


def group_scan(inputs, b_rows, c_rows, steps, rates):
    length, heads, head_dim = inputs.shape
    blocks = length // Q
    x_blocks = inputs.reshape(blocks, Q, heads, head_dim)
    b_blocks = b_rows.reshape(blocks, Q, -1)
    c_blocks = c_rows.reshape(blocks, Q, -1)
    step_blocks = steps.reshape(blocks, Q, heads)
    logs = jnp.cumsum(step_blocks * rates, axis=1)
    causal = (
        lax.broadcasted_iota(jnp.int32, (Q, Q), 0) >= lax.broadcasted_iota(jnp.int32, (Q, Q), 1)
    )[None, :, :, None]
    gaps = logs[:, :, None, :] - logs[:, None, :, :]
    decays = jnp.where(causal, jnp.exp(jnp.where(causal, gaps, 0.0)), 0.0)
    scores = jnp.einsum("bin,bjn->bij", c_blocks, b_blocks, precision=highest)
    kernel = scores[:, :, :, None] * decays * step_blocks[:, None, :, :]
    inner = jnp.einsum("bijh,bjhp->bihp", kernel, x_blocks, precision=highest)
    tails = jnp.exp(logs[:, -1:, :] - logs) * step_blocks
    states = jnp.einsum("bjn,bjh,bjhp->bhpn", b_blocks, tails, x_blocks, precision=highest)

    def advance(state, pair):
        factor, fresh = pair
        return (state * factor[:, None, None] + fresh, state)

    start = jnp.zeros(states.shape[1:], states.dtype)
    closing, entering = lax.scan(advance, start, (jnp.exp(logs[:, -1, :]), states))
    outer = jnp.einsum("bin,bih,bhpn->bihp", c_blocks, jnp.exp(logs), entering, precision=highest)
    return (inner + outer).reshape(length, heads, head_dim)


def mamba_core(u_x, u_bc, u_dt, gate_z, conv_x, conv_bc, head_params):
    length, heads = u_dt.shape
    x_conv = jax.nn.silu(causal_conv(u_x, conv_x))
    bc_conv = jax.nn.silu(causal_conv(u_bc, conv_bc))
    state_dim = bc_conv.shape[1] // 2
    steps = jax.nn.softplus(u_dt + head_params[0])
    rates = -jnp.exp(head_params[1])
    x_heads = x_conv.reshape(length, heads, -1)
    scanned = group_scan(x_heads, bc_conv[:, :state_dim], bc_conv[:, state_dim:], steps, rates)
    scanned = scanned + head_params[2][None, :, None] * x_heads
    return scanned.reshape(length, -1) * jax.nn.silu(gate_z)


def mix_slots(slot_count, u_x, u_bc, u_dt, gate_z, conv_x, conv_bc, head_params):

    def one_slot(part_x, part_bc, part_dt, part_z):
        return mamba_core(part_x, part_bc, part_dt, part_z, conv_x, conv_bc, head_params)

    def by_slot(values):
        return values.reshape((slot_count, -1) + values.shape[1:])

    mixed = jax.vmap(one_slot)(by_slot(u_x), by_slot(u_bc), by_slot(u_dt), by_slot(gate_z))
    return mixed.reshape(u_x.shape)


def fetch_weights(w_zx, w_bc, w_dt, norm_gain, w_out):
    return (
        lax.all_gather(w_zx, "dp", axis=0, tiled=True),
        lax.all_gather(w_bc, "dp", axis=0, tiled=True),
        lax.all_gather(w_dt, "dp", axis=0, tiled=True),
        lax.all_gather(norm_gain, "dp", axis=0, tiled=True),
        lax.all_gather(w_out, "dp", axis=0, tiled=True),
    )


def reduce_grads(parts):
    return lax.psum_scatter(parts, "dp", scatter_dimension=0, tiled=True)


def body(
    tokens,
    cotangent,
    order,
    lengths,
    norm_gain,
    w_zx,
    w_bc,
    w_dt,
    w_out,
    conv_x,
    conv_bc,
    head_params,
    gate_gain,
):
    arrived = (
        lax.all_to_all(tokens, "dp", split_axis=0, concat_axis=0, tiled=True),
        lax.all_to_all(cotangent, "dp", split_axis=0, concat_axis=0, tiled=True),
    )
    arrange = order[0]
    own_x = arrived[0][arrange]
    own_grad = arrived[1][arrange]
    full_x, full_grad = (
        lax.all_gather(own_x, "head", axis=1, tiled=True),
        lax.all_gather(own_grad, "head", axis=1, tiled=True),
    )
    row_count = own_x.shape[0]
    micro_rows = row_count // MICRO
    micro_slots = lengths.shape[0] // MICRO
    quarter = own_x.shape[1]
    place = lax.axis_index("head")
    positions = lax.broadcasted_iota(jnp.int32, (lengths.shape[0], LEN), 1)
    padding = (positions < lengths[:, None]).astype(jnp.float32).reshape(-1)
    saved = []
    outputs = []
    for batch_index in range(MICRO):
        fetched = fetch_weights(w_zx, w_bc, w_dt, norm_gain, w_out)
        proj_zx, proj_bc, proj_dt, gain_one, proj_out = fetched
        start = batch_index * micro_rows
        x_part = full_x[start : start + micro_rows].astype(jnp.float32)
        inv_one = lax.rsqrt(jnp.mean(x_part * x_part, axis=1, keepdims=True) + epsilon)
        normed = (x_part * inv_one * gain_one.astype(jnp.float32)).astype(jnp.bfloat16)
        u_zx = jnp.einsum("rd,dke->rke", normed, proj_zx, preferred_element_type=jnp.float32)
        u_bc = jnp.dot(normed, proj_bc, preferred_element_type=jnp.float32)
        u_dt = jnp.dot(normed, proj_dt, preferred_element_type=jnp.float32)
        mixed, pullback = jax.vjp(
            partial(mix_slots, micro_slots),
            u_zx[:, 1],
            u_bc,
            u_dt,
            u_zx[:, 0],
            conv_x,
            conv_bc,
            head_params,
        )
        row_mask = padding[start : start + micro_rows][:, None]
        squares = lax.psum(jnp.sum(mixed * mixed, axis=1), "head")
        inv_two = lax.rsqrt(squares[:, None] / E + epsilon)
        gated = (mixed * inv_two * gate_gain * row_mask).astype(jnp.bfloat16)
        branch = jnp.einsum("re,de->rd", gated, proj_out, preferred_element_type=jnp.float32)
        shares = lax.psum_scatter(branch, "head", scatter_dimension=1, tiled=True)
        outputs.append(
            (own_x[start : start + micro_rows].astype(jnp.float32) + shares).astype(jnp.bfloat16)
        )
        saved.append((x_part, inv_one, normed, mixed, pullback, inv_two, gated, row_mask))
    backs = []
    for batch_index in range(MICRO):
        fetched = fetch_weights(w_zx, w_bc, w_dt, norm_gain, w_out)
        proj_zx, proj_bc, proj_dt, gain_one, proj_out = fetched
        start = batch_index * micro_rows
        x_part, inv_one, normed, mixed, pullback, inv_two, gated, row_mask = saved[batch_index]
        grad_part = full_grad[start : start + micro_rows]
        grad_out = jnp.einsum("rd,re->de", grad_part, gated, preferred_element_type=jnp.float32)
        grad_gated = jnp.einsum(
            "rd,de->re", grad_part, proj_out, preferred_element_type=jnp.float32
        )
        grad_norm = grad_gated * row_mask
        coefficient = lax.psum(jnp.sum(grad_norm * gate_gain * mixed, axis=1), "head")
        grad_mixed = inv_two * gate_gain * grad_norm - mixed * inv_two**3 * (
            coefficient[:, None] / E
        )
        grad_gain_two = jnp.sum(grad_norm * mixed * inv_two, axis=0)
        grad_ux, grad_ubc, grad_udt, grad_z, grad_convx, grad_convbc, grad_heads = pullback(
            grad_mixed
        )
        grad_ubc, grad_convbc = lax.psum((grad_ubc, grad_convbc), "head")
        round_zx = jnp.stack([grad_z, grad_ux], axis=1).astype(jnp.bfloat16)
        round_bc = grad_ubc.astype(jnp.bfloat16)
        round_dt = grad_udt.astype(jnp.bfloat16)
        grad_wzx = jnp.einsum("rd,rke->dke", normed, round_zx, preferred_element_type=jnp.float32)
        grad_wbc = jnp.einsum("rd,rc->dc", normed, round_bc, preferred_element_type=jnp.float32)
        grad_wdt = jnp.einsum("rd,rc->dc", normed, round_dt, preferred_element_type=jnp.float32)
        head_terms = jnp.einsum(
            "rke,dke->rd", round_zx, proj_zx, preferred_element_type=jnp.float32
        )
        head_terms = head_terms + jnp.einsum(
            "rc,dc->rd", round_dt, proj_dt, preferred_element_type=jnp.float32
        )
        gain_float = gain_one.astype(jnp.float32)
        grad_normed = lax.psum(head_terms, "head")
        grad_normed = grad_normed + jnp.einsum(
            "rc,dc->rd", round_bc, proj_bc, preferred_element_type=jnp.float32
        )
        mean_term = jnp.mean(x_part * gain_float * grad_normed, axis=1, keepdims=True)
        grad_x = inv_one * gain_float * grad_normed - x_part * inv_one**3 * mean_term
        grad_gain_one = jnp.sum(grad_normed * x_part * inv_one, axis=0)
        own_cols = lax.dynamic_slice_in_dim(grad_x, place * quarter, quarter, 1)
        backs.append(
            (own_grad[start : start + micro_rows].astype(jnp.float32) + own_cols).astype(
                jnp.bfloat16
            )
        )
        big_part = (grad_wzx, grad_wbc, grad_wdt, grad_gain_one, grad_out)
        small_part = (grad_convx, grad_convbc, grad_heads, grad_gain_two)
        held = (
            big_part if batch_index == 0 else tuple((old + new for old, new in zip(held, big_part)))
        )
        small_held = (
            small_part
            if batch_index == 0
            else tuple((old + new for old, new in zip(small_held, small_part)))
        )
    held = reduce_grads(held)
    small_total = lax.psum(small_held, "dp")
    out_rows = jnp.concatenate(outputs, axis=0)
    back_rows = jnp.concatenate(backs, axis=0)
    sent_out = jnp.zeros_like(out_rows).at[arrange].set(out_rows)
    sent_back = jnp.zeros_like(back_rows).at[arrange].set(back_rows)
    final_out, final_back = (
        lax.all_to_all(sent_out, "dp", split_axis=0, concat_axis=0, tiled=True),
        lax.all_to_all(sent_back, "dp", split_axis=0, concat_axis=0, tiled=True),
    )
    return (
        final_out,
        final_back,
        held[3],
        held[0],
        held[1],
        held[2],
        held[4],
        small_total[0],
        small_total[1],
        small_total[2],
        small_total[3],
    )


def solution(mesh):
    return jax.shard_map(
        body,
        mesh=mesh,
        in_specs=(
            P("dp", "head"),
            P("dp", "head"),
            P("dp", None),
            P("dp"),
            P("dp"),
            P("dp", None, "head"),
            P("dp", None),
            P("dp", "head"),
            P("dp", "head"),
            P(None, "head"),
            P(),
            P(None, "head"),
            P("head"),
        ),
        out_specs=(
            P("dp", "head"),
            P("dp", "head"),
            P("dp"),
            P("dp", None, "head"),
            P("dp", None),
            P("dp", "head"),
            P("dp", "head"),
            P(None, "head"),
            P(),
            P(None, "head"),
            P("head"),
        ),
        check_vma=False,
    )
```

profile of v0, /device:TPU:0, one launch (start us, length us, event | category | flops | bytes accessed | tf_op | source)
XLA Modules:
  0.0 1538.7 jit_solution(10774276456534877124)
XLA Ops:
  14.6 36.9 %all-to-all-done = bf16[8,256,384]{2,1,0:T(8,128)(2,1)S(1)} async-done(((bf16[8,256,384]{2,1,0:T(8,128)(2,1)}), bf16[8,256,384]{2,1,0:T(8,128)(2,1)S(1)}, u32[]{:S(2)}, u32[]{:S(2)}) %all-to-all-start) | async-done | bytes 1572896 | tf_op jit(solution)/shard_map/all_to_all | solution.py:112
  67.6 40.1 %all-reduce.54 = bf16[1536]{0:T(1024)(128)(2,1)S(1)} all-reduce(bf16[1536]{0:T(1024)(128)(2,1)S(1)} %dynamic-update-slice), channel_id=1, replica_groups=mesh['dp'=8,'head'=4] {'dp'}, use_global_device_ids=true, to_apply=%add.54 | all-reduce | flops 1536 | bytes 6144
  109.0 33.8 %all-gather.2 = bf16[8,192,12]{1,2,0:T(8,128)(2,1)S(1)} all-gather(bf16[1,192,12]{1,2,0:T(8,128)(2,1)S(1)} %bitcast.894), channel_id=1, replica_groups=mesh['dp'=8,'head'=4] {'dp'}, dimensions={0}, use_global_device_ids=true | all-gather | bytes 41472 | tf_op jit(solution)/shard_map/all_gather | solution.py:86
  146.2 36.3 %all_gather.17 = bf16[1536,256]{1,0:T(8,128)(2,1)} all-gather(bf16[192,256]{1,0:T(8,128)(2,1)S(1)} %copy-done.98), channel_id=1, replica_groups=mesh['dp'=8,'head'=4] {'dp'}, dimensions={0}, use_global_device_ids=true | all-gather | bytes 884736 | tf_op jit(solution)/shard_map/all_gather | solution.py:85
  310.0 13.9 while.68
  330.4 14.6 bitcast_add_fusion.9
  386.7 14.6 bitcast_add_fusion.8
  450.1 13.7 fusion.55
  511.5 13.1 while.71
  532.2 12.9 bitcast_add_fusion.6
  545.1 12.7 fusion.113
  606.2 12.0 bitcast_add_fusion.7
  639.3 29.0 %fusion.15 = (f32[4,256,12]{1,2,0:T(8,128)}, f32[4,256,12]{1,2,0:T(8,128)}, f32[4,256,12]{1,2,0:T(8,128)}, f32[4,256,256]{2,1,0:T(8,128)}, f32[4,256,256]{2,1,0:...) fusion(f32[4,256,12]{1,2,0:T(8,128)} %copy.385, ...), kind=kOutput, calls=%fused_computation.49 | convolution fusion | flops 2509692928 | bytes 23625728 | tf_op jit(solution)/shard_map/transpose(jvp(vmap(bijh,bjhp->bihp)))/dot_general | solution.py:43
  706.7 15.3 multiply_reduce_fusion.17
  835.9 65.9 %all-reduce.65 = (bf16[1024,256]{1,0:T(8,128)(2,1)}, bf16[1024,256]{1,0:T(8,128)(2,1)}, f32[5,256]{1,0:T(8,128)S(1)}) all-reduce(f32[1024,256]{1,0:T(8,128)} %fusion.238, f32[1024,256]{1,0:T(8,128)} %fusion.239, f32[5,256]{1,0:T(8,128)S(1)} %add_add_fusion.1), channel_id=1, replica_groups=mesh['dp'=8,'head'=4] {'head'}, use_global_device_ids=true, to_apply=%region_45.47 | all-reduce | flops 525568 | bytes 3155968 | tf_op jit(solution)/shard_map/psum | solution.py:181
  929.9 67.1 %all-reduce.64.cloned.1.call-done = (f32[1024,1536]{1,0:T(8,128)}, f32[1024,1536]{1,0:T(8,128)}) async-done(((f32[1024,1536]{1,0:T(8,128)}, f32[1024,1536]{1,0:T(8,128)}), (f32[1024,1536]{1,0:T(8,128)}, f32[1024,1536]{1,0:T(8,128)})) %all-reduce.64.cloned.1.call-update) | async-done | bytes 12582928 | tf_op jit(solution)/shard_map/psum | solution.py:195
  1011.3 12.5 scatter_custom_fusion.1
  1028.8 28.0 %reduce-scatter.11.cloned.1.call-done = f32[1024,384]{1,0:T(8,128)} async-done(((f32[1024,1536]{1,0:T(8,128)}), f32[1024,384]{1,0:T(8,128)}) %reduce-scatter.11.cloned.1.call-update) | async-done | bytes 1572880 | tf_op jit(solution)/shard_map/reduce_scatter | solution.py:156
  1056.8 61.1 %reduce-scatter.9.cloned.1.call-done = f32[1024,384]{1,0:T(8,128)} async-done(((f32[1024,1536]{1,0:T(8,128)}), f32[1024,384]{1,0:T(8,128)}) %reduce-scatter.9.cloned.1.call-update) | async-done | bytes 1572880 | tf_op jit(solution)/shard_map/reduce_scatter | solution.py:156
  1140.2 56.4 %reduce-scatter.19.cloned.1.call-done = f32[192,12]{1,0:T(8,128)} async-done(((f32[1536,12]{1,0:T(8,128)}), f32[192,12]{1,0:T(8,128)}) %reduce-scatter.19.cloned.1.call-update) | async-done | bytes 9232
  1198.2 38.1 %all-reduce.56 = (f32[1536]{0:T(1024)S(1)}, f32[5,768]{1,0:T(8,128)}, f32[5,256]{1,0:T(8,128)}, f32[3,12]{1,0:T(4,128)}, f32[768]{0:T(1024)}) all-reduce(f32[1536]{0:T(1024)S(1)} %add.499, f32[5,768]{1,0:T(8,128)S(1)} %add_add_fusion, f32[5,256]{1,0:T(8,128)S(1)} %get-tuple-element.776, ...), channel_id=6, replica_groups=mesh['dp'=8,'head'=4] {'dp'}, use_global_device_ids=true, to_apply=%region_50.52.clone | all-reduce | flops 7460 | bytes 59680
  1236.9 126.2 %reduce-scatter.13.cloned.1.call-done = f32[192,2,768]{2,0,1:T(8,128)} async-done(((f32[1536,2,768]{2,0,1:T(8,128)}), f32[192,2,768]{2,0,1:T(8,128)}) %reduce-scatter.13.cloned.1.call-update) | async-done | bytes 1179664 | tf_op jit(solution)/shard_map/reduce_scatter | solution.py:93
  1366.3 65.0 %reduce-scatter.15.cloned.1.call-done = f32[192,256]{1,0:T(8,128)} async-done(((f32[1536,256]{1,0:T(8,128)}), f32[192,256]{1,0:T(8,128)}) %reduce-scatter.15.cloned.1.call-update) | async-done | bytes 196624 | tf_op jit(solution)/shard_map/reduce_scatter | solution.py:93
  1431.3 98.4 %reduce-scatter.17.cloned.1.call-done = f32[192,768]{1,0:T(8,128)} async-done(((f32[1536,768]{1,0:T(8,128)}), f32[192,768]{1,0:T(8,128)}) %reduce-scatter.17.cloned.1.call-update) | async-done | bytes 589840 | tf_op jit(solution)/shard_map/reduce_scatter | solution.py:93
  (711 shorter events, 649.1 us)
Async XLA Ops:
  7.2 44.3 %all-to-all-start = ((bf16[8,256,384]{2,1,0:T(8,128)(2,1)}), bf16[8,256,384]{2,1,0:T(8,128)(2,1)S(1)}, u32[]{:S(2)}, u32[]{:S(2)}) async-start(bf16[8,256,384]{2,1,0:T(8,128)(2,1)} %bitcast.862), calls=%async_computation | async-start | bytes 3145728 | tf_op jit(solution)/shard_map/all_to_all | solution.py:112
  14.5 177.2 %all-gather.12.cloned.1.call-start = ((), (), s32[]{:S(2)}) async-start(), calls=%async_computation.17 | async-start | bytes 7864320 | tf_op jit(solution)/shard_map/all_gather | solution.py:119
  60.6 85.6 %copy-start.98 = (bf16[192,256]{1,0:T(8,128)(2,1)S(1)}, bf16[192,256]{1,0:T(8,128)(2,1)}, u32[]{:S(2)}) copy-start(bf16[192,256]{1,0:T(8,128)(2,1)} %param.28) | copy-start | bytes 294916
  60.6 209.6 %all-gather.8.cloned.1.call-start = ((), (), s32[]{:S(2)}) async-start(), calls=%async_computation.10 | async-start | bytes 5308416 | tf_op jit(solution)/shard_map/all_gather | solution.py:84
  61.6 367.9 %all-gather.10.cloned.1.call-start = ((), (), s32[]{:S(2)}) async-start(), calls=%async_computation.11 | async-start | bytes 2654208 | tf_op jit(solution)/shard_map/all_gather | solution.py:88
  62.3 120.2 %all-to-all-start.2 = ((bf16[8,256,384]{2,1,0:T(8,128)(2,1)}), bf16[8,256,384]{2,1,0:T(8,128)(2,1)S(1)}, u32[]{:S(2)}, u32[]{:S(2)}) async-start(bf16[8,256,384]{2,1,0:T(8,128)(2,1)} %bitcast.80), calls=%async_computation.4 | async-start | bytes 3145728 | tf_op jit(solution)/shard_map/all_to_all | solution.py:113
  66.0 363.5 %all-gather.14.cloned.1.call-start = ((), (), s32[]{:S(2)}) async-start(), calls=%async_computation.18 | async-start | bytes 7864320 | tf_op jit(solution)/shard_map/all_gather | solution.py:120
  109.0 469.0 %copy-start.97 = (f32[768]{0:T(1024)}, f32[768]{0:T(1024)S(1)}, u32[]{:S(2)}) copy-start(f32[768]{0:T(1024)S(1)} %mul.1169) | copy-start | bytes 9220
  144.9 145.8 %copy-start.116 = (f32[768]{0:T(1024)}, f32[768]{0:T(1024)S(1)}, u32[]{:S(2)}) copy-start(f32[768]{0:T(1024)S(1)} %get-tuple-element.713) | copy-start | bytes 9220
  144.9 145.8 %copy-start.118 = (f32[768]{0:T(1024)}, f32[768]{0:T(1024)S(1)}, u32[]{:S(2)}) copy-start(f32[768]{0:T(1024)S(1)} %get-tuple-element.714) | copy-start | bytes 9220
  144.9 145.8 %copy-start.120 = (f32[768]{0:T(1024)}, f32[768]{0:T(1024)S(1)}, u32[]{:S(2)}) copy-start(f32[768]{0:T(1024)S(1)} %get-tuple-element.715) | copy-start | bytes 9220
  191.6 805.3 %all-reduce.64.cloned.1.call-start = ((), (), s32[]{:S(2)}) async-start(), calls=%async_computation.20 | async-start | bytes 25165824 | tf_op jit(solution)/shard_map/psum | solution.py:195
  361.1 184.0 %copy-start = (f32[4,256,12,64]{1,0,3,2:T(4,128)}, f32[4,256,12,64]{1,0,3,2:T(4,128)S(1)}, u32[]{:S(2)}) copy-start(f32[4,256,12,64]{1,0,3,2:T(4,128)S(1)} %reshape.1356) | copy-start | bytes 9437188
  429.4 140.5 %copy-start.130 = (f32[1024]{0:T(1024)}, f32[1024]{0:T(1024)S(1)}, u32[]{:S(2)}) copy-start(f32[1024]{0:T(1024)S(1)} %get-tuple-element.881) | copy-start | bytes 12292
  429.4 148.6 %copy-start.132 = (f32[1024]{0:T(1024)}, f32[1024]{0:T(1024)S(1)}, u32[]{:S(2)}) copy-start(f32[1024]{0:T(1024)S(1)} %get-tuple-element.879) | copy-start | bytes 12292
  753.1 303.7 %reduce-scatter.11.cloned.1.call-start = ((), (), s32[]{:S(2)}) async-start(), calls=%async_computation.13 | async-start | bytes 7864320 | tf_op jit(solution)/shard_map/reduce_scatter | solution.py:156
  761.6 356.3 %reduce-scatter.9.cloned.1.call-start = ((), (), s32[]{:S(2)}) async-start(), calls=%async_computation.12 | async-start | bytes 7864320 | tf_op jit(solution)/shard_map/reduce_scatter | solution.py:156
  770.0 426.5 %reduce-scatter.19.cloned.1.call-start = ((), (), s32[]{:S(2)}) async-start(), calls=%async_computation.19 | async-start | bytes 884736
  784.6 578.5 %reduce-scatter.13.cloned.1.call-start = ((), (), s32[]{:S(2)}) async-start(), calls=%async_computation.14 | async-start | bytes 10616832 | tf_op jit(solution)/shard_map/reduce_scatter | solution.py:93
  795.7 635.6 %reduce-scatter.15.cloned.1.call-start = ((), (), s32[]{:S(2)}) async-start(), calls=%async_computation.15 | async-start | bytes 1769472 | tf_op jit(solution)/shard_map/reduce_scatter | solution.py:93
  906.3 623.4 %reduce-scatter.17.cloned.1.call-start = ((), (), s32[]{:S(2)}) async-start(), calls=%async_computation.16 | async-start | bytes 5308416 | tf_op jit(solution)/shard_map/reduce_scatter | solution.py:93
  1011.3 106.5 %copy-start.34 = (bf16[2048,384]{1,0:T(8,128)(2,1)S(1)}, bf16[2048,384]{1,0:T(8,128)(2,1)}, u32[]{:S(2)}) copy-start(bf16[2048,384]{1,0:T(8,128)(2,1)} %gather_fusion) | copy-start | bytes 4718596
  1023.9 108.9 %all-to-all-start.3 = ((bf16[8,256,384]{2,1,0:T(8,128)(2,1)}), bf16[8,256,384]{2,1,0:T(8,128)(2,1)S(1)}, u32[]{:S(2)}, u32[]{:S(2)}) async-start(bf16[8,256,384]{2,1,0:T(8,128)(2,1)} %bitcast.855), calls=%async_computation.5 | async-start | bytes 3145728 | tf_op jit(solution)/shard_map/all_to_all | solution.py:226
  1132.8 104.1 %all-to-all-start.1 = ((bf16[8,256,384]{2,1,0:T(8,128)(2,1)}), bf16[8,256,384]{2,1,0:T(8,128)(2,1)S(1)}, u32[]{:S(2)}, u32[]{:S(2)}) async-start(bf16[8,256,384]{2,1,0:T(8,128)(2,1)} %bitcast.854), calls=%async_computation.3 | async-start | bytes 3145728 | tf_op jit(solution)/shard_map/all_to_all | solution.py:225
  (176 other events, 1932.8 us)
Sparse Core Ops, SparseCore 0:
  60.7 45.3 all-gather.11
  108.9 92.2 all-gather.7
  203.3 51.4 all-gather.9
  256.2 44.8 all-gather.13
  753.2 243.6 all-reduce.63
  999.3 57.3 reduce-scatter.10
  1059.5 58.3 reduce-scatter.8
  1121.2 75.3 reduce-scatter.18
  1200.6 162.4 reduce-scatter.12
  1367.3 63.9 reduce-scatter.14
  1435.5 94.1 reduce-scatter.16
where the time goes:
time: 1550 us; the launch traced here: 1540 us
  waiting for transfers between devices  540 us (35%)
  matrix products  285 us (18%)
  other arithmetic  234 us (15%)
  blocking collectives  227 us (15%)
  local copies, waits for them, and re-layouts  212 us (14%)
  starting transfers between devices  22 us (1%)
  between operations  17.7 us (1%)
    reduce_scatter x3, waiting for transfers between devices, reduce_grads(): return lax.psum_scatter(parts, 'dp', scatter_dimension=0, tiled=True)  290 us
    dot_general x6, matrix products, group_scan(): inner = jnp.einsum('bijh,bjhp->bihp', kernel, x_blocks, precision=highest)  95.9 us
    reduce_scatter x2, waiting for transfers between devices, body(): shares = lax.psum_scatter(branch, 'head', scatter_dimension=1, tiled=True)  89 us
    unnamed x2, blocking collectives  78.2 us
    psum x1, waiting for transfers between devices, body(): grad_normed = lax.psum(head_terms, 'head')  67.1 us
    psum x1, blocking collectives, body(): grad_ubc, grad_convbc = lax.psum((grad_ubc, grad_convbc), 'head')  65.9 us
    unnamed x12, waiting for transfers between devices  57.2 us
    another operation x42, local copies, waits for them, and re-layouts  53.3 us
  transfers between devices with their start and end apart: 15, of which 8 were waited for; matrix products, arithmetic and copies ran while one was open for 25% of the time, Pallas kernels for 0%

commit v1 on v0

v1 whole, which is shorter than its diff:
```python
import functools

import jax
import jax.numpy as jnp
from jax import lax
from jax.experimental import pallas as pl
from jax.experimental.pallas import tpu as pltpu
from jax.sharding import PartitionSpec as P

LEN = 1024
T = 128
N = 128
HEAD = 64
EPS = 1e-05
NEG = -1e30
F32 = jnp.float32
BF16 = jnp.bfloat16


def dot(a, b):
    return lax.dot_general(a, b, (((1,), (0,)), ((), ())), preferred_element_type=F32)


def dot_nt(a, b):
    return lax.dot_general(a, b, (((1,), (1,)), ((), ())), preferred_element_type=F32)


def dot_exact(a, b):
    return lax.dot_general(
        a, b, (((1,), (0,)), ((), ())), preferred_element_type=F32, precision=lax.Precision.HIGHEST
    )


def iotas(rows, cols):
    return (
        lax.broadcasted_iota(jnp.int32, (rows, cols), 0),
        lax.broadcasted_iota(jnp.int32, (rows, cols), 1),
    )


def sigmoid(v):
    return 1.0 / (1.0 + jnp.exp(-v))


def softplus(v):
    return jnp.maximum(v, 0.0) + jnp.log1p(jnp.exp(-jnp.abs(v)))


def to_col(row):
    return jnp.broadcast_to(row, (T, T)).T


def to_row(col):
    return jnp.broadcast_to(col, (T, T)).T[0:1]


def lanes(value, pick):
    return jnp.broadcast_to(value[:, pick : pick + 1], (value.shape[0], 128))


def step_terms(ubd, head_ref, heads):
    row, col = iotas(T, T)
    raw = jnp.where(col < heads, ubd[:, 2 * N :] + head_ref[0:1], 0.0)
    steps = jnp.where(col < heads, softplus(raw), 0.0)
    rates = -jnp.exp(head_ref[1:2])
    tril = (row >= col).astype(F32)
    logs = dot_exact(tril, steps * rates)
    return raw, steps, rates, logs


def forward_kernel(heads, x_ref, z_ref, ubd_ref, par_ref, pbc_ref, head_ref, y_ref, ss_ref, c_ref, cb_ref, st_ref, ext_x, ext_b, state):
    @pl.when(pl.program_id(1) == 0)
    def _():
        ext_x[0:8] = jnp.zeros_like(ext_x[0:8])
        ext_b[0:8] = jnp.zeros_like(ext_b[0:8])
        state[...] = jnp.zeros_like(state)

    def conv(ext, values, taps):
        ext[8 : 8 + T] = values
        total = taps[4:5] + taps[3:4] * values
        for k in range(3):
            total = total + taps[k : k + 1] * ext[5 + k : 5 + k + T]
        ext[0:8] = ext[T : T + 8]
        return total

    row, col = iotas(T, T)
    low = col < HEAD
    low_row = lax.broadcasted_iota(jnp.int32, (1, 128), 1) < HEAD
    causal = row >= col
    ubd = ubd_ref[...]
    c = conv(ext_x, x_ref[...].astype(F32), par_ref)
    c_ref[...] = c.astype(BF16)
    cb = conv(ext_b, ubd[:, : 2 * N], pbc_ref)
    cb_ref[...] = cb
    bc = cb * sigmoid(cb)
    b_rows = bc[:, :N]
    b_t = b_rows.T.astype(BF16)
    b_low, c_low = b_rows.astype(BF16), bc[:, N:].astype(BF16)
    _, steps, _, logs = step_terms(ubd, head_ref, heads)
    logs_t = logs.T
    scores = dot_nt(c_low, b_low)
    entering = state[...].astype(BF16)
    st_ref[0] = entering
    outer = dot(c_low, entering)
    squares = jnp.zeros((T, 128), F32)
    for pair in range(heads // 2):
        span = slice(128 * pair, 128 * pair + 128)
        h0, h1 = 2 * pair, 2 * pair + 1
        log0, log1 = lanes(logs, h0), lanes(logs, h1)
        log_pair = jnp.where(low, log0, log1)
        step_pair = jnp.where(low, lanes(steps, h0), lanes(steps, h1))
        last_pair = log_pair[T - 1 : T]
        cp = c[:, span]
        xp = cp * sigmoid(cp)
        xd = xp * step_pair
        m0 = (scores * jnp.exp(jnp.where(causal, log0 - logs_t[h0 : h0 + 1], NEG))).astype(BF16)
        m1 = (scores * jnp.exp(jnp.where(causal, log1 - logs_t[h1 : h1 + 1], NEG))).astype(BF16)
        stacked = jnp.concatenate([jnp.where(low, xd, 0.0).astype(BF16), jnp.where(low, 0.0, xd).astype(BF16)], axis=0)
        y = dot(jnp.concatenate([m0, m1], axis=1), stacked)
        y = y + jnp.exp(log_pair) * outer[:, span] + par_ref[5:6, span] * xp
        tail = (jnp.exp(last_pair - log_pair) * xd).astype(BF16)
        state[:, span] = jnp.exp(last_pair) * state[:, span] + dot(b_t, tail)
        y_ref[:, span] = y.astype(BF16)
        zp = z_ref[:, span].astype(F32)
        w = y * zp * sigmoid(zp)
        squares = squares + w * w
    ss_ref[0] = to_row(jnp.sum(squares, axis=1, keepdims=True))


def gate_kernel(g_ref, wo_ref, y_ref, z_ref, par_ref, mask_ref, dyn_ref, co_ref):
    dyn = dot(g_ref[...], wo_ref[...])
    for part in range(dyn.shape[0] // T):
        rows = slice(part * T, part * T + T)
        mask = to_col(mask_ref[part])[:, 0:1]
        own = dyn[rows] * mask
        dyn_ref[rows] = own.astype(BF16)
        z = z_ref[rows].astype(F32)
        w = y_ref[rows].astype(F32) * z * sigmoid(z)
        co_ref[part] = to_row(jnp.sum(own * w * par_ref[6:7], axis=1, keepdims=True))


def mid_kernel(width, y_ref, z_ref, dyn_ref, par_ref, mask_ref, ss_ref, co_ref, yg_ref, dz_ref, dy_ref, gg_ref, rd_ref):
    @pl.when(pl.program_id(0) == 0)
    def _():
        gg_ref[...] = jnp.zeros_like(gg_ref)

    gain = par_ref[6:7]
    for part in range(y_ref.shape[0] // T):
        rows = slice(part * T, part * T + T)
        mask = to_col(mask_ref[part])[:, 0:1]
        inv_row = lax.rsqrt(ss_ref[part] / width + EPS)
        inv = to_col(inv_row)[:, 0:1]
        cube = to_col(inv_row * inv_row * inv_row * (co_ref[part] / width))[:, 0:1]
        y = y_ref[rows].astype(F32)
        z = z_ref[rows].astype(F32)
        dyn = dyn_ref[rows].astype(F32)
        s = sigmoid(z)
        act = z * s
        w = y * act
        wi = w * inv
        yg_ref[rows] = (wi * gain * mask).astype(BF16)
        gg_ref[0:1] += jnp.sum(dyn * wi, axis=0, keepdims=True)
        dw = inv * gain * dyn - w * cube
        dy_ref[rows] = (dw * act).astype(BF16)
        dz = dw * y * (s * (1.0 + z * (1.0 - s)))
        dz_ref[rows] = dz.astype(BF16)
        rd_ref[part] = to_row(jnp.sum(dz * z, axis=1, keepdims=True))


def backward_kernel(heads, dy_ref, x_ref, c_ref, cb_ref, ubd_ref, st_ref, par_ref, pbc_ref, head_ref, dx_ref, dbd_ref, gx_ref, gb_ref, gh_ref, rd_ref, d_state, ext_x, ext_b, rows_ref, prod, edy_ref, tail_ref):
    first = (pl.program_id(0) == 0) & (pl.program_id(1) == 0)

    @pl.when(first)
    def _():
        gx_ref[...] = jnp.zeros_like(gx_ref)
        gb_ref[...] = jnp.zeros_like(gb_ref)
        gh_ref[...] = jnp.zeros_like(gh_ref)
        rows_ref[...] = jnp.zeros_like(rows_ref)

    @pl.when(pl.program_id(1) == 0)
    def _():
        ext_x[T : T + 8] = jnp.zeros_like(ext_x[T : T + 8])
        ext_b[T : T + 8] = jnp.zeros_like(ext_b[T : T + 8])
        d_state[...] = jnp.zeros_like(d_state)

    row, col = iotas(T, T)
    low = col < HEAD
    upto = col >= row
    below = row < col
    reach = (row >= col).astype(BF16)
    ubd = ubd_ref[...]
    raw, steps, rates, logs = step_terms(ubd, head_ref, heads)
    logs_t = logs.T
    cb = cb_ref[...]
    sb = sigmoid(cb)
    bc = cb * sb
    b_low, c_low = bc[:, :N].astype(BF16), bc[:, N:].astype(BF16)
    c_t = bc[:, N:].T.astype(BF16)
    scores = dot_nt(b_low, c_low)
    entering = st_ref[0]
    outer = dot(c_low, entering)
    ds_low = d_state[...].astype(BF16)
    back = dot(b_low, ds_low)
    d_scores = jnp.zeros((T, T), F32)
    skip_parts, closing_parts = [], []
    for pair in range(heads // 2):
        span = slice(128 * pair, 128 * pair + 128)
        h0, h1 = 2 * pair, 2 * pair + 1
        log0, log1 = lanes(logs, h0), lanes(logs, h1)
        log_pair = jnp.where(low, log0, log1)
        step_pair = jnp.where(low, lanes(steps, h0), lanes(steps, h1))
        last_pair = log_pair[T - 1 : T]
        cp = c_ref[:, span].astype(F32)
        sp = sigmoid(cp)
        xp = cp * sp
        xd = xp * step_pair
        dy_low = dy_ref[:, span]
        dy = dy_low.astype(F32)
        decay0 = jnp.exp(jnp.where(upto, logs_t[h0 : h0 + 1] - log0, NEG))
        decay1 = jnp.exp(jnp.where(upto, logs_t[h1 : h1 + 1] - log1, NEG))
        m0, m1 = scores * decay0, scores * decay1
        zero = jnp.zeros_like(dy_low)
        x_stack = jnp.concatenate([jnp.where(low, xd, 0.0).astype(BF16), jnp.where(low, 0.0, xd).astype(BF16)], axis=0)
        dm = dot_nt(x_stack, dy_low)
        dm0, dm1 = dm[:T], dm[T:]
        d_scores = d_scores + dm0 * decay0 + dm1 * decay1
        dy_stack = jnp.concatenate([jnp.where(low, dy, 0.0).astype(BF16), jnp.where(low, 0.0, dy).astype(BF16)], axis=0)
        dxd = dot(jnp.concatenate([m0.astype(BF16), m1.astype(BF16)], axis=1), dy_stack)
        flow = jnp.concatenate([(dm0 * m0).astype(BF16), (dm1 * m1).astype(BF16)], axis=0)
        later = dot(flow, reach)
        rows_ref[h0 : h0 + 1] = jnp.sum(jnp.where(below, later[:T], 0.0), axis=0, keepdims=True)
        rows_ref[h1 : h1 + 1] = jnp.sum(jnp.where(below, later[T:], 0.0), axis=0, keepdims=True)
        grow = jnp.exp(log_pair)
        tail = jnp.exp(last_pair - log_pair)
        from_state = tail * back[:, span]
        dxd = dxd + from_state
        edy = grow * dy
        prod[0:T, span] = (edy * outer[:, span]).astype(BF16)
        prod[T : 2 * T, span] = (from_state * xd).astype(BF16)
        prod[2 * T : 3 * T, span] = (xp * dxd).astype(BF16)
        skip_parts.append(jnp.sum(xp * dy, axis=0, keepdims=True))
        edy_low = edy.astype(BF16)
        edy_ref[:, span] = edy_low
        tail_ref[:, span] = (tail * xd).astype(BF16)
        old = d_state[:, span]
        closing = jnp.exp(last_pair)
        closing_parts.append(closing * jnp.sum(old * entering[:, span].astype(F32), axis=0, keepdims=True))
        d_state[:, span] = closing * old + dot(c_t, edy_low)
        dx = dxd * step_pair + par_ref[5:6, span] * dy
        ext_x[0:T, span] = dx * (sp * (1.0 + cp * (1.0 - sp)))
    d_low = d_scores.astype(BF16)
    d_b = dot_nt(tail_ref[...], ds_low) + dot(d_low, c_low)
    d_c = dot_nt(edy_ref[...], entering) + dot(d_scores.T.astype(BF16), b_low)
    width = heads * HEAD
    lane_row, lane_col = iotas(width, 128)
    member = (lane_row // HEAD == lane_col).astype(BF16)
    sums = dot(prod[...], member)
    skip_all = jnp.concatenate(skip_parts, axis=1)
    closing_all = jnp.concatenate(closing_parts, axis=1)
    fill = jnp.zeros((6, width), F32)
    few = dot_exact(jnp.concatenate([skip_all, closing_all, fill], axis=0), member.astype(F32))
    d_logs = dot(upto.astype(BF16), sums[:T].astype(BF16)) + dot((col < row).astype(BF16), sums[T : 2 * T].astype(BF16))
    d_logs = d_logs + rows_ref[...].T + few[1:2]
    d_steps = sums[2 * T :] + rates * d_logs
    d_raw = jnp.where(col < heads, d_steps * sigmoid(raw), 0.0)
    gh_ref[0:1] += jnp.sum(d_raw, axis=0, keepdims=True)
    gh_ref[1:2] += rates * jnp.sum(steps * d_logs, axis=0, keepdims=True)
    gh_ref[2:3] += few[0:1]
    ext_b[0:T, 0:N] = d_b * (sb[:, :N] * (1.0 + cb[:, :N] * (1.0 - sb[:, :N])))
    ext_b[0:T, N:] = d_c * (sb[:, N:] * (1.0 + cb[:, N:] * (1.0 - sb[:, N:])))

    def conv_back(ext, values, taps, grads):
        now = ext[0:T]
        total = taps[3:4] * now
        grads[3:4] += jnp.sum(values * now, axis=0, keepdims=True)
        grads[4:5] += jnp.sum(now, axis=0, keepdims=True)
        for k in range(3):
            moved = ext[3 - k : 3 - k + T]
            total = total + taps[k : k + 1] * moved
            grads[k : k + 1] += jnp.sum(values * moved, axis=0, keepdims=True)
        ext[T : T + 8] = ext[0:8]
        return total

    ux = x_ref[...].astype(F32)
    dux = conv_back(ext_x, ux, par_ref, gx_ref)
    dx_ref[...] = dux.astype(BF16)
    ubc = ubd[:, : 2 * N]
    dubc = conv_back(ext_b, ubc, pbc_ref, gb_ref)
    dbd_ref[:, : 2 * N] = dubc.astype(BF16)
    dbd_ref[:, 2 * N :] = d_raw.astype(BF16)
    total = jnp.sum(dux * ux, axis=1, keepdims=True) + jnp.sum(dubc * ubc, axis=1, keepdims=True)
    total = total + jnp.sum(jnp.where(col < heads, d_raw * ubd[:, 2 * N :], 0.0), axis=1, keepdims=True)
    rd_ref[0] = to_row(total)


def params(*semantics):
    return pltpu.CompilerParams(dimension_semantics=semantics, vmem_limit_bytes=56 * 1024 * 1024)


def run_forward(heads, u_zx, u_bd, par, pbc, hp):
    rows, width = u_zx.shape[0], heads * HEAD
    slots, chunks = rows // LEN, LEN // T
    at = lambda s, i: (s * chunks + i, 0)
    fixed = lambda s, i: (0, 0)
    return pl.pallas_call(
        functools.partial(forward_kernel, heads),
        grid=(slots, chunks),
        in_specs=[
            pl.BlockSpec((T, width), lambda s, i: (s * chunks + i, 1)),
            pl.BlockSpec((T, width), at),
            pl.BlockSpec((T, 3 * N), at),
            pl.BlockSpec((8, width), fixed),
            pl.BlockSpec((8, 2 * N), fixed),
            pl.BlockSpec((8, 128), fixed),
        ],
        out_specs=[
            pl.BlockSpec((T, width), at),
            pl.BlockSpec((1, 1, T), lambda s, i: (s * chunks + i, 0, 0)),
            pl.BlockSpec((T, width), at),
            pl.BlockSpec((T, 2 * N), at),
            pl.BlockSpec((1, N, width), lambda s, i: (s * chunks + i, 0, 0)),
        ],
        out_shape=[
            jax.ShapeDtypeStruct((rows, width), BF16),
            jax.ShapeDtypeStruct((rows // T, 1, T), F32),
            jax.ShapeDtypeStruct((rows, width), BF16),
            jax.ShapeDtypeStruct((rows, 2 * N), F32),
            jax.ShapeDtypeStruct((rows // T, N, width), BF16),
        ],
        scratch_shapes=[pltpu.VMEM((T + 8, width), F32), pltpu.VMEM((T + 8, 2 * N), F32), pltpu.VMEM((N, width), F32)],
        compiler_params=params("arbitrary", "arbitrary"),
        cost_estimate=pl.CostEstimate(flops=rows * width * 2 * 1200, bytes_accessed=rows * width * 8, transcendentals=rows * width * 6),
        name="scan_forward",
    )(u_zx, u_zx, u_bd, par, pbc, hp)


def run_gate(full_grad, w_out, y, u_zx, par, mask):
    rows, width = y.shape
    deep = full_grad.shape[1]
    step = 256
    at = lambda i: (i, 0)
    fixed = lambda i: (0, 0)
    thin = pl.BlockSpec((step // T, 1, T), lambda i: (i, 0, 0))
    return pl.pallas_call(
        gate_kernel,
        grid=(rows // step,),
        in_specs=[
            pl.BlockSpec((step, deep), at),
            pl.BlockSpec((deep, width), fixed),
            pl.BlockSpec((step, width), at),
            pl.BlockSpec((step, width), at),
            pl.BlockSpec((8, width), fixed),
            thin,
        ],
        out_specs=[pl.BlockSpec((step, width), at), thin],
        out_shape=[jax.ShapeDtypeStruct((rows, width), BF16), jax.ShapeDtypeStruct((rows // T, 1, T), F32)],
        compiler_params=params("arbitrary"),
        cost_estimate=pl.CostEstimate(flops=rows * width * deep * 2, bytes_accessed=rows * (width * 6 + deep * 2), transcendentals=rows * width),
        name="gate_back",
    )(full_grad, w_out, y, u_zx, par, mask)


def run_mid(all_width, y, u_zx, dyn, par, mask, ss, co):
    rows, width = y.shape
    step = 256
    at = lambda i: (i, 0)
    fixed = lambda i: (0, 0)
    thin = pl.BlockSpec((step // T, 1, T), lambda i: (i, 0, 0))
    wide = pl.BlockSpec((step, width), at)
    return pl.pallas_call(
        functools.partial(mid_kernel, float(all_width)),
        grid=(rows // step,),
        in_specs=[wide, wide, wide, pl.BlockSpec((8, width), fixed), thin, thin, thin],
        out_specs=[wide, wide, wide, pl.BlockSpec((8, width), fixed), thin],
        out_shape=[jax.ShapeDtypeStruct((rows, width), BF16)] * 3
        + [jax.ShapeDtypeStruct((8, width), F32), jax.ShapeDtypeStruct((rows // T, 1, T), F32)],
        compiler_params=params("arbitrary"),
        cost_estimate=pl.CostEstimate(flops=rows * width * 30, bytes_accessed=rows * width * 12, transcendentals=rows * width),
        name="gate_mid",
    )(y, u_zx, dyn, par, mask, ss, co)


def run_backward(heads, dy, u_zx, c, cb, u_bd, st, par, pbc, hp):
    rows, width = dy.shape
    slots, chunks = rows // LEN, LEN // T
    place = lambda s, i: s * chunks + chunks - 1 - i
    at = lambda s, i: (place(s, i), 0)
    at3 = lambda s, i: (place(s, i), 0, 0)
    fixed = lambda s, i: (0, 0)
    return pl.pallas_call(
        functools.partial(backward_kernel, heads),
        grid=(slots, chunks),
        in_specs=[
            pl.BlockSpec((T, width), at),
            pl.BlockSpec((T, width), lambda s, i: (place(s, i), 1)),
            pl.BlockSpec((T, width), at),
            pl.BlockSpec((T, 2 * N), at),
            pl.BlockSpec((T, 3 * N), at),
            pl.BlockSpec((1, N, width), at3),
            pl.BlockSpec((8, width), fixed),
            pl.BlockSpec((8, 2 * N), fixed),
            pl.BlockSpec((8, 128), fixed),
        ],
        out_specs=[
            pl.BlockSpec((T, width), at),
            pl.BlockSpec((T, 3 * N), at),
            pl.BlockSpec((8, width), fixed),
            pl.BlockSpec((8, 2 * N), fixed),
            pl.BlockSpec((8, 128), fixed),
            pl.BlockSpec((1, 1, T), at3),
        ],
        out_shape=[
            jax.ShapeDtypeStruct((rows, width), BF16),
            jax.ShapeDtypeStruct((rows, 3 * N), BF16),
            jax.ShapeDtypeStruct((8, width), F32),
            jax.ShapeDtypeStruct((8, 2 * N), F32),
            jax.ShapeDtypeStruct((8, 128), F32),
            jax.ShapeDtypeStruct((rows // T, 1, T), F32),
        ],
        scratch_shapes=[
            pltpu.VMEM((N, width), F32),
            pltpu.VMEM((T + 8, width), F32),
            pltpu.VMEM((T + 8, 2 * N), F32),
            pltpu.VMEM((128, 128), F32),
            pltpu.VMEM((3 * T, width), BF16),
            pltpu.VMEM((T, width), BF16),
            pltpu.VMEM((T, width), BF16),
        ],
        compiler_params=params("arbitrary", "arbitrary"),
        cost_estimate=pl.CostEstimate(flops=rows * width * 2 * 3000, bytes_accessed=rows * width * 12, transcendentals=rows * width * 8),
        name="scan_backward",
    )(dy, u_zx, c, cb, u_bd, st, par, pbc, hp)


def mm(a, b, contract, kind):
    return lax.dot_general(a, b, (contract, ((), ())), preferred_element_type=F32).astype(kind)


def body(tokens, cotangent, order, lengths, norm_gain, w_zx, w_bc, w_dt, w_out, conv_x, conv_bc, head_params, gate_gain):
    rows, quarter = tokens.shape
    heads = head_params.shape[1]
    width = heads * HEAD
    place = lax.axis_index("head")
    groups = lax.axis_size("head")
    all_width = width * groups
    deep = quarter * groups
    arrange = order[0]

    arrived_x = lax.all_to_all(tokens, "dp", split_axis=0, concat_axis=0, tiled=True)
    own_x = arrived_x[arrange]
    own_w = w_zx.shape[0]
    packed = jnp.concatenate(
        [
            w_zx.reshape(own_w, 2 * width),
            w_bc,
            w_dt,
            norm_gain[:, None],
            jnp.zeros((own_w, 127 - heads), BF16),
        ],
        axis=1,
    )
    w_in = lax.all_gather(packed, "dp", axis=0, tiled=True)
    full_x = lax.all_gather(own_x, "head", axis=1, tiled=True)
    arrived_g = lax.all_to_all(cotangent, "dp", split_axis=0, concat_axis=0, tiled=True)
    own_g = arrived_g[arrange]
    full_g = lax.all_gather(own_g, "head", axis=1, tiled=True)
    w_o = lax.all_gather(w_out, "dp", axis=0, tiled=True)

    gain = w_in[:, 2 * width + 2 * N + heads].astype(F32)
    xf = full_x.astype(F32)
    inv_one = lax.rsqrt(jnp.mean(xf * xf, axis=1, keepdims=True) + EPS)
    normed = (xf * inv_one * gain).astype(BF16)
    u_zx = mm(normed, w_in[:, : 2 * width], ((1,), (0,)), BF16)
    u_bd = mm(normed, w_in[:, 2 * width :], ((1,), (0,)), F32)

    par = jnp.concatenate([conv_x, jnp.repeat(head_params[2:3], HEAD, axis=1), gate_gain[None], jnp.zeros((1, width), F32)], axis=0)
    pbc = jnp.concatenate([conv_bc, jnp.zeros((3, 2 * N), F32)], axis=0)
    hp = jnp.pad(head_params, ((0, 5), (0, 128 - heads)))
    positions = lax.broadcasted_iota(jnp.int32, (lengths.shape[0], LEN), 1)
    mask = (positions < lengths[:, None]).astype(F32).reshape(rows // T, 1, T)

    y, ss, c, cb, st = run_forward(heads, u_zx, u_bd, par, pbc, hp)
    dyn, co = run_gate(full_g, w_o, y, u_zx, par, mask)
    ss, co = lax.psum((ss, co), "head")
    yg, dz, dy, gg, rd_z = run_mid(all_width, y, u_zx, dyn, par, mask, ss, co)

    branch = mm(yg, w_o, ((1,), (1,)), BF16)
    shares = lax.psum_scatter(branch, "head", scatter_dimension=1, tiled=True)
    grad_out = mm(full_g, yg, ((0,), (0,)), BF16)
    grad_out = lax.psum_scatter(grad_out, "dp", scatter_dimension=0, tiled=True)
    grad_z = mm(normed, dz, ((0,), (0,)), BF16)
    grad_z = lax.psum_scatter(grad_z, "dp", scatter_dimension=0, tiled=True)

    out_rows = (own_x.astype(F32) + shares.astype(F32)).astype(BF16)
    sent_out = jnp.zeros_like(out_rows).at[arrange].set(out_rows)
    final_out = lax.all_to_all(sent_out, "dp", split_axis=0, concat_axis=0, tiled=True)

    dux, dbd, gx, gb, gh, rd_x = run_backward(heads, dy, u_zx, c, cb, u_bd, st, par, pbc, hp)

    terms = mm(dz, w_in[:, :width], ((1,), (1,)), F32)
    terms = terms + mm(dux, w_in[:, width : 2 * width], ((1,), (1,)), F32)
    terms = terms + mm(dbd, w_in[:, 2 * width :], ((1,), (1,)), F32)
    dxn = lax.psum_scatter(terms.astype(BF16), "head", scatter_dimension=1, tiled=True).astype(F32)
    row_dot = lax.psum(rd_z + rd_x, "head").reshape(rows, 1)

    grad_x = mm(normed, dux, ((0,), (0,)), BF16)
    grad_x = lax.psum_scatter(grad_x, "dp", scatter_dimension=0, tiled=True)
    grad_bd = mm(normed, dbd, ((0,), (0,)), BF16)
    grad_bd = lax.psum_scatter(grad_bd, "dp", scatter_dimension=0, tiled=True).astype(F32)
    grad_bc = lax.psum(grad_bd[:, : 2 * N], "head")
    grad_dt = grad_bd[:, 2 * N : 2 * N + heads]

    gain_own = lax.dynamic_slice_in_dim(gain, place * quarter, quarter, 0)
    inv_own = inv_one
    xs = own_x.astype(F32)
    grad_rows = own_g.astype(F32) + inv_own * gain_own * dxn - xs * inv_own**2 * (row_dot / deep)
    grad_rows = grad_rows.astype(BF16)
    gain_part = jnp.sum(dxn * xs * inv_own, axis=0)
    sent_back = jnp.zeros_like(grad_rows).at[arrange].set(grad_rows)
    final_back = lax.all_to_all(sent_back, "dp", split_axis=0, concat_axis=0, tiled=True)

    gain_part = lax.dynamic_update_slice_in_dim(jnp.zeros((deep,), F32), gain_part, place * quarter, 0)
    gx, gh, gg = lax.psum((gx[:5], gh[:3, :heads], gg[0]), "dp")
    gain_all, gb = lax.psum((gain_part, gb[:5]), ("dp", "head"))
    own_d = norm_gain.shape[0]
    grad_gain = lax.dynamic_slice_in_dim(gain_all, lax.axis_index("dp") * own_d, own_d, 0)
    grad_zx = jnp.stack([grad_z, grad_x], axis=1).astype(F32)
    return (final_out, final_back, grad_gain, grad_zx, grad_bc, grad_dt, grad_out.astype(F32), gx, gb, gh, gg)


def solution(mesh):
    return jax.shard_map(
        body,
        mesh=mesh,
        in_specs=(
            P("dp", "head"),
            P("dp", "head"),
            P("dp", None),
            P("dp"),
            P("dp"),
            P("dp", None, "head"),
            P("dp", None),
            P("dp", "head"),
            P("dp", "head"),
            P(None, "head"),
            P(),
            P(None, "head"),
            P("head"),
        ),
        out_specs=(
            P("dp", "head"),
            P("dp", "head"),
            P("dp"),
            P("dp", None, "head"),
            P("dp", None),
            P("dp", "head"),
            P("dp", "head"),
            P(None, "head"),
            P(),
            P(None, "head"),
            P("head"),
        ),
        check_vma=False,
    )
```

time: 1550 us -> 879 us (0.57)
  other arithmetic: 234 us -> 33.9 us
  matrix products: 285 us -> 97.7 us
  waiting for transfers between devices: 540 us -> 356 us
  local copies, waits for them, and re-layouts: 212 us -> 59.9 us
  Pallas kernels: 0 us -> 95.7 us
  blocking collectives: 227 us -> 193 us
    dot_general x48 -> x10, matrix products: 285 us -> 97.7 us  [mm(): lax.dot_general(a, b, (contract, ((), ())), preferred_element_type=F32)]
    reduce_scatter x5 -> x4, waiting for transfers between devices: 379 us -> 196 us  [the longest x1 71.6 us: body(): grad_x = lax.psum_scatter(grad_x, 'dp', scatter_dimension=0, tiled=True)]
    pallas_call x0 -> x4, Pallas kernels: none -> 95.7 us  [the longest x1 47.1 us: run_backward(): pl.pallas_call(functools.partial(backward_kernel, heads), grid=(slots, ch...]
    all_gather x4, waiting for transfers between devices: 0.06 us -> 87.9 us  [the longest x1 46.9 us: body(): full_g = lax.all_gather(own_g, 'head', axis=1, tiled=True)]
    unnamed x2 -> x0, blocking collectives: 78.2 us -> none
    all_to_all x0 -> x1, blocking collectives: none -> 75.9 us  [body(): lax.all_to_all(cotangent, 'dp', split_axis=0, concat_axis=0, tiled=True)]
    all_gather x2 -> x0, blocking collectives: 70.1 us -> none  [the longest x1 36.3 us: fetch_weights(): lax.all_gather(w_bc, 'dp', axis=0, tiled=True)]
    psum x1, waiting for transfers between devices: 67.1 us -> 0.01 us  [body(): grad_bc = lax.psum(grad_bd[:, :2 * N], 'head')]
  transfers between devices with their start and end apart: 15 -> 14, of which waited for: 8 -> 8; matrix products, arithmetic and copies ran while one was open for 25% -> 19% of each run, Pallas kernels for 0% -> 8%
where the time goes in v1:
time: 879 us; the launch traced here: 869 us
  waiting for transfers between devices  356 us (41%)
  blocking collectives  193 us (22%)
  matrix products  97.7 us (11%)
  Pallas kernels  95.7 us (11%)
  local copies, waits for them, and re-layouts  59.9 us (7%)
  other arithmetic  33.9 us (4%)
  starting transfers between devices  18.3 us (2%)
  between operations  14.4 us (2%)
    dot_general x10, matrix products, mm(): lax.dot_general(a, b, (contract, ((), ())), preferred_element_type=F32)  97.7 us
    all_to_all x1, blocking collectives, body(): lax.all_to_all(cotangent, 'dp', split_axis=0, concat_axis=0, tiled=True)  75.9 us
    reduce_scatter x1, waiting for transfers between devices, body(): grad_x = lax.psum_scatter(grad_x, 'dp', scatter_dimension=0, tiled=True)  71.6 us
    reduce_scatter x1, waiting for transfers between devices, body(): grad_out = lax.psum_scatter(grad_out, 'dp', scatter_dimension=0, tiled=True)  68.3 us
    all_to_all x1, waiting for transfers between devices, body(): lax.all_to_all(tokens, 'dp', split_axis=0, concat_axis=0, tiled=True)  60.6 us
    psum x1, blocking collectives, body(): gx, gh, gg = lax.psum((gx[:5], gh[:3, :heads], gg[0]), 'dp')  59.6 us
    reduce_scatter x1, waiting for transfers between devices, body(): grad_z = lax.psum_scatter(grad_z, 'dp', scatter_dimension=0, tiled=True)  55.9 us
    pallas_call x1, Pallas kernels, run_backward(): pl.pallas_call(functools.partial(backward_kernel, heads), grid=(slots, ch...  47.1 us
  transfers between devices with their start and end apart: 14, of which 8 were waited for; matrix products, arithmetic and copies ran while one was open for 19% of the time, Pallas kernels for 8%

profile of v1, /device:TPU:0, one launch (start us, length us, event | category | flops | bytes accessed | tf_op | source)
XLA Modules:
  0.0 868.6 jit_solution(2491668594063840549)
XLA Ops:
  19.1 60.6 %all-to-all-done = bf16[8,256,384]{2,1,0:T(8,128)(2,1)S(1)} async-done(((bf16[8,256,384]{2,1,0:T(8,128)(2,1)}), bf16[8,256,384]{2,1,0:T(8,128)(2,1)S(1)}, u32[]{:S(2)}, u32[]{:S(2)}) %all-to-all-start) | async-done | bytes 1572896 | tf_op jit(solution)/shard_map/all_to_all | solution.py:449
  89.6 75.9 %all_to_all.48 = bf16[8,256,384]{2,1,0:T(8,128)(2,1)S(1)} all-to-all(bf16[8,256,384]{2,1,0:T(8,128)(2,1)S(1)} %bitcast.44), channel_id=1, replica_groups=mesh['dp'=8,'head'=4] {'dp'}, dimensions={0} | all-to-all | bytes 3145728 | tf_op jit(solution)/shard_map/all_to_all | solution.py:464
  179.0 34.9 %all-gather.11.cloned.1.call-done = bf16[2048,1536]{1,0:T(8,128)(2,1)} async-done(((bf16[2048,384]{1,0:T(8,128)(2,1)}), bf16[2048,1536]{1,0:T(8,128)(2,1)}) %all-gather.11.cloned.1.call-update) | async-done | bytes 6291472 | tf_op jit(solution)/shard_map/all_gather | solution.py:463
  225.4 12.6 %convolution_convert_fusion.1.x_ref.z_ref = bf16[2048,1536]{1,0:T(8,128)(2,1)} fusion(bf16[1536,1920]{1,0:T(8,128)(2,1)S(1)} %bitcast.48, bf16[2048,1536]{1,0:T(8,128)(2,1)S(1)} %copy-done.3, f32[1536]{0:T(1024)S(1)} %fusion.28, f32[2048]{0:T(1024)S(1)} %get-tuple-element.88), kind=kOutput, calls=%fused_computation.11 | convolution fusion | flops 9679405056 | bytes 17317888 | tf_op jit(solution)/shard_map/dot_general | solution.py:436
  237.9 24.2 %scan_forward.1 = (bf16[2048,768]{1,0:T(8,128)(2,1)}, f32[16,1,128]{2,1,0:T(1,128)}, bf16[2048,768]{1,0:T(8,128)(2,1)}, f32[2048,256]{1,0:T(8,128)}, bf16[16,128,768]{2,1,0:T(8,128)(2,1)}) custom-call(bf16[2048,1536]{1,0:T(8,128)(2,1)} %convolution_convert_fusion.1.x_ref.z_ref, bf16[2048,1536]{1,0:T(8,128)(2,1)} %convolution_convert_fusion.1.x_ref.z_ref, ...), custom_call_target="tpu_custom_call" | custom-call | flops 3774873600 | bytes 12582912 | tf_op jit(solution)/shard_map/scan_forward/pallas_call | solution.py:305
  268.2 46.9 %all-gather.13.cloned.1.call-done.g_ref = bf16[2048,1536]{1,0:T(8,128)(2,1)} async-done(((bf16[2048,384]{1,0:T(8,128)(2,1)}), bf16[2048,1536]{1,0:T(8,128)(2,1)}) %all-gather.13.cloned.1.call-update) | async-done | bytes 6291472 | tf_op jit(solution)/shard_map/all_gather | solution.py:466
  315.1 12.3 %gate_back.1 = (bf16[2048,768]{1,0:T(8,128)(2,1)}, f32[16,1,128]{2,1,0:T(1,128)}) custom-call(bf16[2048,1536]{1,0:T(8,128)(2,1)} %all-gather.13.cloned.1.call-done.g_ref, bf16[1536,768]{1,0:T(8,128)(2,1)} %all-gather.9.cloned.1.call-done.wo_ref, bf16[2048,768]{1,0:T(8,128)(2,1)} %get-tuple-element.29.y_ref, ...), custom_call_target="tpu_custom_call" | custom-call | flops 4831838208 | bytes 15728640 | tf_op jit(solution)/shard_map/gate_back/pallas_call | solution.py:344
  327.4 11.7 %all-reduce.4 = (f32[16,1,128]{2,1,0:T(1,128)}, f32[16,1,128]{2,1,0:T(1,128)}) all-reduce(f32[16,1,128]{2,1,0:T(1,128)S(1)} %copy-done.15, f32[16,1,128]{2,1,0:T(1,128)} %get-tuple-element.32), channel_id=1, replica_groups=mesh['dp'=8,'head'=4] {'head'}, use_global_device_ids=true, to_apply=%region_1.2 | all-reduce | flops 4096 | bytes 32768 | tf_op jit(solution)/shard_map/psum | solution.py:484
  339.1 12.1 %gate_mid.1 = (bf16[2048,768]{1,0:T(8,128)(2,1)}, bf16[2048,768]{1,0:T(8,128)(2,1)}, bf16[2048,768]{1,0:T(8,128)(2,1)}, f32[8,768]{1,0:T(8,128)}, f32[16,1,128]{2,1,0:T(1,128)}) custom-call(bf16[2048,768]{1,0:T(8,128)(2,1)} %get-tuple-element.29.y_ref, bf16[2048,1536]{1,0:T(8,128)(2,1)} %convolution_convert_fusion.1.x_ref.z_ref, ...), custom_call_target="tpu_custom_call" | custom-call | flops 47185920 | bytes 18874368 | tf_op jit(solution)/shard_map/gate_mid/pallas_call | solution.py:370
  351.3 9.1 %convolution_convert_fusion = bf16[2048,1536]{1,0:T(8,128)(2,1)} fusion(bf16[2048,768]{1,0:T(8,128)(2,1)} %get-tuple-element.33, bf16[1536,768]{1,0:T(8,128)(2,1)S(1)} %copy-done.4), kind=kOutput, calls=%fused_computation.10 | convolution fusion | flops 4834983936 | bytes 11796480 | tf_op jit(solution)/shard_map/dot_general | solution.py:436
  369.2 47.1 %scan_backward.1 = (bf16[2048,768]{1,0:T(8,128)(2,1)}, bf16[2048,384]{1,0:T(8,128)(2,1)}, f32[8,768]{1,0:T(8,128)}, f32[8,256]{1,0:T(8,128)}, f32[8,128]{1,0:T(8,128)}, /*index=5*/f32[16,1,128]{2,1,0:T(1,128)}) custom-call(bf16[2048,768]{1,0:T(8,128)(2,1)} %get-tuple-element.35.dy_ref, bf16[2048,1536]{1,0:T(8,128)(2,1)} %convolution_convert_fusion.1.x_ref.z_ref, ...), custom_call_target="tpu_custom_call" | custom-call | flops 9437184000 | bytes 18874368 | tf_op jit(solution)/shard_map/scan_backward/pallas_call | solution.py:390
  416.4 9.7 %fusion.13 = f32[2048,1536]{1,0:T(8,128)} fusion(bf16[2048,768]{1,0:T(8,128)(2,1)S(1)} %copy-done.19, bf16[1536,1920]{1,0:T(8,128)(2,1)} %all-gather.7.cloned.1.call-done), kind=kOutput, calls=%fused_computation.30 | convolution fusion | flops 4831838208 | bytes 18087936 | tf_op jit(solution)/shard_map/dot_general | solution.py:436
  426.1 9.7 %fusion.11 = f32[2048,1536]{1,0:T(8,128)} fusion(bf16[2048,768]{1,0:T(8,128)(2,1)S(1)} %copy-done.21, bf16[1536,1920]{1,0:T(8,128)(2,1)} %all-gather.7.cloned.1.call-done), kind=kOutput, calls=%fused_computation.28 | convolution fusion | flops 4831838208 | bytes 18087936 | tf_op jit(solution)/shard_map/dot_general | solution.py:436
  435.8 13.1 %add_convert_fusion = bf16[2048,1536]{1,0:T(8,128)(2,1)} fusion(f32[2048,1536]{1,0:T(8,128)} %fusion.13, f32[2048,1536]{1,0:T(8,128)} %fusion.11, bf16[2048,384]{1,0:T(8,128)(2,1)S(1)} %copy-done.5, bf16[1536,1920]{1,0:T(8,128)(2,1)} %all-gather.7.cloned.1.call-done), kind=kOutput, calls=%fused_computation.9 | convolution fusion | flops 2425356288 | bytes 34209792 | tf_op jit(solution)/shard_map/dot_general | solution.py:436
  465.7 11.3 %convolution_convert_fusion.4 = bf16[1536,768]{1,0:T(8,128)(2,1)} fusion(bf16[2048,768]{1,0:T(8,128)(2,1)} %get-tuple-element.34, bf16[2048,1536]{1,0:T(8,128)(2,1)} %all-gather.11.cloned.1.call-done, f32[1536]{0:T(1024)S(1)} %fusion.28, f32[2048]{0:T(1024)S(1)} %get-tuple-element.88), kind=kOutput, calls=%fused_computation.19 | convolution fusion | flops 4845600768 | bytes 11810816 | tf_op jit(solution)/shard_map/dot_general | solution.py:436
  487.9 10.7 %scatter_custom_fusion = bf16[2048,384]{1,0:T(8,128)(2,1)} fusion(s32[2048]{0:T(1024)S(1)} %bitcast.54, bf16[2048,384]{1,0:T(8,128)(2,1)S(1)} %copy-done, bf16[2048,384]{1,0:T(8,128)(2,1)S(1)} %copy.36, bf16[]{:T(256)} %constant.13.clone.1), kind=kCustom, calls=%fused_computation.32 | custom fusion | flops 3145728 | bytes 4718594 | tf_op jit(solution)/shard_map/scatter | solution.py:495
  504.4 9.3 %convolution_convert_fusion.2 = bf16[1536,768]{1,0:T(8,128)(2,1)} fusion(bf16[2048,1536]{1,0:T(8,128)(2,1)} %all-gather.13.cloned.1.call-done.g_ref, bf16[2048,768]{1,0:T(8,128)(2,1)} %get-tuple-element.33), kind=kOutput, calls=%fused_computation.17 | convolution fusion | flops 4833017856 | bytes 11796480 | tf_op jit(solution)/shard_map/dot_general | solution.py:436
  524.2 11.4 %scatter_custom_fusion.1 = bf16[2048,384]{1,0:T(8,128)(2,1)} fusion(s32[2048]{0:T(1024)S(1)} %bitcast.55, bf16[2048,384]{1,0:T(8,128)(2,1)} %copy.38, bf16[2048,384]{1,0:T(8,128)(2,1)S(1)} %copy-done, bf16[2048,384]{1,0:T(8,128)(2,1)S(1)} %copy-done.1, f32[2048]{0:T(1024)S(1)} %bitcast.52, f32[2048]{0:T(1024)S(1)} %get-tuple-element.87, ...), kind=kCustom, calls=%fused_computation.33 | custom fusion | flops 7864320 | bytes 6318082 | tf_op jit(solution)/shard_map/scatter | solution.py:519
  535.6 10.3 %all-to-all-done.2 = bf16[8,256,384]{2,1,0:T(8,128)(2,1)} async-done(((bf16[8,256,384]{2,1,0:T(8,128)(2,1)}), bf16[8,256,384]{2,1,0:T(8,128)(2,1)}, u32[]{:S(2)}, u32[]{:S(2)}) %all-to-all-start.2) | async-done | bytes 1572896 | tf_op jit(solution)/shard_map/all_to_all | solution.py:496
  551.2 59.6 %all-reduce.3 = (f32[5,768]{1,0:T(8,128)}, f32[3,12]{1,0:T(4,128)}, f32[768]{0:T(1024)}) all-reduce(f32[5,768]{1,0:T(8,128)S(1)} %bitcast.57, f32[3,12]{1,0:T(4,128)S(1)} %slice.50, f32[768]{0:T(1024)S(1)} %slice_reduce_fusion), channel_id=1, replica_groups=mesh['dp'=8,'head'=4] {'dp'}, use_global_device_ids=true, to_apply=%region_15.16 | all-reduce | flops 4644 | bytes 37152 | tf_op jit(solution)/shard_map/psum | solution.py:523
  613.8 55.9 %reduce-scatter.11.cloned.1.call-done = bf16[192,768]{1,0:T(8,128)(2,1)} async-done(((bf16[1536,768]{1,0:T(8,128)(2,1)}), bf16[192,768]{1,0:T(8,128)(2,1)}) %reduce-scatter.11.cloned.1.call-update) | async-done | bytes 294928 | tf_op jit(solution)/shard_map/reduce_scatter | solution.py:492
  669.7 71.6 %reduce-scatter.13.cloned.1.call-done = bf16[192,768]{1,0:T(8,128)(2,1)} async-done(((bf16[1536,768]{1,0:T(8,128)(2,1)}), bf16[192,768]{1,0:T(8,128)(2,1)}) %reduce-scatter.13.cloned.1.call-update) | async-done | bytes 294928 | tf_op jit(solution)/shard_map/reduce_scatter | solution.py:507
  744.4 68.3 %reduce-scatter.17.cloned.1.call-done = bf16[192,768]{1,0:T(8,128)(2,1)} async-done(((bf16[1536,768]{1,0:T(8,128)(2,1)}), bf16[192,768]{1,0:T(8,128)(2,1)}) %reduce-scatter.17.cloned.1.call-update) | async-done | bytes 294928 | tf_op jit(solution)/shard_map/reduce_scatter | solution.py:490
  815.4 39.6 %all-reduce.2 = (f32[1536]{0:T(1024)S(1)}, f32[5,256]{1,0:T(8,128)}) all-reduce(f32[1536]{0:T(1024)S(1)} %dynamic_update_slice.3, f32[5,256]{1,0:T(8,128)S(1)} %bitcast.58), channel_id=1, replica_groups=mesh['dp'=8,'head'=4] {'dp','head'}, use_global_device_ids=true, to_apply=%region_9.10 | all-reduce | flops 2816 | bytes 22528 | tf_op jit(solution)/shard_map/psum | solution.py:524
  (135 shorter events, 126.2 us)
Async XLA Ops:
  7.2 170.5 %all-gather.7.cloned.1.call-start = ((), (), s32[]{:S(2)}) async-start(), calls=%async_computation.10 | async-start | bytes 6635520 | tf_op jit(solution)/shard_map/all_gather | solution.py:462
  11.8 68.0 %all-to-all-start = ((bf16[8,256,384]{2,1,0:T(8,128)(2,1)}), bf16[8,256,384]{2,1,0:T(8,128)(2,1)S(1)}, u32[]{:S(2)}, u32[]{:S(2)}) async-start(bf16[8,256,384]{2,1,0:T(8,128)(2,1)} %bitcast.2), calls=%async_computation | async-start | bytes 3145728 | tf_op jit(solution)/shard_map/all_to_all | solution.py:449
  19.0 194.9 %all-gather.11.cloned.1.call-start = ((), (), s32[]{:S(2)}) async-start(), calls=%async_computation.17 | async-start | bytes 7864320 | tf_op jit(solution)/shard_map/all_gather | solution.py:463
  88.8 179.4 %all-gather.9.cloned.1.call-start = ((), (), s32[]{:S(2)}) async-start(), calls=%async_computation.11 | async-start | bytes 2654208 | tf_op jit(solution)/shard_map/all_gather | solution.py:467
  89.6 225.5 %all-gather.13.cloned.1.call-start = ((), (), s32[]{:S(2)}) async-start(), calls=%async_computation.18 | async-start | bytes 7864320 | tf_op jit(solution)/shard_map/all_gather | solution.py:466
  165.5 11.5 %copy-start.8 = (f32[5,768]{1,0:T(8,128)S(1)}, f32[5,768]{1,0:T(8,128)}, u32[]{:S(2)}) copy-start(f32[5,768]{1,0:T(8,128)} %param.22) | copy-start | bytes 46084
  174.6 311.3 %reduce-scatter.19.cloned.1.call-start = ((), (), s32[]{:S(2)}) async-start(), calls=%async_computation.19 | async-start | bytes 7864320
  213.9 11.4 %slice-start = ((s8[5898240]{0:T(1024)(128)(4,1)}), s8[4194304]{0:T(1024)(128)(4,1)S(1)}, s32[]{:S(2)}) async-start(s8[5898240]{0:T(1024)(128)(4,1)} %bitcast.47), calls=%async_computation.21 | async-start | bytes 8388608
  315.1 12.3 %copy-start.15 = (f32[16,1,128]{2,1,0:T(1,128)S(1)}, f32[16,1,128]{2,1,0:T(1,128)}, u32[]{:S(2)}) copy-start(f32[16,1,128]{2,1,0:T(1,128)} %get-tuple-element.31) | copy-start | bytes 24580
  339.1 12.1 %copy-start.4 = (bf16[1536,768]{1,0:T(8,128)(2,1)S(1)}, bf16[1536,768]{1,0:T(8,128)(2,1)}, u32[]{:S(2)}) copy-start(bf16[1536,768]{1,0:T(8,128)(2,1)} %all-gather.9.cloned.1.call-done.wo_ref) | copy-start | bytes 7077892
  369.2 152.4 %reduce-scatter.21.cloned.1.call-start = ((), (), s32[]{:S(2)}) async-start(), calls=%async_computation.20 | async-start | bytes 7864320
  369.2 47.1 %copy-start.19 = (bf16[2048,768]{1,0:T(8,128)(2,1)S(1)}, bf16[2048,768]{1,0:T(8,128)(2,1)}, u32[]{:S(2)}) copy-start(bf16[2048,768]{1,0:T(8,128)(2,1)} %get-tuple-element.34) | copy-start | bytes 9437188
  457.7 153.0 %reduce-scatter.15.cloned.1.call-start = ((), (), s32[]{:S(2)}) async-start(), calls=%async_computation.14 | async-start | bytes 1327104 | tf_op jit(solution)/shard_map/reduce_scatter | solution.py:509
  465.7 11.6 %copy-start.22 = (bf16[2048,768]{1,0:T(8,128)(2,1)S(1)}, bf16[2048,768]{1,0:T(8,128)(2,1)}, u32[]{:S(2)}) copy-start(bf16[2048,768]{1,0:T(8,128)(2,1)} %get-tuple-element.39) | copy-start | bytes 9437188
  465.7 204.0 %reduce-scatter.11.cloned.1.call-start = ((), (), s32[]{:S(2)}) async-start(), calls=%async_computation.12 | async-start | bytes 2654208 | tf_op jit(solution)/shard_map/reduce_scatter | solution.py:492
  477.0 264.3 %reduce-scatter.13.cloned.1.call-start = ((), (), s32[]{:S(2)}) async-start(), calls=%async_computation.13 | async-start | bytes 2654208 | tf_op jit(solution)/shard_map/reduce_scatter | solution.py:507
  498.7 47.2 %all-to-all-start.2 = ((bf16[8,256,384]{2,1,0:T(8,128)(2,1)}), bf16[8,256,384]{2,1,0:T(8,128)(2,1)}, u32[]{:S(2)}, u32[]{:S(2)}) async-start(bf16[8,256,384]{2,1,0:T(8,128)(2,1)} %bitcast.8), calls=%async_computation.2 | async-start | bytes 3145728 | tf_op jit(solution)/shard_map/all_to_all | solution.py:496
  504.4 308.4 %reduce-scatter.17.cloned.1.call-start = ((), (), s32[]{:S(2)}) async-start(), calls=%async_computation.16 | async-start | bytes 2654208 | tf_op jit(solution)/shard_map/reduce_scatter | solution.py:490
  535.6 14.7 %copy-start.18 = (f32[8,128]{1,0:T(8,128)S(1)}, f32[8,128]{1,0:T(8,128)}, u32[]{:S(2)}) copy-start(f32[8,128]{1,0:T(8,128)} %get-tuple-element.45) | copy-start | bytes 12292
  535.6 15.5 %copy-start.9 = (f32[8,768]{1,0:T(8,128)S(1)}, f32[8,768]{1,0:T(8,128)}, u32[]{:S(2)}) copy-start(f32[8,768]{1,0:T(8,128)} %get-tuple-element.43) | copy-start | bytes 73732
  545.9 309.8 %all-to-all-start.3 = ((bf16[8,256,384]{2,1,0:T(8,128)(2,1)}), bf16[8,256,384]{2,1,0:T(8,128)(2,1)}, u32[]{:S(2)}, u32[]{:S(2)}) async-start(bf16[8,256,384]{2,1,0:T(8,128)(2,1)} %bitcast.42), calls=%async_computation.3 | async-start | bytes 3145728 | tf_op jit(solution)/shard_map/all_to_all | solution.py:520
  550.2 264.4 %copy-start.2 = (bf16[2048,384]{1,0:T(8,128)(2,1)S(1)}, bf16[2048,384]{1,0:T(8,128)(2,1)}, u32[]{:S(2)}) copy-start(bf16[2048,384]{1,0:T(8,128)(2,1)} %copy.38) | copy-start | bytes 4718596
  550.2 305.5 %all-reduce.7.cloned.1.call-start = ((), (), s32[]{:S(2)}) async-start(), calls=%async_computation.15 | async-start | bytes 393216 | tf_op jit(solution)/shard_map/psum | solution.py:510
  742.5 72.9 %copy-start.14 = (f32[8,256]{1,0:T(8,128)S(1)}, f32[8,256]{1,0:T(8,128)}, u32[]{:S(2)}) copy-start(f32[8,256]{1,0:T(8,128)} %get-tuple-element.44) | copy-start | bytes 24580
  (15 other events, 110.1 us)
Sparse Core Ops, SparseCore 0:
  11.9 154.4 all-gather.6
  168.5 45.3 all-gather.10
  216.1 52.0 all-gather.8
  270.2 44.8 all-gather.12
  369.3 58.8 reduce-scatter.18
  457.8 58.9 reduce-scatter.20
  520.8 77.4 reduce-scatter.14
  601.7 67.9 reduce-scatter.10
  673.2 68.0 reduce-scatter.12
  744.7 68.0 reduce-scatter.16
  815.6 30.8 all-reduce.6

commit v2 on v1

--- a/solution.py
+++ b/solution.py
@@ -127,6 +127,14 @@
     ss_ref[0] = to_row(jnp.sum(squares, axis=1, keepdims=True))
 
 
+def norm_kernel(x_ref, gain_ref, out_ref, inv_ref):
+    x = x_ref[...].astype(F32)
+    inv = lax.rsqrt(jnp.sum(x * x, axis=1, keepdims=True) / x.shape[1] + EPS)
+    out_ref[...] = (x * inv * gain_ref[0:1]).astype(BF16)
+    for part in range(x.shape[0] // T):
+        inv_ref[part] = to_row(inv[part * T : part * T + T])
+
+
 def gate_kernel(g_ref, wo_ref, y_ref, z_ref, par_ref, mask_ref, dyn_ref, co_ref):
     dyn = dot(g_ref[...], wo_ref[...])
     for part in range(dyn.shape[0] // T):
@@ -167,7 +175,41 @@
         rd_ref[part] = to_row(jnp.sum(dz * z, axis=1, keepdims=True))
 
 
-def backward_kernel(heads, dy_ref, x_ref, c_ref, cb_ref, ubd_ref, st_ref, par_ref, pbc_ref, head_ref, dx_ref, dbd_ref, gx_ref, gb_ref, gh_ref, rd_ref, d_state, ext_x, ext_b, rows_ref, prod, edy_ref, tail_ref):
+def background(moves, last, srcs, dsts, sems):
+    place = {"dp": lax.axis_index("dp"), "head": lax.axis_index("head")}
+
+    def peer(axis, flip):
+        return tuple(place[name] ^ flip if name == axis else place[name] for name in ("dp", "head"))
+
+    copies = [
+        pltpu.make_async_remote_copy(
+            src_ref=src, dst_ref=dst, send_sem=sems.at[0, i], recv_sem=sems.at[1, i], device_id=peer(*move), device_id_type=MESH
+        )
+        for i, (move, src, dst) in enumerate(zip(moves, srcs, dsts))
+    ]
+    first = (pl.program_id(0) == 0) & (pl.program_id(1) == 0)
+
+    @pl.when(first)
+    def _():
+        greet([peer(*move) for move in dict.fromkeys(moves)])
+        for copy in copies:
+            copy.start()
+
+    @pl.when(last)
+    def _():
+        for copy in copies:
+            copy.wait()
+
+
+def backward_kernel(heads, extra, moves, dy_ref, x_ref, c_ref, cb_ref, ubd_ref, st_ref, par_ref, pbc_ref, head_ref, *refs):
+    count = len(moves)
+    srcs, refs = refs[:count], refs[count + extra :]
+    dx_ref, dbd_ref, gx_ref, gb_ref, gh_ref, rd_ref = refs[:6]
+    dsts, refs = refs[6 : 6 + count], refs[6 + count :]
+    d_state, ext_x, ext_b, rows_ref, prod, edy_ref, tail_ref = refs[:7]
+    if moves:
+        ended = (pl.program_id(0) == pl.num_programs(0) - 1) & (pl.program_id(1) == pl.num_programs(1) - 1)
+        background(moves, ended, srcs, dsts, refs[7])
     first = (pl.program_id(0) == 0) & (pl.program_id(1) == 0)
 
     @pl.when(first)
@@ -293,7 +335,11 @@
     rd_ref[0] = to_row(total)
 
 
-def params(*semantics):
+def params(*semantics, number=0):
+    if number:
+        return pltpu.CompilerParams(
+            dimension_semantics=semantics, vmem_limit_bytes=56 * 1024 * 1024, collective_id=number, has_side_effects=True
+        )
     return pltpu.CompilerParams(dimension_semantics=semantics, vmem_limit_bytes=56 * 1024 * 1024)
 
 
@@ -334,6 +380,22 @@
     )(u_zx, u_zx, u_bd, par, pbc, hp)
 
 
+def run_norm(x, gain):
+    rows, deep = x.shape
+    step = 256
+    at = lambda i: (i, 0)
+    return pl.pallas_call(
+        norm_kernel,
+        grid=(rows // step,),
+        in_specs=[pl.BlockSpec((step, deep), at), pl.BlockSpec((8, deep), lambda i: (0, 0))],
+        out_specs=[pl.BlockSpec((step, deep), at), pl.BlockSpec((step // T, 1, T), lambda i: (i, 0, 0))],
+        out_shape=[jax.ShapeDtypeStruct((rows, deep), BF16), jax.ShapeDtypeStruct((rows // T, 1, T), F32)],
+        compiler_params=params("arbitrary"),
+        cost_estimate=pl.CostEstimate(flops=rows * deep * 6, bytes_accessed=rows * deep * 4, transcendentals=rows),
+        name="norm_rows",
+    )(x, gain)
+
+
 def run_gate(full_grad, w_out, y, u_zx, par, mask):
     rows, width = y.shape
     deep = full_grad.shape[1]
@@ -380,15 +442,17 @@
     )(y, u_zx, dyn, par, mask, ss, co)
 
 
-def run_backward(heads, dy, u_zx, c, cb, u_bd, st, par, pbc, hp):
-    rows, width = dy.shape
-    slots, chunks = rows // LEN, LEN // T
-    place = lambda s, i: s * chunks + chunks - 1 - i
+def run_backward(heads, slot, slots, dy, u_zx, c, cb, u_bd, st, par, pbc, hp, deps, swaps=(), number=0):
+    width = dy.shape[1]
+    chunks = LEN // T
+    rows = slots * LEN
+    here = lambda s, i: s * chunks + chunks - 1 - i
+    place = lambda s, i: (slot + s) * chunks + chunks - 1 - i
     at = lambda s, i: (place(s, i), 0)
     at3 = lambda s, i: (place(s, i), 0, 0)
     fixed = lambda s, i: (0, 0)
     return pl.pallas_call(
-        functools.partial(backward_kernel, heads),
+        functools.partial(backward_kernel, heads, len(deps), tuple(move for move, _ in swaps)),
         grid=(slots, chunks),
         in_specs=[
             pl.BlockSpec((T, width), at),
@@ -400,15 +464,17 @@
             pl.BlockSpec((8, width), fixed),
             pl.BlockSpec((8, 2 * N), fixed),
             pl.BlockSpec((8, 128), fixed),
-        ],
+        ]
+        + [pl.BlockSpec(memory_space=pl.ANY)] * (len(swaps) + len(deps)),
         out_specs=[
-            pl.BlockSpec((T, width), at),
-            pl.BlockSpec((T, 3 * N), at),
+            pl.BlockSpec((T, width), lambda s, i: (here(s, i), 0)),
+            pl.BlockSpec((T, 3 * N), lambda s, i: (here(s, i), 0)),
             pl.BlockSpec((8, width), fixed),
             pl.BlockSpec((8, 2 * N), fixed),
             pl.BlockSpec((8, 128), fixed),
-            pl.BlockSpec((1, 1, T), at3),
-        ],
+            pl.BlockSpec((1, 1, T), lambda s, i: (here(s, i), 0, 0)),
+        ]
+        + [pl.BlockSpec(memory_space=pl.ANY)] * len(swaps),
         out_shape=[
             jax.ShapeDtypeStruct((rows, width), BF16),
             jax.ShapeDtypeStruct((rows, 3 * N), BF16),
@@ -416,7 +482,8 @@
             jax.ShapeDtypeStruct((8, 2 * N), F32),
             jax.ShapeDtypeStruct((8, 128), F32),
             jax.ShapeDtypeStruct((rows // T, 1, T), F32),
-        ],
+        ]
+        + [jax.ShapeDtypeStruct(value.shape, value.dtype) for _, value in swaps],
         scratch_shapes=[
             pltpu.VMEM((N, width), F32),
             pltpu.VMEM((T + 8, width), F32),
@@ -425,15 +492,257 @@
             pltpu.VMEM((3 * T, width), BF16),
             pltpu.VMEM((T, width), BF16),
             pltpu.VMEM((T, width), BF16),
-        ],
-        compiler_params=params("arbitrary", "arbitrary"),
+        ]
+        + ([pltpu.SemaphoreType.DMA((2, len(swaps)))] if swaps else []),
+        compiler_params=params("arbitrary", "arbitrary", number=number),
         cost_estimate=pl.CostEstimate(flops=rows * width * 2 * 3000, bytes_accessed=rows * width * 12, transcendentals=rows * width * 8),
         name="scan_backward",
-    )(dy, u_zx, c, cb, u_bd, st, par, pbc, hp)
+    )(dy, u_zx, c, cb, u_bd, st, par, pbc, hp, *[value for _, value in swaps], *deps)
+
+
+def pieces_kernel(count, me_ref, *refs):
+    values, weights, outs = refs[:count], refs[count : 2 * count], refs[2 * count :]
+    quarter = outs[0].shape[1]
+    for k, out in enumerate(outs):
+        at = pl.ds(pl.multiple_of((me_ref[0] ^ k) * quarter, 128), quarter)
+        total = None
+        for value, weight in zip(values, weights):
+            term = dot_nt(value[...], weight[at, :])
+            total = term if total is None else total + term
+        out[...] = total.astype(out.dtype)
+
+
+def run_pieces(me, values, weights, quarter, first, rows, name):
+    step = 256
+    specs = [pl.BlockSpec((step, v.shape[1]), lambda i, m: (first // step + i, 0)) for v in values]
+    specs += [pl.BlockSpec(w.shape, lambda i, m: (0, 0)) for w in weights]
+    depth = sum(v.shape[1] for v in values)
+    return pl.pallas_call(
+        functools.partial(pieces_kernel, len(values)),
+        grid_spec=pltpu.PrefetchScalarGridSpec(
+            num_scalar_prefetch=1,
+            grid=(rows // step,),
+            in_specs=specs,
+            out_specs=[pl.BlockSpec((step, quarter), lambda i, m: (i, 0))] * 4,
+        ),
+        out_shape=[jax.ShapeDtypeStruct((rows, quarter), BF16)] * 4,
+        compiler_params=params("arbitrary"),
+        cost_estimate=pl.CostEstimate(flops=rows * depth * quarter * 8, bytes_accessed=rows * (depth + 4 * quarter) * 2, transcendentals=0),
+        name=name,
+    )(me, *values, *weights)
+
+
+MESH = pl.DeviceIdType.MESH
+
+
+def greet(peers):
+    barrier = pltpu.get_barrier_semaphore()
+    for peer in peers:
+        pl.semaphore_signal(barrier, inc=1, device_id=peer, device_id_type=MESH)
+    pl.semaphore_wait(barrier, len(peers))
+
+
+def entry_kernel(parts, *refs):
+    x_ref, g_ref, wi_ref, wo_ref, fx_ref, fg_ref, fwi_ref, fwo_ref = refs[:8]
+    row_sems, far_sems, near_sems, back_sems, across_sems, side_sems, local_sems = refs[8:]
+    size = x_ref.shape[0]
+    quarter = x_ref.shape[2]
+    me, own = lax.axis_index("dp"), lax.axis_index("head")
+    columns = lambda head: pl.ds(pl.multiple_of(head * quarter, 128), quarter)
+
+    def remote(src, dst, sems, slot, peer):
+        return pltpu.make_async_remote_copy(
+            src_ref=src, dst_ref=dst, send_sem=sems.at[(0,) + slot], recv_sem=sems.at[(1,) + slot], device_id=peer, device_id_type=MESH
+        )
+
+    def rows_copy(which, k):
+        src, dst = ((x_ref, fx_ref), (g_ref, fg_ref))[which]
+        return remote(src.at[me ^ k], dst.at[me, :, columns(own)], row_sems, (which, k), (me ^ k, own))
+
+    def far_copy(which, k):
+        ref = (fx_ref, fg_ref)[which]
+        block = ref.at[me ^ k, :, columns(own)]
+        return remote(block, block, far_sems, (which, k), (me, own ^ 2))
+
+    def near_copy(which, k):
+        ref = (fx_ref, fg_ref)[which]
+        block = ref.at[me ^ k, :, columns(own)]
+        return remote(block, block, near_sems, (which, k), (me, own ^ 1))
+
+    def back_copy(which, k):
+        ref = (fx_ref, fg_ref)[which]
+        block = ref.at[me ^ k, :, columns(own ^ 2)]
+        return remote(block, block, back_sems, (which, k), (me, own ^ 1))
+
+    line = size // 2
+
+    def across_copy(which, part, j):
+        src, dst = ((wi_ref, fwi_ref), (wo_ref, fwo_ref))[which]
+        return remote(src.at[part], dst.at[me, part], across_sems, (which, part, j), (me ^ (2 * j), own))
+
+    def side_copy(which, part, j):
+        src, dst = ((wi_ref, fwi_ref), (wo_ref, fwo_ref))[which]
+        here = dst.at[me ^ (2 * j), part]
+        return remote(src.at[part] if j == 0 else here, here, side_sems, (which, part, j), (me ^ 1, own))
+
+    greet([(me ^ k, own) for k in range(1, size)] + [(me, own ^ 1), (me, own ^ 2)])
+
+    order = sorted(range(1, size), key=lambda k: (-(k & ~1), k & 1))
+    locals_ = []
+    for which, (src, dst) in enumerate(((x_ref, fx_ref), (g_ref, fg_ref))):
+        locals_.append(pltpu.make_async_copy(src.at[me], dst.at[me, :, columns(own)], local_sems.at[which]))
+    for which, (src, dst) in enumerate(((wi_ref, fwi_ref), (wo_ref, fwo_ref))):
+        locals_.append(pltpu.make_async_copy(src, dst.at[me], local_sems.at[2 + which]))
+
+    def send_rows(which):
+        for k in order:
+            rows_copy(which, k).start()
+
+    def forward(which, done):
+        locals_[which].wait()
+        far_copy(which, 0).start()
+        near_copy(which, 0).start()
+        waiting = [0]
+        for k in order:
+            rows_copy(which, k).wait_recv()
+            far_copy(which, k).start()
+            near_copy(which, k).start()
+            waiting.append(k)
+        return waiting
+
+    def spread(which):
+        for part in range(parts):
+            side_copy(which, part, 0).start()
+        for part in range(min(2, parts)):
+            for j in range(1, line):
+                across_copy(which, part, j).start()
+        for part in range(parts):
+            for j in range(1, line):
+                across_copy(which, part, j).wait_recv()
+                side_copy(which, part, j).start()
+            if part + 2 < parts:
+                for j in range(1, line):
+                    across_copy(which, part + 2, j).start()
+
+    def finish_rows(which, waiting):
+        for k in waiting:
+            far_copy(which, k).wait_recv()
+            back_copy(which, k).start()
+
+    for copy in locals_:
+        copy.start()
+    send_rows(0)
+    waiting = forward(0, None)
+    finish_now = lambda: finish_rows(0, waiting)
+    for part in range(parts):
+        side_copy(0, part, 0).start()
+    for part in range(min(2, parts)):
+        for j in range(1, line):
+            across_copy(0, part, j).start()
+    finish_now()
+    for part in range(parts):
+        for j in range(1, line):
+            across_copy(0, part, j).wait_recv()
+            side_copy(0, part, j).start()
+        if part + 2 < parts:
+            for j in range(1, line):
+                across_copy(0, part + 2, j).start()
+    send_rows(1)
+    waiting = forward(1, None)
+    spread(1)
+    finish_rows(1, waiting)
+    for copy in locals_[2:]:
+        copy.wait()
+    for which in range(2):
+        for k in range(size):
+            near_copy(which, k).wait_recv()
+            back_copy(which, k).wait_recv()
+            near_copy(which, k).wait_send()
+            back_copy(which, k).wait_send()
+            far_copy(which, k).wait_send()
+            if k:
+                rows_copy(which, k).wait_send()
+        for part in range(parts):
+            for j in range(line):
+                side_copy(which, part, j).wait()
+                if j:
+                    across_copy(which, part, j).wait_send()
+
+
+def run_entry(tokens, cotangent, w_in, w_out):
+    size = lax.axis_size("dp")
+    parts = 4
+    rows, quarter = tokens.shape
+    deep = quarter * 4
+    block = rows // size
+    shard = w_in.shape[0]
+    line = size // 2
+    cut = lambda w: w.reshape(parts, shard // parts, w.shape[1])
+    full = lambda w: jax.ShapeDtypeStruct((size, parts, shard // parts, w.shape[1]), BF16)
+    sems = pltpu.SemaphoreType.DMA
+    outs = pl.pallas_call(
+        functools.partial(entry_kernel, parts),
+        in_specs=[pl.BlockSpec(memory_space=pl.ANY)] * 4,
+        out_specs=[pl.BlockSpec(memory_space=pl.ANY)] * 4,
+        out_shape=[jax.ShapeDtypeStruct((size, block, deep), BF16)] * 2 + [full(w_in), full(w_out)],
+        scratch_shapes=[sems((2, 2, size))] * 4 + [sems((2, 2, parts, line))] * 2 + [sems((4,))],
+        compiler_params=pltpu.CompilerParams(collective_id=0, has_side_effects=True, vmem_limit_bytes=1024 * 1024),
+        name="entry",
+    )(tokens.reshape(size, block, quarter), cotangent.reshape(size, block, quarter), cut(w_in), cut(w_out))
+    return (
+        outs[0].reshape(rows, deep),
+        outs[1].reshape(rows, deep),
+        outs[2].reshape(size * shard, w_in.shape[1]),
+        outs[3].reshape(size * shard, w_out.shape[1]),
+    )
 
 
 def mm(a, b, contract, kind):
     return lax.dot_general(a, b, (contract, ((), ())), preferred_element_type=F32).astype(kind)
+
+
+def swap(value, axis, bit):
+    size = lax.axis_size(axis)
+    return lax.ppermute(value, axis, [(i, i ^ (1 << bit)) for i in range(size)])
+
+
+def bits_of(axis):
+    return lax.axis_size(axis).bit_length() - 1
+
+
+def scatter_rows(value, axis):
+    place = lax.axis_index(axis)
+    count = bits_of(axis)
+    size = lax.axis_size(axis)
+    current = value.reshape(size, -1, value.shape[1])
+    bit = 0
+    while count - bit > 2:
+        current = current.reshape(-1, 2, current.shape[1], current.shape[2])
+        mine = (place >> bit) & 1
+        keep = lax.dynamic_index_in_dim(current, mine, 1, keepdims=False)
+        send = lax.dynamic_index_in_dim(current, 1 - mine, 1, keepdims=False)
+        current = keep.astype(F32) + swap(send.astype(BF16), axis, bit).astype(F32)
+        bit += 1
+    high = place >> bit
+    total = lax.dynamic_index_in_dim(current, high, 0, keepdims=False).astype(F32)
+    low_current = current.astype(BF16)
+    for k in (2, 3, 1)[: 2 ** (count - bit)]:
+        send = lax.dynamic_index_in_dim(low_current, high ^ k, 0, keepdims=False)
+        total = total + lax.ppermute(send, axis, [(i, i ^ (k << bit)) for i in range(size)]).astype(F32)
+    return total
+
+
+def sum_all(value, axis):
+    for bit in range(bits_of(axis)):
+        value = value + swap(value, axis, bit)
+    return value
+
+
+def head_sum(pieces):
+    from_third, from_first = swap((pieces[3], pieces[1]), "head", 0)
+    passed = (pieces[2].astype(F32) + from_third.astype(F32)).astype(BF16)
+    arrived = swap(passed, "head", 1)
+    return pieces[0].astype(F32) + from_first.astype(F32) + arrived.astype(F32)
 
 
 def body(tokens, cotangent, order, lengths, norm_gain, w_zx, w_bc, w_dt, w_out, conv_x, conv_bc, head_params, gate_gain):
@@ -441,13 +750,11 @@
     heads = head_params.shape[1]
     width = heads * HEAD
     place = lax.axis_index("head")
+    me = place.astype(jnp.int32).reshape(1)
     groups = lax.axis_size("head")
     all_width = width * groups
     deep = quarter * groups
     arrange = order[0]
-
-    arrived_x = lax.all_to_all(tokens, "dp", split_axis=0, concat_axis=0, tiled=True)
-    own_x = arrived_x[arrange]
     own_w = w_zx.shape[0]
     packed = jnp.concatenate(
         [
@@ -459,19 +766,17 @@
         ],
         axis=1,
     )
-    w_in = lax.all_gather(packed, "dp", axis=0, tiled=True)
-    full_x = lax.all_gather(own_x, "head", axis=1, tiled=True)
-    arrived_g = lax.all_to_all(cotangent, "dp", split_axis=0, concat_axis=0, tiled=True)
-    own_g = arrived_g[arrange]
-    full_g = lax.all_gather(own_g, "head", axis=1, tiled=True)
-    w_o = lax.all_gather(w_out, "dp", axis=0, tiled=True)
+    came_x, came_g, w_in, w_o = run_entry(tokens, cotangent, packed, w_out)
+    full_x = came_x[arrange]
+    full_g = came_g[arrange]
+    w_zx_in, w_bd = w_in[:, : 2 * width], w_in[:, 2 * width :]
 
     gain = w_in[:, 2 * width + 2 * N + heads].astype(F32)
-    xf = full_x.astype(F32)
-    inv_one = lax.rsqrt(jnp.mean(xf * xf, axis=1, keepdims=True) + EPS)
-    normed = (xf * inv_one * gain).astype(BF16)
-    u_zx = mm(normed, w_in[:, : 2 * width], ((1,), (0,)), BF16)
-    u_bd = mm(normed, w_in[:, 2 * width :], ((1,), (0,)), F32)
+    normed, inv_one = run_norm(full_x, jnp.broadcast_to(gain[None], (8, deep)))
+    inv_one = inv_one.reshape(rows, 1)
+    own_x = lax.dynamic_slice_in_dim(full_x, place * quarter, quarter, 1)
+    u_zx = mm(normed, w_zx_in, ((1,), (0,)), BF16)
+    u_bd = mm(normed, w_bd, ((1,), (0,)), F32)
 
     par = jnp.concatenate([conv_x, jnp.repeat(head_params[2:3], HEAD, axis=1), gate_gain[None], jnp.zeros((1, width), F32)], axis=0)
     pbc = jnp.concatenate([conv_bc, jnp.zeros((3, 2 * N), F32)], axis=0)
@@ -484,48 +789,70 @@
     ss, co = lax.psum((ss, co), "head")
     yg, dz, dy, gg, rd_z = run_mid(all_width, y, u_zx, dyn, par, mask, ss, co)
 
-    branch = mm(yg, w_o, ((1,), (1,)), BF16)
-    shares = lax.psum_scatter(branch, "head", scatter_dimension=1, tiled=True)
     grad_out = mm(full_g, yg, ((0,), (0,)), BF16)
-    grad_out = lax.psum_scatter(grad_out, "dp", scatter_dimension=0, tiled=True)
-    grad_z = mm(normed, dz, ((0,), (0,)), BF16)
-    grad_z = lax.psum_scatter(grad_z, "dp", scatter_dimension=0, tiled=True)
-
-    out_rows = (own_x.astype(F32) + shares.astype(F32)).astype(BF16)
-    sent_out = jnp.zeros_like(out_rows).at[arrange].set(out_rows)
-    final_out = lax.all_to_all(sent_out, "dp", split_axis=0, concat_axis=0, tiled=True)
-
-    dux, dbd, gx, gb, gh, rd_x = run_backward(heads, dy, u_zx, c, cb, u_bd, st, par, pbc, hp)
-
-    terms = mm(dz, w_in[:, :width], ((1,), (1,)), F32)
-    terms = terms + mm(dux, w_in[:, width : 2 * width], ((1,), (1,)), F32)
-    terms = terms + mm(dbd, w_in[:, 2 * width :], ((1,), (1,)), F32)
-    dxn = lax.psum_scatter(terms.astype(BF16), "head", scatter_dimension=1, tiled=True).astype(F32)
+    out_pieces = run_pieces(me, [yg], [w_o], quarter, 0, rows, "branch_pieces")
+    grad_out = scatter_rows(grad_out, "dp")
+    from_third, from_first = swap((out_pieces[3], out_pieces[1]), "head", 0)
+    passed = (out_pieces[2].astype(F32) + from_third.astype(F32)).astype(BF16)
+    grad_z = scatter_rows(mm(normed, dz, ((0,), (0,)), BF16), "dp")
+
+    slots = rows // LEN
+    deps = list(out_pieces)
+    parts = []
+    for slot in range(slots):
+        if slot == 0:
+            own = run_backward(heads, slot, 1, dy, u_zx, c, cb, u_bd, st, par, pbc, hp, deps, [(("head", 2), passed)], 1)
+            shares = (out_pieces[0].astype(F32) + from_first.astype(F32) + own[6].astype(F32)).astype(BF16)
+            sent_out = jnp.zeros_like(shares).at[arrange].set(shares)
+            final_out = lax.all_to_all(sent_out, "dp", split_axis=0, concat_axis=0, tiled=True)
+            final_out = (tokens.astype(F32) + final_out.astype(F32)).astype(BF16)
+        else:
+            own = run_backward(heads, slot, 1, dy, u_zx, c, cb, u_bd, st, par, pbc, hp, deps)
+        start = slot * LEN
+        d_pieces = run_pieces(
+            me,
+            [lax.slice_in_dim(dz, start, start + LEN, axis=0), own[0], own[1]],
+            [w_in[:, :width], w_in[:, width : 2 * width], w_bd],
+            quarter,
+            0,
+            LEN,
+            "input_pieces",
+        )
+        parts.append((own, head_sum(d_pieces)))
+        deps = list(d_pieces)
+    dxn = jnp.concatenate([part[1] for part in parts], axis=0)
+    rd_x = jnp.concatenate([part[0][5] for part in parts], axis=0)
+    gx, gb, gh = (sum(part[0][i] for part in parts) for i in (2, 3, 4))
     row_dot = lax.psum(rd_z + rd_x, "head").reshape(rows, 1)
 
-    grad_x = mm(normed, dux, ((0,), (0,)), BF16)
-    grad_x = lax.psum_scatter(grad_x, "dp", scatter_dimension=0, tiled=True)
-    grad_bd = mm(normed, dbd, ((0,), (0,)), BF16)
-    grad_bd = lax.psum_scatter(grad_bd, "dp", scatter_dimension=0, tiled=True).astype(F32)
-    grad_bc = lax.psum(grad_bd[:, : 2 * N], "head")
+    def over_slots(pick):
+        return sum(
+            mm(lax.slice_in_dim(normed, slot * LEN, slot * LEN + LEN, axis=0), parts[slot][0][pick], ((0,), (0,)), F32) for slot in range(slots)
+        ).astype(BF16)
+
+    grad_x = scatter_rows(over_slots(0), "dp")
+    grad_bd = scatter_rows(over_slots(1), "dp")
+    grad_bc = sum_all(grad_bd[:, : 2 * N], "head")
     grad_dt = grad_bd[:, 2 * N : 2 * N + heads]
 
     gain_own = lax.dynamic_slice_in_dim(gain, place * quarter, quarter, 0)
-    inv_own = inv_one
-    xs = own_x.astype(F32)
-    grad_rows = own_g.astype(F32) + inv_own * gain_own * dxn - xs * inv_own**2 * (row_dot / deep)
-    grad_rows = grad_rows.astype(BF16)
-    gain_part = jnp.sum(dxn * xs * inv_own, axis=0)
+    hat = own_x.astype(F32) * inv_one
+    grad_rows = (inv_one * (gain_own * dxn - hat * (row_dot / deep))).astype(BF16)
+    gain_part = jnp.sum(dxn * hat, axis=0)
     sent_back = jnp.zeros_like(grad_rows).at[arrange].set(grad_rows)
     final_back = lax.all_to_all(sent_back, "dp", split_axis=0, concat_axis=0, tiled=True)
-
+    final_back = (cotangent.astype(F32) + final_back.astype(F32)).astype(BF16)
+
+    small = jnp.concatenate([gx[:5].reshape(-1), gg[0], gh[:3].reshape(-1)])
+    small = sum_all(small, "dp")
+    gx, gg, gh = small[: 5 * width].reshape(5, width), small[5 * width : 6 * width], small[6 * width :].reshape(3, 128)[:, :heads]
     gain_part = lax.dynamic_update_slice_in_dim(jnp.zeros((deep,), F32), gain_part, place * quarter, 0)
-    gx, gh, gg = lax.psum((gx[:5], gh[:3, :heads], gg[0]), "dp")
-    gain_all, gb = lax.psum((gain_part, gb[:5]), ("dp", "head"))
+    shared = sum_all(sum_all(jnp.concatenate([gb[:5].reshape(-1), gain_part]), "head"), "dp")
+    gb, gain_all = shared[: 10 * N].reshape(5, 2 * N), shared[10 * N :]
     own_d = norm_gain.shape[0]
     grad_gain = lax.dynamic_slice_in_dim(gain_all, lax.axis_index("dp") * own_d, own_d, 0)
-    grad_zx = jnp.stack([grad_z, grad_x], axis=1).astype(F32)
-    return (final_out, final_back, grad_gain, grad_zx, grad_bc, grad_dt, grad_out.astype(F32), gx, gb, gh, gg)
+    grad_zx = jnp.stack([grad_z, grad_x], axis=1)
+    return (final_out, final_back, grad_gain, grad_zx, grad_bc, grad_dt, grad_out, gx, gb, gh, gg)
 
 
 def solution(mesh):

time: 879 us -> 733 us (0.83)
  waiting for transfers between devices: 356 us -> 83.3 us
  Pallas kernels: 95.7 us -> 347 us
  blocking collectives: 193 us -> 17.9 us
  starting transfers between devices: 18.3 us -> 63.9 us
  matrix products: 97.7 us -> 57.8 us
  other arithmetic: 33.9 us -> 68.7 us
  local copies, waits for them, and re-layouts: 59.9 us -> 81.5 us
  between operations: 14.4 us -> 1.81 us
    pallas_call x1 -> x7, Pallas kernels: 47.1 us -> 298 us  [the longest x1 173 us: run_entry(): pl.pallas_call(functools.partial(entry_kernel, parts), in_specs=[pl.Block...]
    reduce_scatter x4 -> x0, waiting for transfers between devices: 196 us -> none  [the longest x1 71.6 us: body(): grad_x = lax.psum_scatter(grad_x, 'dp', scatter_dimension=0, tiled=True)]
    psum x2 -> x0, blocking collectives: 99.2 us -> none  [the longest x1 59.6 us: body(): gx, gh, gg = lax.psum((gx[:5], gh[:3, :heads], gg[0]), 'dp')]
    all_gather x4 -> x0, waiting for transfers between devices: 87.9 us -> none  [the longest x1 46.9 us: body(): full_g = lax.all_gather(own_g, 'head', axis=1, tiled=True)]
    ppermute x0 -> x34, waiting for transfers between devices: none -> 83.3 us  [the longest x12 44.3 us: scatter_rows(): lax.ppermute(send, axis, [(i, i ^ k << bit) for i in range(size)])]
    all_to_all x1 -> x0, blocking collectives: 75.9 us -> none  [body(): lax.all_to_all(cotangent, 'dp', split_axis=0, concat_axis=0, tiled=True)]
    all_to_all x1 -> x0, waiting for transfers between devices: 60.6 us -> none  [body(): lax.all_to_all(tokens, 'dp', split_axis=0, concat_axis=0, tiled=True)]
    ppermute x0 -> x34, starting transfers between devices: none -> 49 us  [the longest x22 25.8 us: swap(): return lax.ppermute(value, axis, [(i, i ^ 1 << bit) for i in range(size)])]
  transfers between devices with their start and end apart: 14 -> 36, of which waited for: 8 -> 10; matrix products, arithmetic and copies ran while one was open for 19% -> 15% of each run, Pallas kernels for 8% -> 16%
where the time goes in v2:
time: 733 us; the launch traced here: 722 us
  Pallas kernels  347 us (47%)
  waiting for transfers between devices  83.3 us (11%)
  local copies, waits for them, and re-layouts  81.5 us (11%)
  other arithmetic  68.7 us (9%)
  starting transfers between devices  63.9 us (9%)
  matrix products  57.8 us (8%)
  blocking collectives  17.9 us (2%)
    pallas_call x1, Pallas kernels, run_entry(): pl.pallas_call(functools.partial(entry_kernel, parts), in_specs=[pl.Block...  173 us
    pallas_call x2, Pallas kernels, run_backward(): pl.pallas_call(functools.partial(backward_kernel, heads, len(deps), tuple...  77.8 us
    dot_general x8, matrix products, mm(): lax.dot_general(a, b, (contract, ((), ())), preferred_element_type=F32)  57.8 us
    ppermute x12, waiting for transfers between devices, scatter_rows(): lax.ppermute(send, axis, [(i, i ^ k << bit) for i in range(size)])  44.3 us
    ppermute x22, waiting for transfers between devices, swap(): return lax.ppermute(value, axis, [(i, i ^ 1 << bit) for i in range(size)])  39 us
    pallas_call x3, Pallas kernels, run_pieces(): pl.pallas_call(functools.partial(pieces_kernel, len(values)), grid_spec=p...  38 us
    ppermute x22, starting transfers between devices, swap(): return lax.ppermute(value, axis, [(i, i ^ 1 << bit) for i in range(size)])  25.8 us
    pallas_call x1, Pallas kernels, run_forward(): pl.pallas_call(functools.partial(forward_kernel, heads), grid=(slots, chu...  24.2 us
  transfers between devices with their start and end apart: 36, of which 10 were waited for; matrix products, arithmetic and copies ran while one was open for 15% of the time, Pallas kernels for 16%

profile of v2, /device:TPU:0, one launch (start us, length us, event | category | flops | bytes accessed | tf_op | source)
XLA Modules:
  0.0 722.2 jit_solution(11244163422819358171)
XLA Ops:
  7.9 173.2 %entry.1 = (bf16[8,256,1536]{2,1,0:T(8,128)(2,1)S(1)}, bf16[8,256,1536]{2,1,0:T(8,128)(2,1)S(1)}, bf16[8,4,48,1920]{3,2,1,0:T(8,128)(2,1)S(1)}, bf16[8,4,48,768]{3,2,1,0:T(8,128)(2,1)S(1)}) custom-call(bf16[8,256,384]{2,1,0:T(8,128)(2,1)S(1)} %bitcast.133, bf16[8,256,384]{2,1,0:T(8,128)(2,1)S(1)} %bitcast.134, bf16[4,48,1920]{2,1,0:T(8,128)(2,1)S(1)} %concatenate.34.refs_2_, ...), custom_call_target="tpu_custom_call" | custom-call | tf_op jit(solution)/shard_map/entry/pallas_call | solution.py:683
  190.8 16.9 %gather_fusion = bf16[2048,1536]{1,0:T(8,128)(2,1)} fusion(bf16[2048,1536]{1,0:T(8,128)(2,1)} %bitcast.126, s32[2048]{0:T(1024)S(1)} %broadcast_clamp_fusion), kind=kCustom, calls=%fused_computation | custom fusion | bytes 12591104 | tf_op jit(solution)/shard_map/gather | solution.py:770
  208.3 9.2 %norm_rows.1 = (bf16[2048,1536]{1,0:T(8,128)(2,1)}, f32[16,1,128]{2,1,0:T(1,128)}) custom-call(bf16[2048,1536]{1,0:T(8,128)(2,1)} %gather_fusion, f32[8,1536]{1,0:T(8,128)} %broadcast_in_dim.15.gain_ref), custom_call_target="tpu_custom_call" | custom-call | flops 18874368 | bytes 12582912 | tf_op jit(solution)/shard_map/norm_rows/pallas_call | solution.py:387
  217.5 8.0 %fusion.29.ubd_ref = f32[2048,384]{1,0:T(8,128)} fusion(bf16[2048,1536]{1,0:T(8,128)(2,1)} %get-tuple-element.56, bf16[1536,1920]{1,0:T(8,128)(2,1)S(1)} %bitcast.131), kind=kOutput, calls=%fused_computation.94 | convolution fusion | flops 2415919104 | bytes 10616832 | tf_op jit(solution)/shard_map/dot_general | solution.py:701
  225.5 11.8 %convolution_convert_fusion.x_ref.z_ref = bf16[2048,1536]{1,0:T(8,128)(2,1)} fusion(bf16[2048,1536]{1,0:T(8,128)(2,1)S(1)} %copy-done.37, bf16[1536,1920]{1,0:T(8,128)(2,1)S(1)} %bitcast.132), kind=kOutput, calls=%fused_computation.4 | convolution fusion | flops 9666822144 | bytes 17301504 | tf_op jit(solution)/shard_map/dot_general | solution.py:701
  238.9 17.1 %gather_fusion.1 = bf16[2048,1536]{1,0:T(8,128)(2,1)} fusion(bf16[2048,1536]{1,0:T(8,128)(2,1)} %bitcast.125, s32[2048]{0:T(1024)S(1)} %broadcast_clamp_fusion), kind=kCustom, calls=%fused_computation.1 | custom fusion | bytes 12591104 | tf_op jit(solution)/shard_map/gather | solution.py:771
  257.5 24.2 %scan_forward.1 = (bf16[2048,768]{1,0:T(8,128)(2,1)}, f32[16,1,128]{2,1,0:T(1,128)}, bf16[2048,768]{1,0:T(8,128)(2,1)}, f32[2048,256]{1,0:T(8,128)}, bf16[16,128,768]{2,1,0:T(8,128)(2,1)}) custom-call(bf16[2048,1536]{1,0:T(8,128)(2,1)} %convolution_convert_fusion.x_ref.z_ref, bf16[2048,1536]{1,0:T(8,128)(2,1)} %convolution_convert_fusion.x_ref.z_ref, ...), custom_call_target="tpu_custom_call" | custom-call | flops 3774873600 | bytes 12582912 | tf_op jit(solution)/shard_map/scan_forward/pallas_call | solution.py:351
  281.6 12.3 %gate_back.1 = (bf16[2048,768]{1,0:T(8,128)(2,1)}, f32[16,1,128]{2,1,0:T(1,128)}) custom-call(bf16[2048,1536]{1,0:T(8,128)(2,1)} %gather_fusion.1, bf16[1536,768]{1,0:T(8,128)(2,1)} %bitcast.135, bf16[2048,768]{1,0:T(8,128)(2,1)} %get-tuple-element.57.y_ref, bf16[2048,1536]{1,0:T(8,128)(2,1)} %convolution_convert_fusion.x_ref.z_ref, ...), custom_call_target="tpu_custom_call" | custom-call | flops 4831838208 | bytes 15728640 | tf_op jit(solution)/shard_map/gate_back/pallas_call | solution.py:406
  293.9 11.3 %all-reduce.2 = (f32[16,1,128]{2,1,0:T(1,128)}, f32[16,1,128]{2,1,0:T(1,128)}) all-reduce(f32[16,1,128]{2,1,0:T(1,128)S(1)} %copy-done.31, f32[16,1,128]{2,1,0:T(1,128)} %get-tuple-element.62), channel_id=1, replica_groups=mesh['dp'=8,'head'=4] {'head'}, use_global_device_ids=true, to_apply=%region_0.1 | all-reduce | flops 4096 | bytes 32768 | tf_op jit(solution)/shard_map/psum | solution.py:789
  305.3 12.6 %gate_mid.1 = (bf16[2048,768]{1,0:T(8,128)(2,1)}, bf16[2048,768]{1,0:T(8,128)(2,1)}, bf16[2048,768]{1,0:T(8,128)(2,1)}, f32[8,768]{1,0:T(8,128)}, f32[16,1,128]{2,1,0:T(1,128)}) custom-call(bf16[2048,768]{1,0:T(8,128)(2,1)} %get-tuple-element.57.y_ref, bf16[2048,1536]{1,0:T(8,128)(2,1)} %convolution_convert_fusion.x_ref.z_ref, ...), custom_call_target="tpu_custom_call" | custom-call | flops 47185920 | bytes 18874368 | tf_op jit(solution)/shard_map/gate_mid/pallas_call | solution.py:432
  317.9 8.4 %convolution_convert_fusion.1 = bf16[1536,768]{1,0:T(8,128)(2,1)} fusion(bf16[2048,1536]{1,0:T(8,128)(2,1)S(1)} %copy-done.10, bf16[2048,768]{1,0:T(8,128)(2,1)} %get-tuple-element.63.refs_0_), kind=kOutput, calls=%fused_computation.7 | convolution fusion | flops 4833017856 | bytes 11796480 | tf_op jit(solution)/shard_map/dot_general | solution.py:701
  329.0 8.2 %convolution_convert_fusion.2 = bf16[1536,768]{1,0:T(8,128)(2,1)S(1)} fusion(bf16[2048,1536]{1,0:T(8,128)(2,1)} %get-tuple-element.56, bf16[2048,768]{1,0:T(8,128)(2,1)} %get-tuple-element.74), kind=kOutput, calls=%fused_computation.8 | convolution fusion | flops 4833017856 | bytes 11796480 | tf_op jit(solution)/shard_map/dot_general | solution.py:701
  339.1 10.9 %branch_pieces.1 = (bf16[2048,384]{1,0:T(8,128)(2,1)}, bf16[2048,384]{1,0:T(8,128)(2,1)}, bf16[2048,384]{1,0:T(8,128)(2,1)}, bf16[2048,384]{1,0:T(8,128)(2,1)}) custom-call(s32[1]{0:T(128)} %bitcast.2.me_ref, bf16[2048,768]{1,0:T(8,128)(2,1)} %get-tuple-element.63.refs_0_, bf16[1536,768]{1,0:T(8,128)(2,1)} %bitcast.136), custom_call_target="tpu_custom_call" | custom-call | flops 4831838208 | bytes 9437184 | tf_op jit(solution)/shard_map/branch_pieces/pallas_call | solution.py:520
  366.8 13.5 %collective-permute-done.13 = bf16[4,192,768]{2,1,0:T(8,128)(2,1)} collective-permute-done((bf16[4,192,768]{2,1,0:T(8,128)(2,1)S(1)}, bf16[4,192,768]{2,1,0:T(8,128)(2,1)}, u32[]{:S(2)}, u32[]{:S(2)}) %collective-permute-start.13) | collective-permute-done | bytes 1179680 | tf_op jit(solution)/shard_map/ppermute | solution.py:706
  402.0 13.1 %collective-permute-done.14 = bf16[192,768]{1,0:T(8,128)(2,1)S(1)} collective-permute-done((bf16[192,768]{1,0:T(8,128)(2,1)}, bf16[192,768]{1,0:T(8,128)(2,1)S(1)}, u32[]{:S(2)}, u32[]{:S(2)}) %collective-permute-start.14) | collective-permute-done | bytes 294944 | tf_op jit(solution)/shard_map/ppermute | solution.py:731
  420.2 53.3 %scan_backward.2 = (bf16[1024,768]{1,0:T(8,128)(2,1)}, bf16[1024,384]{1,0:T(8,128)(2,1)}, f32[8,768]{1,0:T(8,128)}, f32[8,256]{1,0:T(8,128)}, f32[8,128]{1,0:T(8...) custom-call(bf16[2048,768]{1,0:T(8,128)(2,1)} %get-tuple-element.66.dy_ref, ...), custom_call_target="tpu_custom_call" | custom-call | flops 4718592000 | bytes 9437184 | tf_op jit(solution)/shard_map/scan_backward/pallas_call | solution.py:454
  473.6 11.5 %scatter_custom_fusion = bf16[2048,384]{1,0:T(8,128)(2,1)} fusion(s32[2048]{0:T(1024)S(1)} %bitcast.156, bf16[2048,384]{1,0:T(8,128)(2,1)} %get-tuple-element.72, bf16[2048,384]{1,0:T(8,128)(2,1)} %collective-permute-done, bf16[2048,384]{1,0:T(8,128)(2,1)S(1)} %copy-done.11, bf16[]{:T(256)} %constant.89.clone.1), kind=kCustom, calls=%fused_computation.30 | custom fusion | flops 4718592 | bytes 6291458 | tf_op jit(solution)/shard_map/scatter | solution.py:806
  485.1 10.4 %all-to-all-start = ((bf16[8,256,384]{2,1,0:T(8,128)(2,1)}), bf16[8,256,384]{2,1,0:T(8,128)(2,1)}, u32[]{:S(2)}, u32[]{:S(2)}) async-start(bf16[8,256,384]{2,1,0:T(8,128)(2,1)} %bitcast.14), calls=%async_computation | async-start | bytes 3145728 | tf_op jit(solution)/shard_map/all_to_all | solution.py:807
  502.1 13.4 %input_pieces.2 = (bf16[1024,384]{1,0:T(8,128)(2,1)}, bf16[1024,384]{1,0:T(8,128)(2,1)}, bf16[1024,384]{1,0:T(8,128)(2,1)}, bf16[1024,384]{1,0:T(8,128)(2,1)}) custom-call(s32[1]{0:T(128)} %bitcast.2.me_ref, bf16[1024,768]{1,0:T(8,128)(2,1)} %get-tuple-element.131.refs_0_, bf16[1024,768]{1,0:T(8,128)(2,1)} %get-tuple-element.75.refs_1_, ...), custom_call_target="tpu_custom_call" | custom-call | flops 6039797760 | bytes 7077888 | tf_op jit(solution)/shard_map/input_pieces/pallas_call | solution.py:520
  516.0 24.4 %scan_backward.3 = (bf16[1024,768]{1,0:T(8,128)(2,1)}, bf16[1024,384]{1,0:T(8,128)(2,1)}, f32[8,768]{1,0:T(8,128)}, f32[8,256]{1,0:T(8,128)}, f32[8,128]{1,0:T(8,128)}, /*index=5*/f32[8,1,128]{2,1,0:T(1,128)}) custom-call(bf16[2048,768]{1,0:T(8,128)(2,1)} %get-tuple-element.66.dy_ref, bf16[2048,1536]{1,0:T(8,128)(2,1)} %convolution_convert_fusion.x_ref.z_ref, ...), custom_call_target="tpu_custom_call" | custom-call | flops 4718592000 | bytes 9437184 | tf_op jit(solution)/shard_map/scan_backward/pallas_call | solution.py:454
  549.4 13.7 %input_pieces.3 = (bf16[1024,384]{1,0:T(8,128)(2,1)}, bf16[1024,384]{1,0:T(8,128)(2,1)}, bf16[1024,384]{1,0:T(8,128)(2,1)}, bf16[1024,384]{1,0:T(8,128)(2,1)}) custom-call(s32[1]{0:T(128)} %bitcast.2.me_ref, bf16[1024,768]{1,0:T(8,128)(2,1)} %get-tuple-element.132.refs_0_, bf16[1024,768]{1,0:T(8,128)(2,1)} %get-tuple-element.81.refs_1_, ...), custom_call_target="tpu_custom_call" | custom-call | flops 6039797760 | bytes 7077888 | tf_op jit(solution)/shard_map/input_pieces/pallas_call | solution.py:520
  617.8 11.7 %collective-permute-done.7 = bf16[1024,384]{1,0:T(8,128)(2,1)} collective-permute-done((bf16[1024,384]{1,0:T(8,128)(2,1)S(1)}, bf16[1024,384]{1,0:T(8,128)(2,1)}, u32[]{:S(2)}, u32[]{:S(2)}) %collective-permute-start.7) | collective-permute-done | bytes 786464 | tf_op jit(solution)/shard_map/ppermute | solution.py:706
  631.2 12.5 %scatter_custom_fusion.1 = bf16[2048,384]{1,0:T(8,128)(2,1)} fusion(s32[2048]{0:T(1024)} %bitcast.157, f32[1024,384]{1,0:T(8,128)S(1)} %convert_add_fusion.5, f32[]{:T(128)} %constant.114, f32[1024,384]{1,0:T(8,128)S(1)} %convert_add_fusion.6, f32[2048]{0:T(1024)S(1)} %bitcast.154, f32[384]{0:T(512)S(1)} %dynamic-slice_reduce_fusion, ...), kind=kCustom, calls=%fused_computation.31 | custom fusion | flops 6291456 | bytes 6310916 | tf_op jit(solution)/shard_map/scatter | solution.py:842
  676.5 29.1 %collective-permute-done.18 = bf16[192,768]{1,0:T(8,128)(2,1)S(1)} collective-permute-done((bf16[192,768]{1,0:T(8,128)(2,1)S(1)}, bf16[192,768]{1,0:T(8,128)(2,1)S(1)}, u32[]{:S(2)}, u32[]{:S(2)}) %collective-permute-start.18) | collective-permute-done | bytes 294944 | tf_op jit(solution)/shard_map/ppermute | solution.py:731
  (259 shorter events, 189.6 us)
Async XLA Ops:
  328.6 30.7 %collective-permute-start.27 = (bf16[4,192,768]{2,1,0:T(8,128)(2,1)}, bf16[4,192,768]{2,1,0:T(8,128)(2,1)}, u32[]{:S(2)}, u32[]{:S(2)}) collective-permute-start(bf16[4,192,768]{2,1,0:T(8,128)(2,1)} %dynamic-slice_bitcast_fusion), channel_id=1, source_target_pairs={{0,4},{4,0},{8,12},{12,8},{16,20},{20,16},{24,28},{28,24},{1,5},{5... | collective-permute-start | bytes 3538952 | tf_op jit(solution)/shard_map/ppermute | solution.py:706
  337.3 43.0 %collective-permute-start.13 = (bf16[4,192,768]{2,1,0:T(8,128)(2,1)S(1)}, bf16[4,192,768]{2,1,0:T(8,128)(2,1)}, u32[]{:S(2)}, u32[]{:S(2)}) collective-permute-start(bf16[4,192,768]{2,1,0:T(8,128)(2,1)S(1)} %dynamic-slice_bitcast_fusion.2), channel_id=1, source_target_pairs={{0,4},{4,0},{8,12},{12,8},{16,20},{20,16},{24,28},{28,24},{1,5},{5... | collective-permute-start | bytes 3538952 | tf_op jit(solution)/shard_map/ppermute | solution.py:706
  350.0 123.5 %collective-permute-start = (bf16[2048,384]{1,0:T(8,128)(2,1)}, bf16[2048,384]{1,0:T(8,128)(2,1)}, u32[]{:S(2)}, u32[]{:S(2)}) collective-permute-start(bf16[2048,384]{1,0:T(8,128)(2,1)} %get-tuple-element.65.refs_2_), channel_id=1, source_target_pairs={{0,1},{1,0},{2,3},{3,2},{4,5},{5,4},{6,7},{7,6},{8,9},{9,8},{10,11... | collective-permute-start | bytes 4718600 | tf_op jit(solution)/shard_map/ppermute | solution.py:706
  350.0 67.1 %collective-permute-start.1 = (bf16[2048,384]{1,0:T(8,128)(2,1)}, bf16[2048,384]{1,0:T(8,128)(2,1)}, u32[]{:S(2)}, u32[]{:S(2)}) collective-permute-start(bf16[2048,384]{1,0:T(8,128)(2,1)} %get-tuple-element.71.refs_4_), channel_id=1, source_target_pairs={{0,1},{1,0},{2,3},{3,2},{4,5},{5,4},{6,7},{7,6},{8,9},{9,8},{10,11... | collective-permute-start | bytes 4718600 | tf_op jit(solution)/shard_map/ppermute | solution.py:706
  362.5 26.0 %collective-permute-start.28 = (bf16[192,768]{1,0:T(8,128)(2,1)S(1)}, bf16[192,768]{1,0:T(8,128)(2,1)}, u32[]{:S(2)}, u32[]{:S(2)}) collective-permute-start(bf16[192,768]{1,0:T(8,128)(2,1)S(1)} %get-tuple-element.133), channel_id=1, source_target_pairs={{0,16},{4,20},{8,24},{12,28},{16,0},{20,4},{24,8},{28,12},{1,17},{... | collective-permute-start | bytes 884744 | tf_op jit(solution)/shard_map/ppermute | solution.py:731
  388.4 26.7 %collective-permute-start.14 = (bf16[192,768]{1,0:T(8,128)(2,1)}, bf16[192,768]{1,0:T(8,128)(2,1)S(1)}, u32[]{:S(2)}, u32[]{:S(2)}) collective-permute-start(bf16[192,768]{1,0:T(8,128)(2,1)} %get-tuple-element.136), channel_id=1, source_target_pairs={{0,16},{4,20},{8,24},{12,28},{16,0},{20,4},{24,8},{28,12},{1,17},{... | collective-permute-start | bytes 884744 | tf_op jit(solution)/shard_map/ppermute | solution.py:731
  388.4 26.7 %collective-permute-start.16 = (bf16[192,768]{1,0:T(8,128)(2,1)S(1)}, bf16[192,768]{1,0:T(8,128)(2,1)S(1)}, u32[]{:S(2)}, u32[]{:S(2)}) collective-permute-start(bf16[192,768]{1,0:T(8,128)(2,1)S(1)} %get-tuple-element.137), channel_id=1, source_target_pairs={{0,8},{4,12},{8,0},{12,4},{16,24},{20,28},{24,16},{28,20},{1,9},{5... | collective-permute-start | bytes 884744 | tf_op jit(solution)/shard_map/ppermute | solution.py:731
  391.2 24.0 %collective-permute-start.15 = (bf16[192,768]{1,0:T(8,128)(2,1)S(1)}, bf16[192,768]{1,0:T(8,128)(2,1)S(1)}, u32[]{:S(2)}, u32[]{:S(2)}) collective-permute-start(bf16[192,768]{1,0:T(8,128)(2,1)S(1)} %get-tuple-element.138), channel_id=1, source_target_pairs={{0,24},{4,28},{8,16},{12,20},{16,8},{20,12},{24,0},{28,4},{1,25},{... | collective-permute-start | bytes 884744 | tf_op jit(solution)/shard_map/ppermute | solution.py:731
  485.1 158.7 %all-to-all-start = ((bf16[8,256,384]{2,1,0:T(8,128)(2,1)}), bf16[8,256,384]{2,1,0:T(8,128)(2,1)}, u32[]{:S(2)}, u32[]{:S(2)}) async-start(bf16[8,256,384]{2,1,0:T(8,128)(2,1)} %bitcast.14), calls=%async_computation | async-start | bytes 3145728 | tf_op jit(solution)/shard_map/all_to_all | solution.py:807
  515.5 89.6 %collective-permute-start.2 = (bf16[1024,384]{1,0:T(8,128)(2,1)}, bf16[1024,384]{1,0:T(8,128)(2,1)}, u32[]{:S(2)}, u32[]{:S(2)}) collective-permute-start(bf16[1024,384]{1,0:T(8,128)(2,1)} %get-tuple-element.78.refs_1_), channel_id=1, source_target_pairs={{0,1},{1,0},{2,3},{3,2},{4,5},{5,4},{6,7},{7,6},{8,9},{9,8},{10,11... | collective-permute-start | bytes 2359304 | tf_op jit(solution)/shard_map/ppermute | solution.py:706
  515.5 73.3 %collective-permute-start.3 = (bf16[1024,384]{1,0:T(8,128)(2,1)}, bf16[1024,384]{1,0:T(8,128)(2,1)}, u32[]{:S(2)}, u32[]{:S(2)}) collective-permute-start(bf16[1024,384]{1,0:T(8,128)(2,1)} %get-tuple-element.80.refs_3_), channel_id=1, source_target_pairs={{0,1},{1,0},{2,3},{3,2},{4,5},{5,4},{6,7},{7,6},{8,9},{9,8},{10,11... | collective-permute-start | bytes 2359304 | tf_op jit(solution)/shard_map/ppermute | solution.py:706
  541.9 37.5 %collective-permute-start.31 = (f32[4992]{0:T(1024)S(1)}, f32[4992]{0:T(1024)S(1)}, u32[]{:S(2)}, u32[]{:S(2)}) collective-permute-start(f32[4992]{0:T(1024)S(1)} %pad_maximum_fusion.2), channel_id=1, source_target_pairs={{0,4},{4,0},{8,12},{12,8},{16,20},{20,16},{24,28},{28,24},{1,5},{5... | collective-permute-start | bytes 59912 | tf_op jit(solution)/shard_map/ppermute | solution.py:706
  563.2 29.6 %collective-permute-start.6 = (bf16[1024,384]{1,0:T(8,128)(2,1)}, bf16[1024,384]{1,0:T(8,128)(2,1)}, u32[]{:S(2)}, u32[]{:S(2)}) collective-permute-start(bf16[1024,384]{1,0:T(8,128)(2,1)} %get-tuple-element.86), channel_id=1, source_target_pairs={{0,1},{1,0},{2,3},{3,2},{4,5},{5,4},{6,7},{7,6},{8,9},{9,8},{10,11... | collective-permute-start | bytes 2359304 | tf_op jit(solution)/shard_map/ppermute | solution.py:706
  588.2 27.2 %collective-permute-start.5 = (bf16[1024,384]{1,0:T(8,128)(2,1)}, bf16[1024,384]{1,0:T(8,128)(2,1)}, u32[]{:S(2)}, u32[]{:S(2)}) collective-permute-start(bf16[1024,384]{1,0:T(8,128)(2,1)} %get-tuple-element.84), channel_id=1, source_target_pairs={{0,1},{1,0},{2,3},{3,2},{4,5},{5,4},{6,7},{7,6},{8,9},{9,8},{10,11... | collective-permute-start | bytes 2359304 | tf_op jit(solution)/shard_map/ppermute | solution.py:706
  588.8 61.5 %collective-permute-start.17 = (bf16[4,192,768]{2,1,0:T(8,128)(2,1)}, bf16[4,192,768]{2,1,0:T(8,128)(2,1)}, u32[]{:S(2)}, u32[]{:S(2)}) collective-permute-start(bf16[4,192,768]{2,1,0:T(8,128)(2,1)} %dynamic-slice_bitcast_fusion.1), channel_id=1, source_target_pairs={{0,4},{4,0},{8,12},{12,8},{16,20},{20,16},{24,28},{28,24},{1,5},{5... | collective-permute-start | bytes 3538952 | tf_op jit(solution)/shard_map/ppermute | solution.py:706
  599.5 30.1 %collective-permute-start.7 = (bf16[1024,384]{1,0:T(8,128)(2,1)S(1)}, bf16[1024,384]{1,0:T(8,128)(2,1)}, u32[]{:S(2)}, u32[]{:S(2)}) collective-permute-start(bf16[1024,384]{1,0:T(8,128)(2,1)S(1)} %add_convert_fusion.4), channel_id=1, source_target_pairs={{0,2},{1,3},{2,0},{3,1},{4,6},{5,7},{6,4},{7,5},{8,10},{9,11},{10,... | collective-permute-start | bytes 2359304 | tf_op jit(solution)/shard_map/ppermute | solution.py:706
  605.1 43.1 %collective-permute-start.23 = (bf16[192,384]{0,1:T(8,128)(2,1)}, bf16[192,384]{0,1:T(8,128)(2,1)}, u32[]{:S(2)}, u32[]{:S(2)}) collective-permute-start(bf16[192,384]{0,1:T(8,128)(2,1)} %bitcast.150), channel_id=1, source_target_pairs={{0,24},{4,28},{8,16},{12,20},{16,8},{20,12},{24,0},{28,4},{1,25},{... | collective-permute-start | bytes 442376 | tf_op jit(solution)/shard_map/ppermute | solution.py:731
  613.4 34.9 %collective-permute-start.24 = (bf16[192,384]{0,1:T(8,128)(2,1)}, bf16[192,384]{0,1:T(8,128)(2,1)}, u32[]{:S(2)}, u32[]{:S(2)}) collective-permute-start(bf16[192,384]{0,1:T(8,128)(2,1)} %bitcast.149), channel_id=1, source_target_pairs={{0,8},{4,12},{8,0},{12,4},{16,24},{20,28},{24,16},{28,20},{1,9},{5... | collective-permute-start | bytes 442376 | tf_op jit(solution)/shard_map/ppermute | solution.py:731
  615.4 32.9 %collective-permute-start.22 = (bf16[192,384]{0,1:T(8,128)(2,1)S(1)}, bf16[192,384]{0,1:T(8,128)(2,1)}, u32[]{:S(2)}, u32[]{:S(2)}) collective-permute-start(bf16[192,384]{0,1:T(8,128)(2,1)S(1)} %bitcast.148), channel_id=1, source_target_pairs={{0,16},{4,20},{8,24},{12,28},{16,0},{20,4},{24,8},{28,12},{1,17},{... | collective-permute-start | bytes 442376 | tf_op jit(solution)/shard_map/ppermute | solution.py:731
  643.7 75.1 %all-to-all-start.1 = ((bf16[8,256,384]{2,1,0:T(8,128)(2,1)}), bf16[8,256,384]{2,1,0:T(8,128)(2,1)}, u32[]{:S(2)}, u32[]{:S(2)}) async-start(bf16[8,256,384]{2,1,0:T(8,128)(2,1)} %bitcast.138), calls=%async_computation.1 | async-start | bytes 3145728 | tf_op jit(solution)/shard_map/all_to_all | solution.py:843
  659.2 46.4 %collective-permute-start.18 = (bf16[192,768]{1,0:T(8,128)(2,1)S(1)}, bf16[192,768]{1,0:T(8,128)(2,1)S(1)}, u32[]{:S(2)}, u32[]{:S(2)}) collective-permute-start(bf16[192,768]{1,0:T(8,128)(2,1)S(1)} %get-tuple-element.139), channel_id=1, source_target_pairs={{0,16},{4,20},{8,24},{12,28},{16,0},{20,4},{24,8},{28,12},{1,17},{... | collective-permute-start | bytes 884744 | tf_op jit(solution)/shard_map/ppermute | solution.py:731
  662.1 43.4 %collective-permute-start.20 = (bf16[192,768]{1,0:T(8,128)(2,1)S(1)}, bf16[192,768]{1,0:T(8,128)(2,1)S(1)}, u32[]{:S(2)}, u32[]{:S(2)}) collective-permute-start(bf16[192,768]{1,0:T(8,128)(2,1)S(1)} %get-tuple-element.140), channel_id=1, source_target_pairs={{0,8},{4,12},{8,0},{12,4},{16,24},{20,28},{24,16},{28,20},{1,9},{5... | collective-permute-start | bytes 884744 | tf_op jit(solution)/shard_map/ppermute | solution.py:731
  663.6 41.9 %collective-permute-start.19 = (bf16[192,768]{1,0:T(8,128)(2,1)S(1)}, bf16[192,768]{1,0:T(8,128)(2,1)S(1)}, u32[]{:S(2)}, u32[]{:S(2)}) collective-permute-start(bf16[192,768]{1,0:T(8,128)(2,1)S(1)} %get-tuple-element.141), channel_id=1, source_target_pairs={{0,24},{4,28},{8,16},{12,20},{16,8},{20,12},{24,0},{28,4},{1,25},{... | collective-permute-start | bytes 884744 | tf_op jit(solution)/shard_map/ppermute | solution.py:731
  675.7 31.0 %collective-permute-start.11 = (f32[2816]{0:T(1024)S(1)}, f32[2816]{0:T(1024)S(1)}, u32[]{:S(2)}, u32[]{:S(2)}) collective-permute-start(f32[2816]{0:T(1024)S(1)} %add.225), channel_id=1, source_target_pairs={{0,8},{4,12},{8,0},{12,4},{16,24},{20,28},{24,16},{28,20},{1,9},{5... | collective-permute-start | bytes 33800 | tf_op jit(solution)/shard_map/ppermute | solution.py:706
  (59 other events, 1174.9 us)

commit v3 on v1

--- a/solution.py
+++ b/solution.py
@@ -13,6 +13,8 @@
 HEAD = 64
 EPS = 1e-05
 NEG = -1e30
+LIMIT = 60 * 1024 * 1024
+AXES = ("dp", "head")
 F32 = jnp.float32
 BF16 = jnp.bfloat16
 
@@ -36,6 +38,161 @@
         lax.broadcasted_iota(jnp.int32, (rows, cols), 0),
         lax.broadcasted_iota(jnp.int32, (rows, cols), 1),
     )
+
+
+MESH = pl.DeviceIdType.MESH
+
+
+def greet(peers):
+    barrier = pltpu.get_barrier_semaphore()
+    for peer in peers:
+        pl.semaphore_signal(barrier, inc=1, device_id=peer, device_id_type=MESH)
+    pl.semaphore_wait(barrier, len(peers))
+
+
+def place_of():
+    return {name: lax.axis_index(name) for name in AXES}
+
+
+def move_copies(move, src, dst):
+    kind, axis = move[0], move[1]
+    place = place_of()
+    me = place[axis]
+
+    def peer(flip):
+        return tuple(place[name] ^ flip if name == axis else place[name] for name in AXES)
+
+    if kind == "whole":
+        return [(peer(move[2]), src, dst)], []
+    if kind == "rows":
+        return [(peer(move[2]), src.at[pl.ds(move[3], move[4])], dst)], []
+    if kind == "half":
+        return [(peer(1 << move[2]), src.at[:, 1 - ((me >> move[2]) & 1)], dst)], []
+    if kind == "direct":
+        high = me >> move[2]
+        return [(peer(j << move[2]), src.at[high ^ j], dst.at[j - 1]) for j in range(1, dst.shape[0] + 1)], []
+    if kind == "all":
+        groups = lax.axis_size("head")
+        flips = [divmod(flat, groups) for flat in range(1, dst.shape[0] + 1)]
+        return [((place["dp"] ^ f, place["head"] ^ e), src, dst.at[i]) for i, (f, e) in enumerate(flips)], []
+    if kind == "spread":
+        return [(peer(flip), src, dst.at[flip - 1]) for flip in range(1, dst.shape[0] + 1)], []
+    remote = [(peer(k), src.at[me ^ k], dst.at[me]) for k in turn_order(src.shape[0])]
+    return remote, [(src.at[me], dst.at[me])]
+
+
+def turn_order(size):
+    return sorted(range(1, size), key=lambda k: (-(k & ~1), k & 1))
+
+
+def move_shape(move, shape):
+    kind = move[0]
+    if kind == "rows":
+        return (move[4],) + shape[1:]
+    if kind == "half":
+        return (shape[0],) + shape[2:]
+    if kind == "direct":
+        return (shape[0] - 1,) + shape[1:]
+    if kind == "spread":
+        return (lax.axis_size(move[1]) - 1,) + shape
+    if kind == "all":
+        return (lax.axis_size("dp") * lax.axis_size("head") - 1,) + shape
+    return shape
+
+
+def move_counts(moves, values):
+    remote = local = 0
+    for move, value in zip(moves, values):
+        size = lax.axis_size(move[1])
+        world = lax.axis_size("dp") * lax.axis_size("head")
+        count = {"direct": value.shape[0] - 1, "spread": size - 1, "turn": size - 1, "all": world - 1}.get(move[0], 1)
+        remote, local = remote + count, local + (move[0] == "turn")
+    return remote, local
+
+
+def move_scratch(moves, values):
+    remote, local = move_counts(moves, values)
+    return [pltpu.SemaphoreType.DMA((2, remote)), pltpu.SemaphoreType.DMA((max(local, 1),))] if moves else []
+
+
+def move_outs(moves, values):
+    return [jax.ShapeDtypeStruct(move_shape(move, value.shape), value.dtype) for move, value in zip(moves, values)]
+
+
+def make_moves(moves, srcs, dsts, sems, local_sems):
+    remote, local = [], []
+    for move, src, dst in zip(moves, srcs, dsts):
+        here, there = move_copies(move, src, dst)
+        remote += here
+        local += there
+    copies = [
+        pltpu.make_async_remote_copy(src_ref=a, dst_ref=b, send_sem=sems.at[0, i], recv_sem=sems.at[1, i], device_id=peer, device_id_type=MESH)
+        for i, (peer, a, b) in enumerate(remote)
+    ]
+    copies += [pltpu.make_async_copy(a, b, local_sems.at[i]) for i, (a, b) in enumerate(local)]
+    return move_peers(moves, dsts), copies
+
+
+def move_peers(moves, dsts):
+    flips = {}
+    for move, dst in zip(moves, dsts):
+        kind, axis = move[0], move[1]
+        if kind in ("whole", "rows"):
+            own = [move[2]]
+        elif kind == "half":
+            own = [1 << move[2]]
+        elif kind == "direct":
+            own = [j << move[2] for j in range(1, dst.shape[0] + 1)]
+        elif kind == "all":
+            groups = lax.axis_size("head")
+            for flat in range(1, dst.shape[0] + 1):
+                flips[divmod(flat, groups)] = None
+            continue
+        elif kind == "spread":
+            own = range(1, dst.shape[0] + 1)
+        else:
+            own = range(1, dst.shape[0])
+        for flip in own:
+            flips[(flip, 0) if axis == "dp" else (0, flip)] = None
+    place = place_of()
+    return [(place["dp"] ^ f, place["head"] ^ e) for f, e in flips]
+
+
+def background(first, last, moves, srcs, dsts, sems, local_sems):
+    peers, copies = make_moves(moves, srcs, dsts, sems, local_sems)
+
+    @pl.when(first)
+    def _():
+        greet(peers)
+        for copy in copies:
+            copy.start()
+
+    @pl.when(last)
+    def _():
+        for copy in copies:
+            copy.wait()
+
+
+def exchange_kernel(moves, *refs):
+    count = len(moves)
+    peers, copies = make_moves(moves, refs[:count], refs[count : 2 * count], refs[2 * count], refs[2 * count + 1])
+    greet(peers)
+    for copy in copies:
+        copy.start()
+    for copy in copies:
+        copy.wait()
+
+
+def run_exchange(moves, values, number):
+    return pl.pallas_call(
+        functools.partial(exchange_kernel, tuple(moves)),
+        in_specs=[pl.BlockSpec(memory_space=pl.ANY)] * len(moves),
+        out_specs=[pl.BlockSpec(memory_space=pl.ANY)] * len(moves),
+        out_shape=move_outs(moves, values),
+        scratch_shapes=move_scratch(moves, values),
+        compiler_params=pltpu.CompilerParams(collective_id=number, has_side_effects=True, vmem_limit_bytes=LIMIT),
+        name="exchange",
+    )(*values)
 
 
 def sigmoid(v):
@@ -68,7 +225,76 @@
     return raw, steps, rates, logs
 
 
-def forward_kernel(heads, x_ref, z_ref, ubd_ref, par_ref, pbc_ref, head_ref, y_ref, ss_ref, c_ref, cb_ref, st_ref, ext_x, ext_b, state):
+def forward_moves(steps, rows_ref, w_ref, full_ref, fw_ref, pass_sems, across_sems, side_sems, local_sems):
+    size, quarter = rows_ref.shape[0], rows_ref.shape[2]
+    line = size // 2
+    parts = w_ref.shape[0]
+    me, own = lax.axis_index("dp"), lax.axis_index("head")
+    step = pl.program_id(0) * pl.num_programs(1) + pl.program_id(1)
+    far, near, back = row_forward(size, quarter, rows_ref, full_ref, pass_sems)
+    across, side = shard_spread(w_ref, fw_ref, across_sems, side_sems)
+    mine = pl.ds(pl.multiple_of(own * quarter, 128), quarter)
+    held = [
+        pltpu.make_async_copy(rows_ref, full_ref.at[:, :, mine], local_sems.at[0]),
+        pltpu.make_async_copy(w_ref, fw_ref.at[me], local_sems.at[1]),
+    ]
+
+    @pl.when(step == 0)
+    def _():
+        greet([(me ^ 1, own)] + [(me ^ (2 * j), own) for j in range(1, line)] + [(me, own ^ 1), (me, own ^ 2)])
+        for copy in held:
+            copy.start()
+        for k in range(size):
+            near(k).start()
+        for k in range(size // 2):
+            far(k).start()
+        for part in range(parts):
+            side(part, 0).start()
+        for part in range(min(2, parts)):
+            for j in range(1, line):
+                across(part, j).start()
+
+    for part in range(parts):
+
+        @pl.when(step == min(steps - 1, (part + 2) * steps // (parts + 1)))
+        def _():
+            for j in range(1, line):
+                across(part, j).wait_recv()
+                side(part, j).start()
+            if part + 2 < parts:
+                for j in range(1, line):
+                    across(part + 2, j).start()
+
+    groups = 4
+    for group in range(groups):
+        members = range(group * size // groups, (group + 1) * size // groups)
+
+        @pl.when(step == min(steps - 1, ((group + 1) * 3 * steps) // (2 * groups)))
+        def _():
+            for k in members:
+                far(k).wait_recv()
+                back(k).start()
+                if k < size // 2:
+                    far(k + size // 2).start()
+
+    @pl.when(step == steps - 1)
+    def _():
+        for copy in held:
+            copy.wait()
+        for k in range(size):
+            near(k).wait()
+            back(k).wait()
+            far(k).wait_send()
+        for part in range(parts):
+            for j in range(line):
+                side(part, j).wait()
+                if j:
+                    across(part, j).wait_send()
+
+
+def forward_kernel(heads, steps, x_ref, z_ref, ubd_ref, par_ref, pbc_ref, head_ref, rows_ref, w_ref, y_ref, ss_ref, c_ref, cb_ref, st_ref, full_ref, fw_ref, ext_x, ext_b, state, *sems):
+    forward_moves(steps, rows_ref, w_ref, full_ref, fw_ref, *sems)
+
     @pl.when(pl.program_id(1) == 0)
     def _():
         ext_x[0:8] = jnp.zeros_like(ext_x[0:8])
@@ -127,6 +353,40 @@
     ss_ref[0] = to_row(jnp.sum(squares, axis=1, keepdims=True))
 
 
+def row_picks(order_ref, count):
+    lane = lax.broadcasted_iota(jnp.int32, (T, T), 1).astype(F32)
+    blocks = []
+    for part in range(order_ref.shape[0]):
+        wanted = to_col(order_ref[part])
+        blocks.append(jnp.concatenate([(wanted == lane + float(T * j)).astype(F32).astype(BF16) for j in range(count)], axis=1))
+    return jnp.concatenate(blocks, axis=0)
+
+
+def project_kernel(heads, moves, order_ref, x_ref, w_ref, src_ref, out_ref, inv_ref, uzx_ref, ubd_ref, dst_ref, gain_ref, *sems):
+    deep, width = x_ref.shape[1], 2 * heads * HEAD
+    at_step = pl.program_id(0)
+    background(at_step == 0, at_step == pl.num_programs(0) - 1, moves, (src_ref,), (dst_ref,), *sems)
+
+    @pl.when(pl.program_id(0) == 0)
+    def _():
+        for j in range(deep // T):
+            span = slice(j * T, j * T + T)
+            gain_ref[0:1, span] = w_ref[span, width + 2 * N : width + 3 * N].astype(F32).T[heads : heads + 1]
+
+    x = dot(row_picks(order_ref, x_ref.shape[0] // T), x_ref[...])
+    inv = lax.rsqrt(jnp.sum(x * x, axis=1, keepdims=True) / deep + EPS)
+    normed = (x * inv * gain_ref[0:1]).astype(BF16)
+    out_ref[...] = normed
+    for part in range(x.shape[0] // T):
+        inv_ref[part] = to_row(inv[part * T : part * T + T])
+    uzx_ref[...] = dot(normed, w_ref[:, :width]).astype(BF16)
+    ubd_ref[...] = dot(normed, w_ref[:, width:])
+
+
+def sort_kernel(order_ref, rows_ref, out_ref):
+    out_ref[...] = dot(row_picks(order_ref, rows_ref.shape[0] // T), rows_ref[...]).astype(BF16)
+
+
 def gate_kernel(g_ref, wo_ref, y_ref, z_ref, par_ref, mask_ref, dyn_ref, co_ref):
     dyn = dot(g_ref[...], wo_ref[...])
     for part in range(dyn.shape[0] // T):
@@ -139,18 +399,63 @@
         co_ref[part] = to_row(jnp.sum(own * w * par_ref[6:7], axis=1, keepdims=True))
 
 
-def mid_kernel(width, y_ref, z_ref, dyn_ref, par_ref, mask_ref, ss_ref, co_ref, yg_ref, dz_ref, dy_ref, gg_ref, rd_ref):
-    @pl.when(pl.program_id(0) == 0)
+def home_kernel(last, deep, order_ref, a_ref, b_ref, *refs):
+    out_ref, held_ref = refs[-2:]
+    step = pl.program_id(0)
+    many = held_ref.shape[0] // a_ref.shape[0]
+    size = a_ref.shape[0]
+
+    @pl.when(step < many)
+    def _():
+        value = a_ref[...].astype(F32) + b_ref[...].astype(F32)
+        if last:
+            normed_ref, inv_ref, gain_ref, rdz_ref, rdx_ref, more_ref = refs[:6]
+            gain = gain_ref[0:1]
+            hat = normed_ref[...].astype(F32) / gain
+            parts = []
+            for part in range(size // T):
+                inv_row = inv_ref[part]
+                dots = rdz_ref[part] + rdx_ref[part] + more_ref[0, part] + more_ref[1, part] + more_ref[2, part]
+                rows = slice(part * T, part * T + T)
+                inv = to_col(inv_row)[:, 0:1]
+                mean = to_col(dots / deep)[:, 0:1]
+                parts.append(inv * (gain * value[rows] - hat[rows] * mean))
+            value = jnp.concatenate(parts, axis=0)
+        held_ref[pl.ds(pl.multiple_of(step * size, size), size), :] = value.astype(BF16)
+
+    @pl.when(step >= many)
+    def _():
+        base = ((step - many) * size).astype(F32)
+        row = lax.broadcasted_iota(jnp.int32, (size, T), 0).astype(F32) + base
+        picks = jnp.concatenate([(row == order_ref[j]).astype(F32).astype(BF16) for j in range(order_ref.shape[0])], axis=1)
+        out_ref[...] = dot(picks, held_ref[...]).astype(BF16)
+
+
+def mid_kernel(width, moves, y_ref, z_ref, dyn_ref, par_ref, mask_ref, ss_ref, co_ref, yg_ref, dz_ref, dy_ref, gg_ref, rd_ref, got_ss, got_co, sems, local_sems):
+    step = pl.program_id(0)
+
+    @pl.when(step == 0)
     def _():
         gg_ref[...] = jnp.zeros_like(gg_ref)
+        peers, copies = make_moves(moves, (ss_ref, co_ref), (got_ss, got_co), sems, local_sems)
+        greet(peers)
+        for copy in copies:
+            copy.start()
+        for copy in copies:
+            copy.wait()
 
     gain = par_ref[6:7]
-    for part in range(y_ref.shape[0] // T):
+    parts = y_ref.shape[0] // T
+    for part in range(parts):
         rows = slice(part * T, part * T + T)
+        here = step * parts + part
+        ss, co = ss_ref[here], co_ref[here]
+        for other in range(got_ss.shape[0]):
+            ss, co = ss + got_ss[other, here], co + got_co[other, here]
         mask = to_col(mask_ref[part])[:, 0:1]
-        inv_row = lax.rsqrt(ss_ref[part] / width + EPS)
+        inv_row = lax.rsqrt(ss / width + EPS)
         inv = to_col(inv_row)[:, 0:1]
-        cube = to_col(inv_row * inv_row * inv_row * (co_ref[part] / width))[:, 0:1]
+        cube = to_col(inv_row * inv_row * inv_row * (co / width))[:, 0:1]
         y = y_ref[rows].astype(F32)
         z = z_ref[rows].astype(F32)
         dyn = dyn_ref[rows].astype(F32)
@@ -167,7 +472,16 @@
         rd_ref[part] = to_row(jnp.sum(dz * z, axis=1, keepdims=True))
 
 
-def backward_kernel(heads, dy_ref, x_ref, c_ref, cb_ref, ubd_ref, st_ref, par_ref, pbc_ref, head_ref, dx_ref, dbd_ref, gx_ref, gb_ref, gh_ref, rd_ref, d_state, ext_x, ext_b, rows_ref, prod, edy_ref, tail_ref):
+def backward_kernel(heads, extra, moves, dy_ref, x_ref, c_ref, cb_ref, ubd_ref, st_ref, par_ref, pbc_ref, head_ref, *refs):
+    count = len(moves)
+    srcs, refs = refs[:count], refs[count + extra :]
+    dx_ref, dbd_ref, rd_ref, gx_ref, gb_ref, gh_ref = refs[:6]
+    dsts, refs = refs[6 : 6 + count], refs[6 + count :]
+    d_state, ext_x, ext_b, rows_ref, prod, edy_ref, tail_ref = refs[:7]
+    if moves:
+        began = (pl.program_id(0) == 0) & (pl.program_id(1) == 0)
+        ended = (pl.program_id(0) == pl.num_programs(0) - 1) & (pl.program_id(1) == pl.num_programs(1) - 1)
+        background(began, ended, moves, srcs, dsts, *refs[7:])
     first = (pl.program_id(0) == 0) & (pl.program_id(1) == 0)
 
     @pl.when(first)
@@ -293,17 +607,25 @@
     rd_ref[0] = to_row(total)
 
 
-def params(*semantics):
-    return pltpu.CompilerParams(dimension_semantics=semantics, vmem_limit_bytes=56 * 1024 * 1024)
-
-
-def run_forward(heads, u_zx, u_bd, par, pbc, hp):
+def params(*semantics, number=0):
+    if number:
+        return pltpu.CompilerParams(
+            dimension_semantics=semantics, vmem_limit_bytes=LIMIT, collective_id=number, has_side_effects=True
+        )
+    return pltpu.CompilerParams(dimension_semantics=semantics, vmem_limit_bytes=LIMIT)
+
+
+def run_forward(heads, u_zx, u_bd, par, pbc, hp, came, w_out, number):
     rows, width = u_zx.shape[0], heads * HEAD
     slots, chunks = rows // LEN, LEN // T
     at = lambda s, i: (s * chunks + i, 0)
     fixed = lambda s, i: (0, 0)
+    size, block, quarter = came.shape
+    line = size // 2
+    anywhere = pl.BlockSpec(memory_space=pl.ANY)
+    sems = pltpu.SemaphoreType.DMA
     return pl.pallas_call(
-        functools.partial(forward_kernel, heads),
+        functools.partial(forward_kernel, heads, slots * chunks),
         grid=(slots, chunks),
         in_specs=[
             pl.BlockSpec((T, width), lambda s, i: (s * chunks + i, 1)),
@@ -312,6 +634,8 @@
             pl.BlockSpec((8, width), fixed),
             pl.BlockSpec((8, 2 * N), fixed),
             pl.BlockSpec((8, 128), fixed),
+            anywhere,
+            anywhere,
         ],
         out_specs=[
             pl.BlockSpec((T, width), at),
@@ -319,6 +643,8 @@
             pl.BlockSpec((T, width), at),
             pl.BlockSpec((T, 2 * N), at),
             pl.BlockSpec((1, N, width), lambda s, i: (s * chunks + i, 0, 0)),
+            anywhere,
+            anywhere,
         ],
         out_shape=[
             jax.ShapeDtypeStruct((rows, width), BF16),
@@ -326,17 +652,71 @@
             jax.ShapeDtypeStruct((rows, width), BF16),
             jax.ShapeDtypeStruct((rows, 2 * N), F32),
             jax.ShapeDtypeStruct((rows // T, N, width), BF16),
+            jax.ShapeDtypeStruct((size, block, quarter * 4), BF16),
+            full_shape(size, w_out),
         ],
-        scratch_shapes=[pltpu.VMEM((T + 8, width), F32), pltpu.VMEM((T + 8, 2 * N), F32), pltpu.VMEM((N, width), F32)],
-        compiler_params=params("arbitrary", "arbitrary"),
+        scratch_shapes=[
+            pltpu.VMEM((T + 8, width), F32),
+            pltpu.VMEM((T + 8, 2 * N), F32),
+            pltpu.VMEM((N, width), F32),
+            sems((2, 3, size)),
+            sems((2, PARTS, line)),
+            sems((2, PARTS, line)),
+            sems((2,)),
+        ],
+        compiler_params=params("arbitrary", "arbitrary", number=number),
         cost_estimate=pl.CostEstimate(flops=rows * width * 2 * 1200, bytes_accessed=rows * width * 8, transcendentals=rows * width * 6),
         name="scan_forward",
-    )(u_zx, u_zx, u_bd, par, pbc, hp)
-
-
-def run_gate(full_grad, w_out, y, u_zx, par, mask):
+    )(u_zx, u_zx, u_bd, par, pbc, hp, came, cut_shard(w_out))
+
+
+def run_project(heads, order, x, w_in, moved, number):
+    rows, deep = x.shape
+    wide = w_in.shape[1]
+    width = 2 * heads * HEAD
+    step = 256
+    moves = (("turn", "dp"),)
+    anywhere = pl.BlockSpec(memory_space=pl.ANY)
+    at = lambda i: (i, 0)
+    fixed = lambda i: (0, 0)
+    thin = pl.BlockSpec((step // T, 1, T), lambda i: (i, 0, 0))
+    return pl.pallas_call(
+        functools.partial(project_kernel, heads, moves),
+        grid=(rows // step,),
+        in_specs=[thin, pl.BlockSpec((rows, deep), fixed), pl.BlockSpec((deep, wide), fixed), anywhere],
+        out_specs=[pl.BlockSpec((step, deep), at), thin, pl.BlockSpec((step, width), at), pl.BlockSpec((step, wide - width), at), anywhere],
+        out_shape=[
+            jax.ShapeDtypeStruct((rows, deep), BF16),
+            jax.ShapeDtypeStruct((rows // T, 1, T), F32),
+            jax.ShapeDtypeStruct((rows, width), BF16),
+            jax.ShapeDtypeStruct((rows, wide - width), F32),
+        ]
+        + move_outs(moves, (moved,)),
+        scratch_shapes=[pltpu.VMEM((8, deep), F32)] + move_scratch(moves, (moved,)),
+        compiler_params=params("arbitrary", number=number),
+        cost_estimate=pl.CostEstimate(flops=rows * deep * (rows + wide) * 2, bytes_accessed=rows * deep * 8, transcendentals=rows),
+        name="project",
+    )(order, x, w_in, moved)
+
+
+def run_sort(order, values):
+    rows, wide = values.shape
+    step = 512
+    return pl.pallas_call(
+        sort_kernel,
+        grid=(rows // step,),
+        in_specs=[pl.BlockSpec((step // T, 1, T), lambda i: (i, 0, 0)), pl.BlockSpec((rows, wide), lambda i: (0, 0))],
+        out_specs=pl.BlockSpec((step, wide), lambda i: (i, 0)),
+        out_shape=jax.ShapeDtypeStruct((rows, wide), BF16),
+        compiler_params=params("arbitrary"),
+        cost_estimate=pl.CostEstimate(flops=rows * rows * wide * 2, bytes_accessed=rows * wide * 4, transcendentals=0),
+        name="sort_rows",
+    )(order, values)
+
+
+def run_gate(grads, w_out, y, u_zx, par, mask):
     rows, width = y.shape
-    deep = full_grad.shape[1]
+    deep = grads.shape[1]
     step = 256
     at = lambda i: (i, 0)
     fixed = lambda i: (0, 0)
@@ -355,41 +735,72 @@
         out_specs=[pl.BlockSpec((step, width), at), thin],
         out_shape=[jax.ShapeDtypeStruct((rows, width), BF16), jax.ShapeDtypeStruct((rows // T, 1, T), F32)],
         compiler_params=params("arbitrary"),
-        cost_estimate=pl.CostEstimate(flops=rows * width * deep * 2, bytes_accessed=rows * (width * 6 + deep * 2), transcendentals=rows * width),
+        cost_estimate=pl.CostEstimate(flops=rows * deep * width * 2, bytes_accessed=rows * deep * 2 + rows * width * 6, transcendentals=rows * width),
         name="gate_back",
-    )(full_grad, w_out, y, u_zx, par, mask)
-
-
-def run_mid(all_width, y, u_zx, dyn, par, mask, ss, co):
+    )(grads, w_out, y, u_zx, par, mask)
+
+
+def run_home(order, sums, extra, deep, name):
+    rows, quarter = sums[0].shape
+    step = 512
+    many = rows // step
+    into = lambda i: (jnp.minimum(i, many - 1), 0)
+    into3 = lambda i: (jnp.minimum(i, many - 1), 0, 0)
+    thin = pl.BlockSpec((step // T, 1, T), into3)
+    specs = [pl.BlockSpec((rows // T, 1, T), lambda i: (0, 0, 0))] + [pl.BlockSpec((step, quarter), into)] * 2
+    values = list(sums)
+    if extra is not None:
+        specs += [pl.BlockSpec((step, quarter), into), thin, pl.BlockSpec((8, quarter), lambda i: (0, 0)), thin, thin]
+        specs += [pl.BlockSpec((3, step // T, 1, T), lambda i: (0, jnp.minimum(i, many - 1), 0, 0))]
+        values += list(extra)
+    return pl.pallas_call(
+        functools.partial(home_kernel, extra is not None, float(deep)),
+        grid=(2 * many,),
+        in_specs=specs,
+        out_specs=pl.BlockSpec((step, quarter), lambda i: (jnp.maximum(i - many, 0), 0)),
+        out_shape=jax.ShapeDtypeStruct((rows, quarter), BF16),
+        scratch_shapes=[pltpu.VMEM((rows, quarter), BF16)],
+        compiler_params=params("arbitrary"),
+        cost_estimate=pl.CostEstimate(flops=rows * rows * quarter * 2, bytes_accessed=rows * quarter * 10, transcendentals=0),
+        name=name,
+    )(order, *values)
+
+
+def run_mid(all_width, y, u_zx, dyn, par, mask, ss, co, number):
     rows, width = y.shape
     step = 256
     at = lambda i: (i, 0)
     fixed = lambda i: (0, 0)
     thin = pl.BlockSpec((step // T, 1, T), lambda i: (i, 0, 0))
+    whole = pl.BlockSpec((rows // T, 1, T), lambda i: (0, 0, 0))
     wide = pl.BlockSpec((step, width), at)
+    moves = (("spread", "head"), ("spread", "head"))
+    others = lax.axis_size("head") - 1
     return pl.pallas_call(
-        functools.partial(mid_kernel, float(all_width)),
+        functools.partial(mid_kernel, float(all_width), moves),
         grid=(rows // step,),
-        in_specs=[wide, wide, wide, pl.BlockSpec((8, width), fixed), thin, thin, thin],
+        in_specs=[wide, wide, wide, pl.BlockSpec((8, width), fixed), thin, whole, whole],
         out_specs=[wide, wide, wide, pl.BlockSpec((8, width), fixed), thin],
         out_shape=[jax.ShapeDtypeStruct((rows, width), BF16)] * 3
         + [jax.ShapeDtypeStruct((8, width), F32), jax.ShapeDtypeStruct((rows // T, 1, T), F32)],
-        compiler_params=params("arbitrary"),
+        scratch_shapes=[pltpu.VMEM((others, rows // T, 1, T), F32)] * 2 + move_scratch(moves, (ss, co)),
+        compiler_params=params("arbitrary", number=number),
         cost_estimate=pl.CostEstimate(flops=rows * width * 30, bytes_accessed=rows * width * 12, transcendentals=rows * width),
         name="gate_mid",
     )(y, u_zx, dyn, par, mask, ss, co)
 
 
-def run_backward(heads, dy, u_zx, c, cb, u_bd, st, par, pbc, hp):
+def run_backward(heads, slot, dy, u_zx, c, cb, u_bd, st, par, pbc, hp, before, moves, values, number):
     rows, width = dy.shape
-    slots, chunks = rows // LEN, LEN // T
-    place = lambda s, i: s * chunks + chunks - 1 - i
+    chunks = LEN // T
+    place = lambda s, i: slot * chunks + chunks - 1 - i
     at = lambda s, i: (place(s, i), 0)
     at3 = lambda s, i: (place(s, i), 0, 0)
     fixed = lambda s, i: (0, 0)
+    anywhere = pl.BlockSpec(memory_space=pl.ANY)
     return pl.pallas_call(
-        functools.partial(backward_kernel, heads),
-        grid=(slots, chunks),
+        functools.partial(backward_kernel, heads, len(before), tuple(moves)),
+        grid=(1, chunks),
         in_specs=[
             pl.BlockSpec((T, width), at),
             pl.BlockSpec((T, width), lambda s, i: (place(s, i), 1)),
@@ -400,23 +811,26 @@
             pl.BlockSpec((8, width), fixed),
             pl.BlockSpec((8, 2 * N), fixed),
             pl.BlockSpec((8, 128), fixed),
-        ],
+        ]
+        + [anywhere] * (len(moves) + len(before)),
         out_specs=[
             pl.BlockSpec((T, width), at),
             pl.BlockSpec((T, 3 * N), at),
+            pl.BlockSpec((1, 1, T), at3),
             pl.BlockSpec((8, width), fixed),
             pl.BlockSpec((8, 2 * N), fixed),
             pl.BlockSpec((8, 128), fixed),
-            pl.BlockSpec((1, 1, T), at3),
-        ],
+        ]
+        + [anywhere] * len(moves),
         out_shape=[
             jax.ShapeDtypeStruct((rows, width), BF16),
             jax.ShapeDtypeStruct((rows, 3 * N), BF16),
+            jax.ShapeDtypeStruct((rows // T, 1, T), F32),
             jax.ShapeDtypeStruct((8, width), F32),
             jax.ShapeDtypeStruct((8, 2 * N), F32),
             jax.ShapeDtypeStruct((8, 128), F32),
-            jax.ShapeDtypeStruct((rows // T, 1, T), F32),
-        ],
+        ]
+        + move_outs(moves, values),
         scratch_shapes=[
             pltpu.VMEM((N, width), F32),
             pltpu.VMEM((T + 8, width), F32),
@@ -425,11 +839,328 @@
             pltpu.VMEM((3 * T, width), BF16),
             pltpu.VMEM((T, width), BF16),
             pltpu.VMEM((T, width), BF16),
-        ],
-        compiler_params=params("arbitrary", "arbitrary"),
-        cost_estimate=pl.CostEstimate(flops=rows * width * 2 * 3000, bytes_accessed=rows * width * 12, transcendentals=rows * width * 8),
+        ]
+        + move_scratch(moves, values),
+        input_output_aliases={9 + len(moves) + i: i for i in range(len(before))},
+        compiler_params=params("arbitrary", "arbitrary", number=number),
+        cost_estimate=pl.CostEstimate(flops=LEN * width * 2 * 3000, bytes_accessed=LEN * width * 12, transcendentals=LEN * width * 8),
         name="scan_backward",
-    )(dy, u_zx, c, cb, u_bd, st, par, pbc, hp)
+    )(dy, u_zx, c, cb, u_bd, st, par, pbc, hp, *values, *before)
+
+
+def pieces_kernel(count, many, moves, *refs):
+    total = len(moves)
+    values, weights, srcs = refs[:count], refs[count : 2 * count], refs[2 * count : 2 * count + total]
+    refs = refs[2 * count + total :]
+    far_ref, own_ref = refs[:2]
+    dsts, refs = refs[2 : 2 + total], refs[2 + total :]
+    sent_ref, came_ref, near_sems = refs[:3]
+    step = pl.program_id(0)
+    rows, quarter = far_ref.shape
+    dp, own = lax.axis_index("dp"), lax.axis_index("head")
+    near = (dp, own ^ 1)
+    peers, copies = make_moves(moves, srcs, dsts, *refs[3:]) if moves else ([], [])
+
+    @pl.when(step == 0)
+    def _():
+        greet(peers if near_in(moves) else [near] + peers)
+        for copy in copies:
+            copy.start()
+
+    def product(k):
+        at = pl.ds(pl.multiple_of((own ^ k) * quarter, 128), quarter)
+        out = None
+        for value, weight in zip(values, weights):
+            term = dot_nt(value[...], weight[at, :])
+            out = term if out is None else out + term
+        return out
+
+    def near_copy(block):
+        return pltpu.make_async_remote_copy(
+            src_ref=sent_ref.at[block],
+            dst_ref=came_ref.at[block],
+            send_sem=near_sems.at[0, block],
+            recv_sem=near_sems.at[1, block],
+            device_id=near,
+            device_id_type=MESH,
+        )
+
+    @pl.when(step < many)
+    def _():
+        sent_ref[step, :, :quarter] = product(3).astype(BF16)
+        sent_ref[step, :, quarter:] = product(1).astype(BF16)
+        near_copy(step).start()
+
+    @pl.when(step >= many)
+    def _():
+        block = step - many
+        far, mine = product(2), product(0)
+        near_copy(block).wait_recv()
+        far_ref[...] = (far + came_ref[block, :, :quarter].astype(F32)).astype(BF16)
+        own_ref[...] = (mine + came_ref[block, :, quarter:].astype(F32)).astype(BF16)
+
+    @pl.when(step == 2 * many - 1)
+    def _():
+        for block in range(many):
+            near_copy(block).wait_send()
+        for copy in copies:
+            copy.wait()
+
+
+def near_in(moves):
+    return any(move[0] == "spread" and move[1] == "head" for move in moves)
+
+
+def run_pieces(values, weights, quarter, name, moves, moved, number):
+    rows = values[0].shape[0]
+    step = 256
+    many = rows // step
+    anywhere = pl.BlockSpec(memory_space=pl.ANY)
+    specs = [pl.BlockSpec((step, v.shape[1]), lambda i: (lax.rem(i, many), 0)) for v in values]
+    for weight, block, wide in weights:
+        specs.append(pl.BlockSpec((weight.shape[0], wide), lambda i, block=block: (0, block)))
+    depth = sum(v.shape[1] for v in values)
+    return pl.pallas_call(
+        functools.partial(pieces_kernel, len(values), many, tuple(moves)),
+        grid=(2 * many,),
+        in_specs=specs + [anywhere] * len(moves),
+        out_specs=[pl.BlockSpec((step, quarter), lambda i: (jnp.maximum(i - many, 0), 0))] * 2 + [anywhere] * len(moves),
+        out_shape=[jax.ShapeDtypeStruct((rows, quarter), BF16)] * 2 + move_outs(moves, moved),
+        scratch_shapes=[pltpu.VMEM((many, step, 2 * quarter), BF16)] * 2 + [pltpu.SemaphoreType.DMA((2, many))] + move_scratch(moves, moved),
+        compiler_params=params("arbitrary", number=number),
+        cost_estimate=pl.CostEstimate(flops=rows * depth * quarter * 8, bytes_accessed=rows * (depth + 4 * quarter) * 2, transcendentals=0),
+        name=name,
+    )(*values, *[w for w, _, _ in weights], *moved)
+
+
+def grads_kernel(count, parts, moves, *refs):
+    total = len(moves)
+    lefts, rights, srcs = refs[:count], refs[count : 2 * count], refs[2 * count : 2 * count + total]
+    refs = refs[2 * count + total :]
+    outs, dsts, sems = refs[:count], refs[count : count + total], refs[count + total :]
+    step = pl.program_id(0)
+    if moves:
+        background(step == 0, step == count * parts - 1, moves, srcs, dsts, *sems)
+    for which in range(count):
+
+        @pl.when((step >= which * parts) & (step < (which + 1) * parts))
+        def _():
+            out = lax.dot_general(lefts[which][...], rights[which][...], (((0,), (0,)), ((), ())), preferred_element_type=F32)
+            outs[which][...] = out.astype(BF16)
+
+
+def run_grads(pairs, name, moves=(), moved=(), number=0):
+    rows, deep = pairs[0][0].shape
+    step = 512
+    parts = deep // step
+    count = len(pairs)
+    anywhere = pl.BlockSpec(memory_space=pl.ANY)
+    into = lambda which: lambda i: jnp.clip(i - which * parts, 0, parts - 1)
+    specs = [pl.BlockSpec((rows, step), lambda i, at=into(w): (0, at(i))) for w in range(count)]
+    specs += [pl.BlockSpec(right.shape, lambda i: (0, 0)) for _, right in pairs]
+    return pl.pallas_call(
+        functools.partial(grads_kernel, count, parts, tuple(moves)),
+        grid=(count * parts,),
+        in_specs=specs + [anywhere] * len(moves),
+        out_specs=[pl.BlockSpec((step, right.shape[1]), lambda i, at=into(w): (at(i), 0)) for w, (_, right) in enumerate(pairs)]
+        + [anywhere] * len(moves),
+        out_shape=[jax.ShapeDtypeStruct((deep, right.shape[1]), BF16) for _, right in pairs] + move_outs(moves, moved),
+        scratch_shapes=move_scratch(moves, moved),
+        compiler_params=params("arbitrary", number=number),
+        cost_estimate=pl.CostEstimate(
+            flops=sum(rows * deep * right.shape[1] * 2 for _, right in pairs), bytes_accessed=rows * deep * 2 * count, transcendentals=0
+        ),
+        name=name,
+    )(*[left for left, _ in pairs], *[right for _, right in pairs], *moved)
+
+
+def last_kernel(moves, *refs):
+    count = len(moves)
+    srcs, pair_ref = refs[:count], refs[count]
+    dsts, out_ref = refs[count + 1 : 2 * count + 1], refs[2 * count + 1]
+    kept_ref, line_ref, came_ref, own_ref, pair_sems, sems, local_sems = refs[2 * count + 2 :]
+    me, head = lax.axis_index("dp"), lax.axis_index("head")
+    peers, copies = make_moves(moves, srcs, dsts, sems, local_sems)
+
+    def remote(src, dst, slot, peer):
+        return pltpu.make_async_remote_copy(
+            src_ref=src, dst_ref=dst, send_sem=pair_sems.at[0, slot], recv_sem=pair_sems.at[1, slot], device_id=(peer, head), device_id_type=MESH
+        )
+
+    high = me >> 1
+    half = remote(pair_ref.at[:, 1 - (me & 1)], came_ref, 0, me ^ 1)
+    line = [remote(kept_ref.at[high ^ j], line_ref.at[j - 1], j, me ^ (2 * j)) for j in range(1, own_ref.shape[0])]
+    own = pltpu.make_async_copy(pair_ref.at[:, me & 1], own_ref, pair_sems.at[2, 0])
+    greet(peers)
+    half.start()
+    own.start()
+    for copy in copies:
+        copy.start()
+    own.wait()
+    half.wait()
+    for j in range(own_ref.shape[0]):
+        kept_ref[j] = (own_ref[j].astype(F32) + came_ref[j].astype(F32)).astype(BF16)
+    for copy in line:
+        copy.start()
+    for copy in line:
+        copy.wait()
+    total = kept_ref[high].astype(F32)
+    for j in range(1, own_ref.shape[0]):
+        total = total + line_ref[j - 1].astype(F32)
+    out_ref[...] = total
+    for copy in copies:
+        copy.wait()
+
+
+def run_last(moves, values, paired, number):
+    many, _, block, wide = paired.shape
+    anywhere = pl.BlockSpec(memory_space=pl.ANY)
+    own = pltpu.VMEM((many, block, wide), BF16)
+    return pl.pallas_call(
+        functools.partial(last_kernel, tuple(moves)),
+        in_specs=[anywhere] * (len(moves) + 1),
+        out_specs=[anywhere] * len(moves) + [pl.BlockSpec(memory_space=pltpu.VMEM)],
+        out_shape=move_outs(moves, values) + [jax.ShapeDtypeStruct((block, wide), F32)],
+        scratch_shapes=[own, pltpu.VMEM((many - 1, block, wide), BF16), own, own, pltpu.SemaphoreType.DMA((3, many))] + move_scratch(moves, values),
+        compiler_params=pltpu.CompilerParams(collective_id=number, has_side_effects=True, vmem_limit_bytes=LIMIT),
+        name="last_exchange",
+    )(*values, paired)
+
+
+def row_forward(size, quarter, own_ref, full_ref, sems):
+    me, own = lax.axis_index("dp"), lax.axis_index("head")
+    columns = lambda head: pl.ds(pl.multiple_of(head * quarter, 128), quarter)
+
+    def copy(src, dst, stage, k, head):
+        return pltpu.make_async_remote_copy(
+            src_ref=src, dst_ref=dst, send_sem=sems.at[0, stage, k], recv_sem=sems.at[1, stage, k], device_id=(me, head), device_id_type=MESH
+        )
+
+    def source(k):
+        return full_ref.at[me ^ k, :, columns(own)] if own_ref is None else own_ref.at[me ^ k]
+
+    def far(k):
+        return copy(source(k), full_ref.at[me ^ k, :, columns(own)], 0, k, own ^ 2)
+
+    def near(k):
+        return copy(source(k), full_ref.at[me ^ k, :, columns(own)], 1, k, own ^ 1)
+
+    def back(k):
+        block = full_ref.at[me ^ k, :, columns(own ^ 2)]
+        return copy(block, block, 2, k, own ^ 1)
+
+    return far, near, back
+
+
+def shard_spread(src, dst, across_sems, side_sems):
+    me, own = lax.axis_index("dp"), lax.axis_index("head")
+
+    def copy(a, b, sems, part, j, peer):
+        return pltpu.make_async_remote_copy(
+            src_ref=a, dst_ref=b, send_sem=sems.at[0, part, j], recv_sem=sems.at[1, part, j], device_id=(peer, own), device_id_type=MESH
+        )
+
+    def across(part, j):
+        return copy(src.at[part], dst.at[me, part], across_sems, part, j, me ^ (2 * j))
+
+    def side(part, j):
+        here = dst.at[me ^ (2 * j), part]
+        return copy(src.at[part] if j == 0 else here, here, side_sems, part, j, me ^ 1)
+
+    return across, side
+
+
+def entry_kernel(parts, x_ref, w_ref, fx_ref, fw_ref, row_sems, pass_sems, across_sems, side_sems, local_sems):
+    size, quarter = x_ref.shape[0], x_ref.shape[2]
+    line = size // 2
+    me, own = lax.axis_index("dp"), lax.axis_index("head")
+    mine = pl.ds(pl.multiple_of(own * quarter, 128), quarter)
+    far, near, back = row_forward(size, quarter, None, fx_ref, pass_sems)
+    across, side = shard_spread(w_ref, fw_ref, across_sems, side_sems)
+
+    def rows(k):
+        return pltpu.make_async_remote_copy(
+            src_ref=x_ref.at[me ^ k],
+            dst_ref=fx_ref.at[me, :, mine],
+            send_sem=row_sems.at[0, k],
+            recv_sem=row_sems.at[1, k],
+            device_id=(me ^ k, own),
+            device_id_type=MESH,
+        )
+
+    greet([(me ^ k, own) for k in range(1, size)] + [(me, own ^ 1), (me, own ^ 2)])
+    held = [
+        pltpu.make_async_copy(x_ref.at[me], fx_ref.at[me, :, mine], local_sems.at[0]),
+        pltpu.make_async_copy(w_ref, fw_ref.at[me], local_sems.at[1]),
+    ]
+    for copy in held:
+        copy.start()
+    order = turn_order(size)
+    for k in order:
+        rows(k).start()
+    for part in range(parts):
+        side(part, 0).start()
+    held[0].wait()
+    far(0).start()
+    near(0).start()
+    for k in order:
+        rows(k).wait_recv()
+        far(k).start()
+        near(k).start()
+    for part in range(min(2, parts)):
+        for j in range(1, line):
+            across(part, j).start()
+    for k in [0] + order:
+        far(k).wait_recv()
+        back(k).start()
+    for part in range(parts):
+        for j in range(1, line):
+            across(part, j).wait_recv()
+            side(part, j).start()
+        if part + 2 < parts:
+            for j in range(1, line):
+                across(part + 2, j).start()
+    held[1].wait()
+    for k in range(size):
+        near(k).wait()
+        back(k).wait()
+        far(k).wait_send()
+        if k:
+            rows(k).wait_send()
+    for part in range(parts):
+        for j in range(line):
+            side(part, j).wait()
+            if j:
+                across(part, j).wait_send()
+
+
+PARTS = 4
+
+
+def cut_shard(w):
+    return w.reshape(PARTS, w.shape[0] // PARTS, w.shape[1])
+
+
+def full_shape(size, w):
+    return jax.ShapeDtypeStruct((size, PARTS, w.shape[0] // PARTS, w.shape[1]), BF16)
+
+
+def run_entry(tokens, w_in, number):
+    size = lax.axis_size("dp")
+    rows, quarter = tokens.shape
+    line = size // 2
+    anywhere = pl.BlockSpec(memory_space=pl.ANY)
+    sems = pltpu.SemaphoreType.DMA
+    came, full = pl.pallas_call(
+        functools.partial(entry_kernel, PARTS),
+        in_specs=[anywhere] * 2,
+        out_specs=[anywhere] * 2,
+        out_shape=[jax.ShapeDtypeStruct((size, rows // size, quarter * 4), BF16), full_shape(size, w_in)],
+        scratch_shapes=[sems((2, size)), sems((2, 3, size)), sems((2, PARTS, line)), sems((2, PARTS, line)), sems((2,))],
+        compiler_params=pltpu.CompilerParams(collective_id=number, has_side_effects=True, vmem_limit_bytes=LIMIT),
+        name="entry",
+    )(tokens.reshape(size, rows // size, quarter), cut_shard(w_in))
+    return came.reshape(rows, quarter * 4), full.reshape(size * w_in.shape[0], w_in.shape[1])
 
 
 def mm(a, b, contract, kind):
@@ -441,37 +1172,19 @@
     heads = head_params.shape[1]
     width = heads * HEAD
     place = lax.axis_index("head")
-    groups = lax.axis_size("head")
-    all_width = width * groups
-    deep = quarter * groups
-    arrange = order[0]
-
-    arrived_x = lax.all_to_all(tokens, "dp", split_axis=0, concat_axis=0, tiled=True)
-    own_x = arrived_x[arrange]
+    size = lax.axis_size("dp")
+    here = lax.axis_index("dp")
+    all_width = width * lax.axis_size("head")
+    deep = quarter * lax.axis_size("head")
     own_w = w_zx.shape[0]
+    arrange = order.astype(F32).reshape(rows // T, 1, T)
+
     packed = jnp.concatenate(
-        [
-            w_zx.reshape(own_w, 2 * width),
-            w_bc,
-            w_dt,
-            norm_gain[:, None],
-            jnp.zeros((own_w, 127 - heads), BF16),
-        ],
-        axis=1,
+        [w_zx.reshape(own_w, 2 * width), w_bc, w_dt, norm_gain[:, None], jnp.zeros((own_w, 127 - heads), BF16)], axis=1
     )
-    w_in = lax.all_gather(packed, "dp", axis=0, tiled=True)
-    full_x = lax.all_gather(own_x, "head", axis=1, tiled=True)
-    arrived_g = lax.all_to_all(cotangent, "dp", split_axis=0, concat_axis=0, tiled=True)
-    own_g = arrived_g[arrange]
-    full_g = lax.all_gather(own_g, "head", axis=1, tiled=True)
-    w_o = lax.all_gather(w_out, "dp", axis=0, tiled=True)
-
-    gain = w_in[:, 2 * width + 2 * N + heads].astype(F32)
-    xf = full_x.astype(F32)
-    inv_one = lax.rsqrt(jnp.mean(xf * xf, axis=1, keepdims=True) + EPS)
-    normed = (xf * inv_one * gain).astype(BF16)
-    u_zx = mm(normed, w_in[:, : 2 * width], ((1,), (0,)), BF16)
-    u_bd = mm(normed, w_in[:, 2 * width :], ((1,), (0,)), F32)
+    blocks = lambda value: value.reshape(size, rows // size, quarter)
+    came_x, w_in = run_entry(tokens, packed, 1)
+    normed, inv_one, u_zx, u_bd, own_g = run_project(heads, arrange, came_x, w_in, blocks(cotangent), 2)
 
     par = jnp.concatenate([conv_x, jnp.repeat(head_params[2:3], HEAD, axis=1), gate_gain[None], jnp.zeros((1, width), F32)], axis=0)
     pbc = jnp.concatenate([conv_bc, jnp.zeros((3, 2 * N), F32)], axis=0)
@@ -479,53 +1192,88 @@
     positions = lax.broadcasted_iota(jnp.int32, (lengths.shape[0], LEN), 1)
     mask = (positions < lengths[:, None]).astype(F32).reshape(rows // T, 1, T)
 
-    y, ss, c, cb, st = run_forward(heads, u_zx, u_bd, par, pbc, hp)
+    sorted_g = run_sort(arrange, own_g.reshape(rows, quarter))
+    y, ss, c, cb, st, full_g, w_o = run_forward(heads, u_zx, u_bd, par, pbc, hp, blocks(sorted_g), w_out, 3)
+    w_o = w_o.reshape(deep, width)
+    full_g = full_g.reshape(rows, deep)
     dyn, co = run_gate(full_g, w_o, y, u_zx, par, mask)
-    ss, co = lax.psum((ss, co), "head")
-    yg, dz, dy, gg, rd_z = run_mid(all_width, y, u_zx, dyn, par, mask, ss, co)
-
-    branch = mm(yg, w_o, ((1,), (1,)), BF16)
-    shares = lax.psum_scatter(branch, "head", scatter_dimension=1, tiled=True)
-    grad_out = mm(full_g, yg, ((0,), (0,)), BF16)
-    grad_out = lax.psum_scatter(grad_out, "dp", scatter_dimension=0, tiled=True)
-    grad_z = mm(normed, dz, ((0,), (0,)), BF16)
-    grad_z = lax.psum_scatter(grad_z, "dp", scatter_dimension=0, tiled=True)
-
-    out_rows = (own_x.astype(F32) + shares.astype(F32)).astype(BF16)
-    sent_out = jnp.zeros_like(out_rows).at[arrange].set(out_rows)
-    final_out = lax.all_to_all(sent_out, "dp", split_axis=0, concat_axis=0, tiled=True)
-
-    dux, dbd, gx, gb, gh, rd_x = run_backward(heads, dy, u_zx, c, cb, u_bd, st, par, pbc, hp)
-
-    terms = mm(dz, w_in[:, :width], ((1,), (1,)), F32)
-    terms = terms + mm(dux, w_in[:, width : 2 * width], ((1,), (1,)), F32)
-    terms = terms + mm(dbd, w_in[:, 2 * width :], ((1,), (1,)), F32)
-    dxn = lax.psum_scatter(terms.astype(BF16), "head", scatter_dimension=1, tiled=True).astype(F32)
-    row_dot = lax.psum(rd_z + rd_x, "head").reshape(rows, 1)
-
-    grad_x = mm(normed, dux, ((0,), (0,)), BF16)
-    grad_x = lax.psum_scatter(grad_x, "dp", scatter_dimension=0, tiled=True)
-    grad_bd = mm(normed, dbd, ((0,), (0,)), BF16)
-    grad_bd = lax.psum_scatter(grad_bd, "dp", scatter_dimension=0, tiled=True).astype(F32)
-    grad_bc = lax.psum(grad_bd[:, : 2 * N], "head")
-    grad_dt = grad_bd[:, 2 * N : 2 * N + heads]
-
-    gain_own = lax.dynamic_slice_in_dim(gain, place * quarter, quarter, 0)
-    inv_own = inv_one
-    xs = own_x.astype(F32)
-    grad_rows = own_g.astype(F32) + inv_own * gain_own * dxn - xs * inv_own**2 * (row_dot / deep)
-    grad_rows = grad_rows.astype(BF16)
-    gain_part = jnp.sum(dxn * xs * inv_own, axis=0)
-    sent_back = jnp.zeros_like(grad_rows).at[arrange].set(grad_rows)
-    final_back = lax.all_to_all(sent_back, "dp", split_axis=0, concat_axis=0, tiled=True)
-
-    gain_part = lax.dynamic_update_slice_in_dim(jnp.zeros((deep,), F32), gain_part, place * quarter, 0)
-    gx, gh, gg = lax.psum((gx[:5], gh[:3, :heads], gg[0]), "dp")
-    gain_all, gb = lax.psum((gain_part, gb[:5]), ("dp", "head"))
-    own_d = norm_gain.shape[0]
-    grad_gain = lax.dynamic_slice_in_dim(gain_all, lax.axis_index("dp") * own_d, own_d, 0)
-    grad_zx = jnp.stack([grad_z, grad_x], axis=1).astype(F32)
-    return (final_out, final_back, grad_gain, grad_zx, grad_bc, grad_dt, grad_out.astype(F32), gx, gb, gh, gg)
+    yg, dz, dy, gg, rd_z = run_mid(all_width, y, u_zx, dyn, par, mask, ss, co, 4)
+
+    def keep(paired, came, bit):
+        own = lax.dynamic_index_in_dim(paired, (here >> bit) & 1, 1, keepdims=False)
+        return (own.astype(F32) + came.astype(F32)).astype(BF16)
+
+    def total(kept, came, shift):
+        own = lax.dynamic_index_in_dim(kept, here >> shift, 0, keepdims=False)
+        return own.astype(F32) + jnp.sum(came.astype(F32), axis=0)
+
+    def pairs(grads):
+        return grads.reshape(size // 2, 2, own_w, grads.shape[1])
+
+    def fours(grads):
+        return grads.reshape(size // 4, 2, -1, own_w, grads.shape[-1])
+
+    scan = functools.partial(run_backward, heads)
+    shared = (dy, u_zx, c, cb, u_bd, st, par, pbc, hp)
+    half_rows = rows // 2
+    out_far, out_own = run_pieces([yg], [(w_o, 0, width)], quarter, "branch_pieces", [], [], 5)
+    grad_o, grad_z, far0 = run_grads([(full_g, yg), (normed, dz)], "gate_grads", [("rows", "head", 2, 0, half_rows)], [out_far], 6)
+    grad_o, grad_z = pairs(grad_o), fours(grad_z)
+    *back0, gx0, gb0, gh0, came_o, came_z, far1 = scan(
+        0, *shared, (), [("half", "dp", 0), ("half", "dp", 1), ("rows", "head", 2, half_rows, half_rows)], [grad_o, grad_z, out_far], 7
+    )
+    sent_out = run_home(arrange, [out_own, jnp.concatenate([far0, far1], axis=0)], None, deep, "home_out")
+    kept_o = keep(grad_o, came_o, 0).reshape(size // 4, 2, own_w, width)
+    kept_z = keep(grad_z, came_z, 1)
+    *back1, gx1, gb1, gh1, got_out, came_z, came_o = scan(
+        1, *shared, back0, [("turn", "dp"), ("half", "dp", 0), ("half", "dp", 1)], [blocks(sent_out), kept_z, kept_o], 8
+    )
+    dux, dbd, rd_x = back1
+    kept_z, kept_o = keep(kept_z, came_z, 0), keep(kept_o, came_o, 1)
+    grad_x, grad_bd = run_grads([(normed, dux), (normed, dbd)], "scan_grads")
+    grad_x, grad_bd = pairs(grad_x), pairs(grad_bd)
+    gb = gb0 + gb1
+    d_far, d_own, line_o, line_z, came_x2, got_rows, got_gb = run_pieces(
+        [dz, dux, dbd],
+        [(w_in, 0, width), (w_in, 1, width), (w_in, 2 * width // (3 * N), 3 * N)],
+        quarter,
+        "input_pieces",
+        [("direct", "dp", 2), ("direct", "dp", 2), ("half", "dp", 0), ("spread", "head"), ("spread", "head")],
+        [kept_o, kept_z, grad_x, rd_z + rd_x, gb],
+        9,
+    )
+    kept_x = keep(grad_x, came_x2, 0)
+    gb = gb[:5] + jnp.sum(got_gb, axis=0)[:5]
+    gh = gh0 + gh1
+    ends = jnp.concatenate([gb[3], gb[4]] + [gh[i, :32] for i in range(3)] + [jnp.zeros((width - 4 * N - 96,), F32)])
+    small = jnp.concatenate([(gx0 + gx1)[:5], gg[:1], jnp.concatenate([gb[0], gb[1], gb[2]])[None], ends[None]], axis=0)
+    d_arrived, line_x, got_small, grad_bd = run_last(
+        [("whole", "head", 2), ("direct", "dp", 1), ("spread", "dp")], [d_far, kept_x, small], grad_bd, 10
+    )
+
+    gain_all = w_in[:, 2 * width + 2 * N + heads].astype(F32)
+    gain_own = jnp.broadcast_to(lax.dynamic_slice_in_dim(gain_all, place * quarter, quarter, 0)[None], (8, quarter))
+    normed_own = lax.dynamic_slice_in_dim(normed, place * quarter, quarter, 1)
+    sent_back = run_home(arrange, [d_own, d_arrived], [normed_own, inv_one, gain_own, rd_z, rd_x, got_rows], deep, "home_back")
+    got_back = lax.all_to_all(sent_back, "dp", split_axis=0, concat_axis=0, tiled=True)
+    final_back = (cotangent.astype(F32) + got_back.astype(F32)).astype(BF16)
+
+    final_out = (tokens.astype(F32) + got_out.reshape(rows, quarter).astype(F32)).astype(BF16)
+    grad_out, grad_z = total(kept_o, line_o, 2), total(kept_z, line_z, 2)
+    grad_x = total(kept_x, line_x, 1)
+    small = small + jnp.sum(got_small, axis=0)
+    grad_zx = jnp.stack([grad_z, grad_x], axis=1)
+    of_gain = jnp.sum(grad_z * w_zx[:, 0].astype(F32), axis=1) + jnp.sum(grad_x * w_zx[:, 1].astype(F32), axis=1)
+    of_gain = of_gain + jnp.sum(grad_bd[:, : 2 * N] * w_bc.astype(F32), axis=1)
+    of_gain = of_gain + jnp.sum(grad_bd[:, 2 * N : 2 * N + heads] * w_dt.astype(F32), axis=1)
+    last = jnp.concatenate([grad_bd[:, : 2 * N], jnp.broadcast_to(of_gain[:, None], (own_w, 128))], axis=1)
+    others, = run_exchange([("spread", "head")], [last], 11)
+    last = last + jnp.sum(others, axis=0)
+    grad_gain = last[:, 2 * N] / norm_gain.astype(F32)
+    gx, gg = small[0:5], small[5]
+    gb = jnp.concatenate([small[6].reshape(3, 2 * N), small[7, : 4 * N].reshape(2, 2 * N)], axis=0)
+    gh = small[7, 4 * N : 4 * N + 96].reshape(3, 32)[:, :heads]
+    return (final_out, final_back, grad_gain, grad_zx, last[:, : 2 * N], grad_bd[:, 2 * N : 2 * N + heads], grad_out, gx, gb, gh, gg)
 
 
 def solution(mesh):

time: 879 us -> 586 us (0.67)
  Pallas kernels: 95.7 us -> 517 us
  waiting for transfers between devices: 356 us -> 0.01 us
  blocking collectives: 193 us -> 0 us
  matrix products: 97.7 us -> 0 us
  local copies, waits for them, and re-layouts: 59.9 us -> 26.1 us
  starting transfers between devices: 18.3 us -> 4.97 us
  between operations: 14.4 us -> 1.16 us
    pallas_call x3 -> x15, Pallas kernels: 83.4 us -> 505 us  [the longest x1 117 us: run_entry(): pl.pallas_call(functools.partial(entry_kernel, PARTS), in_specs=[anywhere...]
    reduce_scatter x4 -> x0, waiting for transfers between devices: 196 us -> none  [the longest x1 71.6 us: body(): grad_x = lax.psum_scatter(grad_x, 'dp', scatter_dimension=0, tiled=True)]
    psum x4 -> x0, blocking collectives: 117 us -> none  [the longest x1 59.6 us: body(): gx, gh, gg = lax.psum((gx[:5], gh[:3, :heads], gg[0]), 'dp')]
    dot_general x10 -> x0, matrix products: 97.7 us -> none  [mm(): lax.dot_general(a, b, (contract, ((), ())), preferred_element_type=F32)]
    all_gather x4 -> x0, waiting for transfers between devices: 87.9 us -> none  [the longest x1 46.9 us: body(): full_g = lax.all_gather(own_g, 'head', axis=1, tiled=True)]
    all_to_all x1 -> x0, blocking collectives: 75.9 us -> none  [body(): lax.all_to_all(cotangent, 'dp', split_axis=0, concat_axis=0, tiled=True)]
    all_to_all x2 -> x0, waiting for transfers between devices: 70.9 us -> none  [the longest x1 60.6 us: body(): lax.all_to_all(tokens, 'dp', split_axis=0, concat_axis=0, tiled=True)]
    unnamed x61 -> x75, local copies, waits for them, and re-layouts: 33.3 us -> 6.88 us
  transfers between devices with their start and end apart: 14 -> 1, of which waited for: 8 -> 0; matrix products, arithmetic and copies ran while one was open for 19% -> 4% of each run, Pallas kernels for 8% -> 3%
where the time goes in v3:
time: 586 us; the launch traced here: 584 us
  Pallas kernels  517 us (88%)
  other arithmetic  34 us (6%)
  local copies, waits for them, and re-layouts  26.1 us (4%)
    pallas_call x1, Pallas kernels, run_entry(): pl.pallas_call(functools.partial(entry_kernel, PARTS), in_specs=[anywhere...  117 us
    pallas_call x2, Pallas kernels, run_backward(): pl.pallas_call(functools.partial(backward_kernel, heads, len(before), tup...  78.5 us
    pallas_call x1, Pallas kernels, run_forward(): pl.pallas_call(functools.partial(forward_kernel, heads, slots * chunks),...  64.7 us
    pallas_call x2, Pallas kernels, run_pieces(): pl.pallas_call(functools.partial(pieces_kernel, len(values), many, tuple(...  51 us
    pallas_call x1, Pallas kernels, run_project(): pl.pallas_call(functools.partial(project_kernel, heads, moves), grid=(row...  49.2 us
    pallas_call x1, Pallas kernels, run_last(): pl.pallas_call(functools.partial(last_kernel, tuple(moves)), in_specs=[an...  45 us
    pallas_call x2, Pallas kernels, run_grads(): pl.pallas_call(functools.partial(grads_kernel, count, parts, tuple(moves)...  42.6 us
    pallas_call x2, Pallas kernels, run_home(): pl.pallas_call(functools.partial(home_kernel, extra is not None, float(de...  18.7 us
  transfers between devices with their start and end apart: 1, of which 0 were waited for; matrix products, arithmetic and copies ran while one was open for 4% of the time, Pallas kernels for 3%

profile of v3, /device:TPU:0, one launch (start us, length us, event | category | flops | bytes accessed | tf_op | source)
XLA Modules:
  0.0 583.6 jit_solution(12513766471869302985)
XLA Ops:
  0.7 2.1 concatenate.36
  7.6 116.6 %entry.1 = (bf16[8,256,1536]{2,1,0:T(8,128)(2,1)}, bf16[8,4,48,1920]{3,2,1,0:T(8,128)(2,1)}) custom-call(bf16[8,256,384]{2,1,0:T(8,128)(2,1)} %bitcast.98, bf16[4,48,1920]{2,1,0:T(8,128)(2,1)} %concatenate.40.w_ref), custom_call_target="tpu_custom_call" | custom-call | tf_op jit(solution)/shard_map/entry/pallas_call | solution.py:1154
  126.1 49.2 %project.1 = (bf16[2048,1536]{1,0:T(8,128)(2,1)}, f32[16,1,128]{2,1,0:T(1,128)}, bf16[2048,1536]{1,0:T(8,128)(2,1)}, f32[2048,384]{1,0:T(8,128)}, bf16[8,256,384]{2,1,0:T(8,128)(2,1)}) custom-call(f32[16,1,128]{2,1,0:T(1,128)} %convert_bitcast_fusion.2.order_ref, bf16[2048,1536]{1,0:T(8,128)(2,1)} %bitcast.126, bf16[1536,1920]{1,0:T(8,128)(2,1)} %bitcast.116, ...), custom_call_target="tpu_custom_call" | custom-call | flops 24964497408 | bytes 25165824 | tf_op jit(solution)/shard_map/project/pallas_call | solution.py:683
  175.3 7.4 %sort_rows.1 = bf16[2048,384]{1,0:T(8,128)(2,1)} custom-call(f32[16,1,128]{2,1,0:T(1,128)} %convert_bitcast_fusion.2.order_ref, bf16[2048,384]{1,0:T(8,128)(2,1)} %bitcast.129), custom_call_target="tpu_custom_call" | custom-call | flops 3221225472 | bytes 3145728 | tf_op jit(solution)/shard_map/sort_rows/pallas_call | solution.py:705
  185.7 64.7 %scan_forward.1 = (bf16[2048,768]{1,0:T(8,128)(2,1)}, f32[16,1,128]{2,1,0:T(1,128)}, bf16[2048,768]{1,0:T(8,128)(2,1)}, f32[2048,256]{1,0:T(8,128)}, bf16[16,128...) custom-call(bf16[2048,1536]{1,0:T(8,128)(2,1)} %get-tuple-element.70.x_ref.z_ref, ...), custom_call_target="tpu_custom_call" | custom-call | flops 3774873600 | bytes 12582912 | tf_op jit(solution)/shard_map/scan_forward/pallas_call | solution.py:627
  250.4 12.3 %gate_back.1 = (bf16[2048,768]{1,0:T(8,128)(2,1)}, f32[16,1,128]{2,1,0:T(1,128)}) custom-call(bf16[2048,1536]{1,0:T(8,128)(2,1)} %bitcast.96, bf16[1536,768]{1,0:T(8,128)(2,1)} %bitcast.103, bf16[2048,768]{1,0:T(8,128)(2,1)} %get-tuple-element.73.y_ref, bf16[2048,1536]{1,0:T(8,128)(2,1)} %get-tuple-element.70.x_ref.z_ref, ...), custom_call_target="tpu_custom_call" | custom-call | flops 4831838208 | bytes 15728640 | tf_op jit(solution)/shard_map/gate_back/pallas_call | solution.py:724
  262.7 15.9 %gate_mid.1 = (bf16[2048,768]{1,0:T(8,128)(2,1)}, bf16[2048,768]{1,0:T(8,128)(2,1)}, bf16[2048,768]{1,0:T(8,128)(2,1)}, f32[8,768]{1,0:T(8,128)}, f32[16,1,128]{2,1,0:T(1,128)}) custom-call(bf16[2048,768]{1,0:T(8,128)(2,1)} %get-tuple-element.73.y_ref, bf16[2048,1536]{1,0:T(8,128)(2,1)} %get-tuple-element.70.x_ref.z_ref, ...), custom_call_target="tpu_custom_call" | custom-call | flops 47185920 | bytes 18874368 | tf_op jit(solution)/shard_map/gate_mid/pallas_call | solution.py:779
  278.7 16.4 %branch_pieces.1 = (bf16[2048,384]{1,0:T(8,128)(2,1)}, bf16[2048,384]{1,0:T(8,128)(2,1)}) custom-call(bf16[2048,768]{1,0:T(8,128)(2,1)} %get-tuple-element.83.refs_0_.refs_2_, bf16[1536,768]{1,0:T(8,128)(2,1)} %bitcast.104), custom_call_target="tpu_custom_call" | custom-call | flops 4831838208 | bytes 9437184 | tf_op jit(solution)/shard_map/branch_pieces/pallas_call | solution.py:923
  295.1 27.5 %gate_grads.1 = (bf16[1536,768]{1,0:T(8,128)(2,1)}, bf16[1536,768]{1,0:T(8,128)(2,1)}, bf16[1024,384]{1,0:T(8,128)(2,1)}) custom-call(bf16[2048,1536]{1,0:T(8,128)(2,1)} %bitcast.97, bf16[2048,1536]{1,0:T(8,128)(2,1)} %get-tuple-element.85.refs_1_.refs_0_, bf16[2048,768]{1,0:T(8,128)(2,1)} %get-tuple-element.83.refs_0_.refs_2_, ...), custom_call_target="tpu_custom_call" | custom-call | flops 9663676416 | bytes 12582912 | tf_op jit(solution)/shard_map/gate_grads/pallas_call | solution.py:961
  322.6 33.9 %scan_backward.2 = (bf16[2048,768]{1,0:T(8,128)(2,1)}, bf16[2048,384]{1,0:T(8,128)(2,1)}, f32[16,1,128]{2,1,0:T(1,128)}, f32[8,768]{1,0:T(8,128)}, f32[8,256]{1,...) custom-call(bf16[2048,768]{1,0:T(8,128)(2,1)} %get-tuple-element.79., ...), custom_call_target="tpu_custom_call" | custom-call | flops 4718592000 | bytes 9437184 | tf_op jit(solution)/shard_map/scan_backward/pallas_call | solution.py:801
  360.2 2.7 fusion.3
  364.2 8.7 %home_out.1 = bf16[2048,384]{1,0:T(8,128)(2,1)} custom-call(f32[16,1,128]{2,1,0:T(1,128)} %convert_bitcast_fusion.2.order_ref, bf16[2048,384]{1,0:T(8,128)(2,1)} %get-tuple-element.84.a_ref, bf16[2048,384]{1,0:T(8,128)(2,1)} %pad_maximum_fusion.b_ref), custom_call_target="tpu_custom_call" | custom-call | flops 3221225472 | bytes 7864320 | tf_op jit(solution)/shard_map/home_out/pallas_call | solution.py:756
  372.9 44.6 %scan_backward.3 = (bf16[2048,768]{1,0:T(8,128)(2,1)}, bf16[2048,384]{1,0:T(8,128)(2,1)}, f32[16,1,128]{2,1,0:T(1,128)}, f32[8,768]{1,0:T(8,128)}, f32[8,256]{1,...) custom-call(bf16[2048,768]{1,0:T(8,128)(2,1)} %get-tuple-element.79., ...), custom_call_target="tpu_custom_call", output_to_operand_aliasing={{0}: (12, {}), {1}: (13, {}), {2}: (14, {})} | custom-call | flops 4718592000 | bytes 9437184 | tf_op jit(solution)/shard_map/scan_backward/pallas_call | solution.py:801
  420.1 15.1 %scan_grads.1 = (bf16[1536,768]{1,0:T(8,128)(2,1)}, bf16[1536,384]{1,0:T(8,128)(2,1)}) custom-call(bf16[2048,1536]{1,0:T(8,128)(2,1)} %get-tuple-element.85.refs_1_.refs_0_, bf16[2048,1536]{1,0:T(8,128)(2,1)} %get-tuple-element.85.refs_1_.refs_0_, bf16[2048,768]{1,0:T(8,128)(2,1)} %get-tuple-element.98.refs_2_.refs_1_, ...), custom_call_target="tpu_custom_call" | custom-call | flops 7247757312 | bytes 12582912 | tf_op jit(solution)/shard_map/scan_grads/pallas_call | solution.py:961
  436.5 34.6 %input_pieces.1 = (bf16[2048,384]{1,0:T(8,128)(2,1)}, bf16[2048,384]{1,0:T(8,128)(2,1)}, bf16[1,192,768]{2,1,0:T(8,128)(2,1)}, bf16[1,192,768]{2,1,0:T(8,128)(2,...) custom-call(bf16[2048,768]{1,0:T(8,128)(2,1)} %get-tuple-element.86.refs_3_.refs_0_, ...), custom_call_target="tpu_custom_call" | custom-call | flops 12079595520 | bytes 14155776 | tf_op jit(solution)/shard_map/input_pieces/pallas_call | solution.py:923
  472.8 2.6 fusion.2.refs_1_
  475.3 2.7 constant_dynamic-slice_fusion.refs_0_
  479.7 45.0 %last_exchange.1 = (bf16[2048,384]{1,0:T(8,128)(2,1)}, bf16[3,192,768]{2,1,0:T(8,128)(2,1)}, f32[7,8,768]{2,1,0:T(8,128)}, f32[192,384]{1,0:T(8,128)}) custom-call(bf16[2048,384]{1,0:T(8,128)(2,1)} %get-tuple-element.108.refs_0_, bf16[4,192,768]{2,1,0:T(8,128)(2,1)} %fusion.2.refs_1_, f32[8,768]{1,0:T(8,128)} %pad_maximum_fusion.3.refs_2_, ...), custom_call_target="tpu_custom_call" | custom-call | tf_op jit(solution)/shard_map/last_exchange/pallas_call | solution.py:1019
  525.4 10.0 %home_back.1 = bf16[2048,384]{1,0:T(8,128)(2,1)} custom-call(f32[16,1,128]{2,1,0:T(1,128)} %convert_bitcast_fusion.2.order_ref, bf16[2048,384]{1,0:T(8,128)(2,1)} %get-tuple-element.107.a_ref, bf16[2048,384]{1,0:T(8,128)(2,1)} %get-tuple-element.117.b_ref, bf16[2048,384]{1,0:T(8,128)(2,1)} %constant_dynamic-slice_fusion.refs_0_, ...), custom_call_target="tpu_custom_call" | custom-call | flops 3221225472 | bytes 7864320 | tf_op jit(solution)/shard_map/home_back/pallas_call | solution.py:756
  535.4 5.0 all-to-all-start
  552.9 15.6 %exchange.1 = f32[3,192,384]{2,1,0:T(8,128)} custom-call(f32[192,384]{1,0:T(8,128)} %pad_maximum_fusion.2.refs_0_), custom_call_target="tpu_custom_call" | custom-call | tf_op jit(solution)/shard_map/exchange/pallas_call | solution.py:187
  568.5 2.0 reduce_sum.88
  577.7 2.9 fusion.1
  580.7 3.0 fusion
  (142 shorter events, 42.1 us)
Async XLA Ops:
  175.3 7.5 %copy-start.34 = (f32[3,12]{1,0:T(4,128)S(1)}, f32[3,12]{1,0:T(4,128)}, u32[]{:S(2)}) copy-start(f32[3,12]{1,0:T(4,128)} %param.24) | copy-start | bytes 436
  175.3 7.6 %copy-start.32 = (f32[768]{0:T(1024)S(1)}, f32[768]{0:T(1024)}, u32[]{:S(2)}) copy-start(f32[768]{0:T(1024)} %param.25) | copy-start | bytes 9220
  175.3 8.2 %copy-start.29 = (f32[5,256]{1,0:T(8,128)S(1)}, f32[5,256]{1,0:T(8,128)}, u32[]{:S(2)}) copy-start(f32[5,256]{1,0:T(8,128)} %param.23) | copy-start | bytes 15364
  175.3 8.8 %copy-start.35 = (s32[2]{0:T(128)S(1)}, s32[2]{0:T(128)}, u32[]{:S(2)}) copy-start(s32[2]{0:T(128)} %param.16) | copy-start | bytes 28
  175.3 9.7 %copy-start.24 = (f32[5,768]{1,0:T(8,128)S(1)}, f32[5,768]{1,0:T(8,128)}, u32[]{:S(2)}) copy-start(f32[5,768]{1,0:T(8,128)} %param.22) | copy-start | bytes 46084
  322.6 33.9 %copy-start.5 = (bf16[1536,768]{1,0:T(8,128)(2,1)S(1)}, bf16[1536,768]{1,0:T(8,128)(2,1)}, u32[]{:S(2)}) copy-start(bf16[1536,768]{1,0:T(8,128)(2,1)} %get-tuple-element.90) | copy-start | bytes 7077892
  360.2 2.7 copy-start.13
  372.9 44.6 %copy-start.28 = (f32[8,256]{1,0:T(8,128)S(1)}, f32[8,256]{1,0:T(8,128)}, u32[]{:S(2)}) copy-start(f32[8,256]{1,0:T(8,128)} %get-tuple-element.105) | copy-start | bytes 24580
  372.9 45.9 %copy-start.27 = (f32[16,1,128]{2,1,0:T(1,128)S(1)}, f32[16,1,128]{2,1,0:T(1,128)}, u32[]{:S(2)}) copy-start(f32[16,1,128]{2,1,0:T(1,128)} %get-tuple-element.103.refs_3_) | copy-start | bytes 24580
  420.1 15.1 %copy-start.1 = (bf16[4,192,768]{2,1,0:T(8,128)(2,1)S(1)}, bf16[4,192,768]{2,1,0:T(8,128)(2,1)}, u32[]{:S(2)}) copy-start(bf16[4,192,768]{2,1,0:T(8,128)(2,1)} %fusion.3) | copy-start | bytes 3538948
  420.1 15.1 %copy-start.15 = (bf16[2,192,768]{2,1,0:T(8,128)(2,1)S(1)}, bf16[2,192,768]{2,1,0:T(8,128)(2,1)}, u32[]{:S(2)}) copy-start(bf16[2,192,768]{2,1,0:T(8,128)(2,1)} %get-tuple-element.101) | copy-start | bytes 1769476
  420.1 15.1 %copy-start.16 = (bf16[2,192,768]{2,1,0:T(8,128)(2,1)S(1)}, bf16[2,192,768]{2,1,0:T(8,128)(2,1)}, u32[]{:S(2)}) copy-start(bf16[2,192,768]{2,1,0:T(8,128)(2,1)} %get-tuple-element.100) | copy-start | bytes 1769476
  436.5 35.4 %copy-start.22 = (f32[8,256]{1,0:T(8,128)S(1)}, f32[8,256]{1,0:T(8,128)}, u32[]{:S(2)}) copy-start(f32[8,256]{1,0:T(8,128)} %add.139.refs_10_) | copy-start | bytes 24580
  436.5 35.4 %copy-start.30 = (f32[8,128]{1,0:T(8,128)S(1)}, f32[8,128]{1,0:T(8,128)}, u32[]{:S(2)}) copy-start(f32[8,128]{1,0:T(8,128)} %get-tuple-element.114) | copy-start | bytes 12292
  436.5 35.4 %copy-start.31 = (f32[8,128]{1,0:T(8,128)S(1)}, f32[8,128]{1,0:T(8,128)}, u32[]{:S(2)}) copy-start(f32[8,128]{1,0:T(8,128)} %get-tuple-element.115) | copy-start | bytes 12292
  436.5 36.3 %copy-start.14 = (bf16[1536,768]{1,0:T(8,128)(2,1)S(1)}, bf16[1536,768]{1,0:T(8,128)(2,1)}, u32[]{:S(2)}) copy-start(bf16[1536,768]{1,0:T(8,128)(2,1)} %get-tuple-element.102) | copy-start | bytes 7077892
  475.3 3.7 copy-start.25
  475.3 3.7 copy-start.26
  535.4 5.0 copy-start.20
  535.4 5.7 copy-start.3
  535.4 45.3 %all-to-all-start = ((bf16[8,256,384]{2,1,0:T(8,128)(2,1)}), bf16[8,256,384]{2,1,0:T(8,128)(2,1)S(1)}, u32[]{:S(2)}, u32[]{:S(2)}) async-start(bf16[8,256,384]{2,1,0:T(8,128)(2,1)} %bitcast.105), calls=%async_computation | async-start | bytes 3145728 | tf_op jit(solution)/shard_map/all_to_all | solution.py:1258
  542.9 4.7 copy-start
  568.4 6.8 %copy-start.33 = (bf16[192]{0:T(256)(128)(2,1)S(1)}, bf16[192]{0:T(256)(128)(2,1)}, u32[]{:S(2)}) copy-start(bf16[192]{0:T(256)(128)(2,1)} %param.17) | copy-start | bytes 1156
  570.4 7.3 %copy-start.2 = (bf16[2048,384]{1,0:T(8,128)(2,1)S(1)}, bf16[2048,384]{1,0:T(8,128)(2,1)}, u32[]{:S(2)}) copy-start(bf16[2048,384]{1,0:T(8,128)(2,1)} %param.13) | copy-start | bytes 4718596
  (13 other events, 20.9 us)

commit v4 on v3

--- a/solution.py
+++ b/solution.py
@@ -13,6 +13,7 @@
 HEAD = 64
 EPS = 1e-05
 NEG = -1e30
+LIGHT = 1000
 LIMIT = 60 * 1024 * 1024
 AXES = ("dp", "head")
 F32 = jnp.float32
@@ -225,7 +226,7 @@
     return raw, steps, rates, logs
 
 
-def forward_moves(steps, rows_ref, w_ref, full_ref, fw_ref, pass_sems, across_sems, side_sems, local_sems):
+def forward_moves(steps, rows_ref, w_ref, full_ref, fw_ref, pass_sems, across_sems, side_sems, local_sems, rows_held, w_held):
     size, quarter = rows_ref.shape[0], rows_ref.shape[2]
     line = size // 2
     parts = w_ref.shape[0]
@@ -234,16 +235,17 @@
     far, near, back = row_forward(size, quarter, rows_ref, full_ref, pass_sems)
     across, side = shard_spread(w_ref, fw_ref, across_sems, side_sems)
     mine = pl.ds(pl.multiple_of(own * quarter, 128), quarter)
+    into = [pltpu.make_async_copy(rows_ref, rows_held, local_sems.at[0]), pltpu.make_async_copy(w_ref, w_held, local_sems.at[1])]
     held = [
-        pltpu.make_async_copy(rows_ref, full_ref.at[:, :, mine], local_sems.at[0]),
-        pltpu.make_async_copy(w_ref, fw_ref.at[me], local_sems.at[1]),
+        pltpu.make_async_copy(rows_held, full_ref.at[:, :, mine], local_sems.at[2]),
+        pltpu.make_async_copy(w_held, fw_ref.at[me], local_sems.at[3]),
     ]
 
     @pl.when(step == 0)
     def _():
+        for copy in into:
+            copy.start()
         greet([(me ^ 1, own)] + [(me ^ (2 * j), own) for j in range(1, line)] + [(me, own ^ 1), (me, own ^ 2)])
-        for copy in held:
-            copy.start()
         for k in range(size):
             near(k).start()
         for k in range(size // 2):
@@ -264,6 +266,12 @@
             if part + 2 < parts:
                 for j in range(1, line):
                     across(part + 2, j).start()
+
+    @pl.when(step == 1)
+    def _():
+        for first, second in zip(into, held):
+            first.wait()
+            second.start()
 
     groups = 4
     for group in range(groups):
@@ -362,10 +370,8 @@
     return jnp.concatenate(blocks, axis=0)
 
 
-def project_kernel(heads, moves, order_ref, x_ref, w_ref, src_ref, out_ref, inv_ref, uzx_ref, ubd_ref, dst_ref, gain_ref, *sems):
+def project_kernel(heads, order_ref, x_ref, w_ref, out_ref, inv_ref, uzx_ref, ubd_ref, gain_ref):
     deep, width = x_ref.shape[1], 2 * heads * HEAD
-    at_step = pl.program_id(0)
-    background(at_step == 0, at_step == pl.num_programs(0) - 1, moves, (src_ref,), (dst_ref,), *sems)
 
     @pl.when(pl.program_id(0) == 0)
     def _():
@@ -662,7 +668,9 @@
             sems((2, 3, size)),
             sems((2, PARTS, line)),
             sems((2, PARTS, line)),
-            sems((2,)),
+            sems((4,)),
+            pltpu.VMEM(came.shape, BF16),
+            pltpu.VMEM((PARTS, w_out.shape[0] // PARTS, w_out.shape[1]), BF16),
         ],
         compiler_params=params("arbitrary", "arbitrary", number=number),
         cost_estimate=pl.CostEstimate(flops=rows * width * 2 * 1200, bytes_accessed=rows * width * 8, transcendentals=rows * width * 6),
@@ -670,33 +678,30 @@
     )(u_zx, u_zx, u_bd, par, pbc, hp, came, cut_shard(w_out))
 
 
-def run_project(heads, order, x, w_in, moved, number):
+def run_project(heads, order, x, w_in):
     rows, deep = x.shape
     wide = w_in.shape[1]
     width = 2 * heads * HEAD
     step = 256
-    moves = (("turn", "dp"),)
-    anywhere = pl.BlockSpec(memory_space=pl.ANY)
     at = lambda i: (i, 0)
     fixed = lambda i: (0, 0)
     thin = pl.BlockSpec((step // T, 1, T), lambda i: (i, 0, 0))
     return pl.pallas_call(
-        functools.partial(project_kernel, heads, moves),
+        functools.partial(project_kernel, heads),
         grid=(rows // step,),
-        in_specs=[thin, pl.BlockSpec((rows, deep), fixed), pl.BlockSpec((deep, wide), fixed), anywhere],
-        out_specs=[pl.BlockSpec((step, deep), at), thin, pl.BlockSpec((step, width), at), pl.BlockSpec((step, wide - width), at), anywhere],
+        in_specs=[thin, pl.BlockSpec((rows, deep), fixed), pl.BlockSpec((deep, wide), fixed)],
+        out_specs=[pl.BlockSpec((step, deep), at), thin, pl.BlockSpec((step, width), at), pl.BlockSpec((step, wide - width), at)],
         out_shape=[
             jax.ShapeDtypeStruct((rows, deep), BF16),
             jax.ShapeDtypeStruct((rows // T, 1, T), F32),
             jax.ShapeDtypeStruct((rows, width), BF16),
             jax.ShapeDtypeStruct((rows, wide - width), F32),
-        ]
-        + move_outs(moves, (moved,)),
-        scratch_shapes=[pltpu.VMEM((8, deep), F32)] + move_scratch(moves, (moved,)),
-        compiler_params=params("arbitrary", number=number),
-        cost_estimate=pl.CostEstimate(flops=rows * deep * (rows + wide) * 2, bytes_accessed=rows * deep * 8, transcendentals=rows),
+        ],
+        scratch_shapes=[pltpu.VMEM((8, deep), F32)],
+        compiler_params=params("arbitrary"),
+        cost_estimate=pl.CostEstimate(flops=LIGHT, bytes_accessed=LIGHT, transcendentals=0),
         name="project",
-    )(order, x, w_in, moved)
+    )(order, x, w_in)
 
 
 def run_sort(order, values):
@@ -740,7 +745,7 @@
     )(grads, w_out, y, u_zx, par, mask)
 
 
-def run_home(order, sums, extra, deep, name):
+def run_home(order, sums, extra, deep, name, after=()):
     rows, quarter = sums[0].shape
     step = 512
     many = rows // step
@@ -753,6 +758,8 @@
         specs += [pl.BlockSpec((step, quarter), into), thin, pl.BlockSpec((8, quarter), lambda i: (0, 0)), thin, thin]
         specs += [pl.BlockSpec((3, step // T, 1, T), lambda i: (0, jnp.minimum(i, many - 1), 0, 0))]
         values += list(extra)
+    values += list(after)
+    specs += [pl.BlockSpec(memory_space=pl.ANY)] * len(after)
     return pl.pallas_call(
         functools.partial(home_kernel, extra is not None, float(deep)),
         grid=(2 * many,),
@@ -790,7 +797,7 @@
     )(y, u_zx, dyn, par, mask, ss, co)
 
 
-def run_backward(heads, slot, dy, u_zx, c, cb, u_bd, st, par, pbc, hp, before, moves, values, number):
+def run_backward(heads, slot, dy, u_zx, c, cb, u_bd, st, par, pbc, hp, before, moves, values, number, after=()):
     rows, width = dy.shape
     chunks = LEN // T
     place = lambda s, i: slot * chunks + chunks - 1 - i
@@ -799,7 +806,7 @@
     fixed = lambda s, i: (0, 0)
     anywhere = pl.BlockSpec(memory_space=pl.ANY)
     return pl.pallas_call(
-        functools.partial(backward_kernel, heads, len(before), tuple(moves)),
+        functools.partial(backward_kernel, heads, len(before) + len(after), tuple(moves)),
         grid=(1, chunks),
         in_specs=[
             pl.BlockSpec((T, width), at),
@@ -812,7 +819,7 @@
             pl.BlockSpec((8, 2 * N), fixed),
             pl.BlockSpec((8, 128), fixed),
         ]
-        + [anywhere] * (len(moves) + len(before)),
+        + [anywhere] * (len(moves) + len(before) + len(after)),
         out_specs=[
             pl.BlockSpec((T, width), at),
             pl.BlockSpec((T, 3 * N), at),
@@ -843,15 +850,15 @@
         + move_scratch(moves, values),
         input_output_aliases={9 + len(moves) + i: i for i in range(len(before))},
         compiler_params=params("arbitrary", "arbitrary", number=number),
-        cost_estimate=pl.CostEstimate(flops=LEN * width * 2 * 3000, bytes_accessed=LEN * width * 12, transcendentals=LEN * width * 8),
+        cost_estimate=pl.CostEstimate(flops=LIGHT, bytes_accessed=LIGHT, transcendentals=0),
         name="scan_backward",
-    )(dy, u_zx, c, cb, u_bd, st, par, pbc, hp, *values, *before)
-
-
-def pieces_kernel(count, many, moves, *refs):
+    )(dy, u_zx, c, cb, u_bd, st, par, pbc, hp, *values, *before, *after)
+
+
+def pieces_kernel(count, many, moves, extra, *refs):
     total = len(moves)
     values, weights, srcs = refs[:count], refs[count : 2 * count], refs[2 * count : 2 * count + total]
-    refs = refs[2 * count + total :]
+    refs = refs[2 * count + total + extra :]
     far_ref, own_ref = refs[:2]
     dsts, refs = refs[2 : 2 + total], refs[2 + total :]
     sent_ref, came_ref, near_sems = refs[:3]
@@ -911,9 +918,9 @@
     return any(move[0] == "spread" and move[1] == "head" for move in moves)
 
 
-def run_pieces(values, weights, quarter, name, moves, moved, number):
+def run_pieces(values, weights, quarter, name, moves, moved, number, after=()):
     rows = values[0].shape[0]
-    step = 256
+    step = 512
     many = rows // step
     anywhere = pl.BlockSpec(memory_space=pl.ANY)
     specs = [pl.BlockSpec((step, v.shape[1]), lambda i: (lax.rem(i, many), 0)) for v in values]
@@ -921,22 +928,22 @@
         specs.append(pl.BlockSpec((weight.shape[0], wide), lambda i, block=block: (0, block)))
     depth = sum(v.shape[1] for v in values)
     return pl.pallas_call(
-        functools.partial(pieces_kernel, len(values), many, tuple(moves)),
+        functools.partial(pieces_kernel, len(values), many, tuple(moves), len(after)),
         grid=(2 * many,),
-        in_specs=specs + [anywhere] * len(moves),
+        in_specs=specs + [anywhere] * (len(moves) + len(after)),
         out_specs=[pl.BlockSpec((step, quarter), lambda i: (jnp.maximum(i - many, 0), 0))] * 2 + [anywhere] * len(moves),
         out_shape=[jax.ShapeDtypeStruct((rows, quarter), BF16)] * 2 + move_outs(moves, moved),
         scratch_shapes=[pltpu.VMEM((many, step, 2 * quarter), BF16)] * 2 + [pltpu.SemaphoreType.DMA((2, many))] + move_scratch(moves, moved),
         compiler_params=params("arbitrary", number=number),
-        cost_estimate=pl.CostEstimate(flops=rows * depth * quarter * 8, bytes_accessed=rows * (depth + 4 * quarter) * 2, transcendentals=0),
+        cost_estimate=pl.CostEstimate(flops=LIGHT, bytes_accessed=LIGHT, transcendentals=0),
         name=name,
-    )(*values, *[w for w, _, _ in weights], *moved)
-
-
-def grads_kernel(count, parts, moves, *refs):
+    )(*values, *[w for w, _, _ in weights], *moved, *after)
+
+
+def grads_kernel(count, parts, moves, extra, *refs):
     total = len(moves)
     lefts, rights, srcs = refs[:count], refs[count : 2 * count], refs[2 * count : 2 * count + total]
-    refs = refs[2 * count + total :]
+    refs = refs[2 * count + total + extra :]
     outs, dsts, sems = refs[:count], refs[count : count + total], refs[count + total :]
     step = pl.program_id(0)
     if moves:
@@ -949,7 +956,7 @@
             outs[which][...] = out.astype(BF16)
 
 
-def run_grads(pairs, name, moves=(), moved=(), number=0):
+def run_grads(pairs, name, moves=(), moved=(), number=0, after=()):
     rows, deep = pairs[0][0].shape
     step = 512
     parts = deep // step
@@ -959,19 +966,17 @@
     specs = [pl.BlockSpec((rows, step), lambda i, at=into(w): (0, at(i))) for w in range(count)]
     specs += [pl.BlockSpec(right.shape, lambda i: (0, 0)) for _, right in pairs]
     return pl.pallas_call(
-        functools.partial(grads_kernel, count, parts, tuple(moves)),
+        functools.partial(grads_kernel, count, parts, tuple(moves), len(after)),
         grid=(count * parts,),
-        in_specs=specs + [anywhere] * len(moves),
+        in_specs=specs + [anywhere] * (len(moves) + len(after)),
         out_specs=[pl.BlockSpec((step, right.shape[1]), lambda i, at=into(w): (at(i), 0)) for w, (_, right) in enumerate(pairs)]
         + [anywhere] * len(moves),
         out_shape=[jax.ShapeDtypeStruct((deep, right.shape[1]), BF16) for _, right in pairs] + move_outs(moves, moved),
         scratch_shapes=move_scratch(moves, moved),
         compiler_params=params("arbitrary", number=number),
-        cost_estimate=pl.CostEstimate(
-            flops=sum(rows * deep * right.shape[1] * 2 for _, right in pairs), bytes_accessed=rows * deep * 2 * count, transcendentals=0
-        ),
+        cost_estimate=pl.CostEstimate(flops=LIGHT, bytes_accessed=LIGHT, transcendentals=0),
         name=name,
-    )(*[left for left, _ in pairs], *[right for _, right in pairs], *moved)
+    )(*[left for left, _ in pairs], *[right for _, right in pairs], *moved, *after)
 
 
 def last_kernel(moves, *refs):
@@ -1070,36 +1075,62 @@
     return across, side
 
 
-def entry_kernel(parts, x_ref, w_ref, fx_ref, fw_ref, row_sems, pass_sems, across_sems, side_sems, local_sems):
+def entry_kernel(parts, x_ref, w_ref, fx_ref, fw_ref, row_sems, pass_sems, line_sems, side_sems, local_sems, x_held, w_held):
     size, quarter = x_ref.shape[0], x_ref.shape[2]
     line = size // 2
     me, own = lax.axis_index("dp"), lax.axis_index("head")
+    spot = me >> 1
     mine = pl.ds(pl.multiple_of(own * quarter, 128), quarter)
     far, near, back = row_forward(size, quarter, None, fx_ref, pass_sems)
-    across, side = shard_spread(w_ref, fw_ref, across_sems, side_sems)
+
+    def remote(src, dst, sems, slot, peer):
+        return pltpu.make_async_remote_copy(
+            src_ref=src, dst_ref=dst, send_sem=sems.at[(0,) + slot], recv_sem=sems.at[(1,) + slot], device_id=(peer, own), device_id_type=MESH
+        )
 
     def rows(k):
-        return pltpu.make_async_remote_copy(
-            src_ref=x_ref.at[me ^ k],
-            dst_ref=fx_ref.at[me, :, mine],
-            send_sem=row_sems.at[0, k],
-            recv_sem=row_sems.at[1, k],
-            device_id=(me ^ k, own),
-            device_id_type=MESH,
-        )
-
-    greet([(me ^ k, own) for k in range(1, size)] + [(me, own ^ 1), (me, own ^ 2)])
+        return remote(x_ref.at[me ^ k], fx_ref.at[me, :, mine], row_sems, (k,), me ^ k)
+
+    def along(way, part, j):
+        sign = 1 - 2 * way
+        origin = jnp.clip(me - sign * 2 * (j - 1), 0, size - 1)
+        peer = jnp.clip(me + sign * 2, 0, size - 1)
+        here = fw_ref.at[origin, part]
+        return remote(w_ref.at[part] if j == 1 else here, here, line_sems, (way, part, j - 1), peer)
+
+    def came(way, part, j):
+        sign = 1 - 2 * way
+        here = fw_ref.at[jnp.clip(me - sign * 2 * j, 0, size - 1), part]
+        return remote(here, here, line_sems, (way, part, j - 1), me)
+
+    def side(way, part, j):
+        sign = 1 - 2 * way
+        here = fw_ref.at[jnp.clip(me - sign * 2 * j, 0, size - 1), part]
+        return remote(w_ref.at[part] if j == 0 else here, here, side_sems, (way, part, j), me ^ 1)
+
+    def goes_on(way):
+        return spot < line - 1 if way == 0 else spot > 0
+
+    def arrives(way, j):
+        return spot >= j if way == 0 else spot < line - j
+
+    greet_rows = [(me ^ k, own) for k in range(1, size)] + [(me, own ^ 1), (me, own ^ 2)]
+    into = [pltpu.make_async_copy(x_ref.at[me], x_held, local_sems.at[0]), pltpu.make_async_copy(w_ref, w_held, local_sems.at[1])]
     held = [
-        pltpu.make_async_copy(x_ref.at[me], fx_ref.at[me, :, mine], local_sems.at[0]),
-        pltpu.make_async_copy(w_ref, fw_ref.at[me], local_sems.at[1]),
+        pltpu.make_async_copy(x_held, fx_ref.at[me, :, mine], local_sems.at[2]),
+        pltpu.make_async_copy(w_held, fw_ref.at[me], local_sems.at[3]),
     ]
-    for copy in held:
+    for copy in into:
         copy.start()
+    greet(greet_rows)
     order = turn_order(size)
     for k in order:
         rows(k).start()
     for part in range(parts):
-        side(part, 0).start()
+        side(0, part, 0).start()
+    for first, second in zip(into, held):
+        first.wait()
+        second.start()
     held[0].wait()
     far(0).start()
     near(0).start()
@@ -1107,19 +1138,31 @@
         rows(k).wait_recv()
         far(k).start()
         near(k).start()
-    for part in range(min(2, parts)):
-        for j in range(1, line):
-            across(part, j).start()
+    for way in range(2):
+
+        @pl.when(goes_on(way))
+        def _():
+            for part in range(parts):
+                along(way, part, 1).start()
+
     for k in [0] + order:
         far(k).wait_recv()
         back(k).start()
-    for part in range(parts):
-        for j in range(1, line):
-            across(part, j).wait_recv()
-            side(part, j).start()
-        if part + 2 < parts:
-            for j in range(1, line):
-                across(part + 2, j).start()
+    for j in range(1, line):
+        for part in range(parts):
+            for way in range(2):
+
+                @pl.when(arrives(way, j))
+                def _():
+                    came(way, part, j).wait_recv()
+                    side(way, part, j).start()
+
+                if j + 1 < line:
+
+                    @pl.when(arrives(way, j) & goes_on(way))
+                    def _():
+                        along(way, part, j + 1).start()
+
     held[1].wait()
     for k in range(size):
         near(k).wait()
@@ -1128,10 +1171,24 @@
         if k:
             rows(k).wait_send()
     for part in range(parts):
-        for j in range(line):
-            side(part, j).wait()
-            if j:
-                across(part, j).wait_send()
+        side(0, part, 0).wait()
+        for way in range(2):
+
+            @pl.when(goes_on(way))
+            def _():
+                along(way, part, 1).wait_send()
+
+            for j in range(1, line):
+
+                @pl.when(arrives(way, j))
+                def _():
+                    side(way, part, j).wait()
+
+                if j + 1 < line:
+
+                    @pl.when(arrives(way, j) & goes_on(way))
+                    def _():
+                        along(way, part, j + 1).wait_send()
 
 
 PARTS = 4
@@ -1156,7 +1213,15 @@
         in_specs=[anywhere] * 2,
         out_specs=[anywhere] * 2,
         out_shape=[jax.ShapeDtypeStruct((size, rows // size, quarter * 4), BF16), full_shape(size, w_in)],
-        scratch_shapes=[sems((2, size)), sems((2, 3, size)), sems((2, PARTS, line)), sems((2, PARTS, line)), sems((2,))],
+        scratch_shapes=[
+            sems((2, size)),
+            sems((2, 3, size)),
+            sems((2, 2, PARTS, line)),
+            sems((2, 2, PARTS, line)),
+            sems((4,)),
+            pltpu.VMEM((rows // size, quarter), BF16),
+            pltpu.VMEM((PARTS, w_in.shape[0] // PARTS, w_in.shape[1]), BF16),
+        ],
         compiler_params=pltpu.CompilerParams(collective_id=number, has_side_effects=True, vmem_limit_bytes=LIMIT),
         name="entry",
     )(tokens.reshape(size, rows // size, quarter), cut_shard(w_in))
@@ -1184,7 +1249,9 @@
     )
     blocks = lambda value: value.reshape(size, rows // size, quarter)
     came_x, w_in = run_entry(tokens, packed, 1)
-    normed, inv_one, u_zx, u_bd, own_g = run_project(heads, arrange, came_x, w_in, blocks(cotangent), 2)
+    came_x, later = lax.optimization_barrier((came_x, cotangent))
+    own_g = lax.all_to_all(later, "dp", split_axis=0, concat_axis=0, tiled=True)
+    normed, inv_one, u_zx, u_bd = run_project(heads, arrange, came_x, w_in)
 
     par = jnp.concatenate([conv_x, jnp.repeat(head_params[2:3], HEAD, axis=1), gate_gain[None], jnp.zeros((1, width), F32)], axis=0)
     pbc = jnp.concatenate([conv_bc, jnp.zeros((3, 2 * N), F32)], axis=0)
@@ -1192,7 +1259,7 @@
     positions = lax.broadcasted_iota(jnp.int32, (lengths.shape[0], LEN), 1)
     mask = (positions < lengths[:, None]).astype(F32).reshape(rows // T, 1, T)
 
-    sorted_g = run_sort(arrange, own_g.reshape(rows, quarter))
+    sorted_g = run_sort(arrange, own_g)
     y, ss, c, cb, st, full_g, w_o = run_forward(heads, u_zx, u_bd, par, pbc, hp, blocks(sorted_g), w_out, 3)
     w_o = w_o.reshape(deep, width)
     full_g = full_g.reshape(rows, deep)
@@ -1215,22 +1282,22 @@
 
     scan = functools.partial(run_backward, heads)
     shared = (dy, u_zx, c, cb, u_bd, st, par, pbc, hp)
-    half_rows = rows // 2
     out_far, out_own = run_pieces([yg], [(w_o, 0, width)], quarter, "branch_pieces", [], [], 5)
-    grad_o, grad_z, far0 = run_grads([(full_g, yg), (normed, dz)], "gate_grads", [("rows", "head", 2, 0, half_rows)], [out_far], 6)
+    out_arrived = lax.ppermute(out_far, "head", [(i, i ^ 2) for i in range(lax.axis_size("head"))])
+    grad_o, grad_z = run_grads([(full_g, yg), (normed, dz)], "gate_grads", after=[out_far])
     grad_o, grad_z = pairs(grad_o), fours(grad_z)
-    *back0, gx0, gb0, gh0, came_o, came_z, far1 = scan(
-        0, *shared, (), [("half", "dp", 0), ("half", "dp", 1), ("rows", "head", 2, half_rows, half_rows)], [grad_o, grad_z, out_far], 7
-    )
-    sent_out = run_home(arrange, [out_own, jnp.concatenate([far0, far1], axis=0)], None, deep, "home_out")
+    *back0, gx0, gb0, gh0, came_o, came_z = scan(0, *shared, (), [("half", "dp", 0), ("half", "dp", 1)], [grad_o, grad_z], 7)
+    sent_out = run_home(arrange, [out_own, out_arrived], None, deep, "home_out", [back0[0]])
+    got_out = lax.all_to_all(sent_out, "dp", split_axis=0, concat_axis=0, tiled=True)
     kept_o = keep(grad_o, came_o, 0).reshape(size // 4, 2, own_w, width)
     kept_z = keep(grad_z, came_z, 1)
-    *back1, gx1, gb1, gh1, got_out, came_z, came_o = scan(
-        1, *shared, back0, [("turn", "dp"), ("half", "dp", 0), ("half", "dp", 1)], [blocks(sent_out), kept_z, kept_o], 8
+    *back1, gx1, gb1, gh1 = scan(1, *shared, back0, [], [], 0, [sent_out])
+    dux, dbd, rd_x = back1
+    grad_x, grad_bd, came_z, came_o = run_grads(
+        [(normed, dux), (normed, dbd)], "scan_grads", [("half", "dp", 0), ("half", "dp", 1)], [kept_z, kept_o], 8
     )
-    dux, dbd, rd_x = back1
     kept_z, kept_o = keep(kept_z, came_z, 0), keep(kept_o, came_o, 1)
-    grad_x, grad_bd = run_grads([(normed, dux), (normed, dbd)], "scan_grads")
+    final_out = (tokens.astype(F32) + got_out.astype(F32)).astype(BF16)
     grad_x, grad_bd = pairs(grad_x), pairs(grad_bd)
     gb = gb0 + gb1
     d_far, d_own, line_o, line_z, came_x2, got_rows, got_gb = run_pieces(
@@ -1241,6 +1308,7 @@
         [("direct", "dp", 2), ("direct", "dp", 2), ("half", "dp", 0), ("spread", "head"), ("spread", "head")],
         [kept_o, kept_z, grad_x, rd_z + rd_x, gb],
         9,
+        [final_out],
     )
     kept_x = keep(grad_x, came_x2, 0)
     gb = gb[:5] + jnp.sum(got_gb, axis=0)[:5]
@@ -1258,7 +1326,6 @@
     got_back = lax.all_to_all(sent_back, "dp", split_axis=0, concat_axis=0, tiled=True)
     final_back = (cotangent.astype(F32) + got_back.astype(F32)).astype(BF16)
 
-    final_out = (tokens.astype(F32) + got_out.reshape(rows, quarter).astype(F32)).astype(BF16)
     grad_out, grad_z = total(kept_o, line_o, 2), total(kept_z, line_z, 2)
     grad_x = total(kept_x, line_x, 1)
     small = small + jnp.sum(got_small, axis=0)

time: 586 us -> 532 us (0.908)
  Pallas kernels: 517 us -> 450 us
  starting transfers between devices: 4.97 us -> 15.9 us
  waiting for transfers between devices: 0.01 us -> 9.84 us
  other arithmetic: 34 us -> 25.7 us
    pallas_call x3, Pallas kernels: 128 us -> 92.9 us  [the longest x2 57.5 us: run_backward(): pl.pallas_call(functools.partial(backward_kernel, heads, len(before) + le...]
    pallas_call x1, Pallas kernels: 64.7 us -> 42.9 us  [run_forward(): pl.pallas_call(functools.partial(forward_kernel, heads, slots * chunks),...]
    all_to_all x1, waiting for transfers between devices: 0.01 us -> 9.83 us  [body(): lax.all_to_all(sent_back, 'dp', split_axis=0, concat_axis=0, tiled=True)]
    all_to_all x0 -> x2, starting transfers between devices: none -> 8.99 us  [the longest x1 4.87 us: body(): lax.all_to_all(sent_out, 'dp', split_axis=0, concat_axis=0, tiled=True)]
  transfers between devices with their start and end apart: 1 -> 4, of which waited for: 0 -> 1; matrix products, arithmetic and copies ran while one was open for 4% -> 5% of each run, Pallas kernels for 3% -> 28%
where the time goes in v4:
time: 532 us; the launch traced here: 527 us
  Pallas kernels  450 us (85%)
  other arithmetic  25.7 us (5%)
  local copies, waits for them, and re-layouts  23.9 us (4%)
  starting transfers between devices  15.9 us (3%)
  waiting for transfers between devices  9.84 us (2%)
    pallas_call x1, Pallas kernels, run_entry(): pl.pallas_call(functools.partial(entry_kernel, PARTS), in_specs=[anywhere...  114 us
    pallas_call x2, Pallas kernels, run_backward(): pl.pallas_call(functools.partial(backward_kernel, heads, len(before) + le...  57.5 us
    pallas_call x2, Pallas kernels, run_pieces(): pl.pallas_call(functools.partial(pieces_kernel, len(values), many, tuple(...  46.7 us
    pallas_call x1, Pallas kernels, run_last(): pl.pallas_call(functools.partial(last_kernel, tuple(moves)), in_specs=[an...  44.8 us
    pallas_call x1, Pallas kernels, run_forward(): pl.pallas_call(functools.partial(forward_kernel, heads, slots * chunks),...  42.9 us
    pallas_call x2, Pallas kernels, run_grads(): pl.pallas_call(functools.partial(grads_kernel, count, parts, tuple(moves)...  38.7 us
    pallas_call x1, Pallas kernels, run_project(): pl.pallas_call(functools.partial(project_kernel, heads), grid=(rows // st...  35.3 us
    pallas_call x2, Pallas kernels, run_home(): pl.pallas_call(functools.partial(home_kernel, extra is not None, float(de...  18.7 us
  transfers between devices with their start and end apart: 4, of which 1 were waited for; matrix products, arithmetic and copies ran while one was open for 5% of the time, Pallas kernels for 28%

profile of v4, /device:TPU:0, one launch (start us, length us, event | category | flops | bytes accessed | tf_op | source)
XLA Modules:
  0.0 527.0 jit_solution(16306912231154837777)
XLA Ops:
  6.3 114.3 %entry.1 = (bf16[8,256,1536]{2,1,0:T(8,128)(2,1)}, bf16[8,4,48,1920]{3,2,1,0:T(8,128)(2,1)}) custom-call(bf16[8,256,384]{2,1,0:T(8,128)(2,1)} %bitcast.105, bf16[4,48,1920]{2,1,0:T(8,128)(2,1)} %concatenate.37.w_ref), custom_call_target="tpu_custom_call" | custom-call | tf_op jit(solution)/shard_map/entry/pallas_call | solution.py:1211
  120.6 4.1 all-to-all-start
  125.4 35.3 %project.1 = (bf16[2048,1536]{1,0:T(8,128)(2,1)}, f32[16,1,128]{2,1,0:T(1,128)}, bf16[2048,1536]{1,0:T(8,128)(2,1)}, f32[2048,384]{1,0:T(8,128)}) custom-call(f32[16,1,128]{2,1,0:T(1,128)} %convert_bitcast_fusion.2.order_ref, bf16[2048,1536]{1,0:T(8,128)(2,1)} %bitcast.106, bf16[1536,1920]{1,0:T(8,128)(2,1)} %bitcast.94), custom_call_target="tpu_custom_call" | custom-call | flops 1000 | bytes 1000 | tf_op jit(solution)/shard_map/project/pallas_call | solution.py:689
  164.9 7.4 %sort_rows.1 = bf16[2048,384]{1,0:T(8,128)(2,1)} custom-call(f32[16,1,128]{2,1,0:T(1,128)} %convert_bitcast_fusion.2.order_ref, bf16[2048,384]{1,0:T(8,128)(2,1)} %bitcast.115), custom_call_target="tpu_custom_call" | custom-call | flops 3221225472 | bytes 3145728 | tf_op jit(solution)/shard_map/sort_rows/pallas_call | solution.py:710
  172.3 42.9 %scan_forward.1 = (bf16[2048,768]{1,0:T(8,128)(2,1)}, f32[16,1,128]{2,1,0:T(1,128)}, bf16[2048,768]{1,0:T(8,128)(2,1)}, f32[2048,256]{1,0:T(8,128)}, bf16[16,128...) custom-call(bf16[2048,1536]{1,0:T(8,128)(2,1)} %get-tuple-element.69.x_ref.z_ref, ...), custom_call_target="tpu_custom_call" | custom-call | flops 3774873600 | bytes 12582912 | tf_op jit(solution)/shard_map/scan_forward/pallas_call | solution.py:633
  215.1 12.3 %gate_back.1 = (bf16[2048,768]{1,0:T(8,128)(2,1)}, f32[16,1,128]{2,1,0:T(1,128)}) custom-call(bf16[2048,1536]{1,0:T(8,128)(2,1)} %bitcast.99, bf16[1536,768]{1,0:T(8,128)(2,1)} %bitcast.101, bf16[2048,768]{1,0:T(8,128)(2,1)} %get-tuple-element.72.y_ref, bf16[2048,1536]{1,0:T(8,128)(2,1)} %get-tuple-element.69.x_ref.z_ref, ...), custom_call_target="tpu_custom_call" | custom-call | flops 4831838208 | bytes 15728640 | tf_op jit(solution)/shard_map/gate_back/pallas_call | solution.py:729
  227.4 15.9 %gate_mid.1 = (bf16[2048,768]{1,0:T(8,128)(2,1)}, bf16[2048,768]{1,0:T(8,128)(2,1)}, bf16[2048,768]{1,0:T(8,128)(2,1)}, f32[8,768]{1,0:T(8,128)}, f32[16,1,128]{2,1,0:T(1,128)}) custom-call(bf16[2048,768]{1,0:T(8,128)(2,1)} %get-tuple-element.72.y_ref, bf16[2048,1536]{1,0:T(8,128)(2,1)} %get-tuple-element.69.x_ref.z_ref, ...), custom_call_target="tpu_custom_call" | custom-call | flops 47185920 | bytes 18874368 | tf_op jit(solution)/shard_map/gate_mid/pallas_call | solution.py:786
  243.4 12.2 %branch_pieces.1 = (bf16[2048,384]{1,0:T(8,128)(2,1)}, bf16[2048,384]{1,0:T(8,128)(2,1)}) custom-call(bf16[2048,768]{1,0:T(8,128)(2,1)} %get-tuple-element.78.refs_0_.refs_2_, bf16[1536,768]{1,0:T(8,128)(2,1)} %bitcast.102), custom_call_target="tpu_custom_call" | custom-call | flops 1000 | bytes 1000 | tf_op jit(solution)/shard_map/branch_pieces/pallas_call | solution.py:930
  257.4 16.8 %gate_grads.1 = (bf16[1536,768]{1,0:T(8,128)(2,1)}, bf16[1536,768]{1,0:T(8,128)(2,1)}) custom-call(bf16[2048,1536]{1,0:T(8,128)(2,1)} %bitcast.100, bf16[2048,1536]{1,0:T(8,128)(2,1)} %get-tuple-element.85.refs_1_.refs_0_, bf16[2048,768]{1,0:T(8,128)(2,1)} %get-tuple-element.78.refs_0_.refs_2_, bf16[2048,768]{1,0:T(8,128)(2,1)} %get-tuple-element.86.refs_3_.refs_0_, ...), custom_call_target="tpu_custom_call" | custom-call | flops 1000 | bytes 1000 | tf_op jit(solution)/shard_map/gate_grads/pallas_call | solution.py:968
  274.2 33.1 %scan_backward.2 = (bf16[2048,768]{1,0:T(8,128)(2,1)}, bf16[2048,384]{1,0:T(8,128)(2,1)}, f32[16,1,128]{2,1,0:T(1,128)}, f32[8,768]{1,0:T(8,128)}, f32[8,256]{1,...) custom-call(bf16[2048,768]{1,0:T(8,128)(2,1)} %get-tuple-element.81.dy_ref, ...), custom_call_target="tpu_custom_call" | custom-call | flops 1000 | bytes 1000 | tf_op jit(solution)/shard_map/scan_backward/pallas_call | solution.py:808
  308.4 8.7 %home_out.1.refs_3_ = bf16[2048,384]{1,0:T(8,128)(2,1)} custom-call(f32[16,1,128]{2,1,0:T(1,128)} %convert_bitcast_fusion.2.order_ref, bf16[2048,384]{1,0:T(8,128)(2,1)} %get-tuple-element.79.a_ref, bf16[2048,384]{1,0:T(8,128)(2,1)} %copy-done.35, bf16[2048,768]{1,0:T(8,128)(2,1)} %get-tuple-element.89.refs_0_), custom_call_target="tpu_custom_call" | custom-call | flops 3221225472 | bytes 7864320 | tf_op jit(solution)/shard_map/home_out/pallas_call | solution.py:763
  317.1 4.9 all-to-all-start.1
  323.5 2.8 constant_dynamic-slice_fusion.refs_0_
  332.0 24.4 %scan_backward.3 = (bf16[2048,768]{1,0:T(8,128)(2,1)}, bf16[2048,384]{1,0:T(8,128)(2,1)}, f32[16,1,128]{2,1,0:T(1,128)}, f32[8,768]{1,0:T(8,128)}, f32[8,256]{1,0:T(8,128)}, /*index=5*/f32[8,128]{1,0:T(8,128)}) custom-call(bf16[2048,768]{1,0:T(8,128)(2,1)} %get-tuple-element.81.dy_ref, ...), custom_call_target="tpu_custom_call", output_to_operand_aliasing={{0}: (9, {}), {1}: (10, {}), {2}: (11, {})} | custom-call | flops 1000 | bytes 1000 | tf_op jit(solution)/shard_map/scan_backward/pallas_call | solution.py:808
  356.5 21.9 %scan_grads.1 = (bf16[1536,768]{1,0:T(8,128)(2,1)}, bf16[1536,384]{1,0:T(8,128)(2,1)}, bf16[2,192,768]{2,1,0:T(8,128)(2,1)}, bf16[2,192,768]{2,1,0:T(8,128)(2,1)}) custom-call(bf16[2048,1536]{1,0:T(8,128)(2,1)} %get-tuple-element.85.refs_1_.refs_0_, bf16[2048,1536]{1,0:T(8,128)(2,1)} %get-tuple-element.85.refs_1_.refs_0_, ...), custom_call_target="tpu_custom_call" | custom-call | flops 1000 | bytes 1000 | tf_op jit(solution)/shard_map/scan_grads/pallas_call | solution.py:968
  379.7 2.7 fusion.5
  382.4 3.0 fusion.1.refs_11_
  385.3 34.4 %input_pieces.1 = (bf16[2048,384]{1,0:T(8,128)(2,1)}, bf16[2048,384]{1,0:T(8,128)(2,1)}, bf16[1,192,768]{2,1,0:T(8,128)(2,1)}, bf16[1,192,768]{2,1,0:T(8,128)(2,...) custom-call(bf16[2048,768]{1,0:T(8,128)(2,1)} %get-tuple-element.86.refs_3_.refs_0_, ...), custom_call_target="tpu_custom_call" | custom-call | flops 1000 | bytes 1000 | tf_op jit(solution)/shard_map/input_pieces/pallas_call | solution.py:930
  423.9 44.8 %last_exchange.1 = (bf16[2048,384]{1,0:T(8,128)(2,1)}, bf16[3,192,768]{2,1,0:T(8,128)(2,1)}, f32[7,8,768]{2,1,0:T(8,128)}, f32[192,384]{1,0:T(8,128)}) custom-call(bf16[2048,384]{1,0:T(8,128)(2,1)} %get-tuple-element.104.refs_0_, bf16[4,192,768]{2,1,0:T(8,128)(2,1)} %fusion.2.refs_1_, f32[8,768]{1,0:T(8,128)} %pad_maximum_fusion.2.refs_2_, ...), custom_call_target="tpu_custom_call" | custom-call | tf_op jit(solution)/shard_map/last_exchange/pallas_call | solution.py:1024
  472.3 10.0 %home_back.1 = bf16[2048,384]{1,0:T(8,128)(2,1)} custom-call(f32[16,1,128]{2,1,0:T(1,128)} %convert_bitcast_fusion.2.order_ref, bf16[2048,384]{1,0:T(8,128)(2,1)} %get-tuple-element.103.a_ref, bf16[2048,384]{1,0:T(8,128)(2,1)} %get-tuple-element.113.b_ref, bf16[2048,384]{1,0:T(8,128)(2,1)} %constant_dynamic-slice_fusion.refs_0_, ...), custom_call_target="tpu_custom_call" | custom-call | flops 3221225472 | bytes 7864320 | tf_op jit(solution)/shard_map/home_back/pallas_call | solution.py:763
  482.3 5.2 all-to-all-start.2
  493.4 15.6 %exchange.1 = f32[3,192,384]{2,1,0:T(8,128)} custom-call(f32[192,384]{1,0:T(8,128)} %pad_maximum_fusion.1.refs_0_), custom_call_target="tpu_custom_call" | custom-call | tf_op jit(solution)/shard_map/exchange/pallas_call | solution.py:188
  514.0 9.8 %all-to-all-done.2 = bf16[8,256,384]{2,1,0:T(8,128)(2,1)S(1)} async-done(((bf16[8,256,384]{2,1,0:T(8,128)(2,1)}), bf16[8,256,384]{2,1,0:T(8,128)(2,1)S(1)}, u32[]{:S(2)}, u32[]{:S(2)}) %all-to-all-start.2) | async-done | bytes 1572896 | tf_op jit(solution)/shard_map/all_to_all | solution.py:1326
  523.8 3.0 fusion
  (149 shorter events, 40.0 us)
Async XLA Ops:
  120.6 43.1 %all-to-all-start = ((bf16[8,256,384]{2,1,0:T(8,128)(2,1)}), bf16[8,256,384]{2,1,0:T(8,128)(2,1)S(1)}, u32[]{:S(2)}, u32[]{:S(2)}) async-start(bf16[8,256,384]{2,1,0:T(8,128)(2,1)} %bitcast.7), calls=%async_computation | async-start | bytes 3145728 | tf_op jit(solution)/shard_map/all_to_all | solution.py:1253
  125.4 35.4 %copy-start.34 = (f32[3,12]{1,0:T(4,128)S(1)}, f32[3,12]{1,0:T(4,128)}, u32[]{:S(2)}) copy-start(f32[3,12]{1,0:T(4,128)} %param.24) | copy-start | bytes 436
  125.4 35.5 %copy-start.32 = (f32[768]{0:T(1024)S(1)}, f32[768]{0:T(1024)}, u32[]{:S(2)}) copy-start(f32[768]{0:T(1024)} %param.25) | copy-start | bytes 9220
  125.4 36.1 %copy-start.29 = (f32[5,256]{1,0:T(8,128)S(1)}, f32[5,256]{1,0:T(8,128)}, u32[]{:S(2)}) copy-start(f32[5,256]{1,0:T(8,128)} %param.23) | copy-start | bytes 15364
  125.4 36.7 %copy-start.36 = (s32[2]{0:T(128)S(1)}, s32[2]{0:T(128)}, u32[]{:S(2)}) copy-start(s32[2]{0:T(128)} %param.16) | copy-start | bytes 28
  125.4 37.6 %copy-start.22 = (f32[5,768]{1,0:T(8,128)S(1)}, f32[5,768]{1,0:T(8,128)}, u32[]{:S(2)}) copy-start(f32[5,768]{1,0:T(8,128)} %param.22) | copy-start | bytes 46084
  255.6 51.7 %collective-permute-start = (bf16[2048,384]{1,0:T(8,128)(2,1)}, bf16[2048,384]{1,0:T(8,128)(2,1)S(1)}, u32[]{:S(2)}, u32[]{:S(2)}) collective-permute-start(bf16[2048,384]{1,0:T(8,128)(2,1)} %get-tuple-element.80.refs_4_), channel_id=1, source_target_pairs={{0,2},{1,3},{2,0},{3,1},{4,6},{5,7},{6,4},{7,5},{8,10},{9,11},{10,... | collective-permute-start | bytes 4718600 | tf_op jit(solution)/shard_map/ppermute | solution.py:1286
  317.1 4.9 copy-start.21
  317.1 65.3 %all-to-all-start.1 = ((bf16[8,256,384]{2,1,0:T(8,128)(2,1)}), bf16[8,256,384]{2,1,0:T(8,128)(2,1)}, u32[]{:S(2)}, u32[]{:S(2)}) async-start(bf16[8,256,384]{2,1,0:T(8,128)(2,1)} %bitcast.107), calls=%async_computation.1 | async-start | bytes 3145728 | tf_op jit(solution)/shard_map/all_to_all | solution.py:1291
  323.4 4.7 copy-start.14
  356.4 22.0 %copy-start.26 = (f32[8,256]{1,0:T(8,128)S(1)}, f32[8,256]{1,0:T(8,128)}, u32[]{:S(2)}) copy-start(f32[8,256]{1,0:T(8,128)} %get-tuple-element.101) | copy-start | bytes 24580
  356.4 22.0 %copy-start.27 = (f32[8,256]{1,0:T(8,128)S(1)}, f32[8,256]{1,0:T(8,128)}, u32[]{:S(2)}) copy-start(f32[8,256]{1,0:T(8,128)} %get-tuple-element.102) | copy-start | bytes 24580
  356.5 22.6 %copy-start.20 = (f32[16,1,128]{2,1,0:T(1,128)S(1)}, f32[16,1,128]{2,1,0:T(1,128)}, u32[]{:S(2)}) copy-start(f32[16,1,128]{2,1,0:T(1,128)} %get-tuple-element.100.refs_4_) | copy-start | bytes 24580
  356.5 22.6 %copy-start.25 = (f32[16,1,128]{2,1,0:T(1,128)S(1)}, f32[16,1,128]{2,1,0:T(1,128)}, u32[]{:S(2)}) copy-start(f32[16,1,128]{2,1,0:T(1,128)} %get-tuple-element.99.refs_3_) | copy-start | bytes 24580
  356.5 23.2 %copy-start.30 = (f32[8,128]{1,0:T(8,128)S(1)}, f32[8,128]{1,0:T(8,128)}, u32[]{:S(2)}) copy-start(f32[8,128]{1,0:T(8,128)} %get-tuple-element.110) | copy-start | bytes 12292
  356.5 23.2 %copy-start.31 = (f32[8,128]{1,0:T(8,128)S(1)}, f32[8,128]{1,0:T(8,128)}, u32[]{:S(2)}) copy-start(f32[8,128]{1,0:T(8,128)} %get-tuple-element.111) | copy-start | bytes 12292
  356.5 23.2 %copy-start.23 = (f32[8,768]{1,0:T(8,128)S(1)}, f32[8,768]{1,0:T(8,128)}, u32[]{:S(2)}) copy-start(f32[8,768]{1,0:T(8,128)} %get-tuple-element.106) | copy-start | bytes 73732
  356.5 23.2 %copy-start.24 = (f32[8,768]{1,0:T(8,128)S(1)}, f32[8,768]{1,0:T(8,128)}, u32[]{:S(2)}) copy-start(f32[8,768]{1,0:T(8,128)} %get-tuple-element.107) | copy-start | bytes 73732
  356.5 23.2 %copy-start = (bf16[4,192,768]{2,1,0:T(8,128)(2,1)S(1)}, bf16[4,192,768]{2,1,0:T(8,128)(2,1)}, u32[]{:S(2)}) copy-start(bf16[4,192,768]{2,1,0:T(8,128)(2,1)} %fusion.4) | copy-start | bytes 3538948
  385.3 35.2 %copy-start.18 = (f32[8,256]{1,0:T(8,128)S(1)}, f32[8,256]{1,0:T(8,128)}, u32[]{:S(2)}) copy-start(f32[8,256]{1,0:T(8,128)} %add.139.refs_10_) | copy-start | bytes 24580
  385.3 35.3 %copy-start.3 = (bf16[1536,768]{1,0:T(8,128)(2,1)S(1)}, bf16[1536,768]{1,0:T(8,128)(2,1)}, u32[]{:S(2)}) copy-start(bf16[1536,768]{1,0:T(8,128)(2,1)} %get-tuple-element.98) | copy-start | bytes 7077892
  469.7 17.8 %copy-start.19 = (f32[8,768]{1,0:T(8,128)}, f32[8,768]{1,0:T(8,128)S(1)}, u32[]{:S(2)}) copy-start(f32[8,768]{1,0:T(8,128)S(1)} %fusion.18) | copy-start | bytes 73732
  482.3 7.0 %copy-start.1 = (bf16[4,192,768]{2,1,0:T(8,128)(2,1)S(1)}, bf16[4,192,768]{2,1,0:T(8,128)(2,1)}, u32[]{:S(2)}) copy-start(bf16[4,192,768]{2,1,0:T(8,128)(2,1)} %fusion.2.refs_1_) | copy-start | bytes 3538948
  482.3 41.5 %all-to-all-start.2 = ((bf16[8,256,384]{2,1,0:T(8,128)(2,1)}), bf16[8,256,384]{2,1,0:T(8,128)(2,1)S(1)}, u32[]{:S(2)}, u32[]{:S(2)}) async-start(bf16[8,256,384]{2,1,0:T(8,128)(2,1)} %bitcast.114), calls=%async_computation.2 | async-start | bytes 3145728 | tf_op jit(solution)/shard_map/all_to_all | solution.py:1326
  (17 other events, 40.0 us)

commit v5 on v4

--- a/solution.py
+++ b/solution.py
@@ -226,82 +226,57 @@
     return raw, steps, rates, logs
 
 
-def forward_moves(steps, rows_ref, w_ref, full_ref, fw_ref, pass_sems, across_sems, side_sems, local_sems, rows_held, w_held):
-    size, quarter = rows_ref.shape[0], rows_ref.shape[2]
-    line = size // 2
-    parts = w_ref.shape[0]
+def weight_moves(step, steps, parts, whole, w_ref, fw_ref, across_sems, side_sems, local_sems, w_held):
+    line = fw_ref.shape[0] // 2
     me, own = lax.axis_index("dp"), lax.axis_index("head")
-    step = pl.program_id(0) * pl.num_programs(1) + pl.program_id(1)
-    far, near, back = row_forward(size, quarter, rows_ref, full_ref, pass_sems)
     across, side = shard_spread(w_ref, fw_ref, across_sems, side_sems)
-    mine = pl.ds(pl.multiple_of(own * quarter, 128), quarter)
-    into = [pltpu.make_async_copy(rows_ref, rows_held, local_sems.at[0]), pltpu.make_async_copy(w_ref, w_held, local_sems.at[1])]
-    held = [
-        pltpu.make_async_copy(rows_held, full_ref.at[:, :, mine], local_sems.at[2]),
-        pltpu.make_async_copy(w_held, fw_ref.at[me], local_sems.at[3]),
-    ]
+    if whole:
+        into = pltpu.make_async_copy(w_ref, w_held, local_sems.at[0])
+        held = pltpu.make_async_copy(w_held, fw_ref.at[me], local_sems.at[1])
 
     @pl.when(step == 0)
     def _():
-        for copy in into:
-            copy.start()
-        greet([(me ^ 1, own)] + [(me ^ (2 * j), own) for j in range(1, line)] + [(me, own ^ 1), (me, own ^ 2)])
-        for k in range(size):
-            near(k).start()
-        for k in range(size // 2):
-            far(k).start()
-        for part in range(parts):
+        if whole:
+            into.start()
+        greet([(me ^ 1, own)] + [(me ^ (2 * j), own) for j in range(1, line)])
+        for part in parts:
             side(part, 0).start()
-        for part in range(min(2, parts)):
+        if whole:
+            into.wait()
+            held.start()
+
+    for i, part in enumerate(parts):
+        begin = i * steps // len(parts)
+
+        @pl.when(step == begin)
+        def _():
             for j in range(1, line):
                 across(part, j).start()
 
-    for part in range(parts):
-
-        @pl.when(step == min(steps - 1, (part + 2) * steps // (parts + 1)))
+        @pl.when(step == min(steps - 1, begin + steps // 3 + 2))
         def _():
             for j in range(1, line):
                 across(part, j).wait_recv()
                 side(part, j).start()
-            if part + 2 < parts:
-                for j in range(1, line):
-                    across(part + 2, j).start()
-
-    @pl.when(step == 1)
-    def _():
-        for first, second in zip(into, held):
-            first.wait()
-            second.start()
-
-    groups = 4
-    for group in range(groups):
-        members = range(group * size // groups, (group + 1) * size // groups)
-
-        @pl.when(step == min(steps - 1, ((group + 1) * 3 * steps) // (2 * groups)))
-        def _():
-            for k in members:
-                far(k).wait_recv()
-                back(k).start()
-                if k < size // 2:
-                    far(k + size // 2).start()
 
     @pl.when(step == steps - 1)
     def _():
-        for copy in held:
-            copy.wait()
-        for k in range(size):
-            near(k).wait()
-            back(k).wait()
-            far(k).wait_send()
-        for part in range(parts):
+        if whole:
+            held.wait()
+        for part in parts:
             for j in range(line):
                 side(part, j).wait()
                 if j:
                     across(part, j).wait_send()
 
 
-def forward_kernel(heads, steps, x_ref, z_ref, ubd_ref, par_ref, pbc_ref, head_ref, rows_ref, w_ref, y_ref, ss_ref, c_ref, cb_ref, st_ref, full_ref, fw_ref, ext_x, ext_b, state, *sems):
-    forward_moves(steps, rows_ref, w_ref, full_ref, fw_ref, *sems)
+def weight_scratch(size, w):
+    sems = pltpu.SemaphoreType.DMA
+    return [sems((2, PARTS, size // 2)), sems((2, PARTS, size // 2)), sems((2,)), pltpu.VMEM((PARTS, w.shape[0] // PARTS, w.shape[1]), BF16)]
+
+
+def forward_kernel(heads, steps, x_ref, z_ref, ubd_ref, par_ref, pbc_ref, head_ref, w_ref, before_ref, y_ref, ss_ref, c_ref, cb_ref, st_ref, fw_ref, ext_x, ext_b, state, *sems):
+    weight_moves(pl.program_id(0) * pl.num_programs(1) + pl.program_id(1), steps, range(1, PARTS), False, w_ref, fw_ref, *sems)
 
     @pl.when(pl.program_id(1) == 0)
     def _():
@@ -344,6 +319,7 @@
         log_pair = jnp.where(low, log0, log1)
         step_pair = jnp.where(low, lanes(steps, h0), lanes(steps, h1))
         last_pair = log_pair[T - 1 : T]
+        skip_pair = jnp.where(low_row, lanes(head_ref[2:3], h0), lanes(head_ref[2:3], h1))
         cp = c[:, span]
         xp = cp * sigmoid(cp)
         xd = xp * step_pair
@@ -351,7 +327,7 @@
         m1 = (scores * jnp.exp(jnp.where(causal, log1 - logs_t[h1 : h1 + 1], NEG))).astype(BF16)
         stacked = jnp.concatenate([jnp.where(low, xd, 0.0).astype(BF16), jnp.where(low, 0.0, xd).astype(BF16)], axis=0)
         y = dot(jnp.concatenate([m0, m1], axis=1), stacked)
-        y = y + jnp.exp(log_pair) * outer[:, span] + par_ref[5:6, span] * xp
+        y = y + jnp.exp(log_pair) * outer[:, span] + skip_pair * xp
         tail = (jnp.exp(last_pair - log_pair) * xd).astype(BF16)
         state[:, span] = jnp.exp(last_pair) * state[:, span] + dot(b_t, tail)
         y_ref[:, span] = y.astype(BF16)
@@ -361,25 +337,17 @@
     ss_ref[0] = to_row(jnp.sum(squares, axis=1, keepdims=True))
 
 
-def row_picks(order_ref, count):
-    lane = lax.broadcasted_iota(jnp.int32, (T, T), 1).astype(F32)
-    blocks = []
-    for part in range(order_ref.shape[0]):
-        wanted = to_col(order_ref[part])
-        blocks.append(jnp.concatenate([(wanted == lane + float(T * j)).astype(F32).astype(BF16) for j in range(count)], axis=1))
-    return jnp.concatenate(blocks, axis=0)
-
-
-def project_kernel(heads, order_ref, x_ref, w_ref, out_ref, inv_ref, uzx_ref, ubd_ref, gain_ref):
+def project_kernel(heads, steps, x_ref, w_ref, shard_ref, out_ref, inv_ref, uzx_ref, ubd_ref, gain_ref, fw_ref, *sems):
     deep, width = x_ref.shape[1], 2 * heads * HEAD
+    weight_moves(pl.program_id(0), steps, range(1), True, shard_ref, fw_ref, *sems)
 
     @pl.when(pl.program_id(0) == 0)
     def _():
         for j in range(deep // T):
             span = slice(j * T, j * T + T)
-            gain_ref[0:1, span] = w_ref[span, width + 2 * N : width + 3 * N].astype(F32).T[heads : heads + 1]
-
-    x = dot(row_picks(order_ref, x_ref.shape[0] // T), x_ref[...])
+            gain_ref[:, span] = jnp.broadcast_to(w_ref[span, width + 2 * N : width + 3 * N].astype(F32).T[heads : heads + 1], (8, T))
+
+    x = x_ref[...].astype(F32)
     inv = lax.rsqrt(jnp.sum(x * x, axis=1, keepdims=True) / deep + EPS)
     normed = (x * inv * gain_ref[0:1]).astype(BF16)
     out_ref[...] = normed
@@ -387,10 +355,6 @@
         inv_ref[part] = to_row(inv[part * T : part * T + T])
     uzx_ref[...] = dot(normed, w_ref[:, :width]).astype(BF16)
     ubd_ref[...] = dot(normed, w_ref[:, width:])
-
-
-def sort_kernel(order_ref, rows_ref, out_ref):
-    out_ref[...] = dot(row_picks(order_ref, rows_ref.shape[0] // T), rows_ref[...]).astype(BF16)
 
 
 def gate_kernel(g_ref, wo_ref, y_ref, z_ref, par_ref, mask_ref, dyn_ref, co_ref):
@@ -402,10 +366,10 @@
         dyn_ref[rows] = own.astype(BF16)
         z = z_ref[rows].astype(F32)
         w = y_ref[rows].astype(F32) * z * sigmoid(z)
-        co_ref[part] = to_row(jnp.sum(own * w * par_ref[6:7], axis=1, keepdims=True))
-
-
-def home_kernel(last, deep, order_ref, a_ref, b_ref, *refs):
+        co_ref[part] = to_row(jnp.sum(own * w * par_ref[0:1], axis=1, keepdims=True))
+
+
+def home_kernel(last, deep, me_ref, order_ref, a_ref, b_ref, *refs):
     out_ref, held_ref = refs[-2:]
     step = pl.program_id(0)
     many = held_ref.shape[0] // a_ref.shape[0]
@@ -450,7 +414,7 @@
         for copy in copies:
             copy.wait()
 
-    gain = par_ref[6:7]
+    gain = par_ref[0:1]
     parts = y_ref.shape[0] // T
     for part in range(parts):
         rows = slice(part * T, part * T + T)
@@ -505,6 +469,7 @@
 
     row, col = iotas(T, T)
     low = col < HEAD
+    low_row = lax.broadcasted_iota(jnp.int32, (1, 128), 1) < HEAD
     upto = col >= row
     below = row < col
     reach = (row >= col).astype(BF16)
@@ -530,6 +495,7 @@
         log_pair = jnp.where(low, log0, log1)
         step_pair = jnp.where(low, lanes(steps, h0), lanes(steps, h1))
         last_pair = log_pair[T - 1 : T]
+        skip_pair = jnp.where(low_row, lanes(head_ref[2:3], h0), lanes(head_ref[2:3], h1))
         cp = c_ref[:, span].astype(F32)
         sp = sigmoid(cp)
         xp = cp * sp
@@ -566,7 +532,7 @@
         closing = jnp.exp(last_pair)
         closing_parts.append(closing * jnp.sum(old * entering[:, span].astype(F32), axis=0, keepdims=True))
         d_state[:, span] = closing * old + dot(c_t, edy_low)
-        dx = dxd * step_pair + par_ref[5:6, span] * dy
+        dx = dxd * step_pair + skip_pair * dy
         ext_x[0:T, span] = dx * (sp * (1.0 + cp * (1.0 - sp)))
     d_low = d_scores.astype(BF16)
     d_b = dot_nt(tail_ref[...], ds_low) + dot(d_low, c_low)
@@ -621,15 +587,13 @@
     return pltpu.CompilerParams(dimension_semantics=semantics, vmem_limit_bytes=LIMIT)
 
 
-def run_forward(heads, u_zx, u_bd, par, pbc, hp, came, w_out, number):
+def run_forward(heads, u_zx, u_bd, par, pbc, hp, w_out, before, number):
     rows, width = u_zx.shape[0], heads * HEAD
     slots, chunks = rows // LEN, LEN // T
     at = lambda s, i: (s * chunks + i, 0)
     fixed = lambda s, i: (0, 0)
-    size, block, quarter = came.shape
-    line = size // 2
+    size = lax.axis_size("dp")
     anywhere = pl.BlockSpec(memory_space=pl.ANY)
-    sems = pltpu.SemaphoreType.DMA
     return pl.pallas_call(
         functools.partial(forward_kernel, heads, slots * chunks),
         grid=(slots, chunks),
@@ -637,8 +601,8 @@
             pl.BlockSpec((T, width), lambda s, i: (s * chunks + i, 1)),
             pl.BlockSpec((T, width), at),
             pl.BlockSpec((T, 3 * N), at),
-            pl.BlockSpec((8, width), fixed),
-            pl.BlockSpec((8, 2 * N), fixed),
+            pl.BlockSpec((5, width), fixed),
+            pl.BlockSpec((5, 2 * N), fixed),
             pl.BlockSpec((8, 128), fixed),
             anywhere,
             anywhere,
@@ -650,7 +614,6 @@
             pl.BlockSpec((T, 2 * N), at),
             pl.BlockSpec((1, N, width), lambda s, i: (s * chunks + i, 0, 0)),
             anywhere,
-            anywhere,
         ],
         out_shape=[
             jax.ShapeDtypeStruct((rows, width), BF16),
@@ -658,65 +621,56 @@
             jax.ShapeDtypeStruct((rows, width), BF16),
             jax.ShapeDtypeStruct((rows, 2 * N), F32),
             jax.ShapeDtypeStruct((rows // T, N, width), BF16),
-            jax.ShapeDtypeStruct((size, block, quarter * 4), BF16),
             full_shape(size, w_out),
         ],
         scratch_shapes=[
             pltpu.VMEM((T + 8, width), F32),
             pltpu.VMEM((T + 8, 2 * N), F32),
             pltpu.VMEM((N, width), F32),
-            sems((2, 3, size)),
-            sems((2, PARTS, line)),
-            sems((2, PARTS, line)),
-            sems((4,)),
-            pltpu.VMEM(came.shape, BF16),
-            pltpu.VMEM((PARTS, w_out.shape[0] // PARTS, w_out.shape[1]), BF16),
-        ],
+        ]
+        + weight_scratch(size, w_out),
+        input_output_aliases={7: 5},
         compiler_params=params("arbitrary", "arbitrary", number=number),
         cost_estimate=pl.CostEstimate(flops=rows * width * 2 * 1200, bytes_accessed=rows * width * 8, transcendentals=rows * width * 6),
         name="scan_forward",
-    )(u_zx, u_zx, u_bd, par, pbc, hp, came, cut_shard(w_out))
-
-
-def run_project(heads, order, x, w_in):
+    )(u_zx, u_zx, u_bd, par, pbc, hp, cut_shard(w_out), before)
+
+
+def run_project(heads, x, w_in, w_out, number):
     rows, deep = x.shape
     wide = w_in.shape[1]
     width = 2 * heads * HEAD
+    size = lax.axis_size("dp")
     step = 256
     at = lambda i: (i, 0)
     fixed = lambda i: (0, 0)
+    anywhere = pl.BlockSpec(memory_space=pl.ANY)
     thin = pl.BlockSpec((step // T, 1, T), lambda i: (i, 0, 0))
     return pl.pallas_call(
-        functools.partial(project_kernel, heads),
+        functools.partial(project_kernel, heads, rows // step),
         grid=(rows // step,),
-        in_specs=[thin, pl.BlockSpec((rows, deep), fixed), pl.BlockSpec((deep, wide), fixed)],
-        out_specs=[pl.BlockSpec((step, deep), at), thin, pl.BlockSpec((step, width), at), pl.BlockSpec((step, wide - width), at)],
+        in_specs=[pl.BlockSpec((step, deep), at), pl.BlockSpec((deep, wide), fixed), anywhere],
+        out_specs=[
+            pl.BlockSpec((step, deep), at),
+            thin,
+            pl.BlockSpec((step, width), at),
+            pl.BlockSpec((step, wide - width), at),
+            pl.BlockSpec((8, deep), fixed),
+            anywhere,
+        ],
         out_shape=[
             jax.ShapeDtypeStruct((rows, deep), BF16),
             jax.ShapeDtypeStruct((rows // T, 1, T), F32),
             jax.ShapeDtypeStruct((rows, width), BF16),
             jax.ShapeDtypeStruct((rows, wide - width), F32),
+            jax.ShapeDtypeStruct((8, deep), F32),
+            full_shape(size, w_out),
         ],
-        scratch_shapes=[pltpu.VMEM((8, deep), F32)],
-        compiler_params=params("arbitrary"),
+        scratch_shapes=weight_scratch(size, w_out),
+        compiler_params=params("arbitrary", number=number),
         cost_estimate=pl.CostEstimate(flops=LIGHT, bytes_accessed=LIGHT, transcendentals=0),
         name="project",
-    )(order, x, w_in)
-
-
-def run_sort(order, values):
-    rows, wide = values.shape
-    step = 512
-    return pl.pallas_call(
-        sort_kernel,
-        grid=(rows // step,),
-        in_specs=[pl.BlockSpec((step // T, 1, T), lambda i: (i, 0, 0)), pl.BlockSpec((rows, wide), lambda i: (0, 0))],
-        out_specs=pl.BlockSpec((step, wide), lambda i: (i, 0)),
-        out_shape=jax.ShapeDtypeStruct((rows, wide), BF16),
-        compiler_params=params("arbitrary"),
-        cost_estimate=pl.CostEstimate(flops=rows * rows * wide * 2, bytes_accessed=rows * wide * 4, transcendentals=0),
-        name="sort_rows",
-    )(order, values)
+    )(x, w_in, cut_shard(w_out))
 
 
 def run_gate(grads, w_out, y, u_zx, par, mask):
@@ -734,7 +688,7 @@
             pl.BlockSpec((deep, width), fixed),
             pl.BlockSpec((step, width), at),
             pl.BlockSpec((step, width), at),
-            pl.BlockSpec((8, width), fixed),
+            pl.BlockSpec((1, width), fixed),
             thin,
         ],
         out_specs=[pl.BlockSpec((step, width), at), thin],
@@ -745,32 +699,35 @@
     )(grads, w_out, y, u_zx, par, mask)
 
 
-def run_home(order, sums, extra, deep, name, after=()):
+def run_home(me, order, sums, extra, deep, name, after=()):
     rows, quarter = sums[0].shape
     step = 512
     many = rows // step
-    into = lambda i: (jnp.minimum(i, many - 1), 0)
-    into3 = lambda i: (jnp.minimum(i, many - 1), 0, 0)
-    thin = pl.BlockSpec((step // T, 1, T), into3)
-    specs = [pl.BlockSpec((rows // T, 1, T), lambda i: (0, 0, 0))] + [pl.BlockSpec((step, quarter), into)] * 2
+    into = lambda i, m: (jnp.minimum(i, many - 1), 0)
+    thin = pl.BlockSpec((step // T, 1, T), lambda i, m: (jnp.minimum(i, many - 1), 0, 0))
+    specs = [pl.BlockSpec((rows // T, 1, T), lambda i, m: (0, 0, 0))] + [pl.BlockSpec((step, quarter), into)] * 2
     values = list(sums)
     if extra is not None:
-        specs += [pl.BlockSpec((step, quarter), into), thin, pl.BlockSpec((8, quarter), lambda i: (0, 0)), thin, thin]
-        specs += [pl.BlockSpec((3, step // T, 1, T), lambda i: (0, jnp.minimum(i, many - 1), 0, 0))]
+        specs += [pl.BlockSpec((step, quarter), lambda i, m: (jnp.minimum(i, many - 1), m[0])), thin]
+        specs += [pl.BlockSpec((8, quarter), lambda i, m: (0, m[0])), thin, thin]
+        specs += [pl.BlockSpec((3, step // T, 1, T), lambda i, m: (0, jnp.minimum(i, many - 1), 0, 0))]
         values += list(extra)
     values += list(after)
     specs += [pl.BlockSpec(memory_space=pl.ANY)] * len(after)
     return pl.pallas_call(
         functools.partial(home_kernel, extra is not None, float(deep)),
-        grid=(2 * many,),
-        in_specs=specs,
-        out_specs=pl.BlockSpec((step, quarter), lambda i: (jnp.maximum(i - many, 0), 0)),
+        grid_spec=pltpu.PrefetchScalarGridSpec(
+            num_scalar_prefetch=1,
+            grid=(2 * many,),
+            in_specs=specs,
+            out_specs=pl.BlockSpec((step, quarter), lambda i, m: (jnp.maximum(i - many, 0), 0)),
+            scratch_shapes=[pltpu.VMEM((rows, quarter), BF16)],
+        ),
         out_shape=jax.ShapeDtypeStruct((rows, quarter), BF16),
-        scratch_shapes=[pltpu.VMEM((rows, quarter), BF16)],
         compiler_params=params("arbitrary"),
         cost_estimate=pl.CostEstimate(flops=rows * rows * quarter * 2, bytes_accessed=rows * quarter * 10, transcendentals=0),
         name=name,
-    )(order, *values)
+    )(me, order, *values)
 
 
 def run_mid(all_width, y, u_zx, dyn, par, mask, ss, co, number):
@@ -786,7 +743,7 @@
     return pl.pallas_call(
         functools.partial(mid_kernel, float(all_width), moves),
         grid=(rows // step,),
-        in_specs=[wide, wide, wide, pl.BlockSpec((8, width), fixed), thin, whole, whole],
+        in_specs=[wide, wide, wide, pl.BlockSpec((1, width), fixed), thin, whole, whole],
         out_specs=[wide, wide, wide, pl.BlockSpec((8, width), fixed), thin],
         out_shape=[jax.ShapeDtypeStruct((rows, width), BF16)] * 3
         + [jax.ShapeDtypeStruct((8, width), F32), jax.ShapeDtypeStruct((rows // T, 1, T), F32)],
@@ -815,8 +772,8 @@
             pl.BlockSpec((T, 2 * N), at),
             pl.BlockSpec((T, 3 * N), at),
             pl.BlockSpec((1, N, width), at3),
-            pl.BlockSpec((8, width), fixed),
-            pl.BlockSpec((8, 2 * N), fixed),
+            pl.BlockSpec((5, width), fixed),
+            pl.BlockSpec((5, 2 * N), fixed),
             pl.BlockSpec((8, 128), fixed),
         ]
         + [anywhere] * (len(moves) + len(before) + len(after)),
@@ -857,16 +814,20 @@
 
 def pieces_kernel(count, many, moves, extra, *refs):
     total = len(moves)
-    values, weights, srcs = refs[:count], refs[count : 2 * count], refs[2 * count : 2 * count + total]
-    refs = refs[2 * count + total + extra :]
+    values, weight_ref, srcs = refs[:count], refs[count], refs[count + 1 : count + 1 + total]
+    refs = refs[count + 1 + total + extra :]
     far_ref, own_ref = refs[:2]
     dsts, refs = refs[2 : 2 + total], refs[2 + total :]
-    sent_ref, came_ref, near_sems = refs[:3]
+    sent_ref, came_ref, near_sems, joined_ref = refs[:4]
     step = pl.program_id(0)
     rows, quarter = far_ref.shape
+    start = 0
+    for value in values:
+        joined_ref[:, start : start + value.shape[1]] = value[...]
+        start += value.shape[1]
     dp, own = lax.axis_index("dp"), lax.axis_index("head")
     near = (dp, own ^ 1)
-    peers, copies = make_moves(moves, srcs, dsts, *refs[3:]) if moves else ([], [])
+    peers, copies = make_moves(moves, srcs, dsts, *refs[4:]) if moves else ([], [])
 
     @pl.when(step == 0)
     def _():
@@ -876,11 +837,7 @@
 
     def product(k):
         at = pl.ds(pl.multiple_of((own ^ k) * quarter, 128), quarter)
-        out = None
-        for value, weight in zip(values, weights):
-            term = dot_nt(value[...], weight[at, :])
-            out = term if out is None else out + term
-        return out
+        return dot_nt(joined_ref[...], weight_ref[at, :])
 
     def near_copy(block):
         return pltpu.make_async_remote_copy(
@@ -918,26 +875,24 @@
     return any(move[0] == "spread" and move[1] == "head" for move in moves)
 
 
-def run_pieces(values, weights, quarter, name, moves, moved, number, after=()):
+def run_pieces(values, weight, quarter, name, moves, moved, number, after=()):
     rows = values[0].shape[0]
     step = 512
     many = rows // step
     anywhere = pl.BlockSpec(memory_space=pl.ANY)
     specs = [pl.BlockSpec((step, v.shape[1]), lambda i: (lax.rem(i, many), 0)) for v in values]
-    for weight, block, wide in weights:
-        specs.append(pl.BlockSpec((weight.shape[0], wide), lambda i, block=block: (0, block)))
-    depth = sum(v.shape[1] for v in values)
+    specs.append(pl.BlockSpec(weight.shape, lambda i: (0, 0)))
     return pl.pallas_call(
         functools.partial(pieces_kernel, len(values), many, tuple(moves), len(after)),
         grid=(2 * many,),
         in_specs=specs + [anywhere] * (len(moves) + len(after)),
         out_specs=[pl.BlockSpec((step, quarter), lambda i: (jnp.maximum(i - many, 0), 0))] * 2 + [anywhere] * len(moves),
         out_shape=[jax.ShapeDtypeStruct((rows, quarter), BF16)] * 2 + move_outs(moves, moved),
-        scratch_shapes=[pltpu.VMEM((many, step, 2 * quarter), BF16)] * 2 + [pltpu.SemaphoreType.DMA((2, many))] + move_scratch(moves, moved),
+        scratch_shapes=[pltpu.VMEM((many, step, 2 * quarter), BF16)] * 2 + [pltpu.SemaphoreType.DMA((2, many)), pltpu.VMEM((step, weight.shape[1]), BF16)] + move_scratch(moves, moved),
         compiler_params=params("arbitrary", number=number),
         cost_estimate=pl.CostEstimate(flops=LIGHT, bytes_accessed=LIGHT, transcendentals=0),
         name=name,
-    )(*values, *[w for w, _, _ in weights], *moved, *after)
+    )(*values, weight, *moved, *after)
 
 
 def grads_kernel(count, parts, moves, extra, *refs):
@@ -1075,21 +1030,22 @@
     return across, side
 
 
-def entry_kernel(parts, x_ref, w_ref, fx_ref, fw_ref, row_sems, pass_sems, line_sems, side_sems, local_sems, x_held, w_held):
-    size, quarter = x_ref.shape[0], x_ref.shape[2]
+def entry_kernel(parts, order_ref, x_ref, g_ref, w_ref, fx_ref, fg_ref, fw_ref, row_sems, x_sems, g_sems, line_sems, side_sems, local_sems, land, ready, picks, w_held):
+    size, block, quarter = x_ref.shape
     line = size // 2
     me, own = lax.axis_index("dp"), lax.axis_index("head")
     spot = me >> 1
     mine = pl.ds(pl.multiple_of(own * quarter, 128), quarter)
-    far, near, back = row_forward(size, quarter, None, fx_ref, pass_sems)
+    sources, fulls = (x_ref, g_ref), (fx_ref, fg_ref)
+    forwards = [row_forward(size, quarter, ready.at[i], fulls[i], sems) for i, sems in enumerate((x_sems, g_sems))]
 
     def remote(src, dst, sems, slot, peer):
         return pltpu.make_async_remote_copy(
             src_ref=src, dst_ref=dst, send_sem=sems.at[(0,) + slot], recv_sem=sems.at[(1,) + slot], device_id=(peer, own), device_id_type=MESH
         )
 
-    def rows(k):
-        return remote(x_ref.at[me ^ k], fx_ref.at[me, :, mine], row_sems, (k,), me ^ k)
+    def rows(which, k):
+        return remote(sources[which].at[me ^ k], land.at[which, me], row_sems, (which, k), me ^ k)
 
     def along(way, part, j):
         sign = 1 - 2 * way
@@ -1114,30 +1070,57 @@
     def arrives(way, j):
         return spot >= j if way == 0 else spot < line - j
 
-    greet_rows = [(me ^ k, own) for k in range(1, size)] + [(me, own ^ 1), (me, own ^ 2)]
-    into = [pltpu.make_async_copy(x_ref.at[me], x_held, local_sems.at[0]), pltpu.make_async_copy(w_ref, w_held, local_sems.at[1])]
-    held = [
-        pltpu.make_async_copy(x_held, fx_ref.at[me, :, mine], local_sems.at[2]),
-        pltpu.make_async_copy(w_held, fw_ref.at[me], local_sems.at[3]),
-    ]
+    into = [pltpu.make_async_copy(sources[i].at[me], land.at[i, me], local_sems.at[i]) for i in range(2)]
+    into.append(pltpu.make_async_copy(w_ref, w_held, local_sems.at[2]))
+    held = [pltpu.make_async_copy(ready.at[i], fulls[i].at[:, :, mine], local_sems.at[3 + i]) for i in range(2)]
+    held.append(pltpu.make_async_copy(w_held, fw_ref.at[me], local_sems.at[5]))
     for copy in into:
         copy.start()
-    greet(greet_rows)
+    greet([(me ^ k, own) for k in range(1, size)] + [(me, own ^ 1), (me, own ^ 2)])
     order = turn_order(size)
     for k in order:
-        rows(k).start()
+        rows(0, k).start()
     for part in range(parts):
         side(0, part, 0).start()
-    for first, second in zip(into, held):
-        first.wait()
-        second.start()
-    held[0].wait()
-    far(0).start()
-    near(0).start()
+    for copy in into:
+        copy.wait()
+    held[2].start()
+    total = size * block
+    lane = lax.broadcasted_iota(jnp.int32, (T, T), 1).astype(F32)
+
+    def pick(i, carry):
+        wanted = to_col(order_ref[i])
+        at = pl.ds(pl.multiple_of(i * T, T), T)
+        for j in range(total // T):
+            picks[at, j * T : j * T + T] = (wanted == lane + float(T * j)).astype(F32).astype(BF16)
+        return carry
+
+    lax.fori_loop(0, total // T, pick, 0)
+
+    def arrange(which):
+        step = min(512, total)
+        for i in range(total // step):
+            value = dot(picks[i * step : (i + 1) * step, :], land[which].reshape(total, quarter)).astype(BF16)
+            ready[which, i * step // block : (i + 1) * step // block] = value.reshape(step // block, block, quarter)
+        held[which].start()
+        far, near, _ = forwards[which]
+        for k in range(size):
+            far(k).start()
+            near(k).start()
+
+    def backs(which, some):
+        far, _, back = forwards[which]
+        for k in some:
+            far(k).wait_recv()
+            back(k).start()
+
     for k in order:
-        rows(k).wait_recv()
-        far(k).start()
-        near(k).start()
+        rows(0, k).wait_recv()
+    for k in order:
+        rows(1, k).start()
+    arrange(0)
+    for k in order:
+        rows(1, k).wait_recv()
     for way in range(2):
 
         @pl.when(goes_on(way))
@@ -1145,11 +1128,12 @@
             for part in range(parts):
                 along(way, part, 1).start()
 
-    for k in [0] + order:
-        far(k).wait_recv()
-        back(k).start()
+    arrange(1)
+    backs(0, range(size))
     for j in range(1, line):
         for part in range(parts):
+            if j == line - 1:
+                backs(1, range(part * size // parts, (part + 1) * size // parts))
             for way in range(2):
 
                 @pl.when(arrives(way, j))
@@ -1163,13 +1147,16 @@
                     def _():
                         along(way, part, j + 1).start()
 
-    held[1].wait()
-    for k in range(size):
-        near(k).wait()
-        back(k).wait()
-        far(k).wait_send()
-        if k:
-            rows(k).wait_send()
+    for copy in held:
+        copy.wait()
+    for which in range(2):
+        far, near, back = forwards[which]
+        for k in range(size):
+            near(k).wait()
+            back(k).wait()
+            far(k).wait_send()
+            if k:
+                rows(which, k).wait_send()
     for part in range(parts):
         side(0, part, 0).wait()
         for way in range(2):
@@ -1202,30 +1189,35 @@
     return jax.ShapeDtypeStruct((size, PARTS, w.shape[0] // PARTS, w.shape[1]), BF16)
 
 
-def run_entry(tokens, w_in, number):
+def run_entry(order, tokens, cotangent, w_in, number):
     size = lax.axis_size("dp")
     rows, quarter = tokens.shape
+    block = rows // size
     line = size // 2
     anywhere = pl.BlockSpec(memory_space=pl.ANY)
     sems = pltpu.SemaphoreType.DMA
-    came, full = pl.pallas_call(
+    full = jax.ShapeDtypeStruct((size, block, quarter * 4), BF16)
+    came_x, came_g, came_w = pl.pallas_call(
         functools.partial(entry_kernel, PARTS),
-        in_specs=[anywhere] * 2,
-        out_specs=[anywhere] * 2,
-        out_shape=[jax.ShapeDtypeStruct((size, rows // size, quarter * 4), BF16), full_shape(size, w_in)],
+        in_specs=[pl.BlockSpec(memory_space=pltpu.VMEM)] + [anywhere] * 3,
+        out_specs=[anywhere] * 3,
+        out_shape=[full, full, full_shape(size, w_in)],
         scratch_shapes=[
-            sems((2, size)),
+            sems((2, 2, size)),
+            sems((2, 3, size)),
             sems((2, 3, size)),
             sems((2, 2, PARTS, line)),
             sems((2, 2, PARTS, line)),
-            sems((4,)),
-            pltpu.VMEM((rows // size, quarter), BF16),
+            sems((6,)),
+            pltpu.VMEM((2, size, block, quarter), BF16),
+            pltpu.VMEM((2, size, block, quarter), BF16),
+            pltpu.VMEM((rows, rows), BF16),
             pltpu.VMEM((PARTS, w_in.shape[0] // PARTS, w_in.shape[1]), BF16),
         ],
         compiler_params=pltpu.CompilerParams(collective_id=number, has_side_effects=True, vmem_limit_bytes=LIMIT),
         name="entry",
-    )(tokens.reshape(size, rows // size, quarter), cut_shard(w_in))
-    return came.reshape(rows, quarter * 4), full.reshape(size * w_in.shape[0], w_in.shape[1])
+    )(order, tokens.reshape(size, block, quarter), cotangent.reshape(size, block, quarter), cut_shard(w_in))
+    return came_x.reshape(rows, quarter * 4), came_g.reshape(rows, quarter * 4), came_w.reshape(size * w_in.shape[0], w_in.shape[1])
 
 
 def mm(a, b, contract, kind):
@@ -1236,7 +1228,7 @@
     rows, quarter = tokens.shape
     heads = head_params.shape[1]
     width = heads * HEAD
-    place = lax.axis_index("head")
+    me = lax.axis_index("head").astype(jnp.int32).reshape(1)
     size = lax.axis_size("dp")
     here = lax.axis_index("dp")
     all_width = width * lax.axis_size("head")
@@ -1248,23 +1240,18 @@
         [w_zx.reshape(own_w, 2 * width), w_bc, w_dt, norm_gain[:, None], jnp.zeros((own_w, 127 - heads), BF16)], axis=1
     )
     blocks = lambda value: value.reshape(size, rows // size, quarter)
-    came_x, w_in = run_entry(tokens, packed, 1)
-    came_x, later = lax.optimization_barrier((came_x, cotangent))
-    own_g = lax.all_to_all(later, "dp", split_axis=0, concat_axis=0, tiled=True)
-    normed, inv_one, u_zx, u_bd = run_project(heads, arrange, came_x, w_in)
-
-    par = jnp.concatenate([conv_x, jnp.repeat(head_params[2:3], HEAD, axis=1), gate_gain[None], jnp.zeros((1, width), F32)], axis=0)
-    pbc = jnp.concatenate([conv_bc, jnp.zeros((3, 2 * N), F32)], axis=0)
+    full_x, full_g, w_in = run_entry(arrange, tokens, cotangent, packed, 1)
+    normed, inv_one, u_zx, u_bd, gain, w_o = run_project(heads, full_x, w_in, w_out, 2)
+
+    gated = gate_gain.reshape(1, width)
     hp = jnp.pad(head_params, ((0, 5), (0, 128 - heads)))
     positions = lax.broadcasted_iota(jnp.int32, (lengths.shape[0], LEN), 1)
     mask = (positions < lengths[:, None]).astype(F32).reshape(rows // T, 1, T)
 
-    sorted_g = run_sort(arrange, own_g)
-    y, ss, c, cb, st, full_g, w_o = run_forward(heads, u_zx, u_bd, par, pbc, hp, blocks(sorted_g), w_out, 3)
+    y, ss, c, cb, st, w_o = run_forward(heads, u_zx, u_bd, conv_x, conv_bc, hp, w_out, w_o, 3)
     w_o = w_o.reshape(deep, width)
-    full_g = full_g.reshape(rows, deep)
-    dyn, co = run_gate(full_g, w_o, y, u_zx, par, mask)
-    yg, dz, dy, gg, rd_z = run_mid(all_width, y, u_zx, dyn, par, mask, ss, co, 4)
+    dyn, co = run_gate(full_g, w_o, y, u_zx, gated, mask)
+    yg, dz, dy, gg, rd_z = run_mid(all_width, y, u_zx, dyn, gated, mask, ss, co, 4)
 
     def keep(paired, came, bit):
         own = lax.dynamic_index_in_dim(paired, (here >> bit) & 1, 1, keepdims=False)
@@ -1281,34 +1268,33 @@
         return grads.reshape(size // 4, 2, -1, own_w, grads.shape[-1])
 
     scan = functools.partial(run_backward, heads)
-    shared = (dy, u_zx, c, cb, u_bd, st, par, pbc, hp)
-    out_far, out_own = run_pieces([yg], [(w_o, 0, width)], quarter, "branch_pieces", [], [], 5)
+    shared = (dy, u_zx, c, cb, u_bd, st, conv_x, conv_bc, hp)
+    out_far, out_own = run_pieces([yg], w_o, quarter, "branch_pieces", [], [], 5)
     out_arrived = lax.ppermute(out_far, "head", [(i, i ^ 2) for i in range(lax.axis_size("head"))])
     grad_o, grad_z = run_grads([(full_g, yg), (normed, dz)], "gate_grads", after=[out_far])
     grad_o, grad_z = pairs(grad_o), fours(grad_z)
     *back0, gx0, gb0, gh0, came_o, came_z = scan(0, *shared, (), [("half", "dp", 0), ("half", "dp", 1)], [grad_o, grad_z], 7)
-    sent_out = run_home(arrange, [out_own, out_arrived], None, deep, "home_out", [back0[0]])
+    sent_out = run_home(me, arrange, [out_own, out_arrived], None, deep, "home_out", [back0[0]])
     got_out = lax.all_to_all(sent_out, "dp", split_axis=0, concat_axis=0, tiled=True)
+    *back1, gx1, gb1, gh1 = scan(1, *shared, back0, [], [], 0, [sent_out])
+    kept_z = keep(grad_z, came_z, 1)
     kept_o = keep(grad_o, came_o, 0).reshape(size // 4, 2, own_w, width)
-    kept_z = keep(grad_z, came_z, 1)
-    *back1, gx1, gb1, gh1 = scan(1, *shared, back0, [], [], 0, [sent_out])
     dux, dbd, rd_x = back1
     grad_x, grad_bd, came_z, came_o = run_grads(
         [(normed, dux), (normed, dbd)], "scan_grads", [("half", "dp", 0), ("half", "dp", 1)], [kept_z, kept_o], 8
     )
     kept_z, kept_o = keep(kept_z, came_z, 0), keep(kept_o, came_o, 1)
-    final_out = (tokens.astype(F32) + got_out.astype(F32)).astype(BF16)
     grad_x, grad_bd = pairs(grad_x), pairs(grad_bd)
     gb = gb0 + gb1
     d_far, d_own, line_o, line_z, came_x2, got_rows, got_gb = run_pieces(
         [dz, dux, dbd],
-        [(w_in, 0, width), (w_in, 1, width), (w_in, 2 * width // (3 * N), 3 * N)],
+        w_in,
         quarter,
         "input_pieces",
         [("direct", "dp", 2), ("direct", "dp", 2), ("half", "dp", 0), ("spread", "head"), ("spread", "head")],
         [kept_o, kept_z, grad_x, rd_z + rd_x, gb],
         9,
-        [final_out],
+        [got_out],
     )
     kept_x = keep(grad_x, came_x2, 0)
     gb = gb[:5] + jnp.sum(got_gb, axis=0)[:5]
@@ -1319,11 +1305,9 @@
         [("whole", "head", 2), ("direct", "dp", 1), ("spread", "dp")], [d_far, kept_x, small], grad_bd, 10
     )
 
-    gain_all = w_in[:, 2 * width + 2 * N + heads].astype(F32)
-    gain_own = jnp.broadcast_to(lax.dynamic_slice_in_dim(gain_all, place * quarter, quarter, 0)[None], (8, quarter))
-    normed_own = lax.dynamic_slice_in_dim(normed, place * quarter, quarter, 1)
-    sent_back = run_home(arrange, [d_own, d_arrived], [normed_own, inv_one, gain_own, rd_z, rd_x, got_rows], deep, "home_back")
+    sent_back = run_home(me, arrange, [d_own, d_arrived], [normed, inv_one, gain, rd_z, rd_x, got_rows], deep, "home_back")
     got_back = lax.all_to_all(sent_back, "dp", split_axis=0, concat_axis=0, tiled=True)
+    final_out = (tokens.astype(F32) + got_out.astype(F32)).astype(BF16)
     final_back = (cotangent.astype(F32) + got_back.astype(F32)).astype(BF16)
 
     grad_out, grad_z = total(kept_o, line_o, 2), total(kept_z, line_z, 2)

time: 532 us -> 526 us (0.989)
  waiting for transfers between devices: 9.84 us -> 3.15 us
    pallas_call x1, Pallas kernels: 42.9 us -> 35.2 us  [run_forward(): pl.pallas_call(functools.partial(forward_kernel, heads, slots * chunks),...]
    all_to_all x1, waiting for transfers between devices: 9.83 us -> 3.15 us  [body(): lax.all_to_all(sent_back, 'dp', split_axis=0, concat_axis=0, tiled=True)]
    pallas_call x3 -> x2, Pallas kernels: 157 us -> 160 us  [the longest x1 137 us: run_entry(): pl.pallas_call(functools.partial(entry_kernel, PARTS), in_specs=[pl.Block...]
  transfers between devices with their start and end apart: 4 -> 3, of which waited for: 1 -> 1; matrix products, arithmetic and copies ran while one was open for 5% -> 5% of each run, Pallas kernels for 28% -> 22%
where the time goes in v5:
time: 526 us; the launch traced here: 517 us
  Pallas kernels  447 us (85%)
  other arithmetic  30.9 us (6%)
  local copies, waits for them, and re-layouts  23.9 us (5%)
  starting transfers between devices  10.6 us (2%)
    pallas_call x1, Pallas kernels, run_entry(): pl.pallas_call(functools.partial(entry_kernel, PARTS), in_specs=[pl.Block...  137 us
    pallas_call x2, Pallas kernels, run_backward(): pl.pallas_call(functools.partial(backward_kernel, heads, len(before) + le...  57.8 us
    pallas_call x2, Pallas kernels, run_pieces(): pl.pallas_call(functools.partial(pieces_kernel, len(values), many, tuple(...  47.2 us
    pallas_call x1, Pallas kernels, run_last(): pl.pallas_call(functools.partial(last_kernel, tuple(moves)), in_specs=[an...  44.8 us
    pallas_call x2, Pallas kernels, run_grads(): pl.pallas_call(functools.partial(grads_kernel, count, parts, tuple(moves)...  38.7 us
    pallas_call x1, Pallas kernels, run_forward(): pl.pallas_call(functools.partial(forward_kernel, heads, slots * chunks),...  35.2 us
    pallas_call x1, Pallas kernels, run_project(): pl.pallas_call(functools.partial(project_kernel, heads, rows // step), gr...  23 us
    pallas_call x2, Pallas kernels, run_home(): pl.pallas_call(functools.partial(home_kernel, extra is not None, float(de...  19 us
  transfers between devices with their start and end apart: 3, of which 1 were waited for; matrix products, arithmetic and copies ran while one was open for 5% of the time, Pallas kernels for 22%

profile of v5, /device:TPU:0, one launch (start us, length us, event | category | flops | bytes accessed | tf_op | source)
XLA Modules:
  0.0 516.8 jit_solution(11125841642722106450)
XLA Ops:
  2.0 2.1 concatenate.27
  11.6 137.3 %entry.1 = (bf16[8,256,1536]{2,1,0:T(8,128)(2,1)}, bf16[8,256,1536]{2,1,0:T(8,128)(2,1)}, bf16[8,4,48,1920]{3,2,1,0:T(8,128)(2,1)}) custom-call(f32[16,1,128]{2,1,0:T(1,128)} %convert_bitcast_fusion.2.order_ref, bf16[8,256,384]{2,1,0:T(8,128)(2,1)} %bitcast.99, bf16[8,256,384]{2,1,0:T(8,128)(2,1)} %bitcast.100, bf16[4,48,1920]{2,1,0:T(8,128)(2,1)} %concatenate.31.w_ref), custom_call_target="tpu_custom_call" | custom-call | tf_op jit(solution)/shard_map/entry/pallas_call | solution.py:1200
  148.9 23.0 %project.1 = (bf16[2048,1536]{1,0:T(8,128)(2,1)}, f32[16,1,128]{2,1,0:T(1,128)}, bf16[2048,1536]{1,0:T(8,128)(2,1)}, f32[2048,384]{1,0:T(8,128)}, f32[8,1536]{1,0:T(8,128)}, /*index=5*/bf16[8,4,48,768]{3,2,1,0:T(8,128)(2,1)}) custom-call(bf16[2048,1536]{1,0:T(8,128)(2,1)} %bitcast.98, bf16[1536,1920]{1,0:T(8,128)(2,1)} %bitcast.91, bf16[4,48,768]{2,1,0:T(8,128)(2,1)} %bitcast.110), custom_call_target="tpu_custom_call" | custom-call | flops 1000 | bytes 1000 | tf_op jit(solution)/shard_map/project/pallas_call | solution.py:649
  171.9 35.2 %scan_forward.1 = (bf16[2048,768]{1,0:T(8,128)(2,1)}, f32[16,1,128]{2,1,0:T(1,128)}, bf16[2048,768]{1,0:T(8,128)(2,1)}, f32[2048,256]{1,0:T(8,128)}, bf16[16,128...) custom-call(bf16[2048,1536]{1,0:T(8,128)(2,1)} %get-tuple-element.68.x_ref.z_ref, ...), custom_call_target="tpu_custom_call", output_to_operand_aliasing={{5}: (7, {})} | custom-call | flops 3774873600 | bytes 12582912 | tf_op jit(solution)/shard_map/scan_forward/pallas_call | solution.py:597
  207.1 12.3 %gate_back.1 = (bf16[2048,768]{1,0:T(8,128)(2,1)}, f32[16,1,128]{2,1,0:T(1,128)}) custom-call(bf16[2048,1536]{1,0:T(8,128)(2,1)} %bitcast.89, bf16[1536,768]{1,0:T(8,128)(2,1)} %bitcast.93, bf16[2048,768]{1,0:T(8,128)(2,1)} %get-tuple-element.71.y_ref, bf16[2048,1536]{1,0:T(8,128)(2,1)} %get-tuple-element.68.x_ref.z_ref, f32[1,768]{1,0:T(1,128)} %reshape.214.par_ref, ...), custom_call_target="tpu_custom_call" | custom-call | flops 4831838208 | bytes 15728640 | tf_op jit(solution)/shard_map/gate_back/pallas_call | solution.py:683
  219.4 15.9 %gate_mid.1 = (bf16[2048,768]{1,0:T(8,128)(2,1)}, bf16[2048,768]{1,0:T(8,128)(2,1)}, bf16[2048,768]{1,0:T(8,128)(2,1)}, f32[8,768]{1,0:T(8,128)}, f32[16,1,128]{2,1,0:T(1,128)}) custom-call(bf16[2048,768]{1,0:T(8,128)(2,1)} %get-tuple-element.71.y_ref, bf16[2048,1536]{1,0:T(8,128)(2,1)} %get-tuple-element.68.x_ref.z_ref, ...), custom_call_target="tpu_custom_call" | custom-call | flops 47185920 | bytes 18874368 | tf_op jit(solution)/shard_map/gate_mid/pallas_call | solution.py:743
  235.3 12.5 %branch_pieces.1 = (bf16[2048,384]{1,0:T(8,128)(2,1)}, bf16[2048,384]{1,0:T(8,128)(2,1)}) custom-call(bf16[2048,768]{1,0:T(8,128)(2,1)} %get-tuple-element.77.refs_0_.refs_2_, bf16[1536,768]{1,0:T(8,128)(2,1)} %bitcast.94), custom_call_target="tpu_custom_call" | custom-call | flops 1000 | bytes 1000 | tf_op jit(solution)/shard_map/branch_pieces/pallas_call | solution.py:885
  249.5 16.6 %gate_grads.1 = (bf16[1536,768]{1,0:T(8,128)(2,1)}, bf16[1536,768]{1,0:T(8,128)(2,1)}) custom-call(bf16[2048,1536]{1,0:T(8,128)(2,1)} %bitcast.90, bf16[2048,1536]{1,0:T(8,128)(2,1)} %get-tuple-element.84.refs_1_.refs_0_, bf16[2048,768]{1,0:T(8,128)(2,1)} %get-tuple-element.77.refs_0_.refs_2_, bf16[2048,768]{1,0:T(8,128)(2,1)} %get-tuple-element.85.refs_3_.refs_0_, ...), custom_call_target="tpu_custom_call" | custom-call | flops 1000 | bytes 1000 | tf_op jit(solution)/shard_map/gate_grads/pallas_call | solution.py:923
  266.1 33.4 %scan_backward.2 = (bf16[2048,768]{1,0:T(8,128)(2,1)}, bf16[2048,384]{1,0:T(8,128)(2,1)}, f32[16,1,128]{2,1,0:T(1,128)}, f32[8,768]{1,0:T(8,128)}, f32[8,256]{1,...) custom-call(bf16[2048,768]{1,0:T(8,128)(2,1)} %get-tuple-element.80.dy_ref, ...), custom_call_target="tpu_custom_call" | custom-call | flops 1000 | bytes 1000 | tf_op jit(solution)/shard_map/scan_backward/pallas_call | solution.py:765
  300.7 8.9 %home_out.1.refs_3_ = bf16[2048,384]{1,0:T(8,128)(2,1)} custom-call(s32[1]{0:T(128)} %bitcast.me_ref, f32[16,1,128]{2,1,0:T(1,128)} %convert_bitcast_fusion.2.order_ref, bf16[2048,384]{1,0:T(8,128)(2,1)} %get-tuple-element.78.a_ref, bf16[2048,384]{1,0:T(8,128)(2,1)} %copy-done.30, bf16[2048,768]{1,0:T(8,128)(2,1)} %get-tuple-element.88.refs_0_), custom_call_target="tpu_custom_call" | custom-call | flops 3221225472 | bytes 7864320 | tf_op jit(solution)/shard_map/home_out/pallas_call | solution.py:717
  309.6 3.7 all-to-all-start
  321.7 24.3 %scan_backward.3 = (bf16[2048,768]{1,0:T(8,128)(2,1)}, bf16[2048,384]{1,0:T(8,128)(2,1)}, f32[16,1,128]{2,1,0:T(1,128)}, f32[8,768]{1,0:T(8,128)}, f32[8,256]{1,0:T(8,128)}, /*index=5*/f32[8,128]{1,0:T(8,128)}) custom-call(bf16[2048,768]{1,0:T(8,128)(2,1)} %get-tuple-element.80.dy_ref, ...), custom_call_target="tpu_custom_call", output_to_operand_aliasing={{0}: (9, {}), {1}: (10, {}), {2}: (11, {})} | custom-call | flops 1000 | bytes 1000 | tf_op jit(solution)/shard_map/scan_backward/pallas_call | solution.py:765
  346.1 22.0 %scan_grads.1 = (bf16[1536,768]{1,0:T(8,128)(2,1)}, bf16[1536,384]{1,0:T(8,128)(2,1)}, bf16[2,192,768]{2,1,0:T(8,128)(2,1)}, bf16[2,192,768]{2,1,0:T(8,128)(2,1)}) custom-call(bf16[2048,1536]{1,0:T(8,128)(2,1)} %get-tuple-element.84.refs_1_.refs_0_, bf16[2048,1536]{1,0:T(8,128)(2,1)} %get-tuple-element.84.refs_1_.refs_0_, ...), custom_call_target="tpu_custom_call" | custom-call | flops 1000 | bytes 1000 | tf_op jit(solution)/shard_map/scan_grads/pallas_call | solution.py:923
  369.4 2.7 fusion.4
  373.3 34.7 %input_pieces.1 = (bf16[2048,384]{1,0:T(8,128)(2,1)}, bf16[2048,384]{1,0:T(8,128)(2,1)}, bf16[1,192,768]{2,1,0:T(8,128)(2,1)}, bf16[1,192,768]{2,1,0:T(8,128)(2,...) custom-call(bf16[2048,768]{1,0:T(8,128)(2,1)} %get-tuple-element.85.refs_3_.refs_0_, ...), custom_call_target="tpu_custom_call" | custom-call | flops 1000 | bytes 1000 | tf_op jit(solution)/shard_map/input_pieces/pallas_call | solution.py:885
  408.9 2.9 fusion.1.refs_1_
  412.4 44.8 %last_exchange.1 = (bf16[2048,384]{1,0:T(8,128)(2,1)}, bf16[3,192,768]{2,1,0:T(8,128)(2,1)}, f32[7,8,768]{2,1,0:T(8,128)}, f32[192,384]{1,0:T(8,128)}) custom-call(bf16[2048,384]{1,0:T(8,128)(2,1)} %get-tuple-element.103.refs_0_, bf16[4,192,768]{2,1,0:T(8,128)(2,1)} %fusion.1.refs_1_, f32[8,768]{1,0:T(8,128)} %pad_maximum_fusion.2.refs_2_, ...), custom_call_target="tpu_custom_call" | custom-call | tf_op jit(solution)/shard_map/last_exchange/pallas_call | solution.py:979
  459.6 2.2 convert_reduce_fusion
  461.7 10.1 %home_back.1 = bf16[2048,384]{1,0:T(8,128)(2,1)} custom-call(s32[1]{0:T(128)} %bitcast.me_ref, f32[16,1,128]{2,1,0:T(1,128)} %convert_bitcast_fusion.2.order_ref, bf16[2048,384]{1,0:T(8,128)(2,1)} %get-tuple-element.102.a_ref, bf16[2048,384]{1,0:T(8,128)(2,1)} %get-tuple-element.112.b_ref, bf16[2048,1536]{1,0:T(8,128)(2,1)} %get-tuple-element.84.refs_1_.refs_0_, ...), custom_call_target="tpu_custom_call" | custom-call | flops 3221225472 | bytes 7864320 | tf_op jit(solution)/shard_map/home_back/pallas_call | solution.py:717
  471.9 5.2 all-to-all-start.1
  482.4 15.6 %exchange.1 = f32[3,192,384]{2,1,0:T(8,128)} custom-call(f32[192,384]{1,0:T(8,128)} %pad_maximum_fusion.1.refs_0_), custom_call_target="tpu_custom_call" | custom-call | tf_op jit(solution)/shard_map/exchange/pallas_call | solution.py:188
  507.3 3.0 add_convert_fusion
  510.3 3.1 all-to-all-done.1
  513.4 3.0 fusion
  (124 shorter events, 40.8 us)
Async XLA Ops:
  247.7 51.8 %collective-permute-start = (bf16[2048,384]{1,0:T(8,128)(2,1)}, bf16[2048,384]{1,0:T(8,128)(2,1)S(1)}, u32[]{:S(2)}, u32[]{:S(2)}) collective-permute-start(bf16[2048,384]{1,0:T(8,128)(2,1)} %get-tuple-element.79.refs_4_), channel_id=1, source_target_pairs={{0,2},{1,3},{2,0},{3,1},{4,6},{5,7},{6,4},{7,5},{8,10},{9,11},{10,... | collective-permute-start | bytes 4718600 | tf_op jit(solution)/shard_map/ppermute | solution.py:1273
  309.6 3.7 copy-start.21
  309.6 4.5 copy-start.14
  309.6 62.6 %all-to-all-start = ((bf16[8,256,384]{2,1,0:T(8,128)(2,1)}), bf16[8,256,384]{2,1,0:T(8,128)(2,1)S(1)}, u32[]{:S(2)}, u32[]{:S(2)}) async-start(bf16[8,256,384]{2,1,0:T(8,128)(2,1)} %bitcast.101), calls=%async_computation | async-start | bytes 3145728 | tf_op jit(solution)/shard_map/all_to_all | solution.py:1278
  316.7 3.7 copy-start.13
  346.0 22.2 %copy-start.25 = (f32[8,256]{1,0:T(8,128)S(1)}, f32[8,256]{1,0:T(8,128)}, u32[]{:S(2)}) copy-start(f32[8,256]{1,0:T(8,128)} %get-tuple-element.100) | copy-start | bytes 24580
  346.0 22.2 %copy-start.26 = (f32[8,256]{1,0:T(8,128)S(1)}, f32[8,256]{1,0:T(8,128)}, u32[]{:S(2)}) copy-start(f32[8,256]{1,0:T(8,128)} %get-tuple-element.101) | copy-start | bytes 24580
  346.0 22.8 %copy-start.20 = (f32[16,1,128]{2,1,0:T(1,128)S(1)}, f32[16,1,128]{2,1,0:T(1,128)}, u32[]{:S(2)}) copy-start(f32[16,1,128]{2,1,0:T(1,128)} %get-tuple-element.99.refs_4_) | copy-start | bytes 24580
  346.0 22.7 %copy-start.24 = (f32[16,1,128]{2,1,0:T(1,128)S(1)}, f32[16,1,128]{2,1,0:T(1,128)}, u32[]{:S(2)}) copy-start(f32[16,1,128]{2,1,0:T(1,128)} %get-tuple-element.98.refs_3_) | copy-start | bytes 24580
  346.0 23.3 %copy-start.27 = (f32[8,128]{1,0:T(8,128)S(1)}, f32[8,128]{1,0:T(8,128)}, u32[]{:S(2)}) copy-start(f32[8,128]{1,0:T(8,128)} %get-tuple-element.109) | copy-start | bytes 12292
  346.0 23.3 %copy-start.28 = (f32[8,128]{1,0:T(8,128)S(1)}, f32[8,128]{1,0:T(8,128)}, u32[]{:S(2)}) copy-start(f32[8,128]{1,0:T(8,128)} %get-tuple-element.110) | copy-start | bytes 12292
  346.1 23.3 %copy-start.22 = (f32[8,768]{1,0:T(8,128)S(1)}, f32[8,768]{1,0:T(8,128)}, u32[]{:S(2)}) copy-start(f32[8,768]{1,0:T(8,128)} %get-tuple-element.105) | copy-start | bytes 73732
  346.1 23.3 %copy-start.23 = (f32[8,768]{1,0:T(8,128)S(1)}, f32[8,768]{1,0:T(8,128)}, u32[]{:S(2)}) copy-start(f32[8,768]{1,0:T(8,128)} %get-tuple-element.106) | copy-start | bytes 73732
  346.1 23.4 %copy-start.2 = (bf16[4,192,768]{2,1,0:T(8,128)(2,1)S(1)}, bf16[4,192,768]{2,1,0:T(8,128)(2,1)}, u32[]{:S(2)}) copy-start(bf16[4,192,768]{2,1,0:T(8,128)(2,1)} %fusion.3) | copy-start | bytes 3538948
  373.3 35.4 %copy-start.18 = (f32[8,256]{1,0:T(8,128)S(1)}, f32[8,256]{1,0:T(8,128)}, u32[]{:S(2)}) copy-start(f32[8,256]{1,0:T(8,128)} %add.133.refs_8_) | copy-start | bytes 24580
  458.2 13.6 %copy-start.19 = (f32[8,768]{1,0:T(8,128)}, f32[8,768]{1,0:T(8,128)S(1)}, u32[]{:S(2)}) copy-start(f32[8,768]{1,0:T(8,128)S(1)} %fusion.17) | copy-start | bytes 73732
  471.8 5.2 %copy-start.5 = (bf16[2,192,768]{2,1,0:T(8,128)(2,1)S(1)}, bf16[2,192,768]{2,1,0:T(8,128)(2,1)}, u32[]{:S(2)}) copy-start(bf16[2,192,768]{2,1,0:T(8,128)(2,1)} %get-tuple-element.159.refs_5_) | copy-start | bytes 1769476
  471.9 6.3 %copy-start.4 = (bf16[4,192,768]{2,1,0:T(8,128)(2,1)S(1)}, bf16[4,192,768]{2,1,0:T(8,128)(2,1)}, u32[]{:S(2)}) copy-start(bf16[4,192,768]{2,1,0:T(8,128)(2,1)} %fusion.1.refs_1_) | copy-start | bytes 3538948
  471.9 41.5 %all-to-all-start.1 = ((bf16[8,256,384]{2,1,0:T(8,128)(2,1)}), bf16[8,256,384]{2,1,0:T(8,128)(2,1)S(1)}, u32[]{:S(2)}, u32[]{:S(2)}) async-start(bf16[8,256,384]{2,1,0:T(8,128)(2,1)} %bitcast.108), calls=%async_computation.1 | async-start | bytes 3145728 | tf_op jit(solution)/shard_map/all_to_all | solution.py:1309
  478.3 2.0 copy-start.10
  478.3 2.0 copy-start.12
  478.4 2.2 copy-start.9
  498.0 6.8 %copy-start.29 = (bf16[192]{0:T(256)(128)(2,1)S(1)}, bf16[192]{0:T(256)(128)(2,1)}, u32[]{:S(2)}) copy-start(bf16[192]{0:T(256)(128)(2,1)} %param.17) | copy-start | bytes 1156
  500.0 7.3 %copy-start.1 = (bf16[8,256,384]{2,1,0:T(8,128)(2,1)S(1)}, bf16[8,256,384]{2,1,0:T(8,128)(2,1)}, u32[]{:S(2)}) copy-start(bf16[8,256,384]{2,1,0:T(8,128)(2,1)} %copy-done) | copy-start | bytes 4718596
  (10 other events, 11.9 us)

commit v6 on v5

--- a/solution.py
+++ b/solution.py
@@ -895,14 +895,54 @@
     )(*values, weight, *moved, *after)
 
 
-def grads_kernel(count, parts, moves, extra, *refs):
-    total = len(moves)
-    lefts, rights, srcs = refs[:count], refs[count : 2 * count], refs[2 * count : 2 * count + total]
-    refs = refs[2 * count + total + extra :]
-    outs, dsts, sems = refs[:count], refs[count : count + total], refs[count + total :]
+def second_bits(step, last, paired, came, kept, holds, halves, quarters, bit_sems, load_sems):
+    me, head = lax.axis_index("dp"), lax.axis_index("head")
+    side, mid = me & 1, (me >> 1) & 1
+    own = [paired[0].at[:, :, side], paired[1].at[:, mid]]
+    loads = [pltpu.make_async_copy(own[i], holds[i], load_sems.at[0, i]) for i in range(2)]
+    loads += [pltpu.make_async_copy(came[i], halves[i], load_sems.at[1, i]) for i in range(2)]
+    picks, peers = (mid, side), ((me ^ 2, head), (me ^ 1, head))
+    sends = [
+        pltpu.make_async_remote_copy(
+            src_ref=holds[i].at[:, 1 - picks[i]],
+            dst_ref=quarters[i],
+            send_sem=bit_sems.at[0, i],
+            recv_sem=bit_sems.at[1, i],
+            device_id=peers[i],
+            device_id_type=MESH,
+        )
+        for i in range(2)
+    ]
+
+    @pl.when(step == 0)
+    def _():
+        for copy in loads:
+            copy.start()
+        greet(peers)
+        for copy in loads:
+            copy.wait()
+        for i in range(2):
+            for j in range(holds[i].shape[0]):
+                for k in range(2):
+                    holds[i][j, k] = (holds[i][j, k].astype(F32) + halves[i][j, k].astype(F32)).astype(BF16)
+            sends[i].start()
+
+    @pl.when(step == last)
+    def _():
+        for i in range(2):
+            sends[i].wait()
+            for j in range(holds[i].shape[0]):
+                kept[i][j] = (holds[i][j, picks[i]].astype(F32) + quarters[i][j].astype(F32)).astype(BF16)
+
+
+def grads_kernel(count, parts, extra, reduce, *refs):
+    lefts, rights = refs[:count], refs[count : 2 * count]
+    paired, came = refs[2 * count : 2 * count + 2], refs[2 * count + 2 : 2 * count + 4]
+    refs = refs[2 * count + extra + (4 if reduce else 0) :]
+    outs, refs = refs[:count], refs[count:]
     step = pl.program_id(0)
-    if moves:
-        background(step == 0, step == count * parts - 1, moves, srcs, dsts, *sems)
+    if reduce:
+        second_bits(step, count * parts - 1, paired, came, refs[0:2], refs[2:4], refs[4:6], refs[6:8], refs[8], refs[9])
     for which in range(count):
 
         @pl.when((step >= which * parts) & (step < (which + 1) * parts))
@@ -911,7 +951,7 @@
             outs[which][...] = out.astype(BF16)
 
 
-def run_grads(pairs, name, moves=(), moved=(), number=0, after=()):
+def run_grads(pairs, name, paired=(), came=(), number=0, after=()):
     rows, deep = pairs[0][0].shape
     step = 512
     parts = deep // step
@@ -920,71 +960,100 @@
     into = lambda which: lambda i: jnp.clip(i - which * parts, 0, parts - 1)
     specs = [pl.BlockSpec((rows, step), lambda i, at=into(w): (0, at(i))) for w in range(count)]
     specs += [pl.BlockSpec(right.shape, lambda i: (0, 0)) for _, right in pairs]
+    kept = [(p.shape[0], p.shape[3], p.shape[4]) for p in paired]
+    twice = [pltpu.VMEM((m, 2, r, c), BF16) for m, r, c in kept]
+    sems = pltpu.SemaphoreType.DMA
     return pl.pallas_call(
-        functools.partial(grads_kernel, count, parts, tuple(moves), len(after)),
+        functools.partial(grads_kernel, count, parts, len(after), bool(paired)),
         grid=(count * parts,),
-        in_specs=specs + [anywhere] * (len(moves) + len(after)),
+        in_specs=specs + [anywhere] * (len(paired) + len(came) + len(after)),
         out_specs=[pl.BlockSpec((step, right.shape[1]), lambda i, at=into(w): (at(i), 0)) for w, (_, right) in enumerate(pairs)]
-        + [anywhere] * len(moves),
-        out_shape=[jax.ShapeDtypeStruct((deep, right.shape[1]), BF16) for _, right in pairs] + move_outs(moves, moved),
-        scratch_shapes=move_scratch(moves, moved),
+        + [pl.BlockSpec(shape, lambda i: (0, 0, 0)) for shape in kept],
+        out_shape=[jax.ShapeDtypeStruct((deep, right.shape[1]), BF16) for _, right in pairs] + [jax.ShapeDtypeStruct(shape, BF16) for shape in kept],
+        scratch_shapes=twice + twice + [pltpu.VMEM(shape, BF16) for shape in kept] + ([sems((2, 2)), sems((2, 2))] if paired else []),
         compiler_params=params("arbitrary", number=number),
         cost_estimate=pl.CostEstimate(flops=LIGHT, bytes_accessed=LIGHT, transcendentals=0),
         name=name,
-    )(*[left for left, _ in pairs], *[right for _, right in pairs], *moved, *after)
+    )(*[left for left, _ in pairs], *[right for _, right in pairs], *paired, *came, *after)
 
 
 def last_kernel(moves, *refs):
     count = len(moves)
-    srcs, pair_ref = refs[:count], refs[count]
-    dsts, out_ref = refs[count + 1 : 2 * count + 1], refs[2 * count + 1]
-    kept_ref, line_ref, came_ref, own_ref, pair_sems, sems, local_sems = refs[2 * count + 2 :]
+    srcs, thin_ref, wide_ref, half_ref = refs[:count], *refs[count : count + 3]
+    refs = refs[count + 3 :]
+    dsts, thin_out, wide_out = refs[:count], refs[count], refs[count + 1]
+    thin_own, thin_came, thin_line, wide_own, wide_came, wide_line, load_sems, pair_sems, sems, local_sems = refs[count + 2 :]
     me, head = lax.axis_index("dp"), lax.axis_index("head")
+    side, high = me & 1, me >> 1
+    many = thin_own.shape[0]
     peers, copies = make_moves(moves, srcs, dsts, sems, local_sems)
 
-    def remote(src, dst, slot, peer):
+    def remote(src, dst, which, slot, peer):
         return pltpu.make_async_remote_copy(
-            src_ref=src, dst_ref=dst, send_sem=pair_sems.at[0, slot], recv_sem=pair_sems.at[1, slot], device_id=(peer, head), device_id_type=MESH
+            src_ref=src,
+            dst_ref=dst,
+            send_sem=pair_sems.at[0, which, slot],
+            recv_sem=pair_sems.at[1, which, slot],
+            device_id=(peer, head),
+            device_id_type=MESH,
         )
 
-    high = me >> 1
-    half = remote(pair_ref.at[:, 1 - (me & 1)], came_ref, 0, me ^ 1)
-    line = [remote(kept_ref.at[high ^ j], line_ref.at[j - 1], j, me ^ (2 * j)) for j in range(1, own_ref.shape[0])]
-    own = pltpu.make_async_copy(pair_ref.at[:, me & 1], own_ref, pair_sems.at[2, 0])
+    def blocks(own, line, which):
+        return [remote(own.at[high ^ j], line.at[j - 1], which, j, me ^ (2 * j)) for j in range(1, many)]
+
+    half = remote(thin_ref.at[:, 1 - side], thin_came, 0, 0, me ^ 1)
+    thin_blocks, wide_blocks = blocks(thin_own, thin_line, 0), blocks(wide_own, wide_line, 1)
+    loads = [
+        pltpu.make_async_copy(wide_ref.at[:, side], wide_own, load_sems.at[0]),
+        pltpu.make_async_copy(half_ref, wide_came, load_sems.at[1]),
+        pltpu.make_async_copy(thin_ref.at[:, side], thin_own, load_sems.at[2]),
+    ]
+    for copy in loads:
+        copy.start()
     greet(peers)
     half.start()
-    own.start()
     for copy in copies:
         copy.start()
-    own.wait()
+    for copy in loads:
+        copy.wait()
+    for j in range(many):
+        wide_own[j] = (wide_own[j].astype(F32) + wide_came[j].astype(F32)).astype(BF16)
+    for copy in wide_blocks:
+        copy.start()
     half.wait()
-    for j in range(own_ref.shape[0]):
-        kept_ref[j] = (own_ref[j].astype(F32) + came_ref[j].astype(F32)).astype(BF16)
-    for copy in line:
+    for j in range(many):
+        thin_own[j] = (thin_own[j].astype(F32) + thin_came[j].astype(F32)).astype(BF16)
+    for copy in thin_blocks:
         copy.start()
-    for copy in line:
+    for copy in wide_blocks + thin_blocks:
         copy.wait()
-    total = kept_ref[high].astype(F32)
-    for j in range(1, own_ref.shape[0]):
-        total = total + line_ref[j - 1].astype(F32)
-    out_ref[...] = total
+    thin, wide = thin_own[high].astype(F32), wide_own[high].astype(F32)
+    for j in range(many - 1):
+        thin, wide = thin + thin_line[j].astype(F32), wide + wide_line[j].astype(F32)
+    thin_out[...] = thin
+    wide_out[...] = wide
     for copy in copies:
         copy.wait()
 
 
-def run_last(moves, values, paired, number):
-    many, _, block, wide = paired.shape
+def run_last(moves, values, thin, wide, half, number):
+    many, _, block, slim = thin.shape
+    broad = wide.shape[3]
     anywhere = pl.BlockSpec(memory_space=pl.ANY)
-    own = pltpu.VMEM((many, block, wide), BF16)
+    inside = pl.BlockSpec(memory_space=pltpu.VMEM)
+    space = lambda count, columns: pltpu.VMEM((count, block, columns), BF16)
+    sems = pltpu.SemaphoreType.DMA
     return pl.pallas_call(
         functools.partial(last_kernel, tuple(moves)),
-        in_specs=[anywhere] * (len(moves) + 1),
-        out_specs=[anywhere] * len(moves) + [pl.BlockSpec(memory_space=pltpu.VMEM)],
-        out_shape=move_outs(moves, values) + [jax.ShapeDtypeStruct((block, wide), F32)],
-        scratch_shapes=[own, pltpu.VMEM((many - 1, block, wide), BF16), own, own, pltpu.SemaphoreType.DMA((3, many))] + move_scratch(moves, values),
+        in_specs=[anywhere] * (len(moves) + 3),
+        out_specs=[anywhere] * len(moves) + [inside] * 2,
+        out_shape=move_outs(moves, values) + [jax.ShapeDtypeStruct((block, slim), F32), jax.ShapeDtypeStruct((block, broad), F32)],
+        scratch_shapes=[space(many, slim), space(many, slim), space(many - 1, slim), space(many, broad), space(many, broad), space(many - 1, broad)]
+        + [sems((3,)), sems((2, 2, many))]
+        + move_scratch(moves, values),
         compiler_params=pltpu.CompilerParams(collective_id=number, has_side_effects=True, vmem_limit_bytes=LIMIT),
         name="last_exchange",
-    )(*values, paired)
+    )(*values, thin, wide, half)
 
 
 def row_forward(size, quarter, own_ref, full_ref, sems):
@@ -1253,10 +1322,6 @@
     dyn, co = run_gate(full_g, w_o, y, u_zx, gated, mask)
     yg, dz, dy, gg, rd_z = run_mid(all_width, y, u_zx, dyn, gated, mask, ss, co, 4)
 
-    def keep(paired, came, bit):
-        own = lax.dynamic_index_in_dim(paired, (here >> bit) & 1, 1, keepdims=False)
-        return (own.astype(F32) + came.astype(F32)).astype(BF16)
-
     def total(kept, came, shift):
         own = lax.dynamic_index_in_dim(kept, here >> shift, 0, keepdims=False)
         return own.astype(F32) + jnp.sum(came.astype(F32), axis=0)
@@ -1277,13 +1342,10 @@
     sent_out = run_home(me, arrange, [out_own, out_arrived], None, deep, "home_out", [back0[0]])
     got_out = lax.all_to_all(sent_out, "dp", split_axis=0, concat_axis=0, tiled=True)
     *back1, gx1, gb1, gh1 = scan(1, *shared, back0, [], [], 0, [sent_out])
-    kept_z = keep(grad_z, came_z, 1)
-    kept_o = keep(grad_o, came_o, 0).reshape(size // 4, 2, own_w, width)
     dux, dbd, rd_x = back1
-    grad_x, grad_bd, came_z, came_o = run_grads(
-        [(normed, dux), (normed, dbd)], "scan_grads", [("half", "dp", 0), ("half", "dp", 1)], [kept_z, kept_o], 8
+    grad_x, grad_bd, kept_o, kept_z = run_grads(
+        [(normed, dux), (normed, dbd)], "scan_grads", [fours(grad_o), grad_z], [came_o.reshape(came_z.shape), came_z], 8
     )
-    kept_z, kept_o = keep(kept_z, came_z, 0), keep(kept_o, came_o, 1)
     grad_x, grad_bd = pairs(grad_x), pairs(grad_bd)
     gb = gb0 + gb1
     d_far, d_own, line_o, line_z, came_x2, got_rows, got_gb = run_pieces(
@@ -1296,14 +1358,11 @@
         9,
         [got_out],
     )
-    kept_x = keep(grad_x, came_x2, 0)
     gb = gb[:5] + jnp.sum(got_gb, axis=0)[:5]
     gh = gh0 + gh1
     ends = jnp.concatenate([gb[3], gb[4]] + [gh[i, :32] for i in range(3)] + [jnp.zeros((width - 4 * N - 96,), F32)])
     small = jnp.concatenate([(gx0 + gx1)[:5], gg[:1], jnp.concatenate([gb[0], gb[1], gb[2]])[None], ends[None]], axis=0)
-    d_arrived, line_x, got_small, grad_bd = run_last(
-        [("whole", "head", 2), ("direct", "dp", 1), ("spread", "dp")], [d_far, kept_x, small], grad_bd, 10
-    )
+    d_arrived, got_small, grad_bd, grad_x = run_last([("whole", "head", 2), ("spread", "dp")], [d_far, small], grad_bd, grad_x, came_x2, 10)
 
     sent_back = run_home(me, arrange, [d_own, d_arrived], [normed, inv_one, gain, rd_z, rd_x, got_rows], deep, "home_back")
     got_back = lax.all_to_all(sent_back, "dp", split_axis=0, concat_axis=0, tiled=True)
@@ -1311,7 +1370,6 @@
     final_back = (cotangent.astype(F32) + got_back.astype(F32)).astype(BF16)
 
     grad_out, grad_z = total(kept_o, line_o, 2), total(kept_z, line_z, 2)
-    grad_x = total(kept_x, line_x, 1)
     small = small + jnp.sum(got_small, axis=0)
     grad_zx = jnp.stack([grad_z, grad_x], axis=1)
     of_gain = jnp.sum(grad_z * w_zx[:, 0].astype(F32), axis=1) + jnp.sum(grad_x * w_zx[:, 1].astype(F32), axis=1)

time: 526 us -> 515 us (0.979)
  other arithmetic: 30.9 us -> 21 us
    convert_element_type x4 -> x0, other arithmetic: 8.51 us -> none  [keep(): return (own.astype(F32) + came.astype(F32)).astype(BF16)]
  transfers between devices with their start and end apart: 3 -> 3, of which waited for: 1 -> 1; matrix products, arithmetic and copies ran while one was open for 5% -> 4% of each run, Pallas kernels for 22% -> 23%
where the time goes in v6:
time: 515 us; the launch traced here: 505 us
  Pallas kernels  450 us (87%)
  local copies, waits for them, and re-layouts  21.7 us (4%)
  other arithmetic  21 us (4%)
  starting transfers between devices  9.81 us (2%)
    pallas_call x1, Pallas kernels, run_entry(): pl.pallas_call(functools.partial(entry_kernel, PARTS), in_specs=[pl.Block...  137 us
    pallas_call x2, Pallas kernels, run_backward(): pl.pallas_call(functools.partial(backward_kernel, heads, len(before) + le...  57.7 us
    pallas_call x2, Pallas kernels, run_pieces(): pl.pallas_call(functools.partial(pieces_kernel, len(values), many, tuple(...  46.2 us
    pallas_call x1, Pallas kernels, run_last(): pl.pallas_call(functools.partial(last_kernel, tuple(moves)), in_specs=[an...  46.1 us
    pallas_call x2, Pallas kernels, run_grads(): pl.pallas_call(functools.partial(grads_kernel, count, parts, len(after),...  41.4 us
    pallas_call x1, Pallas kernels, run_forward(): pl.pallas_call(functools.partial(forward_kernel, heads, slots * chunks),...  35.2 us
    pallas_call x1, Pallas kernels, run_project(): pl.pallas_call(functools.partial(project_kernel, heads, rows // step), gr...  23 us
    pallas_call x2, Pallas kernels, run_home(): pl.pallas_call(functools.partial(home_kernel, extra is not None, float(de...  19.1 us
  transfers between devices with their start and end apart: 3, of which 1 were waited for; matrix products, arithmetic and copies ran while one was open for 4% of the time, Pallas kernels for 23%

profile of v6, /device:TPU:0, one launch (start us, length us, event | category | flops | bytes accessed | tf_op | source)
XLA Modules:
  0.0 505.2 jit_solution(14065454436593374893)
XLA Ops:
  2.0 2.1 concatenate.27
  11.6 137.3 %entry.1 = (bf16[8,256,1536]{2,1,0:T(8,128)(2,1)}, bf16[8,256,1536]{2,1,0:T(8,128)(2,1)}, bf16[8,4,48,1920]{3,2,1,0:T(8,128)(2,1)}) custom-call(f32[16,1,128]{2,1,0:T(1,128)} %convert_bitcast_fusion.order_ref, bf16[8,256,384]{2,1,0:T(8,128)(2,1)} %bitcast.70, bf16[8,256,384]{2,1,0:T(8,128)(2,1)} %bitcast.71, bf16[4,48,1920]{2,1,0:T(8,128)(2,1)} %concatenate.31.w_ref), custom_call_target="tpu_custom_call" | custom-call | tf_op jit(solution)/shard_map/entry/pallas_call | solution.py:1269
  148.9 23.0 %project.1 = (bf16[2048,1536]{1,0:T(8,128)(2,1)}, f32[16,1,128]{2,1,0:T(1,128)}, bf16[2048,1536]{1,0:T(8,128)(2,1)}, f32[2048,384]{1,0:T(8,128)}, f32[8,1536]{1,0:T(8,128)}, /*index=5*/bf16[8,4,48,768]{3,2,1,0:T(8,128)(2,1)}) custom-call(bf16[2048,1536]{1,0:T(8,128)(2,1)} %bitcast.69, bf16[1536,1920]{1,0:T(8,128)(2,1)} %bitcast.58, bf16[4,48,768]{2,1,0:T(8,128)(2,1)} %bitcast.77), custom_call_target="tpu_custom_call" | custom-call | flops 1000 | bytes 1000 | tf_op jit(solution)/shard_map/project/pallas_call | solution.py:649
  171.9 35.2 %scan_forward.1 = (bf16[2048,768]{1,0:T(8,128)(2,1)}, f32[16,1,128]{2,1,0:T(1,128)}, bf16[2048,768]{1,0:T(8,128)(2,1)}, f32[2048,256]{1,0:T(8,128)}, bf16[16,128...) custom-call(bf16[2048,1536]{1,0:T(8,128)(2,1)} %get-tuple-element.68.x_ref.z_ref, ...), custom_call_target="tpu_custom_call", output_to_operand_aliasing={{5}: (7, {})} | custom-call | flops 3774873600 | bytes 12582912 | tf_op jit(solution)/shard_map/scan_forward/pallas_call | solution.py:597
  207.0 12.4 %gate_back.1 = (bf16[2048,768]{1,0:T(8,128)(2,1)}, f32[16,1,128]{2,1,0:T(1,128)}) custom-call(bf16[2048,1536]{1,0:T(8,128)(2,1)} %bitcast.56, bf16[1536,768]{1,0:T(8,128)(2,1)} %bitcast.60, bf16[2048,768]{1,0:T(8,128)(2,1)} %get-tuple-element.71.y_ref, bf16[2048,1536]{1,0:T(8,128)(2,1)} %get-tuple-element.68.x_ref.z_ref, f32[1,768]{1,0:T(1,128)} %reshape.183.par_ref, ...), custom_call_target="tpu_custom_call" | custom-call | flops 4831838208 | bytes 15728640 | tf_op jit(solution)/shard_map/gate_back/pallas_call | solution.py:683
  219.4 15.8 %gate_mid.1 = (bf16[2048,768]{1,0:T(8,128)(2,1)}, bf16[2048,768]{1,0:T(8,128)(2,1)}, bf16[2048,768]{1,0:T(8,128)(2,1)}, f32[8,768]{1,0:T(8,128)}, f32[16,1,128]{2,1,0:T(1,128)}) custom-call(bf16[2048,768]{1,0:T(8,128)(2,1)} %get-tuple-element.71.y_ref, bf16[2048,1536]{1,0:T(8,128)(2,1)} %get-tuple-element.68.x_ref.z_ref, ...), custom_call_target="tpu_custom_call" | custom-call | flops 47185920 | bytes 18874368 | tf_op jit(solution)/shard_map/gate_mid/pallas_call | solution.py:743
  235.2 12.5 %branch_pieces.1 = (bf16[2048,384]{1,0:T(8,128)(2,1)}, bf16[2048,384]{1,0:T(8,128)(2,1)}) custom-call(bf16[2048,768]{1,0:T(8,128)(2,1)} %get-tuple-element.77.refs_0_.refs_2_, bf16[1536,768]{1,0:T(8,128)(2,1)} %bitcast.61), custom_call_target="tpu_custom_call" | custom-call | flops 1000 | bytes 1000 | tf_op jit(solution)/shard_map/branch_pieces/pallas_call | solution.py:885
  247.8 1.8 collective-permute-start
  249.6 16.6 %gate_grads.1 = (bf16[1536,768]{1,0:T(8,128)(2,1)}, bf16[1536,768]{1,0:T(8,128)(2,1)}) custom-call(bf16[2048,1536]{1,0:T(8,128)(2,1)} %bitcast.57, bf16[2048,1536]{1,0:T(8,128)(2,1)} %get-tuple-element.84.refs_1_.refs_0_, bf16[2048,768]{1,0:T(8,128)(2,1)} %get-tuple-element.77.refs_0_.refs_2_, bf16[2048,768]{1,0:T(8,128)(2,1)} %get-tuple-element.85.refs_3_.refs_0_, ...), custom_call_target="tpu_custom_call" | custom-call | flops 1000 | bytes 1000 | tf_op jit(solution)/shard_map/gate_grads/pallas_call | solution.py:966
  266.2 33.3 %scan_backward.2 = (bf16[2048,768]{1,0:T(8,128)(2,1)}, bf16[2048,384]{1,0:T(8,128)(2,1)}, f32[16,1,128]{2,1,0:T(1,128)}, f32[8,768]{1,0:T(8,128)}, f32[8,256]{1,...) custom-call(bf16[2048,768]{1,0:T(8,128)(2,1)} %get-tuple-element.80.dy_ref, ...), custom_call_target="tpu_custom_call" | custom-call | flops 1000 | bytes 1000 | tf_op jit(solution)/shard_map/scan_backward/pallas_call | solution.py:765
  300.7 8.7 %home_out.1.refs_3_ = bf16[2048,384]{1,0:T(8,128)(2,1)} custom-call(s32[1]{0:T(128)} %bitcast.me_ref, f32[16,1,128]{2,1,0:T(1,128)} %convert_bitcast_fusion.order_ref, bf16[2048,384]{1,0:T(8,128)(2,1)} %get-tuple-element.78.a_ref, bf16[2048,384]{1,0:T(8,128)(2,1)} %copy-done.23, bf16[2048,768]{1,0:T(8,128)(2,1)} %get-tuple-element.88.refs_0_), custom_call_target="tpu_custom_call" | custom-call | flops 3221225472 | bytes 7864320 | tf_op jit(solution)/shard_map/home_out/pallas_call | solution.py:717
  309.4 3.9 all-to-all-start
  316.5 24.3 %scan_backward.3 = (bf16[2048,768]{1,0:T(8,128)(2,1)}, bf16[2048,384]{1,0:T(8,128)(2,1)}, f32[16,1,128]{2,1,0:T(1,128)}, f32[8,768]{1,0:T(8,128)}, f32[8,256]{1,0:T(8,128)}, /*index=5*/f32[8,128]{1,0:T(8,128)}) custom-call(bf16[2048,768]{1,0:T(8,128)(2,1)} %get-tuple-element.80.dy_ref, ...), custom_call_target="tpu_custom_call", output_to_operand_aliasing={{0}: (9, {}), {1}: (10, {}), {2}: (11, {})} | custom-call | flops 1000 | bytes 1000 | tf_op jit(solution)/shard_map/scan_backward/pallas_call | solution.py:765
  340.9 24.8 %scan_grads.1 = (bf16[1536,768]{1,0:T(8,128)(2,1)}, bf16[1536,384]{1,0:T(8,128)(2,1)}, bf16[2,192,768]{2,1,0:T(8,128)(2,1)}, bf16[2,192,768]{2,1,0:T(8,128)(2,1)}) custom-call(bf16[2048,1536]{1,0:T(8,128)(2,1)} %get-tuple-element.84.refs_1_.refs_0_, bf16[2048,1536]{1,0:T(8,128)(2,1)} %get-tuple-element.84.refs_1_.refs_0_, ...), custom_call_target="tpu_custom_call" | custom-call | flops 1000 | bytes 1000 | tf_op jit(solution)/shard_map/scan_grads/pallas_call | solution.py:966
  368.1 33.7 %input_pieces.1 = (bf16[2048,384]{1,0:T(8,128)(2,1)}, bf16[2048,384]{1,0:T(8,128)(2,1)}, bf16[1,192,768]{2,1,0:T(8,128)(2,1)}, bf16[1,192,768]{2,1,0:T(8,128)(2,...) custom-call(bf16[2048,768]{1,0:T(8,128)(2,1)} %get-tuple-element.85.refs_3_.refs_0_, ...), custom_call_target="tpu_custom_call" | custom-call | flops 1000 | bytes 1000 | tf_op jit(solution)/shard_map/input_pieces/pallas_call | solution.py:885
  403.3 46.1 %last_exchange.1 = (bf16[2048,384]{1,0:T(8,128)(2,1)}, f32[7,8,768]{2,1,0:T(8,128)}, f32[192,384]{1,0:T(8,128)}, f32[192,768]{1,0:T(8,128)}) custom-call(bf16[2048,384]{1,0:T(8,128)(2,1)} %get-tuple-element.103.refs_0_, f32[8,768]{1,0:T(8,128)} %pad_maximum_fusion.2.refs_1_, bf16[4,2,192,384]{3,2,1,0:T(8,128)(2,1)} %bitcast.76, ...), custom_call_target="tpu_custom_call" | custom-call | tf_op jit(solution)/shard_map/last_exchange/pallas_call | solution.py:1046
  451.1 10.4 %home_back.1 = bf16[2048,384]{1,0:T(8,128)(2,1)} custom-call(s32[1]{0:T(128)} %bitcast.me_ref, f32[16,1,128]{2,1,0:T(1,128)} %convert_bitcast_fusion.order_ref, bf16[2048,384]{1,0:T(8,128)(2,1)} %get-tuple-element.102.a_ref, bf16[2048,384]{1,0:T(8,128)(2,1)} %get-tuple-element.112.b_ref, bf16[2048,1536]{1,0:T(8,128)(2,1)} %get-tuple-element.84.refs_1_.refs_0_, ...), custom_call_target="tpu_custom_call" | custom-call | flops 3221225472 | bytes 7864320 | tf_op jit(solution)/shard_map/home_back/pallas_call | solution.py:717
  461.5 4.1 all-to-all-start.1
  468.4 1.9 copy.39
  472.5 15.6 %exchange.1 = f32[3,192,384]{2,1,0:T(8,128)} custom-call(f32[192,384]{1,0:T(8,128)} %pad_maximum_fusion.1.refs_0_), custom_call_target="tpu_custom_call" | custom-call | tf_op jit(solution)/shard_map/exchange/pallas_call | solution.py:188
  488.1 2.0 reduce_sum.76
  495.4 1.9 add_bitcast_fusion
  497.3 3.0 add_convert_fusion
  501.8 3.0 fusion
  (102 shorter events, 30.4 us)
Async XLA Ops:
  247.8 51.8 %collective-permute-start = (bf16[2048,384]{1,0:T(8,128)(2,1)}, bf16[2048,384]{1,0:T(8,128)(2,1)S(1)}, u32[]{:S(2)}, u32[]{:S(2)}) collective-permute-start(bf16[2048,384]{1,0:T(8,128)(2,1)} %get-tuple-element.79.refs_4_), channel_id=1, source_target_pairs={{0,2},{1,3},{2,0},{3,1},{4,6},{5,7},{6,4},{7,5},{8,10},{9,11},{10,... | collective-permute-start | bytes 4718600 | tf_op jit(solution)/shard_map/ppermute | solution.py:1338
  299.6 1.1 copy-start.23
  309.4 3.9 copy-start.14
  309.4 5.4 %copy-start.2 = (bf16[192,2,768]{2,1,0:T(2,128)(2,1)S(1)}, bf16[192,2,768]{2,1,0:T(2,128)(2,1)}, u32[]{:S(2)}) copy-start(bf16[192,2,768]{2,1,0:T(2,128)(2,1)} %param.18) | copy-start | bytes 1769476
  309.4 57.5 %all-to-all-start = ((bf16[8,256,384]{2,1,0:T(8,128)(2,1)}), bf16[8,256,384]{2,1,0:T(8,128)(2,1)S(1)}, u32[]{:S(2)}, u32[]{:S(2)}) async-start(bf16[8,256,384]{2,1,0:T(8,128)(2,1)} %bitcast.72), calls=%async_computation | async-start | bytes 3145728 | tf_op jit(solution)/shard_map/all_to_all | solution.py:1343
  340.8 24.8 %copy-start.18 = (f32[8,256]{1,0:T(8,128)S(1)}, f32[8,256]{1,0:T(8,128)}, u32[]{:S(2)}) copy-start(f32[8,256]{1,0:T(8,128)} %get-tuple-element.100) | copy-start | bytes 24580
  340.8 24.8 %copy-start.19 = (f32[8,256]{1,0:T(8,128)S(1)}, f32[8,256]{1,0:T(8,128)}, u32[]{:S(2)}) copy-start(f32[8,256]{1,0:T(8,128)} %get-tuple-element.101) | copy-start | bytes 24580
  340.8 25.4 %copy-start.13 = (f32[16,1,128]{2,1,0:T(1,128)S(1)}, f32[16,1,128]{2,1,0:T(1,128)}, u32[]{:S(2)}) copy-start(f32[16,1,128]{2,1,0:T(1,128)} %get-tuple-element.99.refs_4_) | copy-start | bytes 24580
  340.8 25.4 %copy-start.17 = (f32[16,1,128]{2,1,0:T(1,128)S(1)}, f32[16,1,128]{2,1,0:T(1,128)}, u32[]{:S(2)}) copy-start(f32[16,1,128]{2,1,0:T(1,128)} %get-tuple-element.98.refs_3_) | copy-start | bytes 24580
  340.8 26.0 %copy-start.20 = (f32[8,128]{1,0:T(8,128)S(1)}, f32[8,128]{1,0:T(8,128)}, u32[]{:S(2)}) copy-start(f32[8,128]{1,0:T(8,128)} %get-tuple-element.108) | copy-start | bytes 12292
  340.8 26.0 %copy-start.21 = (f32[8,128]{1,0:T(8,128)S(1)}, f32[8,128]{1,0:T(8,128)}, u32[]{:S(2)}) copy-start(f32[8,128]{1,0:T(8,128)} %get-tuple-element.109) | copy-start | bytes 12292
  340.8 26.0 %copy-start.15 = (f32[8,768]{1,0:T(8,128)S(1)}, f32[8,768]{1,0:T(8,128)}, u32[]{:S(2)}) copy-start(f32[8,768]{1,0:T(8,128)} %get-tuple-element.104) | copy-start | bytes 73732
  340.9 26.0 %copy-start.16 = (f32[8,768]{1,0:T(8,128)S(1)}, f32[8,768]{1,0:T(8,128)}, u32[]{:S(2)}) copy-start(f32[8,768]{1,0:T(8,128)} %get-tuple-element.105) | copy-start | bytes 73732
  366.9 1.1 copy-start
  368.1 34.5 %copy-start.11 = (f32[8,256]{1,0:T(8,128)S(1)}, f32[8,256]{1,0:T(8,128)}, u32[]{:S(2)}) copy-start(f32[8,256]{1,0:T(8,128)} %add.84.refs_8_) | copy-start | bytes 24580
  450.4 16.2 %copy-start.12 = (f32[8,768]{1,0:T(8,128)}, f32[8,768]{1,0:T(8,128)S(1)}, u32[]{:S(2)}) copy-start(f32[8,768]{1,0:T(8,128)S(1)} %fusion.9) | copy-start | bytes 73732
  461.5 4.1 copy-start.3
  461.5 40.4 %all-to-all-start.1 = ((bf16[8,256,384]{2,1,0:T(8,128)(2,1)}), bf16[8,256,384]{2,1,0:T(8,128)(2,1)S(1)}, u32[]{:S(2)}, u32[]{:S(2)}) async-start(bf16[8,256,384]{2,1,0:T(8,128)(2,1)} %bitcast.74), calls=%async_computation.1 | async-start | bytes 3145728 | tf_op jit(solution)/shard_map/all_to_all | solution.py:1368
  468.4 2.0 copy-start.4
  468.4 2.0 copy-start.5
  468.4 2.0 copy-start.6
  470.4 1.1 copy-start.8
  488.0 6.8 %copy-start.22 = (bf16[192]{0:T(256)(128)(2,1)S(1)}, bf16[192]{0:T(256)(128)(2,1)}, u32[]{:S(2)}) copy-start(bf16[192]{0:T(256)(128)(2,1)} %param.17) | copy-start | bytes 1156
  490.0 7.3 %copy-start.1 = (bf16[8,256,384]{2,1,0:T(8,128)(2,1)S(1)}, bf16[8,256,384]{2,1,0:T(8,128)(2,1)}, u32[]{:S(2)}) copy-start(bf16[8,256,384]{2,1,0:T(8,128)(2,1)} %copy-done) | copy-start | bytes 4718596
  (3 other events, 2.6 us)

commit v7 on v6

--- a/solution.py
+++ b/solution.py
@@ -357,18 +357,6 @@
     ubd_ref[...] = dot(normed, w_ref[:, width:])
 
 
-def gate_kernel(g_ref, wo_ref, y_ref, z_ref, par_ref, mask_ref, dyn_ref, co_ref):
-    dyn = dot(g_ref[...], wo_ref[...])
-    for part in range(dyn.shape[0] // T):
-        rows = slice(part * T, part * T + T)
-        mask = to_col(mask_ref[part])[:, 0:1]
-        own = dyn[rows] * mask
-        dyn_ref[rows] = own.astype(BF16)
-        z = z_ref[rows].astype(F32)
-        w = y_ref[rows].astype(F32) * z * sigmoid(z)
-        co_ref[part] = to_row(jnp.sum(own * w * par_ref[0:1], axis=1, keepdims=True))
-
-
 def home_kernel(last, deep, me_ref, order_ref, a_ref, b_ref, *refs):
     out_ref, held_ref = refs[-2:]
     step = pl.program_id(0)
@@ -397,49 +385,75 @@
     def _():
         base = ((step - many) * size).astype(F32)
         row = lax.broadcasted_iota(jnp.int32, (size, T), 0).astype(F32) + base
-        picks = jnp.concatenate([(row == order_ref[j]).astype(F32).astype(BF16) for j in range(order_ref.shape[0])], axis=1)
+        picks = jnp.concatenate([(row == order_ref[j].astype(F32)).astype(F32).astype(BF16) for j in range(order_ref.shape[0])], axis=1)
         out_ref[...] = dot(picks, held_ref[...]).astype(BF16)
 
 
-def mid_kernel(width, moves, y_ref, z_ref, dyn_ref, par_ref, mask_ref, ss_ref, co_ref, yg_ref, dz_ref, dy_ref, gg_ref, rd_ref, got_ss, got_co, sems, local_sems):
+def gate_kernel(width, moves, g_ref, wo_ref, y_ref, z_ref, gain_ref, mask_ref, ss_ref, yg_ref, dz_ref, dy_ref, gg_ref, rd_ref, held, co_held, got_ss, got_co, sems, local_sems):
     step = pl.program_id(0)
+    many = pl.num_programs(0) // 2
+    size = y_ref.shape[0]
+    parts = size // T
+    others = got_ss.shape[0]
+    peers, copies = make_moves(moves, (ss_ref, co_held), (got_ss, got_co), sems, local_sems)
+    gain = gain_ref[0:1]
 
     @pl.when(step == 0)
     def _():
         gg_ref[...] = jnp.zeros_like(gg_ref)
-        peers, copies = make_moves(moves, (ss_ref, co_ref), (got_ss, got_co), sems, local_sems)
         greet(peers)
-        for copy in copies:
+        for copy in copies[:others]:
             copy.start()
+
+    @pl.when(step < many)
+    def _():
+        dyn = dot(g_ref[...], wo_ref[...])
+        for part in range(parts):
+            rows = slice(part * T, part * T + T)
+            mask = to_col(mask_ref[part])[:, 0:1]
+            own = dyn[rows] * mask
+            held[step, rows] = own.astype(BF16)
+            z = z_ref[rows].astype(F32)
+            w = y_ref[rows].astype(F32) * z * sigmoid(z)
+            co_held[step * parts + part] = to_row(jnp.sum(own * w * gain, axis=1, keepdims=True))
+
+    @pl.when(step == many - 1)
+    def _():
+        for copy in copies[others:]:
+            copy.start()
+
+    @pl.when(step == many)
+    def _():
         for copy in copies:
             copy.wait()
 
-    gain = par_ref[0:1]
-    parts = y_ref.shape[0] // T
-    for part in range(parts):
-        rows = slice(part * T, part * T + T)
-        here = step * parts + part
-        ss, co = ss_ref[here], co_ref[here]
-        for other in range(got_ss.shape[0]):
-            ss, co = ss + got_ss[other, here], co + got_co[other, here]
-        mask = to_col(mask_ref[part])[:, 0:1]
-        inv_row = lax.rsqrt(ss / width + EPS)
-        inv = to_col(inv_row)[:, 0:1]
-        cube = to_col(inv_row * inv_row * inv_row * (co / width))[:, 0:1]
-        y = y_ref[rows].astype(F32)
-        z = z_ref[rows].astype(F32)
-        dyn = dyn_ref[rows].astype(F32)
-        s = sigmoid(z)
-        act = z * s
-        w = y * act
-        wi = w * inv
-        yg_ref[rows] = (wi * gain * mask).astype(BF16)
-        gg_ref[0:1] += jnp.sum(dyn * wi, axis=0, keepdims=True)
-        dw = inv * gain * dyn - w * cube
-        dy_ref[rows] = (dw * act).astype(BF16)
-        dz = dw * y * (s * (1.0 + z * (1.0 - s)))
-        dz_ref[rows] = dz.astype(BF16)
-        rd_ref[part] = to_row(jnp.sum(dz * z, axis=1, keepdims=True))
+    @pl.when(step >= many)
+    def _():
+        for part in range(parts):
+            rows = slice(part * T, part * T + T)
+            block = step - many
+            here = block * parts + part
+            ss, co = ss_ref[here], co_held[here]
+            for other in range(others):
+                ss, co = ss + got_ss[other, here], co + got_co[other, here]
+            mask = to_col(mask_ref[part])[:, 0:1]
+            inv_row = lax.rsqrt(ss / width + EPS)
+            inv = to_col(inv_row)[:, 0:1]
+            cube = to_col(inv_row * inv_row * inv_row * (co / width))[:, 0:1]
+            y = y_ref[rows].astype(F32)
+            z = z_ref[rows].astype(F32)
+            dyn = held[block, rows].astype(F32)
+            s = sigmoid(z)
+            act = z * s
+            w = y * act
+            wi = w * inv
+            yg_ref[rows] = (wi * gain * mask).astype(BF16)
+            gg_ref[0:1] += jnp.sum(dyn * wi, axis=0, keepdims=True)
+            dw = inv * gain * dyn - w * cube
+            dy_ref[rows] = (dw * act).astype(BF16)
+            dz = dw * y * (s * (1.0 + z * (1.0 - s)))
+            dz_ref[rows] = dz.astype(BF16)
+            rd_ref[part] = to_row(jnp.sum(dz * z, axis=1, keepdims=True))
 
 
 def backward_kernel(heads, extra, moves, dy_ref, x_ref, c_ref, cb_ref, ubd_ref, st_ref, par_ref, pbc_ref, head_ref, *refs):
@@ -673,32 +687,6 @@
     )(x, w_in, cut_shard(w_out))
 
 
-def run_gate(grads, w_out, y, u_zx, par, mask):
-    rows, width = y.shape
-    deep = grads.shape[1]
-    step = 256
-    at = lambda i: (i, 0)
-    fixed = lambda i: (0, 0)
-    thin = pl.BlockSpec((step // T, 1, T), lambda i: (i, 0, 0))
-    return pl.pallas_call(
-        gate_kernel,
-        grid=(rows // step,),
-        in_specs=[
-            pl.BlockSpec((step, deep), at),
-            pl.BlockSpec((deep, width), fixed),
-            pl.BlockSpec((step, width), at),
-            pl.BlockSpec((step, width), at),
-            pl.BlockSpec((1, width), fixed),
-            thin,
-        ],
-        out_specs=[pl.BlockSpec((step, width), at), thin],
-        out_shape=[jax.ShapeDtypeStruct((rows, width), BF16), jax.ShapeDtypeStruct((rows // T, 1, T), F32)],
-        compiler_params=params("arbitrary"),
-        cost_estimate=pl.CostEstimate(flops=rows * deep * width * 2, bytes_accessed=rows * deep * 2 + rows * width * 6, transcendentals=rows * width),
-        name="gate_back",
-    )(grads, w_out, y, u_zx, par, mask)
-
-
 def run_home(me, order, sums, extra, deep, name, after=()):
     rows, quarter = sums[0].shape
     step = 512
@@ -730,28 +718,39 @@
     )(me, order, *values)
 
 
-def run_mid(all_width, y, u_zx, dyn, par, mask, ss, co, number):
+def run_gate(all_width, grads, w_out, y, u_zx, gain, mask, ss, number):
     rows, width = y.shape
+    deep = grads.shape[1]
     step = 256
-    at = lambda i: (i, 0)
+    many = rows // step
+    both = lambda i: (lax.rem(i, many), 0)
+    late = lambda i: (jnp.maximum(i - many, 0), 0)
     fixed = lambda i: (0, 0)
-    thin = pl.BlockSpec((step // T, 1, T), lambda i: (i, 0, 0))
-    whole = pl.BlockSpec((rows // T, 1, T), lambda i: (0, 0, 0))
-    wide = pl.BlockSpec((step, width), at)
+    wide, out = pl.BlockSpec((step, width), both), pl.BlockSpec((step, width), late)
     moves = (("spread", "head"), ("spread", "head"))
     others = lax.axis_size("head") - 1
     return pl.pallas_call(
-        functools.partial(mid_kernel, float(all_width), moves),
-        grid=(rows // step,),
-        in_specs=[wide, wide, wide, pl.BlockSpec((1, width), fixed), thin, whole, whole],
-        out_specs=[wide, wide, wide, pl.BlockSpec((8, width), fixed), thin],
+        functools.partial(gate_kernel, float(all_width), moves),
+        grid=(2 * many,),
+        in_specs=[
+            pl.BlockSpec((step, deep), lambda i: (jnp.minimum(i, many - 1), 0)),
+            pl.BlockSpec((deep, width), fixed),
+            wide,
+            wide,
+            pl.BlockSpec((1, width), fixed),
+            pl.BlockSpec((step // T, 1, T), lambda i: (lax.rem(i, many), 0, 0)),
+            pl.BlockSpec((rows // T, 1, T), lambda i: (0, 0, 0)),
+        ],
+        out_specs=[out, out, out, pl.BlockSpec((8, width), fixed), pl.BlockSpec((step // T, 1, T), lambda i: (jnp.maximum(i - many, 0), 0, 0))],
         out_shape=[jax.ShapeDtypeStruct((rows, width), BF16)] * 3
         + [jax.ShapeDtypeStruct((8, width), F32), jax.ShapeDtypeStruct((rows // T, 1, T), F32)],
-        scratch_shapes=[pltpu.VMEM((others, rows // T, 1, T), F32)] * 2 + move_scratch(moves, (ss, co)),
+        scratch_shapes=[pltpu.VMEM((many, step, width), BF16), pltpu.VMEM((rows // T, 1, T), F32)]
+        + [pltpu.VMEM((others, rows // T, 1, T), F32)] * 2
+        + move_scratch(moves, (ss, ss)),
         compiler_params=params("arbitrary", number=number),
-        cost_estimate=pl.CostEstimate(flops=rows * width * 30, bytes_accessed=rows * width * 12, transcendentals=rows * width),
-        name="gate_mid",
-    )(y, u_zx, dyn, par, mask, ss, co)
+        cost_estimate=pl.CostEstimate(flops=LIGHT, bytes_accessed=LIGHT, transcendentals=0),
+        name="gate",
+    )(grads, w_out, y, u_zx, gain, mask, ss)
 
 
 def run_backward(heads, slot, dy, u_zx, c, cb, u_bd, st, par, pbc, hp, before, moves, values, number, after=()):
@@ -1099,7 +1098,7 @@
     return across, side
 
 
-def entry_kernel(parts, order_ref, x_ref, g_ref, w_ref, fx_ref, fg_ref, fw_ref, row_sems, x_sems, g_sems, line_sems, side_sems, local_sems, land, ready, picks, w_held):
+def entry_kernel(parts, order_ref, x_ref, g_ref, zx_ref, rest_ref, fx_ref, fg_ref, fw_ref, row_sems, x_sems, g_sems, line_sems, side_sems, local_sems, land, ready, picks, w_held):
     size, block, quarter = x_ref.shape
     line = size // 2
     me, own = lax.axis_index("dp"), lax.axis_index("head")
@@ -1121,7 +1120,7 @@
         origin = jnp.clip(me - sign * 2 * (j - 1), 0, size - 1)
         peer = jnp.clip(me + sign * 2, 0, size - 1)
         here = fw_ref.at[origin, part]
-        return remote(w_ref.at[part] if j == 1 else here, here, line_sems, (way, part, j - 1), peer)
+        return remote(w_held.at[part] if j == 1 else here, here, line_sems, (way, part, j - 1), peer)
 
     def came(way, part, j):
         sign = 1 - 2 * way
@@ -1131,7 +1130,7 @@
     def side(way, part, j):
         sign = 1 - 2 * way
         here = fw_ref.at[jnp.clip(me - sign * 2 * j, 0, size - 1), part]
-        return remote(w_ref.at[part] if j == 0 else here, here, side_sems, (way, part, j), me ^ 1)
+        return remote(w_held.at[part] if j == 0 else here, here, side_sems, (way, part, j), me ^ 1)
 
     def goes_on(way):
         return spot < line - 1 if way == 0 else spot > 0
@@ -1140,7 +1139,9 @@
         return spot >= j if way == 0 else spot < line - j
 
     into = [pltpu.make_async_copy(sources[i].at[me], land.at[i, me], local_sems.at[i]) for i in range(2)]
-    into.append(pltpu.make_async_copy(w_ref, w_held, local_sems.at[2]))
+    edge = zx_ref.shape[2]
+    into.append(pltpu.make_async_copy(zx_ref, w_held.at[:, :, pl.ds(0, edge)], local_sems.at[2]))
+    into.append(pltpu.make_async_copy(rest_ref, w_held.at[:, :, pl.ds(edge, rest_ref.shape[2])], local_sems.at[6]))
     held = [pltpu.make_async_copy(ready.at[i], fulls[i].at[:, :, mine], local_sems.at[3 + i]) for i in range(2)]
     held.append(pltpu.make_async_copy(w_held, fw_ref.at[me], local_sems.at[5]))
     for copy in into:
@@ -1149,16 +1150,16 @@
     order = turn_order(size)
     for k in order:
         rows(0, k).start()
+    for copy in into:
+        copy.wait()
     for part in range(parts):
         side(0, part, 0).start()
-    for copy in into:
-        copy.wait()
     held[2].start()
     total = size * block
     lane = lax.broadcasted_iota(jnp.int32, (T, T), 1).astype(F32)
 
     def pick(i, carry):
-        wanted = to_col(order_ref[i])
+        wanted = to_col(order_ref[i].astype(F32))
         at = pl.ds(pl.multiple_of(i * T, T), T)
         for j in range(total // T):
             picks[at, j * T : j * T + T] = (wanted == lane + float(T * j)).astype(F32).astype(BF16)
@@ -1258,8 +1259,9 @@
     return jax.ShapeDtypeStruct((size, PARTS, w.shape[0] // PARTS, w.shape[1]), BF16)
 
 
-def run_entry(order, tokens, cotangent, w_in, number):
+def run_entry(order, tokens, cotangent, w_zx, w_rest, number):
     size = lax.axis_size("dp")
+    shard, wide = w_zx.shape[0], w_zx.shape[1] + w_rest.shape[1]
     rows, quarter = tokens.shape
     block = rows // size
     line = size // 2
@@ -1268,25 +1270,25 @@
     full = jax.ShapeDtypeStruct((size, block, quarter * 4), BF16)
     came_x, came_g, came_w = pl.pallas_call(
         functools.partial(entry_kernel, PARTS),
-        in_specs=[pl.BlockSpec(memory_space=pltpu.VMEM)] + [anywhere] * 3,
+        in_specs=[pl.BlockSpec(memory_space=pltpu.VMEM)] + [anywhere] * 4,
         out_specs=[anywhere] * 3,
-        out_shape=[full, full, full_shape(size, w_in)],
+        out_shape=[full, full, jax.ShapeDtypeStruct((size, PARTS, shard // PARTS, wide), BF16)],
         scratch_shapes=[
             sems((2, 2, size)),
             sems((2, 3, size)),
             sems((2, 3, size)),
             sems((2, 2, PARTS, line)),
             sems((2, 2, PARTS, line)),
-            sems((6,)),
+            sems((7,)),
             pltpu.VMEM((2, size, block, quarter), BF16),
             pltpu.VMEM((2, size, block, quarter), BF16),
             pltpu.VMEM((rows, rows), BF16),
-            pltpu.VMEM((PARTS, w_in.shape[0] // PARTS, w_in.shape[1]), BF16),
+            pltpu.VMEM((PARTS, shard // PARTS, wide), BF16),
         ],
         compiler_params=pltpu.CompilerParams(collective_id=number, has_side_effects=True, vmem_limit_bytes=LIMIT),
         name="entry",
-    )(order, tokens.reshape(size, block, quarter), cotangent.reshape(size, block, quarter), cut_shard(w_in))
-    return came_x.reshape(rows, quarter * 4), came_g.reshape(rows, quarter * 4), came_w.reshape(size * w_in.shape[0], w_in.shape[1])
+    )(order, tokens.reshape(size, block, quarter), cotangent.reshape(size, block, quarter), cut_shard(w_zx), cut_shard(w_rest))
+    return came_x.reshape(rows, quarter * 4), came_g.reshape(rows, quarter * 4), came_w.reshape(size * shard, wide)
 
 
 def mm(a, b, contract, kind):
@@ -1303,13 +1305,11 @@
     all_width = width * lax.axis_size("head")
     deep = quarter * lax.axis_size("head")
     own_w = w_zx.shape[0]
-    arrange = order.astype(F32).reshape(rows // T, 1, T)
-
-    packed = jnp.concatenate(
-        [w_zx.reshape(own_w, 2 * width), w_bc, w_dt, norm_gain[:, None], jnp.zeros((own_w, 127 - heads), BF16)], axis=1
-    )
+    arrange = order.reshape(rows // T, 1, T)
+
+    rest = jnp.concatenate([w_bc, w_dt, norm_gain[:, None], jnp.zeros((own_w, 127 - heads), BF16)], axis=1)
     blocks = lambda value: value.reshape(size, rows // size, quarter)
-    full_x, full_g, w_in = run_entry(arrange, tokens, cotangent, packed, 1)
+    full_x, full_g, w_in = run_entry(arrange, tokens, cotangent, w_zx.reshape(own_w, 2 * width), rest, 1)
     normed, inv_one, u_zx, u_bd, gain, w_o = run_project(heads, full_x, w_in, w_out, 2)
 
     gated = gate_gain.reshape(1, width)
@@ -1319,8 +1319,7 @@
 
     y, ss, c, cb, st, w_o = run_forward(heads, u_zx, u_bd, conv_x, conv_bc, hp, w_out, w_o, 3)
     w_o = w_o.reshape(deep, width)
-    dyn, co = run_gate(full_g, w_o, y, u_zx, gated, mask)
-    yg, dz, dy, gg, rd_z = run_mid(all_width, y, u_zx, dyn, gated, mask, ss, co, 4)
+    yg, dz, dy, gg, rd_z = run_gate(all_width, full_g, w_o, y, u_zx, gated, mask, ss, 4)
 
     def total(kept, came, shift):
         own = lax.dynamic_index_in_dim(kept, here >> shift, 0, keepdims=False)
@@ -1338,8 +1337,14 @@
     out_arrived = lax.ppermute(out_far, "head", [(i, i ^ 2) for i in range(lax.axis_size("head"))])
     grad_o, grad_z = run_grads([(full_g, yg), (normed, dz)], "gate_grads", after=[out_far])
     grad_o, grad_z = pairs(grad_o), fours(grad_z)
-    *back0, gx0, gb0, gh0, came_o, came_z = scan(0, *shared, (), [("half", "dp", 0), ("half", "dp", 1)], [grad_o, grad_z], 7)
-    sent_out = run_home(me, arrange, [out_own, out_arrived], None, deep, "home_out", [back0[0]])
+    def other_half(paired, bit):
+        send = lax.dynamic_index_in_dim(paired, 1 - ((here >> bit) & 1), 1, keepdims=False)
+        return send, lax.ppermute(send, "dp", [(i, i ^ (1 << bit)) for i in range(size)])
+
+    send_o, came_o = other_half(grad_o, 0)
+    send_z, came_z = other_half(grad_z, 1)
+    *back0, gx0, gb0, gh0 = scan(0, *shared, (), [], [], 0, [send_o, send_z])
+    sent_out = run_home(me, arrange, [out_own, out_arrived], None, deep, "home_out", [back0[0], came_o, came_z])
     got_out = lax.all_to_all(sent_out, "dp", split_axis=0, concat_axis=0, tiled=True)
     *back1, gx1, gb1, gh1 = scan(1, *shared, back0, [], [], 0, [sent_out])
     dux, dbd, rd_x = back1

time: 515 us -> 510 us (level)
  Pallas kernels: 450 us -> 439 us
    pallas_call x2, Pallas kernels: 57.7 us -> 48.6 us  [run_backward(): pl.pallas_call(functools.partial(backward_kernel, heads, len(before) + le...]
    pallas_call x2 -> x1, Pallas kernels: 28.2 us -> 26.4 us  [run_gate(): pl.pallas_call(functools.partial(gate_kernel, float(all_width), moves), g...]
  transfers between devices with their start and end apart: 3 -> 5, of which waited for: 1 -> 3; matrix products, arithmetic and copies ran while one was open for 4% -> 5% of each run, Pallas kernels for 23% -> 21%
where the time goes in v7:
time: 510 us; the launch traced here: 501 us
  Pallas kernels  439 us (86%)
  local copies, waits for them, and re-layouts  22.5 us (4%)
  other arithmetic  21.4 us (4%)
  starting transfers between devices  12.5 us (2%)
    pallas_call x1, Pallas kernels, run_entry(): pl.pallas_call(functools.partial(entry_kernel, PARTS), in_specs=[pl.Block...  137 us
    pallas_call x2, Pallas kernels, run_backward(): pl.pallas_call(functools.partial(backward_kernel, heads, len(before) + le...  48.6 us
    pallas_call x2, Pallas kernels, run_pieces(): pl.pallas_call(functools.partial(pieces_kernel, len(values), many, tuple(...  46.2 us
    pallas_call x1, Pallas kernels, run_last(): pl.pallas_call(functools.partial(last_kernel, tuple(moves)), in_specs=[an...  46 us
    pallas_call x2, Pallas kernels, run_grads(): pl.pallas_call(functools.partial(grads_kernel, count, parts, len(after),...  41.7 us
    pallas_call x1, Pallas kernels, run_forward(): pl.pallas_call(functools.partial(forward_kernel, heads, slots * chunks),...  35.4 us
    pallas_call x1, Pallas kernels, run_gate(): pl.pallas_call(functools.partial(gate_kernel, float(all_width), moves), g...  26.4 us
    pallas_call x1, Pallas kernels, run_project(): pl.pallas_call(functools.partial(project_kernel, heads, rows // step), gr...  22.8 us
  transfers between devices with their start and end apart: 5, of which 3 were waited for; matrix products, arithmetic and copies ran while one was open for 5% of the time, Pallas kernels for 21%

profile of v7, /device:TPU:0, one launch (start us, length us, event | category | flops | bytes accessed | tf_op | source)
XLA Modules:
  0.0 500.9 jit_solution(11570321487026885176)
XLA Ops:
  0.7 2.8 reshape_reshape.6.zx_ref
  10.9 137.3 %entry.1 = (bf16[8,256,1536]{2,1,0:T(8,128)(2,1)}, bf16[8,256,1536]{2,1,0:T(8,128)(2,1)}, bf16[8,4,48,1920]{3,2,1,0:T(8,128)(2,1)}) custom-call(s32[16,1,128]{2,1,0:T(1,128)} %bitcast.88, bf16[8,256,384]{2,1,0:T(8,128)(2,1)} %bitcast.71, bf16[8,256,384]{2,1,0:T(8,128)(2,1)} %bitcast.72, bf16[4,48,1536]{2,1,0:T(8,128)(2,1)} %reshape_reshape.6.zx_ref, ...), custom_call_target="tpu_custom_call" | custom-call | tf_op jit(solution)/shard_map/entry/pallas_call | solution.py:1271
  148.2 22.8 %project.1 = (bf16[2048,1536]{1,0:T(8,128)(2,1)}, f32[16,1,128]{2,1,0:T(1,128)}, bf16[2048,1536]{1,0:T(8,128)(2,1)}, f32[2048,384]{1,0:T(8,128)}, f32[8,1536]{1,0:T(8,128)}, /*index=5*/bf16[8,4,48,768]{3,2,1,0:T(8,128)(2,1)}) custom-call(bf16[2048,1536]{1,0:T(8,128)(2,1)} %bitcast.70, bf16[1536,1920]{1,0:T(8,128)(2,1)} %bitcast.63, bf16[4,48,768]{2,1,0:T(8,128)(2,1)} %bitcast.82), custom_call_target="tpu_custom_call" | custom-call | flops 1000 | bytes 1000 | tf_op jit(solution)/shard_map/project/pallas_call | solution.py:663
  171.0 35.4 %scan_forward.1 = (bf16[2048,768]{1,0:T(8,128)(2,1)}, f32[16,1,128]{2,1,0:T(1,128)}, bf16[2048,768]{1,0:T(8,128)(2,1)}, f32[2048,256]{1,0:T(8,128)}, bf16[16,128...) custom-call(bf16[2048,1536]{1,0:T(8,128)(2,1)} %get-tuple-element.65.x_ref.z_ref, ...), custom_call_target="tpu_custom_call", output_to_operand_aliasing={{5}: (7, {})} | custom-call | flops 3774873600 | bytes 12582912 | tf_op jit(solution)/shard_map/scan_forward/pallas_call | solution.py:611
  206.4 26.4 %gate.1 = (bf16[2048,768]{1,0:T(8,128)(2,1)}, bf16[2048,768]{1,0:T(8,128)(2,1)}, bf16[2048,768]{1,0:T(8,128)(2,1)}, f32[8,768]{1,0:T(8,128)}, f32[16,1,128]{2,1,0:T(1,128)}) custom-call(bf16[2048,1536]{1,0:T(8,128)(2,1)} %bitcast.61, bf16[1536,768]{1,0:T(8,128)(2,1)} %bitcast.65, bf16[2048,768]{1,0:T(8,128)(2,1)} %get-tuple-element.69.y_ref, ...), custom_call_target="tpu_custom_call" | custom-call | flops 1000 | bytes 1000 | tf_op jit(solution)/shard_map/gate/pallas_call | solution.py:732
  232.8 12.5 %branch_pieces.1 = (bf16[2048,384]{1,0:T(8,128)(2,1)}, bf16[2048,384]{1,0:T(8,128)(2,1)}) custom-call(bf16[2048,768]{1,0:T(8,128)(2,1)} %get-tuple-element.71.refs_0_.refs_2_, bf16[1536,768]{1,0:T(8,128)(2,1)} %bitcast.66), custom_call_target="tpu_custom_call" | custom-call | flops 1000 | bytes 1000 | tf_op jit(solution)/shard_map/branch_pieces/pallas_call | solution.py:884
  247.0 16.6 %gate_grads.1 = (bf16[1536,768]{1,0:T(8,128)(2,1)}, bf16[1536,768]{1,0:T(8,128)(2,1)}) custom-call(bf16[2048,1536]{1,0:T(8,128)(2,1)} %bitcast.62, bf16[2048,1536]{1,0:T(8,128)(2,1)} %get-tuple-element.78.refs_1_.refs_0_, bf16[2048,768]{1,0:T(8,128)(2,1)} %get-tuple-element.71.refs_0_.refs_2_, bf16[2048,768]{1,0:T(8,128)(2,1)} %get-tuple-element.79.refs_3_.refs_0_, ...), custom_call_target="tpu_custom_call" | custom-call | flops 1000 | bytes 1000 | tf_op jit(solution)/shard_map/gate_grads/pallas_call | solution.py:965
  266.9 1.8 collective-permute-start.1
  268.7 24.3 %scan_backward.2 = (bf16[2048,768]{1,0:T(8,128)(2,1)}, bf16[2048,384]{1,0:T(8,128)(2,1)}, f32[16,1,128]{2,1,0:T(1,128)}, f32[8,768]{1,0:T(8,128)}, f32[8,256]{1,0:T(8,128)}, /*index=5*/f32[8,128]{1,0:T(8,128)}) custom-call(bf16[2048,768]{1,0:T(8,128)(2,1)} %get-tuple-element.74.dy_ref, bf16[2048,1536]{1,0:T(8,128)(2,1)} %get-tuple-element.65.x_ref.z_ref, ...), custom_call_target="tpu_custom_call" | custom-call | flops 1000 | bytes 1000 | tf_op jit(solution)/shard_map/scan_backward/pallas_call | solution.py:764
  296.0 8.7 %home_out.1.refs_3_ = bf16[2048,384]{1,0:T(8,128)(2,1)} custom-call(s32[1]{0:T(128)} %bitcast.me_ref, s32[16,1,128]{2,1,0:T(1,128)} %bitcast.89, bf16[2048,384]{1,0:T(8,128)(2,1)} %get-tuple-element.72.a_ref, bf16[2048,384]{1,0:T(8,128)(2,1)} %collective-permute-done.b_ref, bf16[2048,768]{1,0:T(8,128)(2,1)} %get-tuple-element.82.refs_0_, ...), custom_call_target="tpu_custom_call" | custom-call | flops 3221225472 | bytes 7864320 | tf_op jit(solution)/shard_map/home_out/pallas_call | solution.py:705
  304.7 4.1 all-to-all-start
  311.4 24.3 %scan_backward.3 = (bf16[2048,768]{1,0:T(8,128)(2,1)}, bf16[2048,384]{1,0:T(8,128)(2,1)}, f32[16,1,128]{2,1,0:T(1,128)}, f32[8,768]{1,0:T(8,128)}, f32[8,256]{1,0:T(8,128)}, /*index=5*/f32[8,128]{1,0:T(8,128)}) custom-call(bf16[2048,768]{1,0:T(8,128)(2,1)} %get-tuple-element.74.dy_ref, ...), custom_call_target="tpu_custom_call", output_to_operand_aliasing={{0}: (9, {}), {1}: (10, {}), {2}: (11, {})} | custom-call | flops 1000 | bytes 1000 | tf_op jit(solution)/shard_map/scan_backward/pallas_call | solution.py:764
  335.8 25.1 %scan_grads.1 = (bf16[1536,768]{1,0:T(8,128)(2,1)}, bf16[1536,384]{1,0:T(8,128)(2,1)}, bf16[2,192,768]{2,1,0:T(8,128)(2,1)}, bf16[2,192,768]{2,1,0:T(8,128)(2,1)}) custom-call(bf16[2048,1536]{1,0:T(8,128)(2,1)} %get-tuple-element.78.refs_1_.refs_0_, bf16[2048,1536]{1,0:T(8,128)(2,1)} %get-tuple-element.78.refs_1_.refs_0_, ...), custom_call_target="tpu_custom_call" | custom-call | flops 1000 | bytes 1000 | tf_op jit(solution)/shard_map/scan_grads/pallas_call | solution.py:965
  363.4 33.7 %input_pieces.1 = (bf16[2048,384]{1,0:T(8,128)(2,1)}, bf16[2048,384]{1,0:T(8,128)(2,1)}, bf16[1,192,768]{2,1,0:T(8,128)(2,1)}, bf16[1,192,768]{2,1,0:T(8,128)(2,...) custom-call(bf16[2048,768]{1,0:T(8,128)(2,1)} %get-tuple-element.79.refs_3_.refs_0_, ...), custom_call_target="tpu_custom_call" | custom-call | flops 1000 | bytes 1000 | tf_op jit(solution)/shard_map/input_pieces/pallas_call | solution.py:884
  398.6 46.0 %last_exchange.1 = (bf16[2048,384]{1,0:T(8,128)(2,1)}, f32[7,8,768]{2,1,0:T(8,128)}, f32[192,384]{1,0:T(8,128)}, f32[192,768]{1,0:T(8,128)}) custom-call(bf16[2048,384]{1,0:T(8,128)(2,1)} %get-tuple-element.95.refs_0_, f32[8,768]{1,0:T(8,128)} %pad_maximum_fusion.2.refs_1_, bf16[4,2,192,384]{3,2,1,0:T(8,128)(2,1)} %bitcast.81, ...), custom_call_target="tpu_custom_call" | custom-call | tf_op jit(solution)/shard_map/last_exchange/pallas_call | solution.py:1045
  446.2 10.4 %home_back.1 = bf16[2048,384]{1,0:T(8,128)(2,1)} custom-call(s32[1]{0:T(128)} %bitcast.me_ref, s32[16,1,128]{2,1,0:T(1,128)} %bitcast.90, bf16[2048,384]{1,0:T(8,128)(2,1)} %get-tuple-element.94.a_ref, bf16[2048,384]{1,0:T(8,128)(2,1)} %get-tuple-element.104.b_ref, bf16[2048,1536]{1,0:T(8,128)(2,1)} %get-tuple-element.78.refs_1_.refs_0_, ...), custom_call_target="tpu_custom_call" | custom-call | flops 3221225472 | bytes 7864320 | tf_op jit(solution)/shard_map/home_back/pallas_call | solution.py:705
  456.6 4.2 all-to-all-start.1
  463.7 1.9 copy.41
  467.7 15.6 %exchange.1 = f32[3,192,384]{2,1,0:T(8,128)} custom-call(f32[192,384]{1,0:T(8,128)} %pad_maximum_fusion.1.refs_0_), custom_call_target="tpu_custom_call" | custom-call | tf_op jit(solution)/shard_map/exchange/pallas_call | solution.py:188
  483.3 2.0 reduce_sum.76
  490.6 1.9 add_bitcast_fusion
  492.5 3.0 add_convert_fusion
  495.5 2.0 all-to-all-done.1
  497.5 3.0 fusion
  (109 shorter events, 33.8 us)
Async XLA Ops:
  245.3 49.8 %collective-permute-start = (bf16[2048,384]{1,0:T(8,128)(2,1)}, bf16[2048,384]{1,0:T(8,128)(2,1)}, u32[]{:S(2)}, u32[]{:S(2)}) collective-permute-start(bf16[2048,384]{1,0:T(8,128)(2,1)} %get-tuple-element.73.refs_4_), channel_id=1, source_target_pairs={{0,2},{1,3},{2,0},{3,1},{4,6},{5,7},{6,4},{7,5},{8,10},{9,11},{10,... | collective-permute-start | bytes 4718600 | tf_op jit(solution)/shard_map/ppermute | solution.py:1337
  263.6 2.1 copy-start.2
  265.1 3.5 copy-start.4
  265.2 28.2 %collective-permute-start.2 = (bf16[2,2,192,768]{3,2,1,0:T(8,128)(2,1)S(1)}, bf16[2,2,192,768]{3,2,1,0:T(8,128)(2,1)}, u32[]{:S(2)}, u32[]{:S(2)}) collective-permute-start(bf16[2,2,192,768]{3,2,1,0:T(8,128)(2,1)S(1)} %dynamic-slice_bitcast_fusion.refs_1_), channel_id=1, source_target_pairs={{0,8},{4,12},{8,0},{12,4},{16,24},{20,28},{24,16},{28,20},{1,9},{5... | collective-permute-start | bytes 3538952 | tf_op jit(solution)/shard_map/ppermute | solution.py:1342
  266.9 28.1 %collective-permute-start.1 = (bf16[4,192,768]{2,1,0:T(8,128)(2,1)}, bf16[4,192,768]{2,1,0:T(8,128)(2,1)S(1)}, u32[]{:S(2)}, u32[]{:S(2)}) collective-permute-start(bf16[4,192,768]{2,1,0:T(8,128)(2,1)} %dynamic-slice_bitcast_fusion.1.refs_0_), channel_id=1, source_target_pairs={{0,4},{4,0},{8,12},{12,8},{16,20},{20,16},{24,28},{28,24},{1,5},{5... | collective-permute-start | bytes 3538952 | tf_op jit(solution)/shard_map/ppermute | solution.py:1342
  304.7 4.2 copy-start.16
  304.7 5.0 %copy-start.3 = (bf16[192,2,768]{2,1,0:T(2,128)(2,1)S(1)}, bf16[192,2,768]{2,1,0:T(2,128)(2,1)}, u32[]{:S(2)}) copy-start(bf16[192,2,768]{2,1,0:T(2,128)(2,1)} %param.18) | copy-start | bytes 1769476
  304.7 57.5 %all-to-all-start = ((bf16[8,256,384]{2,1,0:T(8,128)(2,1)}), bf16[8,256,384]{2,1,0:T(8,128)(2,1)S(1)}, u32[]{:S(2)}, u32[]{:S(2)}) async-start(bf16[8,256,384]{2,1,0:T(8,128)(2,1)} %bitcast.73), calls=%async_computation | async-start | bytes 3145728 | tf_op jit(solution)/shard_map/all_to_all | solution.py:1348
  335.7 25.2 %copy-start.20 = (f32[8,256]{1,0:T(8,128)S(1)}, f32[8,256]{1,0:T(8,128)}, u32[]{:S(2)}) copy-start(f32[8,256]{1,0:T(8,128)} %get-tuple-element.92) | copy-start | bytes 24580
  335.7 25.2 %copy-start.21 = (f32[8,256]{1,0:T(8,128)S(1)}, f32[8,256]{1,0:T(8,128)}, u32[]{:S(2)}) copy-start(f32[8,256]{1,0:T(8,128)} %get-tuple-element.93) | copy-start | bytes 24580
  335.7 25.8 %copy-start.15 = (f32[16,1,128]{2,1,0:T(1,128)S(1)}, f32[16,1,128]{2,1,0:T(1,128)}, u32[]{:S(2)}) copy-start(f32[16,1,128]{2,1,0:T(1,128)} %get-tuple-element.91.refs_4_) | copy-start | bytes 24580
  335.7 25.8 %copy-start.19 = (f32[16,1,128]{2,1,0:T(1,128)S(1)}, f32[16,1,128]{2,1,0:T(1,128)}, u32[]{:S(2)}) copy-start(f32[16,1,128]{2,1,0:T(1,128)} %get-tuple-element.90.refs_3_) | copy-start | bytes 24580
  335.7 26.4 %copy-start.22 = (f32[8,128]{1,0:T(8,128)S(1)}, f32[8,128]{1,0:T(8,128)}, u32[]{:S(2)}) copy-start(f32[8,128]{1,0:T(8,128)} %get-tuple-element.100) | copy-start | bytes 12292
  335.7 26.4 %copy-start.23 = (f32[8,128]{1,0:T(8,128)S(1)}, f32[8,128]{1,0:T(8,128)}, u32[]{:S(2)}) copy-start(f32[8,128]{1,0:T(8,128)} %get-tuple-element.101) | copy-start | bytes 12292
  335.7 26.4 %copy-start.17 = (f32[8,768]{1,0:T(8,128)S(1)}, f32[8,768]{1,0:T(8,128)}, u32[]{:S(2)}) copy-start(f32[8,768]{1,0:T(8,128)} %get-tuple-element.96) | copy-start | bytes 73732
  335.8 26.4 %copy-start.18 = (f32[8,768]{1,0:T(8,128)S(1)}, f32[8,768]{1,0:T(8,128)}, u32[]{:S(2)}) copy-start(f32[8,768]{1,0:T(8,128)} %get-tuple-element.97) | copy-start | bytes 73732
  363.4 34.4 %copy-start.13 = (f32[8,256]{1,0:T(8,128)S(1)}, f32[8,256]{1,0:T(8,128)}, u32[]{:S(2)}) copy-start(f32[8,256]{1,0:T(8,128)} %add.96.refs_8_) | copy-start | bytes 24580
  445.5 16.3 %copy-start.14 = (f32[8,768]{1,0:T(8,128)}, f32[8,768]{1,0:T(8,128)S(1)}, u32[]{:S(2)}) copy-start(f32[8,768]{1,0:T(8,128)S(1)} %fusion.9) | copy-start | bytes 73732
  456.6 4.2 copy-start.5
  456.6 40.9 %all-to-all-start.1 = ((bf16[8,256,384]{2,1,0:T(8,128)(2,1)}), bf16[8,256,384]{2,1,0:T(8,128)(2,1)S(1)}, u32[]{:S(2)}, u32[]{:S(2)}) async-start(bf16[8,256,384]{2,1,0:T(8,128)(2,1)} %bitcast.79), calls=%async_computation.1 | async-start | bytes 3145728 | tf_op jit(solution)/shard_map/all_to_all | solution.py:1373
  463.7 2.0 copy-start.6
  463.7 2.0 copy-start.7
  483.3 6.8 %copy-start.24 = (bf16[192]{0:T(256)(128)(2,1)S(1)}, bf16[192]{0:T(256)(128)(2,1)}, u32[]{:S(2)}) copy-start(bf16[192]{0:T(256)(128)(2,1)} %param.17) | copy-start | bytes 1156
  485.2 7.3 %copy-start.1 = (bf16[8,256,384]{2,1,0:T(8,128)(2,1)S(1)}, bf16[8,256,384]{2,1,0:T(8,128)(2,1)}, u32[]{:S(2)}) copy-start(bf16[8,256,384]{2,1,0:T(8,128)(2,1)} %copy-done) | copy-start | bytes 4718596
  (6 other events, 6.9 us)

commit v8 on v7

--- a/solution.py
+++ b/solution.py
@@ -217,10 +217,12 @@
 
 
 def step_terms(ubd, head_ref, heads):
+    fill = jnp.zeros((1, 128 - heads), F32)
+    wide_row = lambda i: jnp.concatenate([head_ref[i : i + 1], fill], axis=1)
     row, col = iotas(T, T)
-    raw = jnp.where(col < heads, ubd[:, 2 * N :] + head_ref[0:1], 0.0)
+    raw = jnp.where(col < heads, ubd[:, 2 * N :] + wide_row(0), 0.0)
     steps = jnp.where(col < heads, softplus(raw), 0.0)
-    rates = -jnp.exp(head_ref[1:2])
+    rates = -jnp.exp(wide_row(1))
     tril = (row >= col).astype(F32)
     logs = dot_exact(tril, steps * rates)
     return raw, steps, rates, logs
@@ -396,7 +398,7 @@
     parts = size // T
     others = got_ss.shape[0]
     peers, copies = make_moves(moves, (ss_ref, co_held), (got_ss, got_co), sems, local_sems)
-    gain = gain_ref[0:1]
+    gain = gain_ref[...][None]
 
     @pl.when(step == 0)
     def _():
@@ -617,7 +619,7 @@
             pl.BlockSpec((T, 3 * N), at),
             pl.BlockSpec((5, width), fixed),
             pl.BlockSpec((5, 2 * N), fixed),
-            pl.BlockSpec((8, 128), fixed),
+            pl.BlockSpec((3, heads), fixed),
             anywhere,
             anywhere,
         ],
@@ -737,7 +739,7 @@
             pl.BlockSpec((deep, width), fixed),
             wide,
             wide,
-            pl.BlockSpec((1, width), fixed),
+            pl.BlockSpec((width,), lambda i: (0,)),
             pl.BlockSpec((step // T, 1, T), lambda i: (lax.rem(i, many), 0, 0)),
             pl.BlockSpec((rows // T, 1, T), lambda i: (0, 0, 0)),
         ],
@@ -773,7 +775,7 @@
             pl.BlockSpec((1, N, width), at3),
             pl.BlockSpec((5, width), fixed),
             pl.BlockSpec((5, 2 * N), fixed),
-            pl.BlockSpec((8, 128), fixed),
+            pl.BlockSpec((3, heads), fixed),
         ]
         + [anywhere] * (len(moves) + len(before) + len(after)),
         out_specs=[
@@ -1312,8 +1314,8 @@
     full_x, full_g, w_in = run_entry(arrange, tokens, cotangent, w_zx.reshape(own_w, 2 * width), rest, 1)
     normed, inv_one, u_zx, u_bd, gain, w_o = run_project(heads, full_x, w_in, w_out, 2)
 
-    gated = gate_gain.reshape(1, width)
-    hp = jnp.pad(head_params, ((0, 5), (0, 128 - heads)))
+    gated = gate_gain
+    hp = head_params
     positions = lax.broadcasted_iota(jnp.int32, (lengths.shape[0], LEN), 1)
     mask = (positions < lengths[:, None]).astype(F32).reshape(rows // T, 1, T)
 

time: 510 us -> 508 us (level)
  no operation moved by 1% of the time
where the time goes in v8:
time: 508 us; the launch traced here: 498 us
  Pallas kernels  439 us (86%)
  other arithmetic  21.4 us (4%)
  local copies, waits for them, and re-layouts  19.9 us (4%)
  starting transfers between devices  12.5 us (2%)
    pallas_call x1, Pallas kernels, run_entry(): pl.pallas_call(functools.partial(entry_kernel, PARTS), in_specs=[pl.Block...  137 us
    pallas_call x2, Pallas kernels, run_backward(): pl.pallas_call(functools.partial(backward_kernel, heads, len(before) + le...  48.6 us
    pallas_call x1, Pallas kernels, run_last(): pl.pallas_call(functools.partial(last_kernel, tuple(moves)), in_specs=[an...  46.1 us
    pallas_call x2, Pallas kernels, run_pieces(): pl.pallas_call(functools.partial(pieces_kernel, len(values), many, tuple(...  46.1 us
    pallas_call x2, Pallas kernels, run_grads(): pl.pallas_call(functools.partial(grads_kernel, count, parts, len(after),...  41.7 us
    pallas_call x1, Pallas kernels, run_forward(): pl.pallas_call(functools.partial(forward_kernel, heads, slots * chunks),...  35.4 us
    pallas_call x1, Pallas kernels, run_gate(): pl.pallas_call(functools.partial(gate_kernel, float(all_width), moves), g...  26.4 us
    pallas_call x1, Pallas kernels, run_project(): pl.pallas_call(functools.partial(project_kernel, heads, rows // step), gr...  22.8 us
  transfers between devices with their start and end apart: 5, of which 3 were waited for; matrix products, arithmetic and copies ran while one was open for 5% of the time, Pallas kernels for 21%

profile of v8, /device:TPU:0, one launch (start us, length us, event | category | flops | bytes accessed | tf_op | source)
XLA Modules:
  0.0 498.2 jit_solution(10615024028980437621)
XLA Ops:
  0.7 2.8 reshape_reshape.6.zx_ref
  8.4 137.3 %entry.1 = (bf16[8,256,1536]{2,1,0:T(8,128)(2,1)}, bf16[8,256,1536]{2,1,0:T(8,128)(2,1)}, bf16[8,4,48,1920]{3,2,1,0:T(8,128)(2,1)}) custom-call(s32[16,1,128]{2,1,0:T(1,128)} %bitcast.88, bf16[8,256,384]{2,1,0:T(8,128)(2,1)} %bitcast.72, bf16[8,256,384]{2,1,0:T(8,128)(2,1)} %bitcast.73, bf16[4,48,1536]{2,1,0:T(8,128)(2,1)} %reshape_reshape.6.zx_ref, ...), custom_call_target="tpu_custom_call" | custom-call | tf_op jit(solution)/shard_map/entry/pallas_call | solution.py:1273
  145.7 22.8 %project.1 = (bf16[2048,1536]{1,0:T(8,128)(2,1)}, f32[16,1,128]{2,1,0:T(1,128)}, bf16[2048,1536]{1,0:T(8,128)(2,1)}, f32[2048,384]{1,0:T(8,128)}, f32[8,1536]{1,0:T(8,128)}, /*index=5*/bf16[8,4,48,768]{3,2,1,0:T(8,128)(2,1)}) custom-call(bf16[2048,1536]{1,0:T(8,128)(2,1)} %bitcast.70, bf16[1536,1920]{1,0:T(8,128)(2,1)} %bitcast.63, bf16[4,48,768]{2,1,0:T(8,128)(2,1)} %bitcast.82), custom_call_target="tpu_custom_call" | custom-call | flops 1000 | bytes 1000 | tf_op jit(solution)/shard_map/project/pallas_call | solution.py:665
  168.4 35.4 %scan_forward.1 = (bf16[2048,768]{1,0:T(8,128)(2,1)}, f32[16,1,128]{2,1,0:T(1,128)}, bf16[2048,768]{1,0:T(8,128)(2,1)}, f32[2048,256]{1,0:T(8,128)}, bf16[16,128...) custom-call(bf16[2048,1536]{1,0:T(8,128)(2,1)} %get-tuple-element.65.x_ref.z_ref, ...), custom_call_target="tpu_custom_call", output_to_operand_aliasing={{5}: (7, {})} | custom-call | flops 3774873600 | bytes 12582912 | tf_op jit(solution)/shard_map/scan_forward/pallas_call | solution.py:613
  203.8 26.4 %gate.1 = (bf16[2048,768]{1,0:T(8,128)(2,1)}, bf16[2048,768]{1,0:T(8,128)(2,1)}, bf16[2048,768]{1,0:T(8,128)(2,1)}, f32[8,768]{1,0:T(8,128)}, f32[16,1,128]{2,1,0:T(1,128)}) custom-call(bf16[2048,1536]{1,0:T(8,128)(2,1)} %bitcast.61, bf16[1536,768]{1,0:T(8,128)(2,1)} %bitcast.65, bf16[2048,768]{1,0:T(8,128)(2,1)} %get-tuple-element.69.y_ref, ...), custom_call_target="tpu_custom_call" | custom-call | flops 1000 | bytes 1000 | tf_op jit(solution)/shard_map/gate/pallas_call | solution.py:734
  230.2 12.5 %branch_pieces.1 = (bf16[2048,384]{1,0:T(8,128)(2,1)}, bf16[2048,384]{1,0:T(8,128)(2,1)}) custom-call(bf16[2048,768]{1,0:T(8,128)(2,1)} %get-tuple-element.71.refs_0_.refs_2_, bf16[1536,768]{1,0:T(8,128)(2,1)} %bitcast.66), custom_call_target="tpu_custom_call" | custom-call | flops 1000 | bytes 1000 | tf_op jit(solution)/shard_map/branch_pieces/pallas_call | solution.py:886
  242.7 1.8 collective-permute-start
  244.5 16.6 %gate_grads.1 = (bf16[1536,768]{1,0:T(8,128)(2,1)}, bf16[1536,768]{1,0:T(8,128)(2,1)}) custom-call(bf16[2048,1536]{1,0:T(8,128)(2,1)} %bitcast.62, bf16[2048,1536]{1,0:T(8,128)(2,1)} %get-tuple-element.78.refs_1_.refs_0_, bf16[2048,768]{1,0:T(8,128)(2,1)} %get-tuple-element.71.refs_0_.refs_2_, bf16[2048,768]{1,0:T(8,128)(2,1)} %get-tuple-element.79.refs_3_.refs_0_, ...), custom_call_target="tpu_custom_call" | custom-call | flops 1000 | bytes 1000 | tf_op jit(solution)/shard_map/gate_grads/pallas_call | solution.py:967
  266.1 24.3 %scan_backward.2 = (bf16[2048,768]{1,0:T(8,128)(2,1)}, bf16[2048,384]{1,0:T(8,128)(2,1)}, f32[16,1,128]{2,1,0:T(1,128)}, f32[8,768]{1,0:T(8,128)}, f32[8,256]{1,0:T(8,128)}, /*index=5*/f32[8,128]{1,0:T(8,128)}) custom-call(bf16[2048,768]{1,0:T(8,128)(2,1)} %get-tuple-element.74.dy_ref, bf16[2048,1536]{1,0:T(8,128)(2,1)} %get-tuple-element.65.x_ref.z_ref, ...), custom_call_target="tpu_custom_call" | custom-call | flops 1000 | bytes 1000 | tf_op jit(solution)/shard_map/scan_backward/pallas_call | solution.py:766
  293.5 8.7 %home_out.1.refs_3_ = bf16[2048,384]{1,0:T(8,128)(2,1)} custom-call(s32[1]{0:T(128)} %bitcast.me_ref, s32[16,1,128]{2,1,0:T(1,128)} %bitcast.89, bf16[2048,384]{1,0:T(8,128)(2,1)} %get-tuple-element.72.a_ref, bf16[2048,384]{1,0:T(8,128)(2,1)} %collective-permute-done.b_ref, bf16[2048,768]{1,0:T(8,128)(2,1)} %get-tuple-element.82.refs_0_, ...), custom_call_target="tpu_custom_call" | custom-call | flops 3221225472 | bytes 7864320 | tf_op jit(solution)/shard_map/home_out/pallas_call | solution.py:707
  302.1 4.1 all-to-all-start
  308.8 24.3 %scan_backward.3 = (bf16[2048,768]{1,0:T(8,128)(2,1)}, bf16[2048,384]{1,0:T(8,128)(2,1)}, f32[16,1,128]{2,1,0:T(1,128)}, f32[8,768]{1,0:T(8,128)}, f32[8,256]{1,0:T(8,128)}, /*index=5*/f32[8,128]{1,0:T(8,128)}) custom-call(bf16[2048,768]{1,0:T(8,128)(2,1)} %get-tuple-element.74.dy_ref, ...), custom_call_target="tpu_custom_call", output_to_operand_aliasing={{0}: (9, {}), {1}: (10, {}), {2}: (11, {})} | custom-call | flops 1000 | bytes 1000 | tf_op jit(solution)/shard_map/scan_backward/pallas_call | solution.py:766
  333.2 25.0 %scan_grads.1 = (bf16[1536,768]{1,0:T(8,128)(2,1)}, bf16[1536,384]{1,0:T(8,128)(2,1)}, bf16[2,192,768]{2,1,0:T(8,128)(2,1)}, bf16[2,192,768]{2,1,0:T(8,128)(2,1)}) custom-call(bf16[2048,1536]{1,0:T(8,128)(2,1)} %get-tuple-element.78.refs_1_.refs_0_, bf16[2048,1536]{1,0:T(8,128)(2,1)} %get-tuple-element.78.refs_1_.refs_0_, ...), custom_call_target="tpu_custom_call" | custom-call | flops 1000 | bytes 1000 | tf_op jit(solution)/shard_map/scan_grads/pallas_call | solution.py:967
  360.7 33.6 %input_pieces.1 = (bf16[2048,384]{1,0:T(8,128)(2,1)}, bf16[2048,384]{1,0:T(8,128)(2,1)}, bf16[1,192,768]{2,1,0:T(8,128)(2,1)}, bf16[1,192,768]{2,1,0:T(8,128)(2,...) custom-call(bf16[2048,768]{1,0:T(8,128)(2,1)} %get-tuple-element.79.refs_3_.refs_0_, ...), custom_call_target="tpu_custom_call" | custom-call | flops 1000 | bytes 1000 | tf_op jit(solution)/shard_map/input_pieces/pallas_call | solution.py:886
  395.8 46.1 %last_exchange.1 = (bf16[2048,384]{1,0:T(8,128)(2,1)}, f32[7,8,768]{2,1,0:T(8,128)}, f32[192,384]{1,0:T(8,128)}, f32[192,768]{1,0:T(8,128)}) custom-call(bf16[2048,384]{1,0:T(8,128)(2,1)} %get-tuple-element.95.refs_0_, f32[8,768]{1,0:T(8,128)} %pad_maximum_fusion.2.refs_1_, bf16[4,2,192,384]{3,2,1,0:T(8,128)(2,1)} %bitcast.81, ...), custom_call_target="tpu_custom_call" | custom-call | tf_op jit(solution)/shard_map/last_exchange/pallas_call | solution.py:1047
  443.6 10.4 %home_back.1 = bf16[2048,384]{1,0:T(8,128)(2,1)} custom-call(s32[1]{0:T(128)} %bitcast.me_ref, s32[16,1,128]{2,1,0:T(1,128)} %bitcast.90, bf16[2048,384]{1,0:T(8,128)(2,1)} %get-tuple-element.94.a_ref, bf16[2048,384]{1,0:T(8,128)(2,1)} %get-tuple-element.104.b_ref, bf16[2048,1536]{1,0:T(8,128)(2,1)} %get-tuple-element.78.refs_1_.refs_0_, ...), custom_call_target="tpu_custom_call" | custom-call | flops 3221225472 | bytes 7864320 | tf_op jit(solution)/shard_map/home_back/pallas_call | solution.py:707
  454.0 4.2 all-to-all-start.1
  461.0 1.9 copy.41
  465.0 15.6 %exchange.1 = f32[3,192,384]{2,1,0:T(8,128)} custom-call(f32[192,384]{1,0:T(8,128)} %pad_maximum_fusion.1.refs_0_), custom_call_target="tpu_custom_call" | custom-call | tf_op jit(solution)/shard_map/exchange/pallas_call | solution.py:188
  480.6 2.0 reduce_sum.76
  487.9 1.9 add_bitcast_fusion
  489.9 3.0 add_convert_fusion
  492.8 2.0 all-to-all-done.1
  494.8 3.0 fusion
  (107 shorter events, 31.2 us)
Async XLA Ops:
  242.7 49.8 %collective-permute-start = (bf16[2048,384]{1,0:T(8,128)(2,1)}, bf16[2048,384]{1,0:T(8,128)(2,1)}, u32[]{:S(2)}, u32[]{:S(2)}) collective-permute-start(bf16[2048,384]{1,0:T(8,128)(2,1)} %get-tuple-element.73.refs_4_), channel_id=1, source_target_pairs={{0,2},{1,3},{2,0},{3,1},{4,6},{5,7},{6,4},{7,5},{8,10},{9,11},{10,... | collective-permute-start | bytes 4718600 | tf_op jit(solution)/shard_map/ppermute | solution.py:1339
  261.1 2.1 copy-start.2
  262.6 3.5 copy-start.4
  262.7 28.1 %collective-permute-start.2 = (bf16[2,2,192,768]{3,2,1,0:T(8,128)(2,1)S(1)}, bf16[2,2,192,768]{3,2,1,0:T(8,128)(2,1)}, u32[]{:S(2)}, u32[]{:S(2)}) collective-permute-start(bf16[2,2,192,768]{3,2,1,0:T(8,128)(2,1)S(1)} %dynamic-slice_bitcast_fusion.refs_1_), channel_id=1, source_target_pairs={{0,8},{4,12},{8,0},{12,4},{16,24},{20,28},{24,16},{28,20},{1,9},{5... | collective-permute-start | bytes 3538952 | tf_op jit(solution)/shard_map/ppermute | solution.py:1344
  264.4 28.1 %collective-permute-start.1 = (bf16[4,192,768]{2,1,0:T(8,128)(2,1)}, bf16[4,192,768]{2,1,0:T(8,128)(2,1)S(1)}, u32[]{:S(2)}, u32[]{:S(2)}) collective-permute-start(bf16[4,192,768]{2,1,0:T(8,128)(2,1)} %dynamic-slice_bitcast_fusion.1.refs_0_), channel_id=1, source_target_pairs={{0,4},{4,0},{8,12},{12,8},{16,20},{20,16},{24,28},{28,24},{1,5},{5... | collective-permute-start | bytes 3538952 | tf_op jit(solution)/shard_map/ppermute | solution.py:1344
  302.1 4.2 copy-start.16
  302.1 5.0 %copy-start.3 = (bf16[192,2,768]{2,1,0:T(2,128)(2,1)S(1)}, bf16[192,2,768]{2,1,0:T(2,128)(2,1)}, u32[]{:S(2)}) copy-start(bf16[192,2,768]{2,1,0:T(2,128)(2,1)} %param.18) | copy-start | bytes 1769476
  302.1 57.4 %all-to-all-start = ((bf16[8,256,384]{2,1,0:T(8,128)(2,1)}), bf16[8,256,384]{2,1,0:T(8,128)(2,1)S(1)}, u32[]{:S(2)}, u32[]{:S(2)}) async-start(bf16[8,256,384]{2,1,0:T(8,128)(2,1)} %bitcast.71), calls=%async_computation | async-start | bytes 3145728 | tf_op jit(solution)/shard_map/all_to_all | solution.py:1350
  333.1 25.1 %copy-start.20 = (f32[8,256]{1,0:T(8,128)S(1)}, f32[8,256]{1,0:T(8,128)}, u32[]{:S(2)}) copy-start(f32[8,256]{1,0:T(8,128)} %get-tuple-element.92) | copy-start | bytes 24580
  333.1 25.1 %copy-start.21 = (f32[8,256]{1,0:T(8,128)S(1)}, f32[8,256]{1,0:T(8,128)}, u32[]{:S(2)}) copy-start(f32[8,256]{1,0:T(8,128)} %get-tuple-element.93) | copy-start | bytes 24580
  333.1 25.7 %copy-start.15 = (f32[16,1,128]{2,1,0:T(1,128)S(1)}, f32[16,1,128]{2,1,0:T(1,128)}, u32[]{:S(2)}) copy-start(f32[16,1,128]{2,1,0:T(1,128)} %get-tuple-element.91.refs_4_) | copy-start | bytes 24580
  333.1 25.7 %copy-start.19 = (f32[16,1,128]{2,1,0:T(1,128)S(1)}, f32[16,1,128]{2,1,0:T(1,128)}, u32[]{:S(2)}) copy-start(f32[16,1,128]{2,1,0:T(1,128)} %get-tuple-element.90.refs_3_) | copy-start | bytes 24580
  333.2 26.3 %copy-start.22 = (f32[8,128]{1,0:T(8,128)S(1)}, f32[8,128]{1,0:T(8,128)}, u32[]{:S(2)}) copy-start(f32[8,128]{1,0:T(8,128)} %get-tuple-element.100) | copy-start | bytes 12292
  333.2 26.3 %copy-start.23 = (f32[8,128]{1,0:T(8,128)S(1)}, f32[8,128]{1,0:T(8,128)}, u32[]{:S(2)}) copy-start(f32[8,128]{1,0:T(8,128)} %get-tuple-element.101) | copy-start | bytes 12292
  333.2 26.3 %copy-start.17 = (f32[8,768]{1,0:T(8,128)S(1)}, f32[8,768]{1,0:T(8,128)}, u32[]{:S(2)}) copy-start(f32[8,768]{1,0:T(8,128)} %get-tuple-element.96) | copy-start | bytes 73732
  333.2 26.3 %copy-start.18 = (f32[8,768]{1,0:T(8,128)S(1)}, f32[8,768]{1,0:T(8,128)}, u32[]{:S(2)}) copy-start(f32[8,768]{1,0:T(8,128)} %get-tuple-element.97) | copy-start | bytes 73732
  360.7 34.4 %copy-start.13 = (f32[8,256]{1,0:T(8,128)S(1)}, f32[8,256]{1,0:T(8,128)}, u32[]{:S(2)}) copy-start(f32[8,256]{1,0:T(8,128)} %add.94.refs_8_) | copy-start | bytes 24580
  442.9 16.2 %copy-start.14 = (f32[8,768]{1,0:T(8,128)}, f32[8,768]{1,0:T(8,128)S(1)}, u32[]{:S(2)}) copy-start(f32[8,768]{1,0:T(8,128)S(1)} %fusion.9) | copy-start | bytes 73732
  454.0 4.2 copy-start.5
  454.0 40.9 %all-to-all-start.1 = ((bf16[8,256,384]{2,1,0:T(8,128)(2,1)}), bf16[8,256,384]{2,1,0:T(8,128)(2,1)S(1)}, u32[]{:S(2)}, u32[]{:S(2)}) async-start(bf16[8,256,384]{2,1,0:T(8,128)(2,1)} %bitcast.79), calls=%async_computation.1 | async-start | bytes 3145728 | tf_op jit(solution)/shard_map/all_to_all | solution.py:1375
  461.0 2.0 copy-start.6
  461.0 2.0 copy-start.7
  480.6 6.8 %copy-start.24 = (bf16[192]{0:T(256)(128)(2,1)S(1)}, bf16[192]{0:T(256)(128)(2,1)}, u32[]{:S(2)}) copy-start(bf16[192]{0:T(256)(128)(2,1)} %param.17) | copy-start | bytes 1156
  482.5 7.3 %copy-start.1 = (bf16[8,256,384]{2,1,0:T(8,128)(2,1)S(1)}, bf16[8,256,384]{2,1,0:T(8,128)(2,1)}, u32[]{:S(2)}) copy-start(bf16[8,256,384]{2,1,0:T(8,128)(2,1)} %copy-done) | copy-start | bytes 4718596
  (6 other events, 6.9 us)

commit v9 on v8

--- a/solution.py
+++ b/solution.py
@@ -1157,6 +1157,8 @@
     for part in range(parts):
         side(0, part, 0).start()
     held[2].start()
+    for k in order:
+        rows(1, k).start()
     total = size * block
     lane = lax.broadcasted_iota(jnp.int32, (T, T), 1).astype(F32)
 
@@ -1188,8 +1190,6 @@
 
     for k in order:
         rows(0, k).wait_recv()
-    for k in order:
-        rows(1, k).start()
     arrange(0)
     for k in order:
         rows(1, k).wait_recv()

time: 508 us -> 521 us (1.026)
  Pallas kernels: 439 us -> 454 us
    pallas_call x1, Pallas kernels: 137 us -> 152 us  [run_entry(): pl.pallas_call(functools.partial(entry_kernel, PARTS), in_specs=[pl.Block...]
where the time goes in v9:
time: 521 us; the launch traced here: 512 us
  Pallas kernels  454 us (87%)
  other arithmetic  21.4 us (4%)
  local copies, waits for them, and re-layouts  19.9 us (4%)
  starting transfers between devices  11.6 us (2%)
    pallas_call x1, Pallas kernels, run_entry(): pl.pallas_call(functools.partial(entry_kernel, PARTS), in_specs=[pl.Block...  152 us
    pallas_call x2, Pallas kernels, run_backward(): pl.pallas_call(functools.partial(backward_kernel, heads, len(before) + le...  48.6 us
    pallas_call x2, Pallas kernels, run_pieces(): pl.pallas_call(functools.partial(pieces_kernel, len(values), many, tuple(...  47.2 us
    pallas_call x1, Pallas kernels, run_last(): pl.pallas_call(functools.partial(last_kernel, tuple(moves)), in_specs=[an...  45.7 us
    pallas_call x2, Pallas kernels, run_grads(): pl.pallas_call(functools.partial(grads_kernel, count, parts, len(after),...  42 us
    pallas_call x1, Pallas kernels, run_forward(): pl.pallas_call(functools.partial(forward_kernel, heads, slots * chunks),...  35.2 us
    pallas_call x1, Pallas kernels, run_gate(): pl.pallas_call(functools.partial(gate_kernel, float(all_width), moves), g...  26.4 us
    pallas_call x1, Pallas kernels, run_project(): pl.pallas_call(functools.partial(project_kernel, heads, rows // step), gr...  22.3 us
  transfers between devices with their start and end apart: 5, of which 3 were waited for; matrix products, arithmetic and copies ran while one was open for 5% of the time, Pallas kernels for 21%

profile of v9, /device:TPU:0, one launch (start us, length us, event | category | flops | bytes accessed | tf_op | source)
XLA Modules:
  0.0 512.0 jit_solution(2474521108189391248)
XLA Ops:
  0.7 2.8 reshape_reshape.6.zx_ref
  8.4 152.1 %entry.1 = (bf16[8,256,1536]{2,1,0:T(8,128)(2,1)}, bf16[8,256,1536]{2,1,0:T(8,128)(2,1)}, bf16[8,4,48,1920]{3,2,1,0:T(8,128)(2,1)}) custom-call(s32[16,1,128]{2,1,0:T(1,128)} %bitcast.88, bf16[8,256,384]{2,1,0:T(8,128)(2,1)} %bitcast.72, bf16[8,256,384]{2,1,0:T(8,128)(2,1)} %bitcast.73, bf16[4,48,1536]{2,1,0:T(8,128)(2,1)} %reshape_reshape.6.zx_ref, ...), custom_call_target="tpu_custom_call" | custom-call | tf_op jit(solution)/shard_map/entry/pallas_call | solution.py:1273
  160.5 22.3 %project.1 = (bf16[2048,1536]{1,0:T(8,128)(2,1)}, f32[16,1,128]{2,1,0:T(1,128)}, bf16[2048,1536]{1,0:T(8,128)(2,1)}, f32[2048,384]{1,0:T(8,128)}, f32[8,1536]{1,0:T(8,128)}, /*index=5*/bf16[8,4,48,768]{3,2,1,0:T(8,128)(2,1)}) custom-call(bf16[2048,1536]{1,0:T(8,128)(2,1)} %bitcast.70, bf16[1536,1920]{1,0:T(8,128)(2,1)} %bitcast.63, bf16[4,48,768]{2,1,0:T(8,128)(2,1)} %bitcast.82), custom_call_target="tpu_custom_call" | custom-call | flops 1000 | bytes 1000 | tf_op jit(solution)/shard_map/project/pallas_call | solution.py:665
  182.8 35.2 %scan_forward.1 = (bf16[2048,768]{1,0:T(8,128)(2,1)}, f32[16,1,128]{2,1,0:T(1,128)}, bf16[2048,768]{1,0:T(8,128)(2,1)}, f32[2048,256]{1,0:T(8,128)}, bf16[16,128...) custom-call(bf16[2048,1536]{1,0:T(8,128)(2,1)} %get-tuple-element.65.x_ref.z_ref, ...), custom_call_target="tpu_custom_call", output_to_operand_aliasing={{5}: (7, {})} | custom-call | flops 3774873600 | bytes 12582912 | tf_op jit(solution)/shard_map/scan_forward/pallas_call | solution.py:613
  218.0 26.4 %gate.1 = (bf16[2048,768]{1,0:T(8,128)(2,1)}, bf16[2048,768]{1,0:T(8,128)(2,1)}, bf16[2048,768]{1,0:T(8,128)(2,1)}, f32[8,768]{1,0:T(8,128)}, f32[16,1,128]{2,1,0:T(1,128)}) custom-call(bf16[2048,1536]{1,0:T(8,128)(2,1)} %bitcast.61, bf16[1536,768]{1,0:T(8,128)(2,1)} %bitcast.65, bf16[2048,768]{1,0:T(8,128)(2,1)} %get-tuple-element.69.y_ref, ...), custom_call_target="tpu_custom_call" | custom-call | flops 1000 | bytes 1000 | tf_op jit(solution)/shard_map/gate/pallas_call | solution.py:734
  244.3 12.5 %branch_pieces.1 = (bf16[2048,384]{1,0:T(8,128)(2,1)}, bf16[2048,384]{1,0:T(8,128)(2,1)}) custom-call(bf16[2048,768]{1,0:T(8,128)(2,1)} %get-tuple-element.71.refs_0_.refs_2_, bf16[1536,768]{1,0:T(8,128)(2,1)} %bitcast.66), custom_call_target="tpu_custom_call" | custom-call | flops 1000 | bytes 1000 | tf_op jit(solution)/shard_map/branch_pieces/pallas_call | solution.py:886
  257.4 16.6 %gate_grads.1 = (bf16[1536,768]{1,0:T(8,128)(2,1)}, bf16[1536,768]{1,0:T(8,128)(2,1)}) custom-call(bf16[2048,1536]{1,0:T(8,128)(2,1)} %bitcast.62, bf16[2048,1536]{1,0:T(8,128)(2,1)} %get-tuple-element.78.refs_1_.refs_0_, bf16[2048,768]{1,0:T(8,128)(2,1)} %get-tuple-element.71.refs_0_.refs_2_, bf16[2048,768]{1,0:T(8,128)(2,1)} %get-tuple-element.79.refs_3_.refs_0_, ...), custom_call_target="tpu_custom_call" | custom-call | flops 1000 | bytes 1000 | tf_op jit(solution)/shard_map/gate_grads/pallas_call | solution.py:967
  277.3 2.0 collective-permute-start.1
  279.3 24.3 %scan_backward.2 = (bf16[2048,768]{1,0:T(8,128)(2,1)}, bf16[2048,384]{1,0:T(8,128)(2,1)}, f32[16,1,128]{2,1,0:T(1,128)}, f32[8,768]{1,0:T(8,128)}, f32[8,256]{1,0:T(8,128)}, /*index=5*/f32[8,128]{1,0:T(8,128)}) custom-call(bf16[2048,768]{1,0:T(8,128)(2,1)} %get-tuple-element.74.dy_ref, bf16[2048,1536]{1,0:T(8,128)(2,1)} %get-tuple-element.65.x_ref.z_ref, ...), custom_call_target="tpu_custom_call" | custom-call | flops 1000 | bytes 1000 | tf_op jit(solution)/shard_map/scan_backward/pallas_call | solution.py:766
  303.7 2.0 collective-permute-done.1.refs_1_
  306.7 8.7 %home_out.1.refs_3_ = bf16[2048,384]{1,0:T(8,128)(2,1)} custom-call(s32[1]{0:T(128)} %bitcast.me_ref, s32[16,1,128]{2,1,0:T(1,128)} %bitcast.89, bf16[2048,384]{1,0:T(8,128)(2,1)} %get-tuple-element.72.a_ref, bf16[2048,384]{1,0:T(8,128)(2,1)} %collective-permute-done.b_ref, bf16[2048,768]{1,0:T(8,128)(2,1)} %get-tuple-element.82.refs_0_, ...), custom_call_target="tpu_custom_call" | custom-call | flops 3221225472 | bytes 7864320 | tf_op jit(solution)/shard_map/home_out/pallas_call | solution.py:707
  315.3 4.1 all-to-all-start
  322.0 24.3 %scan_backward.3 = (bf16[2048,768]{1,0:T(8,128)(2,1)}, bf16[2048,384]{1,0:T(8,128)(2,1)}, f32[16,1,128]{2,1,0:T(1,128)}, f32[8,768]{1,0:T(8,128)}, f32[8,256]{1,0:T(8,128)}, /*index=5*/f32[8,128]{1,0:T(8,128)}) custom-call(bf16[2048,768]{1,0:T(8,128)(2,1)} %get-tuple-element.74.dy_ref, ...), custom_call_target="tpu_custom_call", output_to_operand_aliasing={{0}: (9, {}), {1}: (10, {}), {2}: (11, {})} | custom-call | flops 1000 | bytes 1000 | tf_op jit(solution)/shard_map/scan_backward/pallas_call | solution.py:766
  346.4 25.4 %scan_grads.1 = (bf16[1536,768]{1,0:T(8,128)(2,1)}, bf16[1536,384]{1,0:T(8,128)(2,1)}, bf16[2,192,768]{2,1,0:T(8,128)(2,1)}, bf16[2,192,768]{2,1,0:T(8,128)(2,1)}) custom-call(bf16[2048,1536]{1,0:T(8,128)(2,1)} %get-tuple-element.78.refs_1_.refs_0_, bf16[2048,1536]{1,0:T(8,128)(2,1)} %get-tuple-element.78.refs_1_.refs_0_, ...), custom_call_target="tpu_custom_call" | custom-call | flops 1000 | bytes 1000 | tf_op jit(solution)/shard_map/scan_grads/pallas_call | solution.py:967
  374.3 34.7 %input_pieces.1 = (bf16[2048,384]{1,0:T(8,128)(2,1)}, bf16[2048,384]{1,0:T(8,128)(2,1)}, bf16[1,192,768]{2,1,0:T(8,128)(2,1)}, bf16[1,192,768]{2,1,0:T(8,128)(2,...) custom-call(bf16[2048,768]{1,0:T(8,128)(2,1)} %get-tuple-element.79.refs_3_.refs_0_, ...), custom_call_target="tpu_custom_call" | custom-call | flops 1000 | bytes 1000 | tf_op jit(solution)/shard_map/input_pieces/pallas_call | solution.py:886
  410.5 45.7 %last_exchange.1 = (bf16[2048,384]{1,0:T(8,128)(2,1)}, f32[7,8,768]{2,1,0:T(8,128)}, f32[192,384]{1,0:T(8,128)}, f32[192,768]{1,0:T(8,128)}) custom-call(bf16[2048,384]{1,0:T(8,128)(2,1)} %get-tuple-element.95.refs_0_, f32[8,768]{1,0:T(8,128)} %pad_maximum_fusion.2.refs_1_, bf16[4,2,192,384]{3,2,1,0:T(8,128)(2,1)} %bitcast.81, ...), custom_call_target="tpu_custom_call" | custom-call | tf_op jit(solution)/shard_map/last_exchange/pallas_call | solution.py:1047
  457.9 10.4 %home_back.1 = bf16[2048,384]{1,0:T(8,128)(2,1)} custom-call(s32[1]{0:T(128)} %bitcast.me_ref, s32[16,1,128]{2,1,0:T(1,128)} %bitcast.90, bf16[2048,384]{1,0:T(8,128)(2,1)} %get-tuple-element.94.a_ref, bf16[2048,384]{1,0:T(8,128)(2,1)} %get-tuple-element.104.b_ref, bf16[2048,1536]{1,0:T(8,128)(2,1)} %get-tuple-element.78.refs_1_.refs_0_, ...), custom_call_target="tpu_custom_call" | custom-call | flops 3221225472 | bytes 7864320 | tf_op jit(solution)/shard_map/home_back/pallas_call | solution.py:707
  468.3 4.3 all-to-all-start.1
  475.5 1.9 copy.41
  479.4 15.6 %exchange.1 = f32[3,192,384]{2,1,0:T(8,128)} custom-call(f32[192,384]{1,0:T(8,128)} %pad_maximum_fusion.1.refs_0_), custom_call_target="tpu_custom_call" | custom-call | tf_op jit(solution)/shard_map/exchange/pallas_call | solution.py:188
  495.0 2.0 reduce_sum.76
  502.4 1.9 add_bitcast_fusion
  504.3 3.0 add_convert_fusion
  508.7 3.0 fusion
  (107 shorter events, 29.5 us)
Async XLA Ops:
  256.8 48.8 %collective-permute-start = (bf16[2048,384]{1,0:T(8,128)(2,1)}, bf16[2048,384]{1,0:T(8,128)(2,1)}, u32[]{:S(2)}, u32[]{:S(2)}) collective-permute-start(bf16[2048,384]{1,0:T(8,128)(2,1)} %get-tuple-element.73.refs_4_), channel_id=1, source_target_pairs={{0,2},{1,3},{2,0},{3,1},{4,6},{5,7},{6,4},{7,5},{8,10},{9,11},{10,... | collective-permute-start | bytes 4718600 | tf_op jit(solution)/shard_map/ppermute | solution.py:1339
  274.0 2.1 copy-start.2
  275.5 3.8 copy-start.4
  275.5 28.1 %collective-permute-start.2 = (bf16[2,2,192,768]{3,2,1,0:T(8,128)(2,1)S(1)}, bf16[2,2,192,768]{3,2,1,0:T(8,128)(2,1)}, u32[]{:S(2)}, u32[]{:S(2)}) collective-permute-start(bf16[2,2,192,768]{3,2,1,0:T(8,128)(2,1)S(1)} %dynamic-slice_bitcast_fusion.refs_1_), channel_id=1, source_target_pairs={{0,8},{4,12},{8,0},{12,4},{16,24},{20,28},{24,16},{28,20},{1,9},{5... | collective-permute-start | bytes 3538952 | tf_op jit(solution)/shard_map/ppermute | solution.py:1344
  277.3 28.4 %collective-permute-start.1 = (bf16[4,192,768]{2,1,0:T(8,128)(2,1)}, bf16[4,192,768]{2,1,0:T(8,128)(2,1)S(1)}, u32[]{:S(2)}, u32[]{:S(2)}) collective-permute-start(bf16[4,192,768]{2,1,0:T(8,128)(2,1)} %dynamic-slice_bitcast_fusion.1.refs_0_), channel_id=1, source_target_pairs={{0,4},{4,0},{8,12},{12,8},{16,20},{20,16},{24,28},{28,24},{1,5},{5... | collective-permute-start | bytes 3538952 | tf_op jit(solution)/shard_map/ppermute | solution.py:1344
  315.3 4.2 copy-start.16
  315.3 5.0 copy-start.3
  315.3 57.8 %all-to-all-start = ((bf16[8,256,384]{2,1,0:T(8,128)(2,1)}), bf16[8,256,384]{2,1,0:T(8,128)(2,1)S(1)}, u32[]{:S(2)}, u32[]{:S(2)}) async-start(bf16[8,256,384]{2,1,0:T(8,128)(2,1)} %bitcast.71), calls=%async_computation | async-start | bytes 3145728 | tf_op jit(solution)/shard_map/all_to_all | solution.py:1350
  346.3 25.5 %copy-start.20 = (f32[8,256]{1,0:T(8,128)S(1)}, f32[8,256]{1,0:T(8,128)}, u32[]{:S(2)}) copy-start(f32[8,256]{1,0:T(8,128)} %get-tuple-element.92) | copy-start | bytes 24580
  346.3 25.5 %copy-start.21 = (f32[8,256]{1,0:T(8,128)S(1)}, f32[8,256]{1,0:T(8,128)}, u32[]{:S(2)}) copy-start(f32[8,256]{1,0:T(8,128)} %get-tuple-element.93) | copy-start | bytes 24580
  346.3 26.1 %copy-start.15 = (f32[16,1,128]{2,1,0:T(1,128)S(1)}, f32[16,1,128]{2,1,0:T(1,128)}, u32[]{:S(2)}) copy-start(f32[16,1,128]{2,1,0:T(1,128)} %get-tuple-element.91.refs_4_) | copy-start | bytes 24580
  346.3 26.1 %copy-start.19 = (f32[16,1,128]{2,1,0:T(1,128)S(1)}, f32[16,1,128]{2,1,0:T(1,128)}, u32[]{:S(2)}) copy-start(f32[16,1,128]{2,1,0:T(1,128)} %get-tuple-element.90.refs_3_) | copy-start | bytes 24580
  346.4 26.7 %copy-start.22 = (f32[8,128]{1,0:T(8,128)S(1)}, f32[8,128]{1,0:T(8,128)}, u32[]{:S(2)}) copy-start(f32[8,128]{1,0:T(8,128)} %get-tuple-element.100) | copy-start | bytes 12292
  346.4 26.7 %copy-start.23 = (f32[8,128]{1,0:T(8,128)S(1)}, f32[8,128]{1,0:T(8,128)}, u32[]{:S(2)}) copy-start(f32[8,128]{1,0:T(8,128)} %get-tuple-element.101) | copy-start | bytes 12292
  346.4 26.7 %copy-start.17 = (f32[8,768]{1,0:T(8,128)S(1)}, f32[8,768]{1,0:T(8,128)}, u32[]{:S(2)}) copy-start(f32[8,768]{1,0:T(8,128)} %get-tuple-element.96) | copy-start | bytes 73732
  346.4 26.7 %copy-start.18 = (f32[8,768]{1,0:T(8,128)S(1)}, f32[8,768]{1,0:T(8,128)}, u32[]{:S(2)}) copy-start(f32[8,768]{1,0:T(8,128)} %get-tuple-element.97) | copy-start | bytes 73732
  374.3 35.5 %copy-start.13 = (f32[8,256]{1,0:T(8,128)S(1)}, f32[8,256]{1,0:T(8,128)}, u32[]{:S(2)}) copy-start(f32[8,256]{1,0:T(8,128)} %add.94.refs_8_) | copy-start | bytes 24580
  457.2 16.4 %copy-start.14 = (f32[8,768]{1,0:T(8,128)}, f32[8,768]{1,0:T(8,128)S(1)}, u32[]{:S(2)}) copy-start(f32[8,768]{1,0:T(8,128)S(1)} %fusion.9) | copy-start | bytes 73732
  468.3 4.3 copy-start.5
  468.3 40.4 %all-to-all-start.1 = ((bf16[8,256,384]{2,1,0:T(8,128)(2,1)}), bf16[8,256,384]{2,1,0:T(8,128)(2,1)S(1)}, u32[]{:S(2)}, u32[]{:S(2)}) async-start(bf16[8,256,384]{2,1,0:T(8,128)(2,1)} %bitcast.79), calls=%async_computation.1 | async-start | bytes 3145728 | tf_op jit(solution)/shard_map/all_to_all | solution.py:1375
  475.4 2.0 copy-start.6
  475.4 2.0 copy-start.7
  495.0 6.8 %copy-start.24 = (bf16[192]{0:T(256)(128)(2,1)S(1)}, bf16[192]{0:T(256)(128)(2,1)}, u32[]{:S(2)}) copy-start(bf16[192]{0:T(256)(128)(2,1)} %param.17) | copy-start | bytes 1156
  497.0 7.3 %copy-start.1 = (bf16[8,256,384]{2,1,0:T(8,128)(2,1)S(1)}, bf16[8,256,384]{2,1,0:T(8,128)(2,1)}, u32[]{:S(2)}) copy-start(bf16[8,256,384]{2,1,0:T(8,128)(2,1)} %copy-done) | copy-start | bytes 4718596
  (6 other events, 6.9 us)
